TPU v7x, 32 devices: a whole 2x2x4 slice. The times are simulated.
32 devices in a mesh: dp: 4 (over y, x), seq: 8 (over z, core).
Axes of the slice: x: 2, y: 2, z: 4, core: 2. Of those that a mesh axis runs over, the one named last changes fastest.
Arguments:
- block_input: bfloat16 [2, 4, 1024, 576], P(None, 'dp', 'seq'), may hold values from -6 to 6
- out_grad: bfloat16 [2, 4, 1024, 576], P(None, 'dp', 'seq'), may hold values from -6 to 6
- doc_lengths: int32 [2, 4, 6], P(None, 'dp'), may hold values from 200 to 1000, as said below
- attention_weights: float32 [884736], P(('dp', 'seq'))
- feedforward_weights: float32 [2654208], P(('dp', 'seq'))
- norm_gains: float32 [2, 576], replicated, may hold values from 0.5 to 1.5
- attention_moment: float32 [884736], P(('dp', 'seq'))
- attention_square: float32 [884736], P(('dp', 'seq')), as said below
- feedforward_moment: float32 [2654208], P(('dp', 'seq'))
- feedforward_square: float32 [2654208], P(('dp', 'seq')), as said below
- gain_moment: float32 [2, 576], replicated, may hold values from -64 to 64
- gain_square: float32 [2, 576], replicated, may hold values from 212.992 to 3440.64
Outputs:
- block_output: bfloat16 [2, 4, 1024, 576], P(None, 'dp', 'seq')
- input_grad: float32 [2, 4, 1024, 576], P(None, 'dp', 'seq')
- new_attention: float32 [884736], P(('dp', 'seq'))
- new_attention_moment: float32 [884736], P(('dp', 'seq'))
- new_attention_square: float32 [884736], P(('dp', 'seq'))
- new_feedforward: float32 [2654208], P(('dp', 'seq'))
- new_feedforward_moment: float32 [2654208], P(('dp', 'seq'))
- new_feedforward_square: float32 [2654208], P(('dp', 'seq'))
- new_gains: float32 [2, 576], replicated
- new_gain_moment: float32 [2, 576], replicated
- new_gain_square: float32 [2, 576], replicated
Inputs may be any that keep to these rules, and one draw needn't show every extreme that they name: `doc_lengths`: documents lie end to end from each sequence's first token in the given order; those starting at or after 1024 are unused and the last used one is cut at 1024. The first or the second document of every sequence has exactly 1000 tokens. `attention_square`: positive. `feedforward_square`: positive.
All inputs are finite; a program needn't handle non-finite values.
Results may differ from a plain program's by a relative error of at most 0.014.
Values may be sent and summed in bfloat16 or wider, within the bound.
No kernel may reach another device: no remote copies, remote signals or barrier semaphores. Data moves between devices by JAX's collectives and lax.ppermute only.
A program may use at most 128 MiB of HBM per device.

v0:
```python
import jax
import jax.numpy as jnp
from jax import lax
from jax.experimental import pallas as pl
from jax.experimental.pallas import tpu as pltpu
from jax.sharding import PartitionSpec as P

D = 576
QUERY_HEADS = 9
KEY_VALUE_HEADS = 3
GROUP = QUERY_HEADS // KEY_VALUE_HEADS
HEAD_SIZE = 64
FF = 1536
DEVICE_TOKENS = 128
MICRO = 2
DOC_MAX = 1000
STEP = 10
QKV_WIDTH = 960
QUERY_WIDTH = QUERY_HEADS * HEAD_SIZE
KV_WIDTH = KEY_VALUE_HEADS * HEAD_SIZE
OUT_FAN = 14
LANES = 128
HALF = LANES // 2
BLOCKS = 32
VMEM_LIMIT = 52 * 2**20

NORM_EPSILON = 1e-05
THETA = 100000.0
BETA_ONE = 0.9
BETA_TWO = 0.95
ADAM_EPSILON = 1e-08
MATRIX_DECAY = 0.1
RATE_FACTOR = 1.5
GAIN_RATE = 0.2
SCALE = HEAD_SIZE ** (-0.5)
BF16 = jnp.bfloat16
F32 = jnp.float32


def is_power_of_two(count):
    return count & (count - 1) == 0


def exchange(value, axis, bit):
    count = lax.axis_size(axis)
    return lax.ppermute(value, axis, [(place, place ^ bit) for place in range(count)])


def gather_stages():
    seq, dp = lax.axis_size("seq"), lax.axis_size("dp")
    stages = []
    bit = seq // 2
    while bit > 1:
        stages.append(("seq", bit, bit))
        bit //= 2
    bit = dp // 2
    while bit >= 1:
        stages.append(("dp", bit, bit * seq))
        bit //= 2
    if seq > 1:
        stages.append(("seq", 1, 1))
    return stages


def block_order(stages):
    order = [0]
    for unused_axis, unused_bit, flat_bit in stages:
        order = order + [place ^ flat_bit for place in order]
    return order


def doubled(block, stages):
    for axis, bit, unused_flat in stages:
        block = jnp.concatenate([block, exchange(block, axis, bit)], 0)
    return block


def halved(blocks, stages):
    for axis, bit, unused_flat in reversed(stages):
        half = blocks.shape[0] // 2
        received = exchange(blocks[half:], axis, bit)
        blocks = (blocks[:half].astype(F32) + received.astype(F32)).astype(BF16)
    return blocks


def inverse_places(order, place):
    by_relative = [0] * len(order)
    for position, relative in enumerate(order):
        by_relative[relative] = position
    count = len(order)
    return jnp.array(by_relative, jnp.int32)[jnp.arange(count, dtype=jnp.int32) ^ place]


def unit_norm(inputs):
    inverse_rms = lax.rsqrt(jnp.mean(inputs * inputs, axis=-1, keepdims=True) + NORM_EPSILON)
    return (inputs * inverse_rms, inverse_rms)


def norm_backward(d_normed, unit_rows, inverse_rms, gain_row):
    scaled = d_normed * gain_row
    return inverse_rms * (
        scaled - unit_rows * jnp.mean(scaled * unit_rows, axis=-1, keepdims=True)
    )


def matmul(equation, left, right):
    return jnp.einsum(equation, left, right, preferred_element_type=F32)


def params():
    return pltpu.CompilerParams(vmem_limit_bytes=VMEM_LIMIT)


def vmem(count):
    return [pl.BlockSpec(memory_space=pltpu.VMEM)] * count


def smem():
    return pl.BlockSpec(memory_space=pltpu.SMEM)


def dot(left, right):
    return jnp.dot(left, right, preferred_element_type=F32)


def dot_nt(left, right):
    return lax.dot_general(left, right, (((1,), (1,)), ((), ())), preferred_element_type=F32)


def dot_tn(left, right):
    return lax.dot_general(left, right, (((0,), (0,)), ((), ())), preferred_element_type=F32)


def shift_half(low, high):
    lane = lax.broadcasted_iota(jnp.int32, low.shape, 1)
    return pltpu.roll(jnp.where(lane < HALF, low, high), HALF, 1)


def unflatten_odd(flat, base, pairs, whole, planes):
    step = 2 * whole + 1

    def piece(k):
        return flat[pl.ds(base + k, pairs, stride=step), :]

    for j in range(whole + 1):
        planes[j, pl.ds(0, pairs, stride=2), :] = piece(j)
        planes[j, pl.ds(1, pairs, stride=2), :] = shift_half(
            piece(min(whole + 1 + j, 2 * whole)), piece(whole + j)
        )


def flatten_odd(planes, pairs, whole, flat, base):
    step = 2 * whole + 1

    def even(j):
        return planes[j, pl.ds(0, pairs, stride=2), :]

    def odd(j):
        return planes[j, pl.ds(1, pairs, stride=2), :]

    for k in range(step):
        if k < whole:
            rows = even(k)
        elif k == whole:
            first = odd(0)
            lane = lax.broadcasted_iota(jnp.int32, first.shape, 1)
            rows = jnp.where(lane < HALF, even(whole), pltpu.roll(first, HALF, 1))
        else:
            rows = shift_half(odd(k - whole), odd(k - whole - 1))
        flat[pl.ds(base + k, pairs, stride=step), :] = rows


def load_blocks(places, blocks, flat):
    count, rows, unused = blocks.shape
    for index in range(count):
        flat[index * rows : (index + 1) * rows, :] = blocks[places[index]].astype(F32)


def store_blocks(order, flat, blocks):
    count, rows, unused = blocks.shape
    for index in range(count):
        start = pl.multiple_of(order[index] * rows, 8)
        blocks[index] = flat[pl.ds(start, rows), :].astype(BF16)


def planes_to_matrix(planes, whole, matrix):
    for j in range(whole):
        matrix[:, j * LANES : (j + 1) * LANES] = planes[j].astype(BF16)
    matrix[:, whole * LANES : whole * LANES + HALF] = planes[whole, :, :HALF].astype(BF16)


def rotated(rows, cosine, sine):
    half_width = HEAD_SIZE // 2
    first, second = rows[:half_width], rows[half_width:]
    return jnp.concatenate([first * cosine - second * sine, second * cosine + first * sine], 0)


def attention_forward_kernel(
    places,
    weight_blocks,
    window_inputs,
    cosines,
    sines,
    bias,
    gains,
    w_project,
    w_output,
    normed,
    queries,
    keys_across,
    keys,
    values,
    log_totals,
    mixed_across,
    residual,
    flat,
    planes_one,
    planes_two,
    w_across,
    values_across,
):
    load_blocks(places, weight_blocks, flat)
    unflatten_odd(flat, 0, D // 2, 7, planes_one)
    planes_to_matrix(planes_one, 7, w_project)
    for j in range(7):
        w_across[j * LANES : (j + 1) * LANES, :] = jnp.transpose(planes_one[j]).astype(BF16)
    w_across[7 * LANES :, :] = jnp.transpose(planes_one[7])[:HALF].astype(BF16)
    unflatten_odd(flat, D * QKV_WIDTH // LANES, QUERY_WIDTH // 2, 4, planes_two)
    planes_to_matrix(planes_two, 4, w_output)
    blocks = window_inputs.shape[0]
    gain = gains[0:1, :]
    for micro in range(MICRO):
        for block in range(blocks):
            rows = window_inputs[block, micro].astype(F32)
            inverse = lax.rsqrt(jnp.mean(rows * rows, axis=-1, keepdims=True) + NORM_EPSILON)
            normed[micro, block * DEVICE_TOKENS : (block + 1) * DEVICE_TOKENS, :] = (
                rows * inverse * gain
            ).astype(BF16)
        cosine, sine = cosines[micro], sines[micro]
        own_cosine, own_sine = cosine[:, :DEVICE_TOKENS], sine[:, :DEVICE_TOKENS]
        query = dot_nt(w_across[:QUERY_WIDTH, :], normed[micro, :DEVICE_TOKENS, :])
        for head in range(QUERY_HEADS):
            rows = slice(head * HEAD_SIZE, (head + 1) * HEAD_SIZE)
            queries[micro, rows, :] = rotated(query[rows], own_cosine, own_sine).astype(BF16)
        other = dot_nt(w_across[QUERY_WIDTH:, :], normed[micro])
        for head in range(KEY_VALUE_HEADS):
            rows = slice(head * HEAD_SIZE, (head + 1) * HEAD_SIZE)
            key = rotated(other[rows], cosine, sine)
            keys_across[micro, rows, :] = key.astype(BF16)
            keys[micro, head] = jnp.transpose(key).astype(BF16)
            value = other[KV_WIDTH + head * HEAD_SIZE : KV_WIDTH + (head + 1) * HEAD_SIZE]
            values_across[rows, :] = value.astype(BF16)
            values[micro, head] = jnp.transpose(value).astype(BF16)
        for head in range(QUERY_HEADS):
            group = head // GROUP
            rows = slice(head * HEAD_SIZE, (head + 1) * HEAD_SIZE)
            group_rows = slice(group * HEAD_SIZE, (group + 1) * HEAD_SIZE)
            scores = dot(keys[micro, group], queries[micro, rows, :] * SCALE) + bias[micro]
            top = jnp.max(scores, axis=0, keepdims=True)
            weights = jnp.exp(scores - top)
            total = jnp.sum(weights, axis=0, keepdims=True)
            low = (weights * (1.0 / total)).astype(BF16)
            mixed_across[micro, rows, :] = dot(values_across[group_rows, :], low)
            log_totals[micro, head : head + 1, :] = top + jnp.log(total)
        mixed = jnp.transpose(mixed_across[micro]).astype(BF16)
        residual[micro] = window_inputs[0, micro].astype(F32) + dot(mixed, w_output[...])


def attention_forward(places, weight_blocks, window_inputs, cosines, sines, bias, gains):
    window = window_inputs.shape[0] * DEVICE_TOKENS
    shape = jax.ShapeDtypeStruct
    rows = weight_blocks.shape[0] * weight_blocks.shape[1]
    return pl.pallas_call(
        attention_forward_kernel,
        out_shape=(
            shape((D, QKV_WIDTH), BF16),
            shape((QUERY_WIDTH, D), BF16),
            shape((MICRO, window, D), BF16),
            shape((MICRO, QUERY_WIDTH, DEVICE_TOKENS), BF16),
            shape((MICRO, KV_WIDTH, window), BF16),
            shape((MICRO, KEY_VALUE_HEADS, window, HEAD_SIZE), BF16),
            shape((MICRO, KEY_VALUE_HEADS, window, HEAD_SIZE), BF16),
            shape((MICRO, QUERY_HEADS, DEVICE_TOKENS), F32),
            shape((MICRO, QUERY_WIDTH, DEVICE_TOKENS), F32),
            shape((MICRO, DEVICE_TOKENS, D), F32),
        ),
        in_specs=[smem()] + vmem(6),
        out_specs=tuple(vmem(10)),
        scratch_shapes=[
            pltpu.VMEM((rows, LANES), F32),
            pltpu.VMEM((8, D, LANES), F32),
            pltpu.VMEM((5, QUERY_WIDTH, LANES), F32),
            pltpu.VMEM((QKV_WIDTH, D), BF16),
            pltpu.VMEM((KV_WIDTH, window), BF16),
        ],
        compiler_params=params(),
    )(places, weight_blocks, window_inputs, cosines, sines, bias, gains)


def feedforward_kernel(
    places,
    order,
    weight_blocks,
    residual,
    cotangent,
    gains,
    block_output,
    d_residual,
    grad_blocks,
    gain_grad,
    flat,
    planes,
    w_gate_up,
    w_down,
    hidden,
    d_gate_up,
):
    columns = 2 * FF // LANES
    load_blocks(places, weight_blocks, flat)
    for j in range(columns):
        w_gate_up[:, j * LANES : (j + 1) * LANES] = flat[
            pl.ds(j, D, stride=columns), :
        ].astype(BF16)
    unflatten_odd(flat, D * columns, FF // 2, 4, planes)
    planes_to_matrix(planes, 4, w_down)
    gain = gains[1:2, :]
    rows = residual[...]
    inverse = lax.rsqrt(jnp.mean(rows * rows, axis=-1, keepdims=True) + NORM_EPSILON)
    unit = rows * inverse
    normed = (unit * gain).astype(BF16)
    cotangent_low = cotangent[...]
    part = 256
    for start in range(0, FF, part):
        gate = dot(normed, w_gate_up[:, start : start + part])
        up = dot(normed, w_gate_up[:, FF + start : FF + start + part])
        d_hidden = dot_nt(cotangent_low, w_down[start : start + part, :])
        sigmoid = 1.0 / (1.0 + jnp.exp(-gate))
        activated = gate * sigmoid
        hidden[:, start : start + part] = (activated * up).astype(BF16)
        d_gate_up[:, start : start + part] = (
            d_hidden * up * sigmoid * (1.0 + gate * (1.0 - sigmoid))
        ).astype(BF16)
        d_gate_up[:, FF + start : FF + start + part] = (d_hidden * activated).astype(BF16)
    block_output[...] = (rows + dot(hidden[...], w_down[...])).astype(BF16)
    d_normed = dot_nt(d_gate_up[...], w_gate_up[...])
    scaled = d_normed * gain
    d_residual[...] = cotangent_low.astype(F32) + inverse * (
        scaled - unit * jnp.mean(scaled * unit, axis=-1, keepdims=True)
    )
    normed_across = jnp.transpose(unit * gain).astype(BF16)
    total = jnp.zeros((D, LANES), F32)
    for start in range(0, 2 * FF, part):
        grad = dot(normed_across, d_gate_up[:, start : start + part])
        for offset in range(0, part, LANES):
            piece = grad[:, offset : offset + LANES]
            place = start + offset
            total = total + piece * w_gate_up[:, place : place + LANES].astype(F32)
            flat[pl.ds(place // LANES, D, stride=columns), :] = piece
    gain_grad[...] = jnp.sum(total, axis=1, keepdims=True)
    for start in range(0, FF, part):
        grad = dot_tn(hidden[:, start : start + part], cotangent_low)
        for j in range(4):
            planes[j, start : start + part, :] = grad[:, j * LANES : (j + 1) * LANES]
        planes[4, start : start + part, :HALF] = grad[:, 4 * LANES :]
    flatten_odd(planes, FF // 2, 4, flat, D * columns)
    store_blocks(order, flat, grad_blocks)


def feedforward(places, order, weight_blocks, residual, cotangent, gains):
    shape = jax.ShapeDtypeStruct
    tokens = residual.shape[0]
    rows = weight_blocks.shape[0] * weight_blocks.shape[1]
    return pl.pallas_call(
        feedforward_kernel,
        out_shape=(
            shape((tokens, D), BF16),
            shape((tokens, D), F32),
            shape(weight_blocks.shape, BF16),
            shape((D, 1), F32),
        ),
        in_specs=[smem(), smem()] + vmem(4),
        out_specs=tuple(vmem(4)),
        scratch_shapes=[
            pltpu.VMEM((rows, LANES), F32),
            pltpu.VMEM((5, FF, LANES), F32),
            pltpu.VMEM((D, 2 * FF), BF16),
            pltpu.VMEM((FF, D), BF16),
            pltpu.VMEM((tokens, FF), BF16),
            pltpu.VMEM((tokens, 2 * FF), BF16),
        ],
        compiler_params=params(),
    )(places, order, weight_blocks, residual, cotangent, gains)


def attention_backward_kernel(
    order,
    w_project,
    w_output,
    normed,
    queries,
    keys_across,
    keys,
    values,
    log_totals,
    mixed_across,
    d_residual,
    cosines,
    sines,
    bias,
    grad_blocks,
    d_queries,
    d_window,
    gain_grad,
    flat,
    planes,
    d_window_across,
    grad_across,
    grad_output,
):
    blocks = d_window.shape[0]
    for micro in range(MICRO):
        cosine, sine = cosines[micro], sines[micro]
        own_cosine, own_sine = cosine[:, :DEVICE_TOKENS], sine[:, :DEVICE_TOKENS]
        d_branch = d_residual[micro].astype(BF16)
        d_mixed = dot_nt(w_output[...], d_branch).astype(BF16)
        mixed = mixed_across[micro]
        for group in range(KEY_VALUE_HEADS):
            group_rows = slice(group * HEAD_SIZE, (group + 1) * HEAD_SIZE)
            d_key = None
            for head in range(group * GROUP, (group + 1) * GROUP):
                rows = slice(head * HEAD_SIZE, (head + 1) * HEAD_SIZE)
                query = queries[micro, rows, :] * SCALE
                d_mixed_head = d_mixed[rows]
                delta = jnp.sum(d_mixed_head.astype(F32) * mixed[rows], axis=0, keepdims=True)
                scores = dot(keys[micro, group], query) + bias[micro]
                probability = jnp.exp(scores - log_totals[micro, head : head + 1, :])
                d_probs = dot(values[micro, group], d_mixed_head)
                d_scores = (probability * (d_probs - delta)).astype(BF16)
                d_query = dot(keys_across[micro, group_rows, :], d_scores) * SCALE
                d_queries[micro, rows, :] = rotated(d_query, own_cosine, -own_sine).astype(BF16)
                key_part = dot_nt(query, d_scores)
                value_part = dot_nt(d_mixed_head, probability.astype(BF16))
                d_key = key_part if d_key is None else d_key + key_part
                if head == group * GROUP:
                    d_value = value_part
                else:
                    d_value = d_value + value_part
            d_window_across[group_rows, :] = rotated(d_key, cosine, -sine).astype(BF16)
            value_rows = slice(
                KV_WIDTH + group * HEAD_SIZE, KV_WIDTH + (group + 1) * HEAD_SIZE
            )
            d_window_across[value_rows, :] = d_value.astype(BF16)
        for block in range(blocks):
            d_window[block, micro] = d_window_across[
                :, block * DEVICE_TOKENS : (block + 1) * DEVICE_TOKENS
            ]
        query_grad = dot(d_queries[micro], normed[micro, :DEVICE_TOKENS, :])
        window_grad = dot(d_window_across[...], normed[micro])
        output_grad = dot(mixed.astype(BF16), d_branch)
        if micro == 0:
            grad_across[:QUERY_WIDTH, :] = query_grad
            grad_across[QUERY_WIDTH:, :] = window_grad
            grad_output[...] = output_grad
        else:
            grad_across[:QUERY_WIDTH, :] += query_grad
            grad_across[QUERY_WIDTH:, :] += window_grad
            grad_output[...] += output_grad
    total = jnp.zeros((D, LANES), F32)
    for j in range(7):
        piece = jnp.transpose(grad_across[j * LANES : (j + 1) * LANES, :])
        planes[j] = piece
        total = total + piece * w_project[:, j * LANES : (j + 1) * LANES].astype(F32)
    last = jnp.transpose(grad_across[QKV_WIDTH - LANES :, :])
    last = pltpu.roll(last, HALF, 1)
    planes[7] = last
    last_sum = last[:, :HALF] * w_project[:, 7 * LANES :].astype(F32)
    gain_grad[...] = jnp.sum(total, axis=1, keepdims=True) + jnp.sum(
        last_sum, axis=1, keepdims=True
    )
    flatten_odd(planes, D // 2, 7, flat, 0)
    for j in range(4):
        planes[j] = grad_output[:, j * LANES : (j + 1) * LANES]
    planes[4, :, :HALF] = grad_output[:, 4 * LANES :]
    flatten_odd(planes, QUERY_WIDTH // 2, 4, flat, D * QKV_WIDTH // LANES)
    store_blocks(order, flat, grad_blocks)


def attention_backward(order, rows, *operands):
    shape = jax.ShapeDtypeStruct
    window = operands[2].shape[1]
    count = order.shape[0]
    return pl.pallas_call(
        attention_backward_kernel,
        out_shape=(
            shape((count, rows, LANES), BF16),
            shape((MICRO, QUERY_WIDTH, DEVICE_TOKENS), BF16),
            shape((window // DEVICE_TOKENS, MICRO, 2 * KV_WIDTH, DEVICE_TOKENS), BF16),
            shape((D, 1), F32),
        ),
        in_specs=[smem()] + vmem(len(operands)),
        out_specs=tuple(vmem(4)),
        scratch_shapes=[
            pltpu.VMEM((count * rows, LANES), F32),
            pltpu.VMEM((8, D, LANES), F32),
            pltpu.VMEM((2 * KV_WIDTH, window), BF16),
            pltpu.VMEM((QKV_WIDTH, D), F32),
            pltpu.VMEM((QUERY_WIDTH, D), F32),
        ],
        compiler_params=params(),
    )(order, *operands)


def adam_update(weights, moment, square, grad, rate, decay):
    new_moment = BETA_ONE * moment + (1.0 - BETA_ONE) * grad
    new_square = BETA_TWO * square + (1.0 - BETA_TWO) * grad * grad
    mean_hat = new_moment / (1.0 - BETA_ONE**STEP)
    square_hat = new_square / (1.0 - BETA_TWO**STEP)
    new_weights = weights - rate * (
        mean_hat / (jnp.sqrt(square_hat) + ADAM_EPSILON) + decay * weights
    )
    return (new_weights, new_moment, new_square)


def first_of(lengths, index):
    starts = jnp.cumsum(lengths, axis=-1) - lengths
    return jnp.max(
        jnp.where(starts[:, None, :] <= index[None, :, None], starts[:, None, :], 0), axis=-1
    )


def on_device(
    block_input,
    out_grad,
    doc_lengths,
    attention_weights,
    feedforward_weights,
    norm_gains,
    attention_moment,
    attention_square,
    feedforward_moment,
    feedforward_square,
    gain_moment,
    gain_square,
):
    both = ("dp", "seq")
    seq_count = lax.axis_size("seq")
    owner_count = lax.axis_size(both)
    seq_place = lax.axis_index("seq")
    owner_place = lax.axis_index(both)
    attention_length = attention_weights.shape[0]
    feedforward_length = feedforward_weights.shape[0]
    reach = min((DOC_MAX + DEVICE_TOKENS - 2) // DEVICE_TOKENS, seq_count - 1)
    paired = is_power_of_two(seq_count) and reach == seq_count - 1
    butterfly = is_power_of_two(owner_count) and attention_length % (8 * LANES) == 0
    stages = gather_stages()
    order = block_order(stages)
    seq_stages = [stage for stage in stages if stage[0] == "seq"]

    attention_low = attention_weights.astype(BF16)
    feedforward_low = feedforward_weights.astype(BF16)
    own_inputs = block_input[:, 0]
    straight = jnp.arange(BLOCKS, dtype=jnp.int32)
    if butterfly:
        attention_blocks = doubled(
            attention_low.reshape(1, attention_length // LANES, LANES), stages
        )
        attention_places = inverse_places(order, owner_place)
        attention_order = jnp.array(order, jnp.int32) ^ owner_place
    else:
        attention_blocks = lax.all_gather(attention_low, both, axis=0, tiled=True)
        attention_blocks = attention_blocks.reshape(BLOCKS, -1, LANES)
        attention_places = attention_order = straight
    if paired:
        window_inputs = doubled(own_inputs[None], seq_stages)
        window_blocks = seq_place ^ jnp.array(block_order(seq_stages), jnp.int32)
    else:
        window_inputs = jnp.stack(
            [own_inputs]
            + [
                lax.ppermute(
                    own_inputs, "seq", [(p, p + step) for p in range(seq_count - step)]
                )
                for step in range(1, reach + 1)
            ],
            0,
        )
        window_blocks = seq_place - jnp.arange(reach + 1, dtype=jnp.int32)
    tiled_rows = feedforward_length % (8 * LANES) == 0
    if tiled_rows:
        feedforward_low = feedforward_low.reshape(-1, LANES)
    feedforward_blocks = lax.all_gather(feedforward_low, both, axis=0, tiled=True)
    feedforward_blocks = feedforward_blocks.reshape(BLOCKS, -1, LANES)

    token = jnp.arange(DEVICE_TOKENS, dtype=jnp.int32)
    query_index = seq_place * DEVICE_TOKENS + token
    key_index = (window_blocks[:, None] * DEVICE_TOKENS + token[None, :]).reshape(-1)
    lengths = doc_lengths[:, 0]
    first_query = first_of(lengths, query_index)
    first_key = first_of(lengths, key_index)
    half_width = HEAD_SIZE // 2
    inverse = THETA ** (-(jnp.arange(half_width, dtype=F32) * 2.0) / HEAD_SIZE)
    position = (key_index[None] - first_key).astype(F32)
    angles = position[:, None, :] * inverse[None, :, None]
    cosines, sines = jnp.cos(angles), jnp.sin(angles)
    allowed = (key_index[None, :, None] >= first_query[:, None, :]) & (
        key_index[None, :, None] <= query_index[None, None, :]
    )
    bias = jnp.where(allowed, 0.0, -jnp.inf).astype(F32)

    (
        w_project,
        w_output,
        normed_one,
        queries,
        keys_across,
        keys,
        values,
        log_totals,
        mixed_across,
        residual,
    ) = attention_forward(
        attention_places, attention_blocks, window_inputs, cosines, sines, bias, norm_gains
    )
    block_output, d_residual, feedforward_grads, gain_two = feedforward(
        straight,
        straight,
        feedforward_blocks,
        residual.reshape(-1, D),
        out_grad[:, 0].reshape(-1, D),
        norm_gains,
    )
    block_output = block_output.reshape(MICRO, DEVICE_TOKENS, D)
    d_residual = d_residual.reshape(MICRO, DEVICE_TOKENS, D)
    feedforward_grads = feedforward_grads.reshape(-1, LANES)
    if not tiled_rows:
        feedforward_grads = feedforward_grads.reshape(-1)
    feedforward_owned = lax.psum_scatter(
        feedforward_grads, both, scatter_dimension=0, tiled=True
    ).reshape(-1)
    attention_grads, d_queries, d_window, gain_one = attention_backward(
        attention_order,
        D * (QKV_WIDTH + QUERY_WIDTH) // (LANES * BLOCKS),
        w_project,
        w_output,
        normed_one,
        queries,
        keys_across,
        keys,
        values,
        log_totals,
        mixed_across,
        d_residual,
        cosines,
        sines,
        bias,
    )
    if butterfly:
        attention_owned = halved(attention_grads, stages).reshape(-1)
    else:
        attention_owned = lax.psum_scatter(
            attention_grads.reshape(-1), both, scatter_dimension=0, tiled=True
        )
    if paired:
        d_own = halved(d_window, seq_stages)[0]
    else:
        d_own = d_window[0].astype(F32)
        for step in range(1, reach + 1):
            d_own = d_own + lax.ppermute(
                d_window[step], "seq", [(p, p - step) for p in range(step, seq_count)]
            ).astype(F32)
        d_own = d_own.astype(BF16)
    d_normed_one = matmul("met,de->mtd", jnp.concatenate([d_queries, d_own], 1), w_project)
    unit_one, inverse_one = unit_norm(own_inputs.astype(F32))
    input_grad = d_residual + norm_backward(d_normed_one, unit_one, inverse_one, norm_gains[0])

    gains_total = jnp.stack([gain_one[:, 0], gain_two[:, 0]], 0) / norm_gains
    if butterfly:
        for axis, bit, unused_flat in stages:
            gains_total = gains_total + exchange(gains_total, axis, bit)
    else:
        gains_total = lax.psum(gains_total, both)

    attention_place = owner_place * attention_length + jnp.arange(attention_length, dtype=jnp.int32)
    attention_rate = jnp.where(
        attention_place < D * QKV_WIDTH, RATE_FACTOR * D ** (-0.5), RATE_FACTOR * OUT_FAN ** (-0.5)
    )
    feedforward_place = owner_place * feedforward_length + jnp.arange(
        feedforward_length, dtype=jnp.int32
    )
    feedforward_rate = jnp.where(
        feedforward_place < 2 * D * FF, RATE_FACTOR * D ** (-0.5), RATE_FACTOR * FF ** (-0.5)
    )
    new_attention = adam_update(
        attention_weights,
        attention_moment,
        attention_square,
        attention_owned.astype(F32),
        attention_rate,
        MATRIX_DECAY,
    )
    new_feedforward = adam_update(
        feedforward_weights,
        feedforward_moment,
        feedforward_square,
        feedforward_owned.astype(F32),
        feedforward_rate,
        MATRIX_DECAY,
    )
    new_gains = adam_update(norm_gains, gain_moment, gain_square, gains_total, GAIN_RATE, 0.0)
    return (
        block_output[:, None],
        input_grad[:, None],
        *new_attention,
        *new_feedforward,
        *new_gains,
    )


def solution(mesh):
    tokens = P(None, "dp", "seq", None)
    flat = P(("dp", "seq"))
    return jax.shard_map(
        on_device,
        mesh=mesh,
        in_specs=(
            tokens,
            tokens,
            P(None, "dp", None),
            flat,
            flat,
            P(),
            flat,
            flat,
            flat,
            flat,
            P(),
            P(),
        ),
        out_specs=(tokens, tokens, flat, flat, flat, flat, flat, flat, P(), P(), P()),
        check_vma=False,
    )
```

profile of v0, /device:TPU:0, one launch (start us, length us, event | category | flops | bytes accessed | tf_op | source)
XLA Modules:
  0.0 237.7 jit_solution(10335791812168213056)
XLA Ops:
  7.2 1.7 convert_bitcast_fusion
  9.0 1.5 constant_dynamic-update-slice_fusion.4
  10.5 4.0 %collective-permute-start = (bf16[1,216,128]{2,1,0:T(8,128)(2,1)S(1)}, bf16[1,216,128]{2,1,0:T(8,128)(2,1)S(1)}, u32[]{:S(2)}, u32[]{:S(2)}) collective-permute-start(bf16[1,216,128]{2,1,0:T(8,128)(2,1)S(1)} %get-tuple-element.101), channel_id=1, source_target_pairs={{0,4},{1,5},{2,6},{3,7},{4,0},{5,1},{6,2},{7,3},{8,12},{9,13},{10,... | collective-permute-start | bytes 165896 | tf_op jit(solution)/shard_map/ppermute | solution.py:46
  14.5 1.2 copy.49
  15.8 1.0 reduce_window_sum.12
  16.8 0.7 sub.30
  17.6 0.7 xor_multiply_fusion
  18.4 0.6 subtract_convert_fusion
  19.3 7.4 %collective-permute-start.1 = (bf16[2,216,128]{2,1,0:T(8,128)(2,1)S(1)}, bf16[2,216,128]{2,1,0:T(8,128)(2,1)S(1)}, u32[]{:S(2)}, u32[]{:S(2)}) collective-permute-start(bf16[2,216,128]{2,1,0:T(8,128)(2,1)S(1)} %pad_maximum_fusion.5), channel_id=1, source_target_pairs={{0,2},{1,3},{2,0},{3,1},{4,6},{5,7},{6,4},{7,5},{8,10},{9,11},{10,... | collective-permute-start | bytes 331784 | tf_op jit(solution)/shard_map/ppermute | solution.py:46
  26.7 0.6 pad_clamp_fusion
  27.3 9.5 %collective-permute-done.1 = bf16[2,216,128]{2,1,0:T(8,128)(2,1)S(1)} collective-permute-done((bf16[2,216,128]{2,1,0:T(8,128)(2,1)S(1)}, bf16[2,216,128]{2,1,0:T(8,128)(2,1)S(1)}, u32[]{:S(2)}, u32[]{:S(2)}) %collective-permute-start.1) | collective-permute-done | bytes 110624 | tf_op jit(solution)/shard_map/ppermute | solution.py:46
  36.8 0.7 pad_maximum_fusion.4
  37.6 1.1 copy.50
  38.7 5.0 %collective-permute-done.2 = bf16[4,216,128]{2,1,0:T(8,128)(2,1)} collective-permute-done((bf16[4,216,128]{2,1,0:T(8,128)(2,1)}, bf16[4,216,128]{2,1,0:T(8,128)(2,1)}, u32[]{:S(2)}, u32[]{:S(2)}) %collective-permute-start.2) | collective-permute-done | bytes 221216 | tf_op jit(solution)/shard_map/ppermute | solution.py:46
  43.8 1.8 pad_maximum_fusion.3
  45.5 1.4 constant_dynamic-update-slice_fusion.3
  47.0 0.7 constant_dynamic-update-slice_fusion.2
  47.6 0.9 copy.52
  48.5 1.7 constant_dynamic-update-slice_fusion.1
  50.2 8.3 %collective-permute-done.6 = bf16[2,2,128,576]{2,3,1,0:T(8,128)(2,1)S(1)} collective-permute-done((bf16[2,2,128,576]{2,3,1,0:T(8,128)(2,1)}, bf16[2,2,128,576]{2,3,1,0:T(8,128)(2,1)S(1)}, u32[]{:S(2)}, u32[]{:S(2)}) %collective-permute-start.6) | collective-permute-done | bytes 589856 | tf_op jit(solution)/shard_map/ppermute | solution.py:46
  58.6 2.3 pad_maximum_fusion.1
  60.9 1.9 constant_dynamic-update-slice_fusion
  63.3 0.8 copy-done.5
  64.1 1.2 copy.57
  65.3 0.8 gather_fusion
  66.4 1.0 multiply_sine_fusion
  67.4 1.2 and_select_fusion.bias
  68.7 1.4 copy.53
  70.1 2.2 constant_dynamic-update-slice_fusion.5.weight_blocks
  72.2 2.4 %copy.54 = bf16[4,2,128,576]{3,2,1,0:T(8,128)(2,1)} copy(bf16[4,2,128,576]{2,3,1,0:T(8,128)(2,1)} %collective-permute-done.7) | data formatting | bytes 2359296 | tf_op jit(solution)/shard_map/ppermute | solution.py:46
  74.6 3.0 %pad_maximum_fusion.window_inputs = bf16[8,2,128,576]{3,2,1,0:T(8,128)(2,1)} fusion(bf16[4,2,128,576]{3,2,1,0:T(8,128)(2,1)} %copy.54, bf16[2,2,128,576]{3,2,1,0:T(8,128)(2,1)S(1)} %copy.53, bf16[1,2,128,576]{3,2,1,0:T(8,128)(2,1)S(1)} %collective-permute-done.5, bf16[1,2,128,576]{3,2,1,0:T(8,128)(2,1)S(1)} %bitcast.53), kind=kLoop, calls=%fused_computation.1 | loop fusion | flops 3538944 | bytes 4718592 | tf_op jit(solution)/shard_map/concatenate | solution.py:74
  77.6 18.8 %shard_map.230 = (bf16[576,960]{1,0:T(8,128)(2,1)}, bf16[576,576]{1,0:T(8,128)(2,1)}, bf16[2,1024,576]{2,1,0:T(8,128)(2,1)}, bf16[2,576,128]{2,1,0:T(8,128)(2,1)...) custom-call(s32[32]{0:T(128)S(1)} %gather_fusion, ...), custom_call_target="tpu_custom_call" | custom-call | tf_op jit(solution)/shard_map/pallas_call | solution.py:273
  96.4 14.7 %shard_map.231 = (bf16[256,576]{1,0:T(8,128)(2,1)S(1)}, f32[256,576]{1,0:T(8,128)S(1)}, bf16[32,648,128]{2,1,0:T(8,128)(2,1)}, f32[576,1]{1,0:T(8,128)S(1)}) custom-call(s32[32]{0:T(128)S(1)} %iota.32.places.order, s32[32]{0:T(128)S(1)} %iota.32.places.order, bf16[32,648,128]{2,1,0:T(8,128)(2,1)} %bitcast.54, f32[256,576]{1,0:T(8,128)} %bitcast.56, ...), custom_call_target="tpu_custom_call" | custom-call | tf_op jit(solution)/shard_map/pallas_call | solution.py:373
  111.1 0.8 copy-done
  112.0 0.6 copy-done.18
  112.6 19.9 %shard_map.232 = (bf16[32,216,128]{2,1,0:T(8,128)(2,1)}, bf16[2,576,128]{2,1,0:T(8,128)(2,1)S(1)}, bf16[8,2,384,128]{3,2,1,0:T(8,128)(2,1)}, f32[576,1]{1,0:T(8,128)S(1)}) custom-call(s32[32]{0:T(128)S(1)} %broadcast_xor_fusion.order, bf16[576,960]{1,0:T(8,128)(2,1)} %get-tuple-element.32.w_project, bf16[576,576]{1,0:T(8,128)(2,1)} %get-tuple-element.33.w_output, ...), custom_call_target="tpu_custom_call" | custom-call | tf_op jit(solution)/shard_map/pallas_call | solution.py:492
  132.8 1.2 slice.52
  134.1 0.5 collective-permute-start.8
  134.6 2.0 collective-permute-start.16
  136.6 2.2 slice.59
  139.2 1.5 collective-permute-start.17
  140.9 2.1 collective-permute-done.17
  142.9 1.5 collective-permute-start.18
  144.5 2.1 collective-permute-done.18
  146.5 1.7 collective-permute-start.19
  148.3 0.9 copy.60
  149.2 1.0 collective-permute-done.19
  150.2 1.6 add_convert_fusion.1
  151.8 1.5 collective-permute-start.9
  153.3 1.5 add_convert_fusion
  154.8 1.7 collective-permute-start.12
  156.5 0.6 multiply_subtract_fusion.2
  157.1 11.0 %collective-permute-done.9 = bf16[2,2,384,128]{3,2,1,0:T(8,128)(2,1)S(1)} collective-permute-done((bf16[2,2,384,128]{3,2,1,0:T(8,128)(2,1)S(1)}, bf16[2,2,384,128]{3,2,1,0:T(8,128)(2,1)S(1)}, u32[]{:S(2)}, u32[]{:S(2)}) %collective-permute-start.9) | collective-permute-done | bytes 393248 | tf_op jit(solution)/shard_map/ppermute | solution.py:46
  168.3 1.3 collective-permute-start.10
  169.6 5.8 %collective-permute-done.12 = bf16[8,216,128]{2,1,0:T(8,128)(2,1)S(1)} collective-permute-done((bf16[8,216,128]{2,1,0:T(8,128)(2,1)S(1)}, bf16[8,216,128]{2,1,0:T(8,128)(2,1)S(1)}, u32[]{:S(2)}, u32[]{:S(2)}) %collective-permute-start.12) | collective-permute-done | bytes 442400 | tf_op jit(solution)/shard_map/ppermute | solution.py:46
  175.5 1.4 collective-permute-start.13
  176.9 10.9 %collective-permute-done.10 = bf16[1,2,384,128]{3,2,1,0:T(8,128)(2,1)S(1)} collective-permute-done((bf16[1,2,384,128]{3,2,1,0:T(8,128)(2,1)S(1)}, bf16[1,2,384,128]{3,2,1,0:T(8,128)(2,1)S(1)}, u32[]{:S(2)}, u32[]{:S(2)}) %collective-permute-start.10) | collective-permute-done | bytes 196640 | tf_op jit(solution)/shard_map/ppermute | solution.py:46
  187.9 0.7 fusion.3
  188.8 4.7 %collective-permute-done.14 = bf16[2,216,128]{2,1,0:T(8,128)(2,1)S(1)} collective-permute-done((bf16[2,216,128]{2,1,0:T(8,128)(2,1)S(1)}, bf16[2,216,128]{2,1,0:T(8,128)(2,1)S(1)}, u32[]{:S(2)}, u32[]{:S(2)}) %collective-permute-start.14) | collective-permute-done | bytes 110624 | tf_op jit(solution)/shard_map/ppermute | solution.py:46
  194.0 1.1 copy.61
  195.0 6.1 %collective-permute-done.15 = bf16[1,216,128]{2,1,0:T(8,128)(2,1)S(1)} collective-permute-done((bf16[1,216,128]{2,1,0:T(8,128)(2,1)S(1)}, bf16[1,216,128]{2,1,0:T(8,128)(2,1)S(1)}, u32[]{:S(2)}, u32[]{:S(2)}) %collective-permute-start.15) | collective-permute-done | bytes 55328 | tf_op jit(solution)/shard_map/ppermute | solution.py:46
  201.1 0.8 multiply_subtract_fusion.1
  201.9 26.4 %reduce-scatter.4.cloned.1.call-done = bf16[648,128]{1,0:T(8,128)(2,1)} async-done(((bf16[20736,128]{1,0:T(8,128)(2,1)}), bf16[648,128]{1,0:T(8,128)(2,1)}) %reduce-scatter.4.cloned.1.call-update) | async-done | bytes 165904
  228.3 2.1 multiply_subtract_fusion
  (99 shorter events, 3.6 us)
Async XLA Ops:
  7.2 89.2 %all-gather.2.cloned.1.call-start = ((), (), s32[]{:S(2)}) async-start(), calls=%async_computation.1 | async-start | bytes 5474304 | tf_op jit(solution)/shard_map/all_gather | solution.py:591
  8.9 219.4 %reduce-scatter.4.cloned.1.call-start = ((), (), s32[]{:S(2)}) async-start(), calls=%async_computation.2 | async-start | bytes 5474304
  10.5 8.8 %collective-permute-start = (bf16[1,216,128]{2,1,0:T(8,128)(2,1)S(1)}, bf16[1,216,128]{2,1,0:T(8,128)(2,1)S(1)}, u32[]{:S(2)}, u32[]{:S(2)}) collective-permute-start(bf16[1,216,128]{2,1,0:T(8,128)(2,1)S(1)} %get-tuple-element.101), channel_id=1, source_target_pairs={{0,4},{1,5},{2,6},{3,7},{4,0},{5,1},{6,2},{7,3},{8,12},{9,13},{10,... | collective-permute-start | bytes 165896 | tf_op jit(solution)/shard_map/ppermute | solution.py:46
  15.7 21.8 %collective-permute-start.5 = (bf16[1,2,128,576]{3,2,1,0:T(8,128)(2,1)S(1)}, bf16[1,2,128,576]{3,2,1,0:T(8,128)(2,1)S(1)}, u32[]{:S(2)}, u32[]{:S(2)}) collective-permute-start(bf16[1,2,128,576]{3,2,1,0:T(8,128)(2,1)S(1)} %bitcast.50), channel_id=1, source_target_pairs={{0,4},{1,5},{2,6},{3,7},{4,0},{5,1},{6,2},{7,3},{8,12},{9,13},{10,... | collective-permute-start | bytes 884744 | tf_op jit(solution)/shard_map/ppermute | solution.py:46
  19.2 18.3 %copy-start.9 = (bf16[1,216,128]{2,1,0:T(8,128)(2,1)}, bf16[1,216,128]{2,1,0:T(8,128)(2,1)S(1)}, u32[]{:S(2)}) copy-start(bf16[1,216,128]{2,1,0:T(8,128)(2,1)S(1)} %collective-permute-done) | copy-start | bytes 165892
  19.3 17.5 %collective-permute-start.1 = (bf16[2,216,128]{2,1,0:T(8,128)(2,1)S(1)}, bf16[2,216,128]{2,1,0:T(8,128)(2,1)S(1)}, u32[]{:S(2)}, u32[]{:S(2)}) collective-permute-start(bf16[2,216,128]{2,1,0:T(8,128)(2,1)S(1)} %pad_maximum_fusion.5), channel_id=1, source_target_pairs={{0,2},{1,3},{2,0},{3,1},{4,6},{5,7},{6,4},{7,5},{8,10},{9,11},{10,... | collective-permute-start | bytes 331784 | tf_op jit(solution)/shard_map/ppermute | solution.py:46
  37.5 6.2 %collective-permute-start.2 = (bf16[4,216,128]{2,1,0:T(8,128)(2,1)}, bf16[4,216,128]{2,1,0:T(8,128)(2,1)}, u32[]{:S(2)}, u32[]{:S(2)}) collective-permute-start(bf16[4,216,128]{2,1,0:T(8,128)(2,1)} %pad_maximum_fusion.4), channel_id=1, source_target_pairs={{0,16},{8,24},{16,0},{24,8},{1,17},{9,25},{17,1},{25,9},{2,18},{10... | collective-permute-start | bytes 663560 | tf_op jit(solution)/shard_map/ppermute | solution.py:46
  38.7 19.9 %collective-permute-start.6 = (bf16[2,2,128,576]{2,3,1,0:T(8,128)(2,1)}, bf16[2,2,128,576]{2,3,1,0:T(8,128)(2,1)S(1)}, u32[]{:S(2)}, u32[]{:S(2)}) collective-permute-start(bf16[2,2,128,576]{2,3,1,0:T(8,128)(2,1)} %copy.50), channel_id=1, source_target_pairs={{0,2},{1,3},{2,0},{3,1},{4,6},{5,7},{6,4},{7,5},{8,10},{9,11},{10,... | collective-permute-start | bytes 1769480 | tf_op jit(solution)/shard_map/ppermute | solution.py:46
  45.5 15.3 %collective-permute-start.3 = (bf16[8,216,128]{2,1,0:T(8,128)(2,1)}, bf16[8,216,128]{2,1,0:T(8,128)(2,1)}, u32[]{:S(2)}, u32[]{:S(2)}) collective-permute-start(bf16[8,216,128]{2,1,0:T(8,128)(2,1)} %pad_maximum_fusion.3), channel_id=1, source_target_pairs={{0,8},{8,0},{16,24},{24,16},{1,9},{9,1},{17,25},{25,17},{2,10},{10... | collective-permute-start | bytes 1327112 | tf_op jit(solution)/shard_map/ppermute | solution.py:46
  50.2 15.1 %copy-start.3 = (s32[32]{0:T(128)S(1)}, s32[32]{0:T(128)}, u32[]{:S(2)}) copy-start(s32[32]{0:T(128)} %constant.28.clone) | copy-start | bytes 388
  58.6 4.2 %copy-start.4 = (bf16[2,2,128,576]{2,3,1,0:T(8,128)(2,1)}, bf16[2,2,128,576]{2,3,1,0:T(8,128)(2,1)S(1)}, u32[]{:S(2)}) copy-start(bf16[2,2,128,576]{2,3,1,0:T(8,128)(2,1)S(1)} %collective-permute-done.6) | copy-start | bytes 1769476
  60.9 5.6 %copy-start.15 = (f32[2,1024]{1,0:T(2,128)S(1)}, f32[2,1024]{1,0:T(2,128)}, u32[]{:S(2)}) copy-start(f32[2,1024]{1,0:T(2,128)} %subtract_convert_fusion) | copy-start | bytes 24580
  60.9 11.4 %collective-permute-start.7 = (bf16[4,2,128,576]{2,3,1,0:T(8,128)(2,1)}, bf16[4,2,128,576]{2,3,1,0:T(8,128)(2,1)}, u32[]{:S(2)}, u32[]{:S(2)}) collective-permute-start(bf16[4,2,128,576]{2,3,1,0:T(8,128)(2,1)} %pad_maximum_fusion.1), channel_id=1, source_target_pairs={{0,1},{1,0},{2,3},{3,2},{4,5},{5,4},{6,7},{7,6},{8,9},{9,8},{10,11... | collective-permute-start | bytes 3538952 | tf_op jit(solution)/shard_map/ppermute | solution.py:46
  62.8 1.3 copy-start.5
  62.8 7.2 %collective-permute-start.4 = (bf16[16,216,128]{2,1,0:T(8,128)(2,1)}, bf16[16,216,128]{2,1,0:T(8,128)(2,1)}, u32[]{:S(2)}, u32[]{:S(2)}) collective-permute-start(bf16[16,216,128]{2,1,0:T(8,128)(2,1)} %get-tuple-element.102), channel_id=1, source_target_pairs={{0,1},{1,0},{2,3},{3,2},{4,5},{5,4},{6,7},{7,6},{8,9},{9,8},{10,11... | collective-permute-start | bytes 2654216 | tf_op jit(solution)/shard_map/ppermute | solution.py:46
  74.6 3.0 %copy-start.2 = (f32[2,576]{1,0:T(2,128)S(1)}, f32[2,576]{1,0:T(2,128)}, u32[]{:S(2)}) copy-start(f32[2,576]{1,0:T(2,128)} %gains.3) | copy-start | bytes 13828
  111.1 0.8 copy-start
  112.0 0.7 copy-start.18
  134.1 16.1 %collective-permute-start.8 = (bf16[4,2,384,128]{3,2,1,0:T(8,128)(2,1)S(1)}, bf16[4,2,384,128]{3,2,1,0:T(8,128)(2,1)}, u32[]{:S(2)}, u32[]{:S(2)}) collective-permute-start(bf16[4,2,384,128]{3,2,1,0:T(8,128)(2,1)S(1)} %slice.52), channel_id=1, source_target_pairs={{0,1},{1,0},{2,3},{3,2},{4,5},{5,4},{6,7},{7,6},{8,9},{9,8},{10,11... | collective-permute-start | bytes 2359304 | tf_op jit(solution)/shard_map/ppermute | solution.py:46
  134.6 4.6 %collective-permute-start.16 = (f32[2,576]{1,0:T(2,128)S(1)}, f32[2,576]{1,0:T(2,128)S(1)}, u32[]{:S(2)}, u32[]{:S(2)}) collective-permute-start(f32[2,576]{1,0:T(2,128)S(1)} %maximum_divide_fusion), channel_id=1, source_target_pairs={{0,4},{1,5},{2,6},{3,7},{4,0},{5,1},{6,2},{7,3},{8,12},{9,13},{10,... | collective-permute-start | bytes 13832 | tf_op jit(solution)/shard_map/ppermute | solution.py:46
  138.8 14.5 %collective-permute-start.11 = (bf16[16,216,128]{2,1,0:T(8,128)(2,1)}, bf16[16,216,128]{2,1,0:T(8,128)(2,1)}, u32[]{:S(2)}, u32[]{:S(2)}) collective-permute-start(bf16[16,216,128]{2,1,0:T(8,128)(2,1)} %slice.59), channel_id=1, source_target_pairs={{0,1},{1,0},{2,3},{3,2},{4,5},{5,4},{6,7},{7,6},{8,9},{9,8},{10,11... | collective-permute-start | bytes 2654216 | tf_op jit(solution)/shard_map/ppermute | solution.py:46
  139.2 3.7 %collective-permute-start.17 = (f32[2,576]{1,0:T(2,128)S(1)}, f32[2,576]{1,0:T(2,128)S(1)}, u32[]{:S(2)}, u32[]{:S(2)}) collective-permute-start(f32[2,576]{1,0:T(2,128)S(1)} %fusion.28), channel_id=1, source_target_pairs={{0,2},{1,3},{2,0},{3,1},{4,6},{5,7},{6,4},{7,5},{8,10},{9,11},{10,... | collective-permute-start | bytes 13832 | tf_op jit(solution)/shard_map/ppermute | solution.py:46
  142.9 3.6 %collective-permute-start.18 = (f32[2,576]{1,0:T(2,128)S(1)}, f32[2,576]{1,0:T(2,128)S(1)}, u32[]{:S(2)}, u32[]{:S(2)}) collective-permute-start(f32[2,576]{1,0:T(2,128)S(1)} %add.201), channel_id=1, source_target_pairs={{0,16},{8,24},{16,0},{24,8},{1,17},{9,25},{17,1},{25,9},{2,18},{10... | collective-permute-start | bytes 13832 | tf_op jit(solution)/shard_map/ppermute | solution.py:46
  146.5 3.6 %collective-permute-start.19 = (f32[2,576]{1,0:T(2,128)S(1)}, f32[2,576]{1,0:T(2,128)S(1)}, u32[]{:S(2)}, u32[]{:S(2)}) collective-permute-start(f32[2,576]{1,0:T(2,128)S(1)} %add.202), channel_id=1, source_target_pairs={{0,8},{8,0},{16,24},{24,16},{1,9},{9,1},{17,25},{25,17},{2,10},{10... | collective-permute-start | bytes 13832 | tf_op jit(solution)/shard_map/ppermute | solution.py:46
  148.2 5.1 %copy-start.6 = (bf16[32,216,128]{2,1,0:T(8,128)(2,1)S(1)}, bf16[32,216,128]{2,1,0:T(8,128)(2,1)}, u32[]{:S(2)}) copy-start(bf16[32,216,128]{2,1,0:T(8,128)(2,1)} %get-tuple-element.43) | copy-start | bytes 5308420
  150.2 6.4 %collective-permute-start.20 = (f32[2,576]{1,0:T(2,128)S(1)}, f32[2,576]{1,0:T(2,128)S(1)}, u32[]{:S(2)}, u32[]{:S(2)}) collective-permute-start(f32[2,576]{1,0:T(2,128)S(1)} %add.203), channel_id=1, source_target_pairs={{0,1},{1,0},{2,3},{3,2},{4,5},{5,4},{6,7},{7,6},{8,9},{9,8},{10,11... | collective-permute-start | bytes 13832 | tf_op jit(solution)/shard_map/ppermute | solution.py:46
  151.8 4.7 %copy-start.16 = (f32[2,576]{1,0:T(2,128)S(1)}, f32[2,576]{1,0:T(2,128)}, u32[]{:S(2)}) copy-start(f32[2,576]{1,0:T(2,128)} %param.25) | copy-start | bytes 13828
  151.8 4.7 %copy-start.17 = (f32[2,576]{1,0:T(2,128)S(1)}, f32[2,576]{1,0:T(2,128)}, u32[]{:S(2)}) copy-start(f32[2,576]{1,0:T(2,128)} %param.26) | copy-start | bytes 13828
  151.8 16.3 %collective-permute-start.9 = (bf16[2,2,384,128]{3,2,1,0:T(8,128)(2,1)S(1)}, bf16[2,2,384,128]{3,2,1,0:T(8,128)(2,1)S(1)}, u32[]{:S(2)}, u32[]{:S(2)}) collective-permute-start(bf16[2,2,384,128]{3,2,1,0:T(8,128)(2,1)S(1)} %slice.71), channel_id=1, source_target_pairs={{0,2},{1,3},{2,0},{3,1},{4,6},{5,7},{6,4},{7,5},{8,10},{9,11},{10,... | collective-permute-start | bytes 1179656 | tf_op jit(solution)/shard_map/ppermute | solution.py:46
  154.8 20.5 %collective-permute-start.12 = (bf16[8,216,128]{2,1,0:T(8,128)(2,1)S(1)}, bf16[8,216,128]{2,1,0:T(8,128)(2,1)S(1)}, u32[]{:S(2)}, u32[]{:S(2)}) collective-permute-start(bf16[8,216,128]{2,1,0:T(8,128)(2,1)S(1)} %slice.75), channel_id=1, source_target_pairs={{0,8},{8,0},{16,24},{24,16},{1,9},{9,1},{17,25},{25,17},{2,10},{10... | collective-permute-start | bytes 1327112 | tf_op jit(solution)/shard_map/ppermute | solution.py:46
  157.1 30.8 %copy-start.8 = (bf16[576,960]{1,0:T(8,128)(2,1)S(1)}, bf16[576,960]{1,0:T(8,128)(2,1)}, u32[]{:S(2)}) copy-start(bf16[576,960]{1,0:T(8,128)(2,1)} %get-tuple-element.32.w_project) | copy-start | bytes 3317764
  168.3 19.6 %collective-permute-start.10 = (bf16[1,2,384,128]{3,2,1,0:T(8,128)(2,1)S(1)}, bf16[1,2,384,128]{3,2,1,0:T(8,128)(2,1)S(1)}, u32[]{:S(2)}, u32[]{:S(2)}) collective-permute-start(bf16[1,2,384,128]{3,2,1,0:T(8,128)(2,1)S(1)} %slice.73), channel_id=1, source_target_pairs={{0,4},{1,5},{2,6},{3,7},{4,0},{5,1},{6,2},{7,3},{8,12},{9,13},{10,... | collective-permute-start | bytes 589832 | tf_op jit(solution)/shard_map/ppermute | solution.py:46
  175.5 13.1 %collective-permute-start.13 = (bf16[4,216,128]{2,1,0:T(8,128)(2,1)S(1)}, bf16[4,216,128]{2,1,0:T(8,128)(2,1)S(1)}, u32[]{:S(2)}, u32[]{:S(2)}) collective-permute-start(bf16[4,216,128]{2,1,0:T(8,128)(2,1)S(1)} %slice.77), channel_id=1, source_target_pairs={{0,16},{8,24},{16,0},{24,8},{1,17},{9,25},{17,1},{25,9},{2,18},{10... | collective-permute-start | bytes 663560 | tf_op jit(solution)/shard_map/ppermute | solution.py:46
  187.9 5.8 %copy-start.1 = (f32[256,576]{1,0:T(8,128)S(1)}, f32[256,576]{1,0:T(8,128)}, u32[]{:S(2)}) copy-start(f32[256,576]{1,0:T(8,128)} %copy-done) | copy-start | bytes 1769476
  188.7 4.8 %collective-permute-start.14 = (bf16[2,216,128]{2,1,0:T(8,128)(2,1)S(1)}, bf16[2,216,128]{2,1,0:T(8,128)(2,1)S(1)}, u32[]{:S(2)}, u32[]{:S(2)}) collective-permute-start(bf16[2,216,128]{2,1,0:T(8,128)(2,1)S(1)} %slice.79), channel_id=1, source_target_pairs={{0,2},{1,3},{2,0},{3,1},{4,6},{5,7},{6,4},{7,5},{8,10},{9,11},{10,... | collective-permute-start | bytes 331784 | tf_op jit(solution)/shard_map/ppermute | solution.py:46
  193.6 7.5 %collective-permute-start.15 = (bf16[1,216,128]{2,1,0:T(8,128)(2,1)S(1)}, bf16[1,216,128]{2,1,0:T(8,128)(2,1)S(1)}, u32[]{:S(2)}, u32[]{:S(2)}) collective-permute-start(bf16[1,216,128]{2,1,0:T(8,128)(2,1)S(1)} %slice.81), channel_id=1, source_target_pairs={{0,4},{1,5},{2,6},{3,7},{4,0},{5,1},{6,2},{7,3},{8,12},{9,13},{10,... | collective-permute-start | bytes 165896 | tf_op jit(solution)/shard_map/ppermute | solution.py:46
  193.7 7.4 %copy-start.10 = (f32[27648]{0:T(1024)S(1)}, f32[27648]{0:T(1024)}, u32[]{:S(2)}) copy-start(f32[27648]{0:T(1024)} %param.18) | copy-start | bytes 331780
  193.7 7.4 %copy-start.13 = (f32[27648]{0:T(1024)S(1)}, f32[27648]{0:T(1024)}, u32[]{:S(2)}) copy-start(f32[27648]{0:T(1024)} %param.21) | copy-start | bytes 331780
  193.7 7.4 %copy-start.14 = (f32[27648]{0:T(1024)S(1)}, f32[27648]{0:T(1024)}, u32[]{:S(2)}) copy-start(f32[27648]{0:T(1024)} %param.22) | copy-start | bytes 331780
  193.7 34.6 %copy-start.7 = (f32[82944]{0:T(1024)S(1)}, f32[82944]{0:T(1024)}, u32[]{:S(2)}) copy-start(f32[82944]{0:T(1024)} %param.19) | copy-start | bytes 995332
  193.7 34.6 %copy-start.11 = (f32[82944]{0:T(1024)S(1)}, f32[82944]{0:T(1024)}, u32[]{:S(2)}) copy-start(f32[82944]{0:T(1024)} %param.23) | copy-start | bytes 995332
  193.8 34.6 %copy-start.12 = (f32[82944]{0:T(1024)S(1)}, f32[82944]{0:T(1024)}, u32[]{:S(2)}) copy-start(f32[82944]{0:T(1024)} %param.24) | copy-start | bytes 995332
Sparse Core Ops, SparseCore 0:
  11.4 73.7 all-gather.1
  112.1 116.1 reduce-scatter.3
where the time goes:
time: 242 us; the launch traced here: 238 us
  waiting for transfers between devices  93.4 us (39%)
  Pallas kernels  53.3 us (22%)
  starting transfers between devices  25.3 us (10%)
  other arithmetic  25 us (10%)
  local copies, waits for them, and re-layouts  25 us (10%)
  between operations  14.9 us (6%)
    ppermute x21, waiting for transfers between devices, exchange(): lax.ppermute(value, axis, [(place, place ^ bit) for place in range(count)])  67 us
    unnamed x3, waiting for transfers between devices  26.5 us
    ppermute x21, starting transfers between devices, exchange(): lax.ppermute(value, axis, [(place, place ^ bit) for place in range(count)])  25.3 us
    pallas_call x1, Pallas kernels, attention_backward(): pl.pallas_call(attention_backward_kernel, out_shape=(shape((count, rows,...  19.9 us
    pallas_call x1, Pallas kernels, attention_forward(): pl.pallas_call(attention_forward_kernel, out_shape=(shape((D, QKV_WIDTH),...  18.8 us
    pallas_call x1, Pallas kernels, feedforward(): pl.pallas_call(feedforward_kernel, out_shape=(shape((tokens, D), BF16), s...  14.7 us
    unnamed x46, local copies, waits for them, and re-layouts  10.5 us
    concatenate x6, other arithmetic, doubled(): block = jnp.concatenate([block, exchange(block, axis, bit)], 0)  7.87 us
  transfers between devices with their start and end apart: 23, of which 13 were waited for; matrix products, arithmetic and copies ran while one was open for 19% of the time, Pallas kernels for 16%

commit v1 on v0

--- a/solution.py
+++ b/solution.py
@@ -69,26 +69,23 @@
     return order
 
 
-def doubled(block, stages):
-    for axis, bit, unused_flat in stages:
-        block = jnp.concatenate([block, exchange(block, axis, bit)], 0)
-    return block
-
-
-def halved(blocks, stages):
-    for axis, bit, unused_flat in reversed(stages):
-        half = blocks.shape[0] // 2
-        received = exchange(blocks[half:], axis, bit)
-        blocks = (blocks[:half].astype(F32) + received.astype(F32)).astype(BF16)
-    return blocks
-
-
-def inverse_places(order, place):
-    by_relative = [0] * len(order)
-    for position, relative in enumerate(order):
-        by_relative[relative] = position
-    count = len(order)
-    return jnp.array(by_relative, jnp.int32)[jnp.arange(count, dtype=jnp.int32) ^ place]
+def swap_dp(stages):
+    turned = iter([stage for stage in reversed(stages) if stage[0] == "dp"])
+    return [next(turned) if stage[0] == "dp" else stage for stage in stages]
+
+
+def halve_step(blocks, received):
+    half = blocks.shape[0] // 2
+    return (blocks[:half].astype(F32) + received.astype(F32)).astype(BF16)
+
+
+def send_half(blocks, stage):
+    axis, bit, unused_flat = stage
+    return exchange(blocks[blocks.shape[0] // 2 :], axis, bit)
+
+
+def together(*values):
+    return lax.optimization_barrier(values)
 
 
 def unit_norm(inputs):
@@ -170,17 +167,29 @@
         flat[pl.ds(base + k, pairs, stride=step), :] = rows
 
 
-def load_blocks(places, blocks, flat):
+def load_blocks(order, halves, flat):
+    first = 0
+    for blocks in halves:
+        count, rows, unused = blocks.shape
+
+        def move(place, unused, blocks=blocks, rows=rows, first=first):
+            start = pl.multiple_of(order[first + place] * rows, 8)
+            flat[pl.ds(start, rows), :] = blocks[place].astype(F32)
+            return unused
+
+        lax.fori_loop(0, count, move, 0)
+        first += count
+
+
+def store_blocks(order, flat, blocks, owner_rows, first_row):
     count, rows, unused = blocks.shape
-    for index in range(count):
-        flat[index * rows : (index + 1) * rows, :] = blocks[places[index]].astype(F32)
-
-
-def store_blocks(order, flat, blocks):
-    count, rows, unused = blocks.shape
-    for index in range(count):
-        start = pl.multiple_of(order[index] * rows, 8)
+
+    def move(index, unused):
+        start = pl.multiple_of(order[index] * owner_rows + first_row, 8)
         blocks[index] = flat[pl.ds(start, rows), :].astype(BF16)
+        return unused
+
+    lax.fori_loop(0, count, move, 0)
 
 
 def planes_to_matrix(planes, whole, matrix):
@@ -196,9 +205,11 @@
 
 
 def attention_forward_kernel(
-    places,
-    weight_blocks,
-    window_inputs,
+    order,
+    weights_near,
+    weights_far,
+    inputs_near,
+    inputs_far,
     cosines,
     sines,
     bias,
@@ -219,7 +230,7 @@
     w_across,
     values_across,
 ):
-    load_blocks(places, weight_blocks, flat)
+    load_blocks(order, (weights_near, weights_far), flat)
     unflatten_odd(flat, 0, D // 2, 7, planes_one)
     planes_to_matrix(planes_one, 7, w_project)
     for j in range(7):
@@ -227,11 +238,16 @@
     w_across[7 * LANES :, :] = jnp.transpose(planes_one[7])[:HALF].astype(BF16)
     unflatten_odd(flat, D * QKV_WIDTH // LANES, QUERY_WIDTH // 2, 4, planes_two)
     planes_to_matrix(planes_two, 4, w_output)
-    blocks = window_inputs.shape[0]
+    near_count = inputs_near.shape[0]
+    blocks = near_count + inputs_far.shape[0]
     gain = gains[0:1, :]
-    for micro in range(MICRO):
+
+    def one(micro, unused):
         for block in range(blocks):
-            rows = window_inputs[block, micro].astype(F32)
+            if block < near_count:
+                rows = inputs_near[block, micro].astype(F32)
+            else:
+                rows = inputs_far[block - near_count, micro].astype(F32)
             inverse = lax.rsqrt(jnp.mean(rows * rows, axis=-1, keepdims=True) + NORM_EPSILON)
             normed[micro, block * DEVICE_TOKENS : (block + 1) * DEVICE_TOKENS, :] = (
                 rows * inverse * gain
@@ -263,13 +279,16 @@
             mixed_across[micro, rows, :] = dot(values_across[group_rows, :], low)
             log_totals[micro, head : head + 1, :] = top + jnp.log(total)
         mixed = jnp.transpose(mixed_across[micro]).astype(BF16)
-        residual[micro] = window_inputs[0, micro].astype(F32) + dot(mixed, w_output[...])
-
-
-def attention_forward(places, weight_blocks, window_inputs, cosines, sines, bias, gains):
-    window = window_inputs.shape[0] * DEVICE_TOKENS
+        residual[micro] = inputs_near[0, micro].astype(F32) + dot(mixed, w_output[...])
+        return unused
+
+    lax.fori_loop(0, MICRO, one, 0)
+
+
+def attention_forward(order, weight_halves, input_halves, *tables):
+    window = sum(half.shape[0] for half in input_halves) * DEVICE_TOKENS
     shape = jax.ShapeDtypeStruct
-    rows = weight_blocks.shape[0] * weight_blocks.shape[1]
+    rows = sum(half.shape[0] * half.shape[1] for half in weight_halves)
     return pl.pallas_call(
         attention_forward_kernel,
         out_shape=(
@@ -284,7 +303,7 @@
             shape((MICRO, QUERY_WIDTH, DEVICE_TOKENS), F32),
             shape((MICRO, DEVICE_TOKENS, D), F32),
         ),
-        in_specs=[smem()] + vmem(6),
+        in_specs=[smem()] + vmem(4 + len(tables)),
         out_specs=tuple(vmem(10)),
         scratch_shapes=[
             pltpu.VMEM((rows, LANES), F32),
@@ -294,19 +313,22 @@
             pltpu.VMEM((KV_WIDTH, window), BF16),
         ],
         compiler_params=params(),
-    )(places, weight_blocks, window_inputs, cosines, sines, bias, gains)
+    )(order, *weight_halves, *input_halves, *tables)
 
 
 def feedforward_kernel(
-    places,
-    order,
+    straight,
+    order_two,
+    order_three,
     weight_blocks,
     residual,
     cotangent,
     gains,
     block_output,
     d_residual,
-    grad_blocks,
+    grads_one,
+    grads_two,
+    grads_three,
     gain_grad,
     flat,
     planes,
@@ -316,7 +338,7 @@
     d_gate_up,
 ):
     columns = 2 * FF // LANES
-    load_blocks(places, weight_blocks, flat)
+    load_blocks(straight, (weight_blocks,), flat)
     for j in range(columns):
         w_gate_up[:, j * LANES : (j + 1) * LANES] = flat[
             pl.ds(j, D, stride=columns), :
@@ -363,11 +385,20 @@
             planes[j, start : start + part, :] = grad[:, j * LANES : (j + 1) * LANES]
         planes[4, start : start + part, :HALF] = grad[:, 4 * LANES :]
     flatten_odd(planes, FF // 2, 4, flat, D * columns)
-    store_blocks(order, flat, grad_blocks)
-
-
-def feedforward(places, order, weight_blocks, residual, cotangent, gains):
+    owner_rows = weight_blocks.shape[1]
+    first_row = 0
+    for order, blocks in (
+        (straight, grads_one),
+        (order_two, grads_two),
+        (order_three, grads_three),
+    ):
+        store_blocks(order, flat, blocks, owner_rows, first_row)
+        first_row += blocks.shape[1]
+
+
+def feedforward(orders, weight_blocks, residual, cotangent, gains):
     shape = jax.ShapeDtypeStruct
+    part = shape((weight_blocks.shape[0], weight_blocks.shape[1] // 3, LANES), BF16)
     tokens = residual.shape[0]
     rows = weight_blocks.shape[0] * weight_blocks.shape[1]
     return pl.pallas_call(
@@ -375,11 +406,13 @@
         out_shape=(
             shape((tokens, D), BF16),
             shape((tokens, D), F32),
-            shape(weight_blocks.shape, BF16),
+            part,
+            part,
+            part,
             shape((D, 1), F32),
         ),
-        in_specs=[smem(), smem()] + vmem(4),
-        out_specs=tuple(vmem(4)),
+        in_specs=[smem()] * 3 + vmem(4),
+        out_specs=tuple(vmem(6)),
         scratch_shapes=[
             pltpu.VMEM((rows, LANES), F32),
             pltpu.VMEM((5, FF, LANES), F32),
@@ -389,12 +422,10 @@
             pltpu.VMEM((tokens, 2 * FF), BF16),
         ],
         compiler_params=params(),
-    )(places, order, weight_blocks, residual, cotangent, gains)
-
-
-def attention_backward_kernel(
-    order,
-    w_project,
+    )(*orders, weight_blocks, residual, cotangent, gains)
+
+
+def attention_backward_body(
     w_output,
     normed,
     queries,
@@ -407,64 +438,74 @@
     cosines,
     sines,
     bias,
-    grad_blocks,
     d_queries,
     d_window,
-    gain_grad,
-    flat,
-    planes,
     d_window_across,
     grad_across,
     grad_output,
+    d_mixed,
 ):
     blocks = d_window.shape[0]
-    for micro in range(MICRO):
-        cosine, sine = cosines[micro], sines[micro]
-        own_cosine, own_sine = cosine[:, :DEVICE_TOKENS], sine[:, :DEVICE_TOKENS]
-        d_branch = d_residual[micro].astype(BF16)
-        d_mixed = dot_nt(w_output[...], d_branch).astype(BF16)
-        mixed = mixed_across[micro]
-        for group in range(KEY_VALUE_HEADS):
-            group_rows = slice(group * HEAD_SIZE, (group + 1) * HEAD_SIZE)
-            d_key = None
-            for head in range(group * GROUP, (group + 1) * GROUP):
-                rows = slice(head * HEAD_SIZE, (head + 1) * HEAD_SIZE)
-                query = queries[micro, rows, :] * SCALE
-                d_mixed_head = d_mixed[rows]
-                delta = jnp.sum(d_mixed_head.astype(F32) * mixed[rows], axis=0, keepdims=True)
-                scores = dot(keys[micro, group], query) + bias[micro]
-                probability = jnp.exp(scores - log_totals[micro, head : head + 1, :])
-                d_probs = dot(values[micro, group], d_mixed_head)
-                d_scores = (probability * (d_probs - delta)).astype(BF16)
-                d_query = dot(keys_across[micro, group_rows, :], d_scores) * SCALE
-                d_queries[micro, rows, :] = rotated(d_query, own_cosine, -own_sine).astype(BF16)
-                key_part = dot_nt(query, d_scores)
-                value_part = dot_nt(d_mixed_head, probability.astype(BF16))
-                d_key = key_part if d_key is None else d_key + key_part
-                if head == group * GROUP:
-                    d_value = value_part
-                else:
-                    d_value = d_value + value_part
-            d_window_across[group_rows, :] = rotated(d_key, cosine, -sine).astype(BF16)
-            value_rows = slice(
-                KV_WIDTH + group * HEAD_SIZE, KV_WIDTH + (group + 1) * HEAD_SIZE
+    cosine, sine = cosines[...], sines[...]
+    own_cosine, own_sine = cosine[:, :DEVICE_TOKENS], sine[:, :DEVICE_TOKENS]
+    d_branch = d_residual[...].astype(BF16)
+    d_mixed[...] = dot_nt(w_output[...], d_branch).astype(BF16)
+
+    def one(group, unused):
+        group_rows = pl.ds(pl.multiple_of(group * HEAD_SIZE, HEAD_SIZE), HEAD_SIZE)
+        value_rows = pl.ds(pl.multiple_of(KV_WIDTH + group * HEAD_SIZE, HEAD_SIZE), HEAD_SIZE)
+        d_key = d_value = jnp.zeros((HEAD_SIZE, cosine.shape[1]), F32)
+        for offset in range(GROUP):
+            head = group * GROUP + offset
+            rows = pl.ds(pl.multiple_of(head * HEAD_SIZE, HEAD_SIZE), HEAD_SIZE)
+            query = queries[rows, :] * SCALE
+            d_mixed_head = d_mixed[rows, :]
+            delta = jnp.sum(
+                d_mixed_head.astype(F32) * mixed_across[rows, :], axis=0, keepdims=True
             )
-            d_window_across[value_rows, :] = d_value.astype(BF16)
-        for block in range(blocks):
-            d_window[block, micro] = d_window_across[
-                :, block * DEVICE_TOKENS : (block + 1) * DEVICE_TOKENS
-            ]
-        query_grad = dot(d_queries[micro], normed[micro, :DEVICE_TOKENS, :])
-        window_grad = dot(d_window_across[...], normed[micro])
-        output_grad = dot(mixed.astype(BF16), d_branch)
-        if micro == 0:
-            grad_across[:QUERY_WIDTH, :] = query_grad
-            grad_across[QUERY_WIDTH:, :] = window_grad
-            grad_output[...] = output_grad
-        else:
-            grad_across[:QUERY_WIDTH, :] += query_grad
-            grad_across[QUERY_WIDTH:, :] += window_grad
-            grad_output[...] += output_grad
+            scores = dot(keys[group], query) + bias[...]
+            probability = jnp.exp(scores - log_totals[pl.ds(head, 1), :])
+            d_probs = dot(values[group], d_mixed_head)
+            d_scores = (probability * (d_probs - delta)).astype(BF16)
+            d_query = dot(keys_across[group_rows, :], d_scores) * SCALE
+            d_queries[rows, :] = rotated(d_query, own_cosine, -own_sine).astype(BF16)
+            d_key = d_key + dot_nt(query, d_scores)
+            d_value = d_value + dot_nt(d_mixed_head, probability.astype(BF16))
+        d_window_across[group_rows, :] = rotated(d_key, cosine, -sine).astype(BF16)
+        d_window_across[value_rows, :] = d_value.astype(BF16)
+        return unused
+
+    lax.fori_loop(0, KEY_VALUE_HEADS, one, 0)
+    for block in range(blocks):
+        d_window[block] = d_window_across[
+            :, block * DEVICE_TOKENS : (block + 1) * DEVICE_TOKENS
+        ]
+    query_grad = dot(d_queries[...], normed[:DEVICE_TOKENS, :])
+    window_grad = dot(d_window_across[...], normed[...])
+    output_grad = dot(mixed_across[...].astype(BF16), d_branch)
+    grad_across[:QUERY_WIDTH, :] = query_grad
+    grad_across[QUERY_WIDTH:, :] = window_grad
+    grad_output[...] = output_grad
+
+
+def attention_backward_first(*refs):
+    operands, (d_queries, d_window, grad_across, grad_output, across, d_mixed) = (
+        refs[:12],
+        refs[12:],
+    )
+    attention_backward_body(
+        *operands, d_queries, d_window, across, grad_across, grad_output, d_mixed
+    )
+
+
+def attention_backward_second(order, w_project, first_across, first_output, *refs):
+    operands, (grad_blocks, d_queries, d_window, gain_grad) = refs[:12], refs[12:16]
+    flat, planes, across, d_mixed, grad_across, grad_output = refs[16:]
+    attention_backward_body(
+        *operands, d_queries, d_window, across, grad_across, grad_output, d_mixed
+    )
+    grad_across[...] += first_across[...]
+    grad_output[...] += first_output[...]
     total = jnp.zeros((D, LANES), F32)
     for j in range(7):
         piece = jnp.transpose(grad_across[j * LANES : (j + 1) * LANES, :])
@@ -482,32 +523,43 @@
         planes[j] = grad_output[:, j * LANES : (j + 1) * LANES]
     planes[4, :, :HALF] = grad_output[:, 4 * LANES :]
     flatten_odd(planes, QUERY_WIDTH // 2, 4, flat, D * QKV_WIDTH // LANES)
-    store_blocks(order, flat, grad_blocks)
-
-
-def attention_backward(order, rows, *operands):
+    store_blocks(order, flat, grad_blocks, grad_blocks.shape[1], 0)
+
+
+def attention_backward(operands, count, rows, final=()):
     shape = jax.ShapeDtypeStruct
-    window = operands[2].shape[1]
-    count = order.shape[0]
-    return pl.pallas_call(
-        attention_backward_kernel,
-        out_shape=(
-            shape((count, rows, LANES), BF16),
-            shape((MICRO, QUERY_WIDTH, DEVICE_TOKENS), BF16),
-            shape((window // DEVICE_TOKENS, MICRO, 2 * KV_WIDTH, DEVICE_TOKENS), BF16),
-            shape((D, 1), F32),
-        ),
-        in_specs=[smem()] + vmem(len(operands)),
-        out_specs=tuple(vmem(4)),
-        scratch_shapes=[
+    window = operands[1].shape[0]
+    outputs = (
+        shape((QUERY_WIDTH, DEVICE_TOKENS), BF16),
+        shape((window // DEVICE_TOKENS, 2 * KV_WIDTH, DEVICE_TOKENS), BF16),
+    )
+    sums = [(QKV_WIDTH, D), (QUERY_WIDTH, D)]
+    scratch = [
+        pltpu.VMEM((2 * KV_WIDTH, window), BF16),
+        pltpu.VMEM((QUERY_WIDTH, DEVICE_TOKENS), BF16),
+    ]
+    if final:
+        kernel = attention_backward_second
+        outputs = (shape((count, rows, LANES), BF16), *outputs, shape((D, 1), F32))
+        scratch = [
             pltpu.VMEM((count * rows, LANES), F32),
             pltpu.VMEM((8, D, LANES), F32),
-            pltpu.VMEM((2 * KV_WIDTH, window), BF16),
-            pltpu.VMEM((QKV_WIDTH, D), F32),
-            pltpu.VMEM((QUERY_WIDTH, D), F32),
-        ],
+            *scratch,
+            *[pltpu.VMEM(dims, F32) for dims in sums],
+        ]
+        in_specs = [smem()] + vmem(len(final) - 1 + len(operands))
+    else:
+        kernel = attention_backward_first
+        outputs = (*outputs, *[shape(dims, F32) for dims in sums])
+        in_specs = vmem(len(operands))
+    return pl.pallas_call(
+        kernel,
+        out_shape=outputs,
+        in_specs=in_specs,
+        out_specs=tuple(vmem(len(outputs))),
+        scratch_shapes=scratch,
         compiler_params=params(),
-    )(order, *operands)
+    )(*final, *operands)
 
 
 def adam_update(weights, moment, square, grad, rate, decay):
@@ -556,41 +608,19 @@
     order = block_order(stages)
     seq_stages = [stage for stage in stages if stage[0] == "seq"]
 
-    attention_low = attention_weights.astype(BF16)
-    feedforward_low = feedforward_weights.astype(BF16)
     own_inputs = block_input[:, 0]
     straight = jnp.arange(BLOCKS, dtype=jnp.int32)
-    if butterfly:
-        attention_blocks = doubled(
-            attention_low.reshape(1, attention_length // LANES, LANES), stages
-        )
-        attention_places = inverse_places(order, owner_place)
-        attention_order = jnp.array(order, jnp.int32) ^ owner_place
-    else:
-        attention_blocks = lax.all_gather(attention_low, both, axis=0, tiled=True)
-        attention_blocks = attention_blocks.reshape(BLOCKS, -1, LANES)
-        attention_places = attention_order = straight
-    if paired:
-        window_inputs = doubled(own_inputs[None], seq_stages)
-        window_blocks = seq_place ^ jnp.array(block_order(seq_stages), jnp.int32)
-    else:
-        window_inputs = jnp.stack(
-            [own_inputs]
-            + [
-                lax.ppermute(
-                    own_inputs, "seq", [(p, p + step) for p in range(seq_count - step)]
-                )
-                for step in range(1, reach + 1)
-            ],
-            0,
-        )
-        window_blocks = seq_place - jnp.arange(reach + 1, dtype=jnp.int32)
     tiled_rows = feedforward_length % (8 * LANES) == 0
+    feedforward_low = feedforward_weights.astype(BF16)
     if tiled_rows:
         feedforward_low = feedforward_low.reshape(-1, LANES)
     feedforward_blocks = lax.all_gather(feedforward_low, both, axis=0, tiled=True)
     feedforward_blocks = feedforward_blocks.reshape(BLOCKS, -1, LANES)
 
+    if paired:
+        window_blocks = seq_place ^ jnp.array(block_order(seq_stages), jnp.int32)
+    else:
+        window_blocks = seq_place - jnp.arange(reach + 1, dtype=jnp.int32)
     token = jnp.arange(DEVICE_TOKENS, dtype=jnp.int32)
     query_index = seq_place * DEVICE_TOKENS + token
     key_index = (window_blocks[:, None] * DEVICE_TOKENS + token[None, :]).reshape(-1)
@@ -607,6 +637,49 @@
     )
     bias = jnp.where(allowed, 0.0, -jnp.inf).astype(F32)
 
+    attention_low = attention_weights.astype(BF16)
+    if butterfly:
+        orders = [
+            jnp.array(block_order(path), jnp.int32) ^ owner_place
+            for path in (stages, swap_dp(stages))
+        ]
+    else:
+        orders = [straight, straight]
+    if butterfly and paired:
+        weights = attention_low.reshape(1, attention_length // LANES, LANES)
+        window_inputs = own_inputs[None]
+        for index, (axis, bit, unused_flat) in enumerate(stages):
+            far = exchange(weights, axis, bit)
+            if index < len(seq_stages):
+                other_axis, other_bit, unused_flat = seq_stages[index]
+                inputs_far = exchange(window_inputs, other_axis, other_bit)
+                far, inputs_far = together(far, inputs_far)
+                if index == 0:
+                    far, cosines, sines, bias = together(far, cosines, sines, bias)
+                if index < len(seq_stages) - 1:
+                    window_inputs = jnp.concatenate([window_inputs, inputs_far], 0)
+            if index < len(stages) - 1:
+                weights = jnp.concatenate([weights, far], 0)
+        weight_halves = (weights, far)
+        input_halves = (window_inputs, inputs_far)
+    else:
+        weights = lax.all_gather(attention_low, both, axis=0, tiled=True)
+        weights = weights.reshape(BLOCKS, -1, LANES)
+        weight_halves = (weights[: BLOCKS // 2], weights[BLOCKS // 2 :])
+        window_inputs = jnp.stack(
+            [own_inputs]
+            + [
+                lax.ppermute(
+                    own_inputs, "seq", [(p, p + step) for p in range(seq_count - step)]
+                )
+                for step in range(1, reach + 1)
+            ],
+            0,
+        )
+        middle = (reach + 1) // 2
+        input_halves = (window_inputs[:middle], window_inputs[middle:])
+        orders = [straight, straight]
+
     (
         w_project,
         w_output,
@@ -619,11 +692,10 @@
         mixed_across,
         residual,
     ) = attention_forward(
-        attention_places, attention_blocks, window_inputs, cosines, sines, bias, norm_gains
-    )
-    block_output, d_residual, feedforward_grads, gain_two = feedforward(
-        straight,
-        straight,
+        orders[0], weight_halves, input_halves, cosines, sines, bias, norm_gains
+    )
+    block_output, d_residual, part_one, part_two, part_three, gain_two = feedforward(
+        (straight, *orders),
         feedforward_blocks,
         residual.reshape(-1, D),
         out_grad[:, 0].reshape(-1, D),
@@ -631,54 +703,97 @@
     )
     block_output = block_output.reshape(MICRO, DEVICE_TOKENS, D)
     d_residual = d_residual.reshape(MICRO, DEVICE_TOKENS, D)
-    feedforward_grads = feedforward_grads.reshape(-1, LANES)
-    if not tiled_rows:
-        feedforward_grads = feedforward_grads.reshape(-1)
-    feedforward_owned = lax.psum_scatter(
-        feedforward_grads, both, scatter_dimension=0, tiled=True
-    ).reshape(-1)
-    attention_grads, d_queries, d_window, gain_one = attention_backward(
-        attention_order,
-        D * (QKV_WIDTH + QUERY_WIDTH) // (LANES * BLOCKS),
-        w_project,
-        w_output,
-        normed_one,
-        queries,
-        keys_across,
-        keys,
-        values,
-        log_totals,
-        mixed_across,
-        d_residual,
-        cosines,
-        sines,
-        bias,
-    )
-    if butterfly:
-        attention_owned = halved(attention_grads, stages).reshape(-1)
+
+    def operands_of(micro):
+        return (
+            w_output,
+            normed_one[micro],
+            queries[micro],
+            keys_across[micro],
+            keys[micro],
+            values[micro],
+            log_totals[micro],
+            mixed_across[micro],
+            d_residual[micro],
+            cosines[micro],
+            sines[micro],
+            bias[micro],
+        )
+
+    attention_rows = D * (QKV_WIDTH + QUERY_WIDTH) // (LANES * BLOCKS)
+    if butterfly and paired:
+        paths = [stages[::-1], swap_dp(stages)[::-1]]
+        halving_seq = seq_stages[::-1]
+        owned_one = lax.psum_scatter(
+            part_one.reshape(-1, LANES), both, scatter_dimension=0, tiled=True
+        )
+        received = [send_half(p, path[0]) for p, path in zip((part_two, part_three), paths)]
+        first = attention_backward(operands_of(0), BLOCKS, attention_rows)
+        received = together(*received, *first)
+        first = received[2:]
+        parts = [halve_step(part_two, received[0]), halve_step(part_three, received[1])]
+        first_across, *parts = together(first[2], *parts)
+        received = [send_half(p, path[1]) for p, path in zip(parts, paths)]
+        second = attention_backward(
+            operands_of(1),
+            BLOCKS,
+            attention_rows,
+            (orders[0], w_project, first_across, first[3]),
+        )
+        received = together(*received, *second)
+        attention_grads, d_queries_two, d_window_two, gain_one = received[2:]
+        parts = [halve_step(p, r) for p, r in zip(parts, received)]
+        d_queries = jnp.stack([first[0], d_queries_two], 0)
+        d_window = jnp.stack([first[1], d_window_two], 1)
+        gains_total = jnp.stack([gain_one[:, 0], gain_two[:, 0]], 0) / norm_gains
+        for index, stage in enumerate(paths[0]):
+            arrivals = {
+                "attention": send_half(attention_grads, stage),
+                "gains": exchange(gains_total, stage[0], stage[1]),
+            }
+            if index + 2 < len(paths[0]):
+                arrivals["two"] = send_half(parts[0], paths[0][index + 2])
+                arrivals["three"] = send_half(parts[1], paths[1][index + 2])
+            if index < len(halving_seq):
+                arrivals["window"] = send_half(d_window, halving_seq[index])
+            arrivals = lax.optimization_barrier(arrivals)
+            attention_grads = halve_step(attention_grads, arrivals["attention"])
+            gains_total = gains_total + arrivals["gains"]
+            if "two" in arrivals:
+                parts = [
+                    halve_step(parts[0], arrivals["two"]),
+                    halve_step(parts[1], arrivals["three"]),
+                ]
+            if "window" in arrivals:
+                d_window = halve_step(d_window, arrivals["window"])
+        attention_owned = attention_grads.reshape(-1)
+        d_own = d_window[0]
+        feedforward_owned = jnp.concatenate(
+            [owned_one, parts[0][0], parts[1][0]], 0
+        ).reshape(-1)
     else:
+        grads = jnp.concatenate([part_one, part_two, part_three], 1).reshape(-1)
+        feedforward_owned = lax.psum_scatter(grads, both, scatter_dimension=0, tiled=True)
+        first = attention_backward(operands_of(0), BLOCKS, attention_rows)
+        attention_grads, d_queries_two, d_window_two, gain_one = attention_backward(
+            operands_of(1), BLOCKS, attention_rows, (orders[0], w_project, first[2], first[3])
+        )
         attention_owned = lax.psum_scatter(
             attention_grads.reshape(-1), both, scatter_dimension=0, tiled=True
         )
-    if paired:
-        d_own = halved(d_window, seq_stages)[0]
-    else:
+        d_queries = jnp.stack([first[0], d_queries_two], 0)
+        d_window = jnp.stack([first[1], d_window_two], 1)
         d_own = d_window[0].astype(F32)
         for step in range(1, reach + 1):
             d_own = d_own + lax.ppermute(
                 d_window[step], "seq", [(p, p - step) for p in range(step, seq_count)]
             ).astype(F32)
         d_own = d_own.astype(BF16)
+        gains_total = jnp.stack([gain_one[:, 0], gain_two[:, 0]], 0) / norm_gains
+        gains_total = lax.psum(gains_total, both)
     d_normed_one = matmul("met,de->mtd", jnp.concatenate([d_queries, d_own], 1), w_project)
     unit_one, inverse_one = unit_norm(own_inputs.astype(F32))
     input_grad = d_residual + norm_backward(d_normed_one, unit_one, inverse_one, norm_gains[0])
-
-    gains_total = jnp.stack([gain_one[:, 0], gain_two[:, 0]], 0) / norm_gains
-    if butterfly:
-        for axis, bit, unused_flat in stages:
-            gains_total = gains_total + exchange(gains_total, axis, bit)
-    else:
-        gains_total = lax.psum(gains_total, both)
 
     attention_place = owner_place * attention_length + jnp.arange(attention_length, dtype=jnp.int32)
     attention_rate = jnp.where(

time: 242 us -> 285 us (1.18); the launches traced: 238 us -> 284 us
  waiting for transfers between devices: 93.4 us -> 118 us
  starting transfers between devices: 25.3 us -> 33.3 us
  Pallas kernels: 53.3 us -> 59.7 us
  local copies, waits for them, and re-layouts: 25 us -> 29.5 us
  other arithmetic: 25 us -> 28.3 us
    unnamed x3, waiting for transfers between devices: 26.5 us -> 44.1 us
    ppermute x21 -> x31, starting transfers between devices: 25.3 us -> 33.3 us  [exchange(): lax.ppermute(value, axis, [(place, place ^ bit) for place in range(count)])]
    convert_element_type x6 -> x14, other arithmetic: 3.38 us -> 11.2 us  [halve_step(): return (blocks[:half].astype(F32) + received.astype(F32)).astype(BF16)]
    concatenate x6 -> x5, other arithmetic: 7.87 us -> 0.39 us  [the longest x2 0.31 us: on_device(): window_inputs = jnp.concatenate([window_inputs, inputs_far], 0)]
    ppermute x21 -> x31, waiting for transfers between devices: 67 us -> 74.1 us  [exchange(): lax.ppermute(value, axis, [(place, place ^ bit) for place in range(count)])]
    slice x8 -> x18, local copies, waits for them, and re-layouts: 3.51 us -> 8.77 us  [the longest x17 8.73 us: send_half(): return exchange(blocks[blocks.shape[0] // 2:], axis, bit)]
    squeeze x0 -> x8, local copies, waits for them, and re-layouts: none -> 4.71 us  [the longest x1 1.79 us: operands_of(): normed_one[micro]]
    ppermute x3 -> x0, local copies, waits for them, and re-layouts: 4.67 us -> none  [exchange(): lax.ppermute(value, axis, [(place, place ^ bit) for place in range(count)])]
  transfers between devices with their start and end apart: 23 -> 33, of which waited for: 13 -> 13; matrix products, arithmetic and copies ran while one was open for 19% -> 16% of each run, Pallas kernels for 16% -> 16%
where the time goes in v1:
time: 285 us; the launch traced here: 284 us
  waiting for transfers between devices  118 us (41%)
  Pallas kernels  59.7 us (21%)
  starting transfers between devices  33.3 us (12%)
  local copies, waits for them, and re-layouts  29.5 us (10%)
  other arithmetic  28.3 us (10%)
  between operations  14.8 us (5%)
    ppermute x31, waiting for transfers between devices, exchange(): lax.ppermute(value, axis, [(place, place ^ bit) for place in range(count)])  74.1 us
    unnamed x3, waiting for transfers between devices  44.1 us
    ppermute x31, starting transfers between devices, exchange(): lax.ppermute(value, axis, [(place, place ^ bit) for place in range(count)])  33.3 us
    pallas_call x2, Pallas kernels, attention_backward(): pl.pallas_call(kernel, out_shape=outputs, in_specs=in_specs, out_specs=tu...  24.5 us
    pallas_call x1, Pallas kernels, attention_forward(): pl.pallas_call(attention_forward_kernel, out_shape=(shape((D, QKV_WIDTH),...  19.8 us
    pallas_call x1, Pallas kernels, feedforward(): pl.pallas_call(feedforward_kernel, out_shape=(shape((tokens, D), BF16), s...  15.3 us
    convert_element_type x14, other arithmetic, halve_step(): return (blocks[:half].astype(F32) + received.astype(F32)).astype(BF16)  11.2 us
    unnamed x88, local copies, waits for them, and re-layouts  11.1 us
  transfers between devices with their start and end apart: 33, of which 13 were waited for; matrix products, arithmetic and copies ran while one was open for 16% of the time, Pallas kernels for 16%

profile of v1, /device:TPU:0, one launch (start us, length us, event | category | flops | bytes accessed | tf_op | source)
XLA Modules:
  0.0 284.4 jit_solution(14947007600781819260)
XLA Ops:
  7.2 1.7 convert_bitcast_fusion
  9.0 1.5 constant_dynamic-update-slice_fusion.4
  10.5 4.0 %collective-permute-start = (bf16[1,216,128]{2,1,0:T(8,128)(2,1)S(1)}, bf16[1,216,128]{2,1,0:T(8,128)(2,1)S(1)}, u32[]{:S(2)}, u32[]{:S(2)}) collective-permute-start(bf16[1,216,128]{2,1,0:T(8,128)(2,1)S(1)} %get-tuple-element.201), channel_id=1, source_target_pairs={{0,4},{1,5},{2,6},{3,7},{4,0},{5,1},{6,2},{7,3},{8,12},{9,13},{10,... | collective-permute-start | bytes 165896 | tf_op jit(solution)/shard_map/ppermute | solution.py:46
  14.5 1.2 copy.48
  15.8 1.0 reduce_window_sum.12
  18.4 1.0 multiply_sine_fusion
  19.7 16.3 %collective-permute-done.1 = bf16[1,2,128,576]{3,2,1,0:T(8,128)(2,1)S(1)} collective-permute-done((bf16[1,2,128,576]{3,2,1,0:T(8,128)(2,1)S(1)}, bf16[1,2,128,576]{3,2,1,0:T(8,128)(2,1)S(1)}, u32[]{:S(2)}, u32[]{:S(2)}) %collective-permute-start.1) | collective-permute-done | bytes 294944 | tf_op jit(solution)/shard_map/ppermute | solution.py:46
  36.6 1.3 and_select_fusion.bias
  37.9 2.1 collective-permute-start.2
  40.0 19.9 %collective-permute-done.2 = bf16[2,216,128]{2,1,0:T(8,128)(2,1)S(1)} collective-permute-done((bf16[2,216,128]{2,1,0:T(8,128)(2,1)S(1)}, bf16[2,216,128]{2,1,0:T(8,128)(2,1)S(1)}, u32[]{:S(2)}, u32[]{:S(2)}) %collective-permute-start.2) | collective-permute-done | bytes 110624 | tf_op jit(solution)/shard_map/ppermute | solution.py:46
  61.3 1.8 collective-permute-start.4
  63.1 9.7 %collective-permute-done.4 = bf16[4,216,128]{2,1,0:T(8,128)(2,1)S(1)} collective-permute-done((bf16[4,216,128]{2,1,0:T(8,128)(2,1)S(1)}, bf16[4,216,128]{2,1,0:T(8,128)(2,1)S(1)}, u32[]{:S(2)}, u32[]{:S(2)}) %collective-permute-start.4) | collective-permute-done | bytes 221216 | tf_op jit(solution)/shard_map/ppermute | solution.py:46
  73.5 1.4 collective-permute-start.6
  74.9 1.2 copy.55
  77.4 1.6 constant_dynamic-update-slice_fusion.1
  79.0 6.7 %collective-permute-done.6 = bf16[8,216,128]{2,1,0:T(8,128)(2,1)S(1)} collective-permute-done((bf16[8,216,128]{2,1,0:T(8,128)(2,1)S(1)}, bf16[8,216,128]{2,1,0:T(8,128)(2,1)S(1)}, u32[]{:S(2)}, u32[]{:S(2)}) %collective-permute-start.6) | collective-permute-done | bytes 442400 | tf_op jit(solution)/shard_map/ppermute | solution.py:46
  86.6 1.0 slice_bitcast_fusion.6
  87.6 2.4 copy.54.inputs_far
  90.0 0.9 copy-done.30
  91.0 19.8 %shard_map.230 = (bf16[576,960]{1,0:T(8,128)(2,1)}, bf16[576,576]{1,0:T(8,128)(2,1)}, bf16[2,1024,576]{2,1,0:T(8,128)(2,1)}, bf16[2,576,128]{2,1,0:T(8,128)(2,1)...) custom-call(s32[32]{0:T(128)S(1)} %broadcast_xor_fusion.1.order.orde, ...), custom_call_target="tpu_custom_call" | custom-call | tf_op jit(solution)/shard_map/pallas_call | solution.py:292
  110.9 1.0 copy-done.31
  112.0 15.3 %shard_map.231 = (bf16[256,576]{1,0:T(8,128)(2,1)S(1)}, f32[256,576]{1,0:T(8,128)S(1)}, bf16[32,216,128]{2,1,0:T(8,128)(2,1)}, bf16[32,216,128]{2,1,0:T(8,128)(2...) custom-call(s32[32]{0:T(128)S(1)} %iota.26.straight, s32[32]{0:T(128)S(1)} %broadcast_xor_fusion.1.order.order_two, ...), custom_call_target="tpu_custom_call" | custom-call | tf_op jit(solution)/shard_map/pallas_call | solution.py:404
  127.4 1.4 slice.179
  129.3 1.2 slice.180
  130.7 1.8 slice_bitcast_fusion
  132.6 0.9 copy-done.26
  133.5 1.7 slice_bitcast_fusion.2
  135.3 10.8 %shard_map.232 = (bf16[576,128]{1,0:T(8,128)(2,1)S(1)}, bf16[8,384,128]{2,1,0:T(8,128)(2,1)}, f32[960,576]{1,0:T(8,128)}, f32[576,576]{1,0:T(8,128)}) custom-call(bf16[576,576]{1,0:T(8,128)(2,1)} %get-tuple-element.94.refs_0_, bf16[1024,576]{1,0:T(8,128)(2,1)} %get-tuple-element.203.refs_1_, bf16[576,128]{1,0:T(8,128)(2,1)S(1)} %get-tuple-element.217.refs_2_, ...), custom_call_target="tpu_custom_call" | custom-call | tf_op jit(solution)/shard_map/pallas_call | solution.py:555
  146.1 1.5 add_convert_fusion.1
  149.6 2.3 collective-permute-start.11
  152.1 13.7 %shard_map.233 = (bf16[32,216,128]{2,1,0:T(8,128)(2,1)}, bf16[576,128]{1,0:T(8,128)(2,1)S(1)}, bf16[8,384,128]{2,1,0:T(8,128)(2,1)}, f32[576,1]{1,0:T(8,128)S(1)}) custom-call(s32[32]{0:T(128)S(1)} %broadcast_xor_fusion.1.order.order_two, bf16[576,960]{1,0:T(8,128)(2,1)} %get-tuple-element.112.w_project, f32[960,576]{1,0:T(8,128)} %get-tuple-element.113.first_across, ...), custom_call_target="tpu_custom_call" | custom-call | tf_op jit(solution)/shard_map/pallas_call | solution.py:555
  165.9 2.3 slice.208
  168.2 1.0 pad_maximum_fusion.1
  169.7 1.1 add_convert_fusion.5
  171.7 1.1 add_convert_fusion.6
  174.3 1.1 collective-permute-start.14
  175.8 1.0 collective-permute-done.13
  176.8 2.4 collective-permute-done.15
  179.2 2.7 collective-permute-done.14
  182.0 1.4 add_convert_fusion.3
  183.4 1.1 collective-permute-start.21
  184.5 1.0 add_convert_fusion.9
  185.5 1.1 collective-permute-start.20
  186.6 1.0 add_convert_fusion.10
  187.6 1.1 collective-permute-start.19
  188.7 1.5 add_convert_fusion
  190.2 1.5 collective-permute-start.17
  192.4 8.1 %collective-permute-done.18 = f32[2,576]{1,0:T(2,128)S(1)} collective-permute-done((f32[2,576]{1,0:T(2,128)S(1)}, f32[2,576]{1,0:T(2,128)S(1)}, u32[]{:S(2)}, u32[]{:S(2)}) %collective-permute-start.18) | collective-permute-done | bytes 4640 | tf_op jit(solution)/shard_map/ppermute | solution.py:46
  201.4 2.9 %collective-permute-start.26 = (bf16[1,2,384,128]{3,2,0,1:T(8,128)(2,1)}, bf16[1,2,384,128]{3,2,0,1:T(8,128)(2,1)}, u32[]{:S(2)}, u32[]{:S(2)}) collective-permute-start(bf16[1,2,384,128]{3,2,0,1:T(8,128)(2,1)} %slice.256), channel_id=1, source_target_pairs={{0,4},{1,5},{2,6},{3,7},{4,0},{5,1},{6,2},{7,3},{8,12},{9,13},{10,... | collective-permute-start | bytes 589832 | tf_op jit(solution)/shard_map/ppermute | solution.py:46
  205.3 1.4 collective-permute-start.22
  206.7 2.9 %collective-permute-start.24 = (bf16[1,216,128]{2,1,0:T(8,128)(2,1)S(1)}, bf16[1,216,128]{2,1,0:T(8,128)(2,1)}, u32[]{:S(2)}, u32[]{:S(2)}) collective-permute-start(bf16[1,216,128]{2,1,0:T(8,128)(2,1)S(1)} %slice.253), channel_id=1, source_target_pairs={{0,4},{1,5},{2,6},{3,7},{4,0},{5,1},{6,2},{7,3},{8,12},{9,13},{10,... | collective-permute-start | bytes 165896 | tf_op jit(solution)/shard_map/ppermute | solution.py:46
  210.6 0.9 copy.58
  211.5 1.7 collective-permute-done.23
  213.2 2.2 collective-permute-done.25
  216.1 1.0 add_convert_fusion.8
  217.1 2.1 collective-permute-start.27
  220.9 1.0 fusion.17
  222.4 44.1 %reduce-scatter.4.cloned.1.call-done = bf16[216,128]{1,0:T(8,128)(2,1)} async-done(((bf16[6912,128]{1,0:T(8,128)(2,1)}), bf16[216,128]{1,0:T(8,128)(2,1)}) %reduce-scatter.4.cloned.1.call-update) | async-done | bytes 55312
  266.5 2.0 multiply_subtract_fusion
  268.5 1.5 collective-permute-start.30
  270.0 0.9 add_convert_fusion.12
  271.0 1.5 collective-permute-start.29
  272.5 0.9 fusion.8
  273.5 2.6 collective-permute-done.29
  (187 shorter events, 21.0 us)
Async XLA Ops:
  7.2 104.8 %all-gather.2.cloned.1.call-start = ((), (), s32[]{:S(2)}) async-start(), calls=%async_computation.1 | async-start | bytes 5474304 | tf_op jit(solution)/shard_map/all_gather | solution.py:617
  8.9 257.6 %reduce-scatter.4.cloned.1.call-start = ((), (), s32[]{:S(2)}) async-start(), calls=%async_computation.2 | async-start | bytes 1824768
  10.5 9.2 %collective-permute-start = (bf16[1,216,128]{2,1,0:T(8,128)(2,1)S(1)}, bf16[1,216,128]{2,1,0:T(8,128)(2,1)S(1)}, u32[]{:S(2)}, u32[]{:S(2)}) collective-permute-start(bf16[1,216,128]{2,1,0:T(8,128)(2,1)S(1)} %get-tuple-element.201), channel_id=1, source_target_pairs={{0,4},{1,5},{2,6},{3,7},{4,0},{5,1},{6,2},{7,3},{8,12},{9,13},{10,... | collective-permute-start | bytes 165896 | tf_op jit(solution)/shard_map/ppermute | solution.py:46
  15.7 20.3 %collective-permute-start.1 = (bf16[1,2,128,576]{3,2,1,0:T(8,128)(2,1)S(1)}, bf16[1,2,128,576]{3,2,1,0:T(8,128)(2,1)S(1)}, u32[]{:S(2)}, u32[]{:S(2)}) collective-permute-start(bf16[1,2,128,576]{3,2,1,0:T(8,128)(2,1)S(1)} %bitcast.109), channel_id=1, source_target_pairs={{0,4},{1,5},{2,6},{3,7},{4,0},{5,1},{6,2},{7,3},{8,12},{9,13},{10,... | collective-permute-start | bytes 884744 | tf_op jit(solution)/shard_map/ppermute | solution.py:46
  36.4 23.4 %collective-permute-start.3 = (bf16[2,2,128,576]{2,3,1,0:T(8,128)(2,1)S(1)}, bf16[2,2,128,576]{2,3,1,0:T(8,128)(2,1)S(1)}, u32[]{:S(2)}, u32[]{:S(2)}) collective-permute-start(bf16[2,2,128,576]{2,3,1,0:T(8,128)(2,1)S(1)} %copy.51), channel_id=1, source_target_pairs={{0,2},{1,3},{2,0},{3,1},{4,6},{5,7},{6,4},{7,5},{8,10},{9,11},{10,... | collective-permute-start | bytes 1769480 | tf_op jit(solution)/shard_map/ppermute | solution.py:46
  37.9 21.9 %collective-permute-start.2 = (bf16[2,216,128]{2,1,0:T(8,128)(2,1)S(1)}, bf16[2,216,128]{2,1,0:T(8,128)(2,1)S(1)}, u32[]{:S(2)}, u32[]{:S(2)}) collective-permute-start(bf16[2,216,128]{2,1,0:T(8,128)(2,1)S(1)} %pad_maximum_fusion.5), channel_id=1, source_target_pairs={{0,2},{1,3},{2,0},{3,1},{4,6},{5,7},{6,4},{7,5},{8,10},{9,11},{10,... | collective-permute-start | bytes 331784 | tf_op jit(solution)/shard_map/ppermute | solution.py:46
  60.4 12.5 %copy-start.5 = (bf16[4,2,128,576]{3,2,1,0:T(8,128)(2,1)}, bf16[4,2,128,576]{3,2,1,0:T(8,128)(2,1)S(1)}, u32[]{:S(2)}) copy-start(bf16[4,2,128,576]{3,2,1,0:T(8,128)(2,1)S(1)} %pad_maximum_fusion.inputs_near) | copy-start | bytes 3538948
  61.2 11.6 %collective-permute-start.5 = (bf16[4,2,128,576]{2,3,1,0:T(8,128)(2,1)S(1)}, bf16[4,2,128,576]{2,3,1,0:T(8,128)(2,1)}, u32[]{:S(2)}, u32[]{:S(2)}) collective-permute-start(bf16[4,2,128,576]{2,3,1,0:T(8,128)(2,1)S(1)} %copy.53), channel_id=1, source_target_pairs={{0,1},{1,0},{2,3},{3,2},{4,5},{5,4},{6,7},{7,6},{8,9},{9,8},{10,11... | collective-permute-start | bytes 3538952 | tf_op jit(solution)/shard_map/ppermute | solution.py:46
  61.3 25.2 %copy-start.40 = (s32[32]{0:T(128)S(1)}, s32[32]{0:T(128)}, u32[]{:S(2)}) copy-start(s32[32]{0:T(128)} %constant.29.clone) | copy-start | bytes 388
  61.3 25.2 %copy-start.39 = (s32[32]{0:T(128)S(1)}, s32[32]{0:T(128)}, u32[]{:S(2)}) copy-start(s32[32]{0:T(128)} %constant.30.clone) | copy-start | bytes 388
  61.3 11.5 %collective-permute-start.4 = (bf16[4,216,128]{2,1,0:T(8,128)(2,1)S(1)}, bf16[4,216,128]{2,1,0:T(8,128)(2,1)S(1)}, u32[]{:S(2)}, u32[]{:S(2)}) collective-permute-start(bf16[4,216,128]{2,1,0:T(8,128)(2,1)S(1)} %pad_maximum_fusion.4), channel_id=1, source_target_pairs={{0,16},{8,24},{16,0},{24,8},{1,17},{9,25},{17,1},{25,9},{2,18},{10... | collective-permute-start | bytes 663560 | tf_op jit(solution)/shard_map/ppermute | solution.py:46
  73.5 12.1 %collective-permute-start.6 = (bf16[8,216,128]{2,1,0:T(8,128)(2,1)S(1)}, bf16[8,216,128]{2,1,0:T(8,128)(2,1)S(1)}, u32[]{:S(2)}, u32[]{:S(2)}) collective-permute-start(bf16[8,216,128]{2,1,0:T(8,128)(2,1)S(1)} %pad_maximum_fusion.3), channel_id=1, source_target_pairs={{0,8},{8,0},{16,24},{24,16},{1,9},{9,1},{17,25},{25,17},{2,10},{10... | collective-permute-start | bytes 1327112 | tf_op jit(solution)/shard_map/ppermute | solution.py:46
  76.1 10.5 %copy-start.6 = (f32[2,1024,128]{2,1,0:T(8,128)S(1)}, f32[2,1024,128]{2,1,0:T(8,128)}, u32[]{:S(2)}) copy-start(f32[2,1024,128]{2,1,0:T(8,128)} %and_select_fusion.bias) | copy-start | bytes 3145732
  86.5 3.6 %collective-permute-start.7 = (bf16[16,216,128]{2,1,0:T(8,128)(2,1)}, bf16[16,216,128]{2,1,0:T(8,128)(2,1)S(1)}, u32[]{:S(2)}, u32[]{:S(2)}) collective-permute-start(bf16[16,216,128]{2,1,0:T(8,128)(2,1)} %constant_dynamic-update-slice_fusion.weights_near), channel_id=1, source_target_pairs={{0,1},{1,0},{2,3},{3,2},{4,5},{5,4},{6,7},{7,6},{8,9},{9,8},{10,11... | collective-permute-start | bytes 2654216 | tf_op jit(solution)/shard_map/ppermute | solution.py:46
  87.6 3.4 %copy-start.2 = (f32[2,576]{1,0:T(2,128)S(1)}, f32[2,576]{1,0:T(2,128)}, u32[]{:S(2)}) copy-start(f32[2,576]{1,0:T(2,128)} %gains.3) | copy-start | bytes 13828
  127.4 3.2 %copy-start = (f32[576,1]{1,0:T(8,128)}, f32[576,1]{1,0:T(8,128)S(1)}, u32[]{:S(2)}) copy-start(f32[576,1]{1,0:T(8,128)S(1)} %get-tuple-element.124) | copy-start | bytes 6916
  127.4 3.3 %copy-start.17 = (bf16[2,1024,576]{2,1,0:T(8,128)(2,1)S(1)}, bf16[2,1024,576]{2,1,0:T(8,128)(2,1)}, u32[]{:S(2)}) copy-start(bf16[2,1024,576]{2,1,0:T(8,128)(2,1)} %get-tuple-element.95) | copy-start | bytes 7077892
  128.8 17.3 %collective-permute-start.8 = (bf16[16,216,128]{2,1,0:T(8,128)(2,1)S(1)}, bf16[16,216,128]{2,1,0:T(8,128)(2,1)S(1)}, u32[]{:S(2)}, u32[]{:S(2)}) collective-permute-start(bf16[16,216,128]{2,1,0:T(8,128)(2,1)S(1)} %slice.179), channel_id=1, source_target_pairs={{0,1},{1,0},{2,3},{3,2},{4,5},{5,4},{6,7},{7,6},{8,9},{9,8},{10,11... | collective-permute-start | bytes 2654216 | tf_op jit(solution)/shard_map/ppermute | solution.py:46
  130.6 15.5 %collective-permute-start.9 = (bf16[16,216,128]{2,1,0:T(8,128)(2,1)S(1)}, bf16[16,216,128]{2,1,0:T(8,128)(2,1)}, u32[]{:S(2)}, u32[]{:S(2)}) collective-permute-start(bf16[16,216,128]{2,1,0:T(8,128)(2,1)S(1)} %slice.180), channel_id=1, source_target_pairs={{0,1},{1,0},{2,3},{3,2},{4,5},{5,4},{6,7},{7,6},{8,9},{9,8},{10,11... | collective-permute-start | bytes 2654216 | tf_op jit(solution)/shard_map/ppermute | solution.py:46
  130.7 2.8 copy-start.26
  135.3 10.8 %copy-start.20 = (bf16[32,216,128]{2,1,0:T(8,128)(2,1)S(1)}, bf16[32,216,128]{2,1,0:T(8,128)(2,1)}, u32[]{:S(2)}) copy-start(bf16[32,216,128]{2,1,0:T(8,128)(2,1)} %get-tuple-element.93) | copy-start | bytes 5308420
  146.1 2.1 copy-start.3
  147.9 4.1 %copy-start.1 = (f32[576,1]{1,0:T(8,128)S(1)}, f32[576,1]{1,0:T(8,128)}, u32[]{:S(2)}) copy-start(f32[576,1]{1,0:T(8,128)} %copy-done) | copy-start | bytes 6916
  148.2 17.7 %collective-permute-start.10 = (bf16[8,216,128]{2,1,0:T(8,128)(2,1)S(1)}, bf16[8,216,128]{2,1,0:T(8,128)(2,1)}, u32[]{:S(2)}, u32[]{:S(2)}) collective-permute-start(bf16[8,216,128]{2,1,0:T(8,128)(2,1)S(1)} %slice.194), channel_id=1, source_target_pairs={{0,8},{8,0},{16,24},{24,16},{1,9},{9,1},{17,25},{25,17},{2,10},{10... | collective-permute-start | bytes 1327112 | tf_op jit(solution)/shard_map/ppermute | solution.py:46
  149.6 16.3 %collective-permute-start.11 = (bf16[8,216,128]{2,1,0:T(8,128)(2,1)}, bf16[8,216,128]{2,1,0:T(8,128)(2,1)}, u32[]{:S(2)}, u32[]{:S(2)}) collective-permute-start(bf16[8,216,128]{2,1,0:T(8,128)(2,1)} %slice.195), channel_id=1, source_target_pairs={{0,16},{8,24},{16,0},{24,8},{1,17},{9,25},{17,1},{25,9},{2,18},{10... | collective-permute-start | bytes 1327112 | tf_op jit(solution)/shard_map/ppermute | solution.py:46
  165.9 2.4 copy-start.11
  165.9 2.4 copy-start.13
  168.2 13.7 %collective-permute-start.12 = (bf16[16,216,128]{2,1,0:T(8,128)(2,1)}, bf16[16,216,128]{2,1,0:T(8,128)(2,1)}, u32[]{:S(2)}, u32[]{:S(2)}) collective-permute-start(bf16[16,216,128]{2,1,0:T(8,128)(2,1)} %slice.208), channel_id=1, source_target_pairs={{0,1},{1,0},{2,3},{3,2},{4,5},{5,4},{6,7},{7,6},{8,9},{9,8},{10,11... | collective-permute-start | bytes 2654216 | tf_op jit(solution)/shard_map/ppermute | solution.py:46
  168.2 3.4 %copy-start.8 = (bf16[16,216,128]{2,1,0:T(8,128)(2,1)S(1)}, bf16[16,216,128]{2,1,0:T(8,128)(2,1)}, u32[]{:S(2)}) copy-start(bf16[16,216,128]{2,1,0:T(8,128)(2,1)} %copy-done.7) | copy-start | bytes 2654212
  169.2 12.7 %collective-permute-start.16 = (bf16[4,2,384,128]{3,2,0,1:T(8,128)(2,1)}, bf16[4,2,384,128]{3,2,0,1:T(8,128)(2,1)}, u32[]{:S(2)}, u32[]{:S(2)}) collective-permute-start(bf16[4,2,384,128]{3,2,0,1:T(8,128)(2,1)} %pad_maximum_fusion.1), channel_id=1, source_target_pairs={{0,1},{1,0},{2,3},{3,2},{4,5},{5,4},{6,7},{7,6},{8,9},{9,8},{10,11... | collective-permute-start | bytes 2359304 | tf_op jit(solution)/shard_map/ppermute | solution.py:46
  170.9 4.8 %copy-start.15 = (bf16[2,1,128,576]{2,3,1,0:T(8,128)(2,1)S(1)}, bf16[2,1,128,576]{2,3,1,0:T(8,128)(2,1)}, u32[]{:S(2)}) copy-start(bf16[2,1,128,576]{2,3,1,0:T(8,128)(2,1)} %param.15) | copy-start | bytes 884740
  171.6 7.7 %collective-permute-start.15 = (bf16[4,216,128]{2,1,0:T(8,128)(2,1)}, bf16[4,216,128]{2,1,0:T(8,128)(2,1)}, u32[]{:S(2)}, u32[]{:S(2)}) collective-permute-start(bf16[4,216,128]{2,1,0:T(8,128)(2,1)} %slice.241), channel_id=1, source_target_pairs={{0,16},{8,24},{16,0},{24,8},{1,17},{9,25},{17,1},{25,9},{2,18},{10... | collective-permute-start | bytes 663560 | tf_op jit(solution)/shard_map/ppermute | solution.py:46
  173.6 8.4 %copy-start.12 = (bf16[8,384,128]{2,1,0:T(8,128)(2,1)S(1)}, bf16[8,384,128]{2,1,0:T(8,128)(2,1)}, u32[]{:S(2)}) copy-start(bf16[8,384,128]{2,1,0:T(8,128)(2,1)} %get-tuple-element.120) | copy-start | bytes 2359300
  173.6 8.4 %copy-start.14 = (bf16[8,384,128]{2,1,0:T(8,128)(2,1)S(1)}, bf16[8,384,128]{2,1,0:T(8,128)(2,1)}, u32[]{:S(2)}) copy-start(bf16[8,384,128]{2,1,0:T(8,128)(2,1)} %get-tuple-element.121) | copy-start | bytes 2359300
  174.3 7.7 %collective-permute-start.14 = (bf16[4,216,128]{2,1,0:T(8,128)(2,1)}, bf16[4,216,128]{2,1,0:T(8,128)(2,1)}, u32[]{:S(2)}, u32[]{:S(2)}) collective-permute-start(bf16[4,216,128]{2,1,0:T(8,128)(2,1)} %slice.240), channel_id=1, source_target_pairs={{0,8},{8,0},{16,24},{24,16},{1,9},{9,1},{17,25},{25,17},{2,10},{10... | collective-permute-start | bytes 663560 | tf_op jit(solution)/shard_map/ppermute | solution.py:46
  175.6 1.2 collective-permute-start.13
  175.8 8.7 %copy-start.22 = (bf16[8,216,128]{2,1,0:T(8,128)(2,1)S(1)}, bf16[8,216,128]{2,1,0:T(8,128)(2,1)}, u32[]{:S(2)}) copy-start(bf16[8,216,128]{2,1,0:T(8,128)(2,1)} %copy-done.21) | copy-start | bytes 1327108
  182.0 4.6 %copy-start.24 = (bf16[8,216,128]{2,1,0:T(8,128)(2,1)S(1)}, bf16[8,216,128]{2,1,0:T(8,128)(2,1)}, u32[]{:S(2)}) copy-start(bf16[8,216,128]{2,1,0:T(8,128)(2,1)} %copy-done.23) | copy-start | bytes 1327108
  183.4 5.3 %copy-start.18 = (bf16[32,216,128]{2,1,0:T(8,128)(2,1)S(1)}, bf16[32,216,128]{2,1,0:T(8,128)(2,1)}, u32[]{:S(2)}) copy-start(bf16[32,216,128]{2,1,0:T(8,128)(2,1)} %get-tuple-element.122) | copy-start | bytes 5308420
  183.4 17.1 %collective-permute-start.21 = (bf16[2,2,384,128]{3,2,0,1:T(8,128)(2,1)S(1)}, bf16[2,2,384,128]{3,2,0,1:T(8,128)(2,1)S(1)}, u32[]{:S(2)}, u32[]{:S(2)}) collective-permute-start(bf16[2,2,384,128]{3,2,0,1:T(8,128)(2,1)S(1)} %slice.248), channel_id=1, source_target_pairs={{0,2},{1,3},{2,0},{3,1},{4,6},{5,7},{6,4},{7,5},{8,10},{9,11},{10,... | collective-permute-start | bytes 1179656 | tf_op jit(solution)/shard_map/ppermute | solution.py:46
  185.5 15.0 %collective-permute-start.20 = (bf16[2,216,128]{2,1,0:T(8,128)(2,1)S(1)}, bf16[2,216,128]{2,1,0:T(8,128)(2,1)S(1)}, u32[]{:S(2)}, u32[]{:S(2)}) collective-permute-start(bf16[2,216,128]{2,1,0:T(8,128)(2,1)S(1)} %slice.247), channel_id=1, source_target_pairs={{0,2},{1,3},{2,0},{3,1},{4,6},{5,7},{6,4},{7,5},{8,10},{9,11},{10,... | collective-permute-start | bytes 331784 | tf_op jit(solution)/shard_map/ppermute | solution.py:46
  187.6 12.9 %collective-permute-start.19 = (bf16[2,216,128]{2,1,0:T(8,128)(2,1)S(1)}, bf16[2,216,128]{2,1,0:T(8,128)(2,1)S(1)}, u32[]{:S(2)}, u32[]{:S(2)}) collective-permute-start(bf16[2,216,128]{2,1,0:T(8,128)(2,1)S(1)} %slice.245), channel_id=1, source_target_pairs={{0,2},{1,3},{2,0},{3,1},{4,6},{5,7},{6,4},{7,5},{8,10},{9,11},{10,... | collective-permute-start | bytes 331784 | tf_op jit(solution)/shard_map/ppermute | solution.py:46
  190.2 10.3 %collective-permute-start.17 = (bf16[8,216,128]{2,1,0:T(8,128)(2,1)S(1)}, bf16[8,216,128]{2,1,0:T(8,128)(2,1)S(1)}, u32[]{:S(2)}, u32[]{:S(2)}) collective-permute-start(bf16[8,216,128]{2,1,0:T(8,128)(2,1)S(1)} %slice.243), channel_id=1, source_target_pairs={{0,8},{8,0},{16,24},{24,16},{1,9},{9,1},{17,25},{25,17},{2,10},{10... | collective-permute-start | bytes 1327112 | tf_op jit(solution)/shard_map/ppermute | solution.py:46
  191.7 8.9 %collective-permute-start.18 = (f32[2,576]{1,0:T(2,128)S(1)}, f32[2,576]{1,0:T(2,128)S(1)}, u32[]{:S(2)}, u32[]{:S(2)}) collective-permute-start(f32[2,576]{1,0:T(2,128)S(1)} %fusion.33), channel_id=1, source_target_pairs={{0,8},{8,0},{16,24},{24,16},{1,9},{9,1},{17,25},{25,17},{2,10},{10... | collective-permute-start | bytes 13832 | tf_op jit(solution)/shard_map/ppermute | solution.py:46
  201.4 14.7 %collective-permute-start.26 = (bf16[1,2,384,128]{3,2,0,1:T(8,128)(2,1)}, bf16[1,2,384,128]{3,2,0,1:T(8,128)(2,1)}, u32[]{:S(2)}, u32[]{:S(2)}) collective-permute-start(bf16[1,2,384,128]{3,2,0,1:T(8,128)(2,1)} %slice.256), channel_id=1, source_target_pairs={{0,4},{1,5},{2,6},{3,7},{4,0},{5,1},{6,2},{7,3},{8,12},{9,13},{10,... | collective-permute-start | bytes 589832 | tf_op jit(solution)/shard_map/ppermute | solution.py:46
  204.4 11.1 %collective-permute-start.25 = (bf16[1,216,128]{2,1,0:T(8,128)(2,1)S(1)}, bf16[1,216,128]{2,1,0:T(8,128)(2,1)}, u32[]{:S(2)}, u32[]{:S(2)}) collective-permute-start(bf16[1,216,128]{2,1,0:T(8,128)(2,1)S(1)} %slice.255), channel_id=1, source_target_pairs={{0,4},{1,5},{2,6},{3,7},{4,0},{5,1},{6,2},{7,3},{8,12},{9,13},{10,... | collective-permute-start | bytes 165896 | tf_op jit(solution)/shard_map/ppermute | solution.py:46
  205.3 10.8 %collective-permute-start.22 = (bf16[4,216,128]{2,1,0:T(8,128)(2,1)}, bf16[4,216,128]{2,1,0:T(8,128)(2,1)}, u32[]{:S(2)}, u32[]{:S(2)}) collective-permute-start(bf16[4,216,128]{2,1,0:T(8,128)(2,1)} %slice.251), channel_id=1, source_target_pairs={{0,16},{8,24},{16,0},{24,8},{1,17},{9,25},{17,1},{25,9},{2,18},{10... | collective-permute-start | bytes 663560 | tf_op jit(solution)/shard_map/ppermute | solution.py:46
  206.7 9.3 %collective-permute-start.24 = (bf16[1,216,128]{2,1,0:T(8,128)(2,1)S(1)}, bf16[1,216,128]{2,1,0:T(8,128)(2,1)}, u32[]{:S(2)}, u32[]{:S(2)}) collective-permute-start(bf16[1,216,128]{2,1,0:T(8,128)(2,1)S(1)} %slice.253), channel_id=1, source_target_pairs={{0,4},{1,5},{2,6},{3,7},{4,0},{5,1},{6,2},{7,3},{8,12},{9,13},{10,... | collective-permute-start | bytes 165896 | tf_op jit(solution)/shard_map/ppermute | solution.py:46
  209.6 3.6 %collective-permute-start.23 = (f32[2,576]{1,0:T(2,128)S(1)}, f32[2,576]{1,0:T(2,128)S(1)}, u32[]{:S(2)}, u32[]{:S(2)}) collective-permute-start(f32[2,576]{1,0:T(2,128)S(1)} %add.203), channel_id=1, source_target_pairs={{0,16},{8,24},{16,0},{24,8},{1,17},{9,25},{17,1},{25,9},{2,18},{10... | collective-permute-start | bytes 13832 | tf_op jit(solution)/shard_map/ppermute | solution.py:46
  210.3 11.5 %copy-start.4 = (bf16[576,128]{1,0:T(8,128)(2,1)S(1)}, bf16[576,128]{1,0:T(8,128)(2,1)}, u32[]{:S(2)}) copy-start(bf16[576,128]{1,0:T(8,128)(2,1)} %copy-done.3) | copy-start | bytes 442372
  210.3 11.5 %copy-start.16 = (bf16[2,1,128,576]{2,3,1,0:T(8,128)(2,1)S(1)}, bf16[2,1,128,576]{2,3,1,0:T(8,128)(2,1)}, u32[]{:S(2)}) copy-start(bf16[2,1,128,576]{2,3,1,0:T(8,128)(2,1)} %param.15) | copy-start | bytes 884740
  211.5 10.4 %copy-start.28 = (bf16[576,960]{1,0:T(8,128)(2,1)S(1)}, bf16[576,960]{1,0:T(8,128)(2,1)}, u32[]{:S(2)}) copy-start(bf16[576,960]{1,0:T(8,128)(2,1)} %get-tuple-element.112.w_project) | copy-start | bytes 3317764
  216.0 52.5 %collective-permute-start.28 = (f32[2,576]{1,0:T(2,128)S(1)}, f32[2,576]{1,0:T(2,128)S(1)}, u32[]{:S(2)}, u32[]{:S(2)}) collective-permute-start(f32[2,576]{1,0:T(2,128)S(1)} %add.211), channel_id=1, source_target_pairs={{0,2},{1,3},{2,0},{3,1},{4,6},{5,7},{6,4},{7,5},{8,10},{9,11},{10,... | collective-permute-start | bytes 13832 | tf_op jit(solution)/shard_map/ppermute | solution.py:46
  217.1 51.4 %collective-permute-start.27 = (bf16[2,216,128]{2,1,0:T(8,128)(2,1)S(1)}, bf16[2,216,128]{2,1,0:T(8,128)(2,1)}, u32[]{:S(2)}, u32[]{:S(2)}) collective-permute-start(bf16[2,216,128]{2,1,0:T(8,128)(2,1)S(1)} %slice.259), channel_id=1, source_target_pairs={{0,2},{1,3},{2,0},{3,1},{4,6},{5,7},{6,4},{7,5},{8,10},{9,11},{10,... | collective-permute-start | bytes 331784 | tf_op jit(solution)/shard_map/ppermute | solution.py:46
  221.9 44.6 %copy-start.27 = (f32[82944]{0:T(1024)S(1)}, f32[82944]{0:T(1024)}, u32[]{:S(2)}) copy-start(f32[82944]{0:T(1024)} %param.19) | copy-start | bytes 995332
  221.9 44.6 %copy-start.33 = (f32[82944]{0:T(1024)S(1)}, f32[82944]{0:T(1024)}, u32[]{:S(2)}) copy-start(f32[82944]{0:T(1024)} %param.23) | copy-start | bytes 995332
  221.9 44.6 %copy-start.34 = (f32[82944]{0:T(1024)S(1)}, f32[82944]{0:T(1024)}, u32[]{:S(2)}) copy-start(f32[82944]{0:T(1024)} %param.24) | copy-start | bytes 995332
  268.5 7.7 %copy-start.37 = (f32[2,576]{1,0:T(2,128)S(1)}, f32[2,576]{1,0:T(2,128)}, u32[]{:S(2)}) copy-start(f32[2,576]{1,0:T(2,128)} %param.25) | copy-start | bytes 13828
  268.5 7.7 %copy-start.38 = (f32[2,576]{1,0:T(2,128)S(1)}, f32[2,576]{1,0:T(2,128)}, u32[]{:S(2)}) copy-start(f32[2,576]{1,0:T(2,128)} %param.26) | copy-start | bytes 13828
  268.5 8.3 %copy-start.32 = (f32[27648]{0:T(1024)S(1)}, f32[27648]{0:T(1024)}, u32[]{:S(2)}) copy-start(f32[27648]{0:T(1024)} %param.18) | copy-start | bytes 331780
  268.5 8.3 %copy-start.35 = (f32[27648]{0:T(1024)S(1)}, f32[27648]{0:T(1024)}, u32[]{:S(2)}) copy-start(f32[27648]{0:T(1024)} %param.21) | copy-start | bytes 331780
  268.5 8.3 %copy-start.36 = (f32[27648]{0:T(1024)S(1)}, f32[27648]{0:T(1024)}, u32[]{:S(2)}) copy-start(f32[27648]{0:T(1024)} %param.22) | copy-start | bytes 331780
  268.5 4.9 %collective-permute-start.30 = (f32[2,576]{1,0:T(2,128)S(1)}, f32[2,576]{1,0:T(2,128)S(1)}, u32[]{:S(2)}, u32[]{:S(2)}) collective-permute-start(f32[2,576]{1,0:T(2,128)S(1)} %add.213), channel_id=1, source_target_pairs={{0,4},{1,5},{2,6},{3,7},{4,0},{5,1},{6,2},{7,3},{8,12},{9,13},{10,... | collective-permute-start | bytes 13832 | tf_op jit(solution)/shard_map/ppermute | solution.py:46
  271.0 5.1 %collective-permute-start.29 = (bf16[1,216,128]{2,1,0:T(8,128)(2,1)S(1)}, bf16[1,216,128]{2,1,0:T(8,128)(2,1)S(1)}, u32[]{:S(2)}, u32[]{:S(2)}) collective-permute-start(bf16[1,216,128]{2,1,0:T(8,128)(2,1)S(1)} %slice.261), channel_id=1, source_target_pairs={{0,4},{1,5},{2,6},{3,7},{4,0},{5,1},{6,2},{7,3},{8,12},{9,13},{10,... | collective-permute-start | bytes 165896 | tf_op jit(solution)/shard_map/ppermute | solution.py:46
  (10 other events, 11.9 us)
Sparse Core Ops, SparseCore 0:
  11.4 78.1 all-gather.1
  175.9 90.4 reduce-scatter.3

commit v2 on v1

--- a/solution.py
+++ b/solution.py
@@ -74,14 +74,15 @@
     return [next(turned) if stage[0] == "dp" else stage for stage in stages]
 
 
-def halve_step(blocks, received):
-    half = blocks.shape[0] // 2
-    return (blocks[:half].astype(F32) + received.astype(F32)).astype(BF16)
-
-
-def send_half(blocks, stage):
-    axis, bit, unused_flat = stage
-    return exchange(blocks[blocks.shape[0] // 2 :], axis, bit)
+def halve_step(kept, received):
+    half = kept.shape[0] // 2
+    kept, received = kept.astype(F32), received.astype(F32)
+    if half == 0:
+        return (kept + received, None)
+    return (
+        (kept[:half] + received[:half]).astype(BF16),
+        (kept[half:] + received[half:]).astype(BF16),
+    )
 
 
 def together(*values):
@@ -181,11 +182,11 @@
         first += count
 
 
-def store_blocks(order, flat, blocks, owner_rows, first_row):
+def store_blocks(order, flat, blocks, owner_rows, first_row, first_index):
     count, rows, unused = blocks.shape
 
     def move(index, unused):
-        start = pl.multiple_of(order[index] * owner_rows + first_row, 8)
+        start = pl.multiple_of(order[first_index + index] * owner_rows + first_row, 8)
         blocks[index] = flat[pl.ds(start, rows), :].astype(BF16)
         return unused
 
@@ -204,33 +205,12 @@
     return jnp.concatenate([first * cosine - second * sine, second * cosine + first * sine], 0)
 
 
-def attention_forward_kernel(
-    order,
-    weights_near,
-    weights_far,
-    inputs_near,
-    inputs_far,
-    cosines,
-    sines,
-    bias,
-    gains,
-    w_project,
-    w_output,
-    normed,
-    queries,
-    keys_across,
-    keys,
-    values,
-    log_totals,
-    mixed_across,
-    residual,
-    flat,
-    planes_one,
-    planes_two,
-    w_across,
-    values_across,
-):
-    load_blocks(order, (weights_near, weights_far), flat)
+def attention_forward_kernel(order, *refs):
+    weight_pieces, input_pieces, refs = refs[:4], refs[4:8], refs[8:]
+    cosines, sines, bias, gains, w_project, w_output, normed, queries = refs[:8]
+    keys_across, keys, values, log_totals, mixed_across, residual = refs[8:14]
+    flat, planes_one, planes_two, w_across, values_across = refs[14:]
+    load_blocks(order, weight_pieces, flat)
     unflatten_odd(flat, 0, D // 2, 7, planes_one)
     planes_to_matrix(planes_one, 7, w_project)
     for j in range(7):
@@ -238,16 +218,12 @@
     w_across[7 * LANES :, :] = jnp.transpose(planes_one[7])[:HALF].astype(BF16)
     unflatten_odd(flat, D * QKV_WIDTH // LANES, QUERY_WIDTH // 2, 4, planes_two)
     planes_to_matrix(planes_two, 4, w_output)
-    near_count = inputs_near.shape[0]
-    blocks = near_count + inputs_far.shape[0]
+    blocks = [piece.at[place] for piece in input_pieces for place in range(piece.shape[0])]
     gain = gains[0:1, :]
 
     def one(micro, unused):
-        for block in range(blocks):
-            if block < near_count:
-                rows = inputs_near[block, micro].astype(F32)
-            else:
-                rows = inputs_far[block - near_count, micro].astype(F32)
+        for block, inputs in enumerate(blocks):
+            rows = inputs[micro].astype(F32)
             inverse = lax.rsqrt(jnp.mean(rows * rows, axis=-1, keepdims=True) + NORM_EPSILON)
             normed[micro, block * DEVICE_TOKENS : (block + 1) * DEVICE_TOKENS, :] = (
                 rows * inverse * gain
@@ -279,16 +255,16 @@
             mixed_across[micro, rows, :] = dot(values_across[group_rows, :], low)
             log_totals[micro, head : head + 1, :] = top + jnp.log(total)
         mixed = jnp.transpose(mixed_across[micro]).astype(BF16)
-        residual[micro] = inputs_near[0, micro].astype(F32) + dot(mixed, w_output[...])
+        residual[micro] = blocks[0][micro].astype(F32) + dot(mixed, w_output[...])
         return unused
 
     lax.fori_loop(0, MICRO, one, 0)
 
 
-def attention_forward(order, weight_halves, input_halves, *tables):
-    window = sum(half.shape[0] for half in input_halves) * DEVICE_TOKENS
+def attention_forward(order, weight_pieces, input_pieces, *tables):
+    window = sum(piece.shape[0] for piece in input_pieces) * DEVICE_TOKENS
     shape = jax.ShapeDtypeStruct
-    rows = sum(half.shape[0] * half.shape[1] for half in weight_halves)
+    rows = sum(piece.shape[0] * piece.shape[1] for piece in weight_pieces)
     return pl.pallas_call(
         attention_forward_kernel,
         out_shape=(
@@ -303,7 +279,7 @@
             shape((MICRO, QUERY_WIDTH, DEVICE_TOKENS), F32),
             shape((MICRO, DEVICE_TOKENS, D), F32),
         ),
-        in_specs=[smem()] + vmem(4 + len(tables)),
+        in_specs=[smem()] + vmem(8 + len(tables)),
         out_specs=tuple(vmem(10)),
         scratch_shapes=[
             pltpu.VMEM((rows, LANES), F32),
@@ -313,22 +289,23 @@
             pltpu.VMEM((KV_WIDTH, window), BF16),
         ],
         compiler_params=params(),
-    )(order, *weight_halves, *input_halves, *tables)
+    )(order, *weight_pieces, *input_pieces, *tables)
 
 
 def feedforward_kernel(
     straight,
+    order_one,
     order_two,
-    order_three,
     weight_blocks,
     residual,
     cotangent,
     gains,
     block_output,
     d_residual,
-    grads_one,
-    grads_two,
-    grads_three,
+    one_kept,
+    one_sent,
+    two_kept,
+    two_sent,
     gain_grad,
     flat,
     planes,
@@ -346,11 +323,11 @@
     unflatten_odd(flat, D * columns, FF // 2, 4, planes)
     planes_to_matrix(planes, 4, w_down)
     gain = gains[1:2, :]
-    rows = residual[...]
+    rows = jnp.concatenate([residual[micro] for micro in range(MICRO)], 0)
     inverse = lax.rsqrt(jnp.mean(rows * rows, axis=-1, keepdims=True) + NORM_EPSILON)
     unit = rows * inverse
     normed = (unit * gain).astype(BF16)
-    cotangent_low = cotangent[...]
+    cotangent_low = jnp.concatenate([cotangent[micro, 0] for micro in range(MICRO)], 0)
     part = 256
     for start in range(0, FF, part):
         gate = dot(normed, w_gate_up[:, start : start + part])
@@ -386,33 +363,35 @@
         planes[4, start : start + part, :HALF] = grad[:, 4 * LANES :]
     flatten_odd(planes, FF // 2, 4, flat, D * columns)
     owner_rows = weight_blocks.shape[1]
-    first_row = 0
-    for order, blocks in (
-        (straight, grads_one),
-        (order_two, grads_two),
-        (order_three, grads_three),
-    ):
-        store_blocks(order, flat, blocks, owner_rows, first_row)
-        first_row += blocks.shape[1]
+    half = one_kept.shape[0]
+    middle = one_kept.shape[1]
+    store_blocks(order_one, flat, one_sent, owner_rows, 0, half)
+    store_blocks(order_two, flat, two_sent, owner_rows, middle, half)
+    store_blocks(order_one, flat, one_kept, owner_rows, 0, 0)
+    store_blocks(order_two, flat, two_kept, owner_rows, middle, 0)
 
 
 def feedforward(orders, weight_blocks, residual, cotangent, gains):
     shape = jax.ShapeDtypeStruct
-    part = shape((weight_blocks.shape[0], weight_blocks.shape[1] // 3, LANES), BF16)
-    tokens = residual.shape[0]
+    count, owner_rows, unused = weight_blocks.shape
+    middle = owner_rows // 32 * 16
+    one = shape((count // 2, middle, LANES), BF16)
+    two = shape((count // 2, owner_rows - middle, LANES), BF16)
+    tokens = residual.shape[0] * residual.shape[1]
     rows = weight_blocks.shape[0] * weight_blocks.shape[1]
     return pl.pallas_call(
         feedforward_kernel,
         out_shape=(
             shape((tokens, D), BF16),
             shape((tokens, D), F32),
-            part,
-            part,
-            part,
+            one,
+            one,
+            two,
+            two,
             shape((D, 1), F32),
         ),
         in_specs=[smem()] * 3 + vmem(4),
-        out_specs=tuple(vmem(6)),
+        out_specs=tuple(vmem(7)),
         scratch_shapes=[
             pltpu.VMEM((rows, LANES), F32),
             pltpu.VMEM((5, FF, LANES), F32),
@@ -488,22 +467,43 @@
     grad_output[...] = output_grad
 
 
+def micro_views(micro, operands):
+    w_output, *views = operands
+    views = [view.at[micro] for view in views]
+    views[7] = operands[8].at[micro * DEVICE_TOKENS : (micro + 1) * DEVICE_TOKENS, :]
+    return (w_output, *views)
+
+
 def attention_backward_first(*refs):
     operands, (d_queries, d_window, grad_across, grad_output, across, d_mixed) = (
         refs[:12],
         refs[12:],
     )
     attention_backward_body(
-        *operands, d_queries, d_window, across, grad_across, grad_output, d_mixed
-    )
-
-
-def attention_backward_second(order, w_project, first_across, first_output, *refs):
-    operands, (grad_blocks, d_queries, d_window, gain_grad) = refs[:12], refs[12:16]
-    flat, planes, across, d_mixed, grad_across, grad_output = refs[16:]
+        *micro_views(0, operands), d_queries, d_window, across, grad_across, grad_output, d_mixed
+    )
+
+
+def attention_backward_second(order, w_project, *refs):
+    first_queries, first_window, first_across, first_output = refs[:4]
+    operands, refs = refs[4:16], refs[16:]
+    kept, sent, d_queries, window_kept, window_sent, gain_grad, flat, planes = refs[:8]
+    across, d_mixed, own_window, grad_across, grad_output = refs[8:]
     attention_backward_body(
-        *operands, d_queries, d_window, across, grad_across, grad_output, d_mixed
-    )
+        *micro_views(1, operands),
+        d_queries.at[1],
+        own_window,
+        across,
+        grad_across,
+        grad_output,
+        d_mixed,
+    )
+    d_queries[0] = first_queries[...]
+    early = window_kept.shape[0]
+    for block in range(own_window.shape[0]):
+        target, place = (window_kept, block) if block < early else (window_sent, block - early)
+        target[place, 0] = first_window[block]
+        target[place, 1] = own_window[block]
     grad_across[...] += first_across[...]
     grad_output[...] += first_output[...]
     total = jnp.zeros((D, LANES), F32)
@@ -523,16 +523,14 @@
         planes[j] = grad_output[:, j * LANES : (j + 1) * LANES]
     planes[4, :, :HALF] = grad_output[:, 4 * LANES :]
     flatten_odd(planes, QUERY_WIDTH // 2, 4, flat, D * QKV_WIDTH // LANES)
-    store_blocks(order, flat, grad_blocks, grad_blocks.shape[1], 0)
+    store_blocks(order, flat, sent, sent.shape[1], 0, sent.shape[0])
+    store_blocks(order, flat, kept, kept.shape[1], 0, 0)
 
 
 def attention_backward(operands, count, rows, final=()):
     shape = jax.ShapeDtypeStruct
-    window = operands[1].shape[0]
-    outputs = (
-        shape((QUERY_WIDTH, DEVICE_TOKENS), BF16),
-        shape((window // DEVICE_TOKENS, 2 * KV_WIDTH, DEVICE_TOKENS), BF16),
-    )
+    window = operands[1].shape[1]
+    blocks = window // DEVICE_TOKENS
     sums = [(QKV_WIDTH, D), (QUERY_WIDTH, D)]
     scratch = [
         pltpu.VMEM((2 * KV_WIDTH, window), BF16),
@@ -540,17 +538,32 @@
     ]
     if final:
         kernel = attention_backward_second
-        outputs = (shape((count, rows, LANES), BF16), *outputs, shape((D, 1), F32))
+        half = shape((count // 2, rows, LANES), BF16)
+        late = blocks // 2
+        one_block = (MICRO, 2 * KV_WIDTH, DEVICE_TOKENS)
+        outputs = (
+            half,
+            half,
+            shape((MICRO, QUERY_WIDTH, DEVICE_TOKENS), BF16),
+            shape((blocks - late, *one_block), BF16),
+            shape((late, *one_block), BF16),
+            shape((D, 1), F32),
+        )
         scratch = [
             pltpu.VMEM((count * rows, LANES), F32),
             pltpu.VMEM((8, D, LANES), F32),
             *scratch,
+            pltpu.VMEM((blocks, 2 * KV_WIDTH, DEVICE_TOKENS), BF16),
             *[pltpu.VMEM(dims, F32) for dims in sums],
         ]
         in_specs = [smem()] + vmem(len(final) - 1 + len(operands))
     else:
         kernel = attention_backward_first
-        outputs = (*outputs, *[shape(dims, F32) for dims in sums])
+        outputs = (
+            shape((QUERY_WIDTH, DEVICE_TOKENS), BF16),
+            shape((blocks, 2 * KV_WIDTH, DEVICE_TOKENS), BF16),
+            *[shape(dims, F32) for dims in sums],
+        )
         in_specs = vmem(len(operands))
     return pl.pallas_call(
         kernel,
@@ -648,24 +661,27 @@
     if butterfly and paired:
         weights = attention_low.reshape(1, attention_length // LANES, LANES)
         window_inputs = own_inputs[None]
-        for index, (axis, bit, unused_flat) in enumerate(stages):
+        inputs_far = exchange(window_inputs, "seq", seq_stages[0][1])
+        for index, (axis, bit, unused_flat) in enumerate(stages[:-1]):
             far = exchange(weights, axis, bit)
-            if index < len(seq_stages):
-                other_axis, other_bit, unused_flat = seq_stages[index]
-                inputs_far = exchange(window_inputs, other_axis, other_bit)
-                far, inputs_far = together(far, inputs_far)
-                if index == 0:
-                    far, cosines, sines, bias = together(far, cosines, sines, bias)
-                if index < len(seq_stages) - 1:
-                    window_inputs = jnp.concatenate([window_inputs, inputs_far], 0)
-            if index < len(stages) - 1:
+            if index == 0:
+                far, cosines, sines, bias = together(far, cosines, sines, bias)
+            if index < len(stages) - 2:
                 weights = jnp.concatenate([weights, far], 0)
-        weight_halves = (weights, far)
-        input_halves = (window_inputs, inputs_far)
+            if 0 < index < len(seq_stages) - 1:
+                window_inputs = jnp.concatenate([window_inputs, inputs_far], 0)
+                far_weights, window_inputs = together(weights, window_inputs)
+                weights = far_weights
+                inputs_far = exchange(window_inputs, "seq", seq_stages[index][1])
+        axis, bit, unused_flat = stages[-1]
+        weight_pieces = [weights, far]
+        weight_pieces += [exchange(piece, axis, bit) for piece in weight_pieces]
+        input_pieces = [window_inputs, inputs_far]
+        input_pieces += [exchange(piece, axis, bit) for piece in input_pieces]
     else:
         weights = lax.all_gather(attention_low, both, axis=0, tiled=True)
         weights = weights.reshape(BLOCKS, -1, LANES)
-        weight_halves = (weights[: BLOCKS // 2], weights[BLOCKS // 2 :])
+        weight_pieces = jnp.split(weights, 4)
         window_inputs = jnp.stack(
             [own_inputs]
             + [
@@ -676,8 +692,9 @@
             ],
             0,
         )
-        middle = (reach + 1) // 2
-        input_halves = (window_inputs[:middle], window_inputs[middle:])
+        quarter = (reach + 1) // 4
+        cuts = [0, quarter, 2 * quarter, 3 * quarter, reach + 1]
+        input_pieces = [window_inputs[a:b] for a, b in zip(cuts, cuts[1:])]
         orders = [straight, straight]
 
     (
@@ -692,97 +709,85 @@
         mixed_across,
         residual,
     ) = attention_forward(
-        orders[0], weight_halves, input_halves, cosines, sines, bias, norm_gains
-    )
-    block_output, d_residual, part_one, part_two, part_three, gain_two = feedforward(
-        (straight, *orders),
-        feedforward_blocks,
-        residual.reshape(-1, D),
-        out_grad[:, 0].reshape(-1, D),
-        norm_gains,
+        orders[0], weight_pieces, input_pieces, cosines, sines, bias, norm_gains
+    )
+    block_output, d_residual, *parts, gain_two = feedforward(
+        (straight, *orders), feedforward_blocks, residual, out_grad, norm_gains
     )
     block_output = block_output.reshape(MICRO, DEVICE_TOKENS, D)
+    operands = (
+        w_output,
+        normed_one,
+        queries,
+        keys_across,
+        keys,
+        values,
+        log_totals,
+        mixed_across,
+        d_residual,
+        cosines,
+        sines,
+        bias,
+    )
     d_residual = d_residual.reshape(MICRO, DEVICE_TOKENS, D)
-
-    def operands_of(micro):
-        return (
-            w_output,
-            normed_one[micro],
-            queries[micro],
-            keys_across[micro],
-            keys[micro],
-            values[micro],
-            log_totals[micro],
-            mixed_across[micro],
-            d_residual[micro],
-            cosines[micro],
-            sines[micro],
-            bias[micro],
-        )
-
     attention_rows = D * (QKV_WIDTH + QUERY_WIDTH) // (LANES * BLOCKS)
     if butterfly and paired:
         paths = [stages[::-1], swap_dp(stages)[::-1]]
         halving_seq = seq_stages[::-1]
-        owned_one = lax.psum_scatter(
-            part_one.reshape(-1, LANES), both, scatter_dimension=0, tiled=True
-        )
-        received = [send_half(p, path[0]) for p, path in zip((part_two, part_three), paths)]
-        first = attention_backward(operands_of(0), BLOCKS, attention_rows)
-        received = together(*received, *first)
-        first = received[2:]
-        parts = [halve_step(part_two, received[0]), halve_step(part_three, received[1])]
-        first_across, *parts = together(first[2], *parts)
-        received = [send_half(p, path[1]) for p, path in zip(parts, paths)]
+
+        def send(value, stage):
+            return exchange(value, stage[0], stage[1])
+
+        kept, sent = [parts[0], parts[2]], [parts[1], parts[3]]
+        arrived = [send(part, path[0]) for part, path in zip(sent, paths)]
+        first = attention_backward(operands, BLOCKS, attention_rows)
+        arrived = together(*arrived, *first)
+        first = arrived[2:]
+        kept, sent = zip(*[halve_step(part, new) for part, new in zip(kept, arrived)])
+        first_across, *sent = together(first[2], *sent)
+        arrived = [send(part, path[1]) for part, path in zip(sent, paths)]
         second = attention_backward(
-            operands_of(1),
+            operands,
             BLOCKS,
             attention_rows,
-            (orders[0], w_project, first_across, first[3]),
+            (orders[0], w_project, first[0], first[1], first_across, first[3]),
         )
-        received = together(*received, *second)
-        attention_grads, d_queries_two, d_window_two, gain_one = received[2:]
-        parts = [halve_step(p, r) for p, r in zip(parts, received)]
-        d_queries = jnp.stack([first[0], d_queries_two], 0)
-        d_window = jnp.stack([first[1], d_window_two], 1)
+        arrived = together(*arrived, *second)
+        attention_kept, attention_sent, d_queries, window_kept, window_sent, gain_one = arrived[2:]
+        kept, sent = zip(*[halve_step(part, new) for part, new in zip(kept, arrived)])
         gains_total = jnp.stack([gain_one[:, 0], gain_two[:, 0]], 0) / norm_gains
         for index, stage in enumerate(paths[0]):
-            arrivals = {
-                "attention": send_half(attention_grads, stage),
-                "gains": exchange(gains_total, stage[0], stage[1]),
-            }
-            if index + 2 < len(paths[0]):
-                arrivals["two"] = send_half(parts[0], paths[0][index + 2])
-                arrivals["three"] = send_half(parts[1], paths[1][index + 2])
+            arrivals = {}
+            if index + 2 < len(stages):
+                arrivals["one"] = send(sent[0], paths[0][index + 2])
+                arrivals["two"] = send(sent[1], paths[1][index + 2])
+            arrivals["attention"] = send(attention_sent, stage)
             if index < len(halving_seq):
-                arrivals["window"] = send_half(d_window, halving_seq[index])
+                arrivals["window"] = send(window_sent, halving_seq[index])
+            arrivals["gains"] = send(gains_total, stage)
             arrivals = lax.optimization_barrier(arrivals)
-            attention_grads = halve_step(attention_grads, arrivals["attention"])
+            if "one" in arrivals:
+                news = [arrivals["one"], arrivals["two"]]
+                kept, sent = zip(*[halve_step(part, new) for part, new in zip(kept, news)])
+            attention_kept, attention_sent = halve_step(attention_kept, arrivals["attention"])
+            if "window" in arrivals:
+                window_kept, window_sent = halve_step(window_kept, arrivals["window"])
             gains_total = gains_total + arrivals["gains"]
-            if "two" in arrivals:
-                parts = [
-                    halve_step(parts[0], arrivals["two"]),
-                    halve_step(parts[1], arrivals["three"]),
-                ]
-            if "window" in arrivals:
-                d_window = halve_step(d_window, arrivals["window"])
-        attention_owned = attention_grads.reshape(-1)
-        d_own = d_window[0]
-        feedforward_owned = jnp.concatenate(
-            [owned_one, parts[0][0], parts[1][0]], 0
-        ).reshape(-1)
+        attention_owned = attention_kept.reshape(-1)
+        d_own = window_kept[0].astype(BF16)
+        feedforward_owned = jnp.concatenate([kept[0][0], kept[1][0]], 0).reshape(-1)
     else:
-        grads = jnp.concatenate([part_one, part_two, part_three], 1).reshape(-1)
+        halves = [jnp.concatenate(parts[index : index + 2], 0) for index in (0, 2)]
+        grads = jnp.concatenate(halves, 1).reshape(-1)
         feedforward_owned = lax.psum_scatter(grads, both, scatter_dimension=0, tiled=True)
-        first = attention_backward(operands_of(0), BLOCKS, attention_rows)
-        attention_grads, d_queries_two, d_window_two, gain_one = attention_backward(
-            operands_of(1), BLOCKS, attention_rows, (orders[0], w_project, first[2], first[3])
+        first = attention_backward(operands, BLOCKS, attention_rows)
+        kept, sent, d_queries, window_kept, window_sent, gain_one = attention_backward(
+            operands, BLOCKS, attention_rows, (orders[0], w_project, *first)
         )
         attention_owned = lax.psum_scatter(
-            attention_grads.reshape(-1), both, scatter_dimension=0, tiled=True
+            jnp.concatenate([kept, sent], 0).reshape(-1), both, scatter_dimension=0, tiled=True
         )
-        d_queries = jnp.stack([first[0], d_queries_two], 0)
-        d_window = jnp.stack([first[1], d_window_two], 1)
+        d_window = jnp.concatenate([window_kept, window_sent], 0)
         d_own = d_window[0].astype(F32)
         for step in range(1, reach + 1):
             d_own = d_own + lax.ppermute(

time: 285 us -> 216 us (0.76)
  waiting for transfers between devices: 118 us -> 53.9 us
  local copies, waits for them, and re-layouts: 29.5 us -> 16.4 us
  starting transfers between devices: 33.3 us -> 38.2 us
  Pallas kernels: 59.7 us -> 64.1 us
    unnamed x3 -> x1, waiting for transfers between devices: 44.1 us -> 0.02 us
    ppermute x31 -> x33, waiting for transfers between devices: 74.1 us -> 52.1 us  [exchange(): lax.ppermute(value, axis, [(place, place ^ bit) for place in range(count)])]
    slice x18 -> x0, local copies, waits for them, and re-layouts: 8.77 us -> none  [the longest x17 8.73 us: send_half(): return exchange(blocks[blocks.shape[0] // 2:], axis, bit)]
    convert_element_type x14 -> x33, other arithmetic: 11.2 us -> 16.7 us  [the longest x28 14.5 us: halve_step(): kept, received = (kept.astype(F32), received.astype(F32))]
    ppermute x0 -> x3, local copies, waits for them, and re-layouts: none -> 5.41 us  [exchange(): lax.ppermute(value, axis, [(place, place ^ bit) for place in range(count)])]
    ppermute x31 -> x33, starting transfers between devices: 33.3 us -> 38.2 us  [exchange(): lax.ppermute(value, axis, [(place, place ^ bit) for place in range(count)])]
    squeeze x8 -> x0, local copies, waits for them, and re-layouts: 4.71 us -> none  [the longest x1 1.79 us: operands_of(): normed_one[micro]]
    pallas_call x2, Pallas kernels: 24.5 us -> 28 us  [attention_backward(): pl.pallas_call(kernel, out_shape=outputs, in_specs=in_specs, out_specs=tu...]
  transfers between devices with their start and end apart: 33 -> 34, of which waited for: 13 -> 12; matrix products, arithmetic and copies ran while one was open for 16% -> 14% of each run, Pallas kernels for 16% -> 23%
where the time goes in v2:
time: 216 us; the launch traced here: 215 us
  Pallas kernels  64.1 us (30%)
  waiting for transfers between devices  53.9 us (25%)
  starting transfers between devices  38.2 us (18%)
  other arithmetic  27.4 us (13%)
  local copies, waits for them, and re-layouts  16.4 us (8%)
  between operations  14.8 us (7%)
    ppermute x33, waiting for transfers between devices, exchange(): lax.ppermute(value, axis, [(place, place ^ bit) for place in range(count)])  52.1 us
    ppermute x33, starting transfers between devices, exchange(): lax.ppermute(value, axis, [(place, place ^ bit) for place in range(count)])  38.2 us
    pallas_call x2, Pallas kernels, attention_backward(): pl.pallas_call(kernel, out_shape=outputs, in_specs=in_specs, out_specs=tu...  28 us
    pallas_call x1, Pallas kernels, attention_forward(): pl.pallas_call(attention_forward_kernel, out_shape=(shape((D, QKV_WIDTH),...  20.8 us
    pallas_call x1, Pallas kernels, feedforward(): pl.pallas_call(feedforward_kernel, out_shape=(shape((tokens, D), BF16), s...  15.2 us
    convert_element_type x28, other arithmetic, halve_step(): kept, received = (kept.astype(F32), received.astype(F32))  14.5 us
    unnamed x88, local copies, waits for them, and re-layouts  8.15 us
    ppermute x3, local copies, waits for them, and re-layouts, exchange(): lax.ppermute(value, axis, [(place, place ^ bit) for place in range(count)])  5.41 us
  transfers between devices with their start and end apart: 34, of which 12 were waited for; matrix products, arithmetic and copies ran while one was open for 14% of the time, Pallas kernels for 23%

profile of v2, /device:TPU:0, one launch (start us, length us, event | category | flops | bytes accessed | tf_op | source)
XLA Modules:
  0.0 215.3 jit_solution(7951961342810116443)
XLA Ops:
  7.2 1.7 convert_bitcast_fusion
  8.9 0.9 convert_bitcast_fusion.1
  9.8 4.0 %collective-permute-start = (bf16[1,216,128]{2,1,0:T(8,128)(2,1)S(1)}, bf16[1,216,128]{2,1,0:T(8,128)(2,1)S(1)}, u32[]{:S(2)}, u32[]{:S(2)}) collective-permute-start(bf16[1,216,128]{2,1,0:T(8,128)(2,1)S(1)} %convert_bitcast_fusion.1), channel_id=1, source_target_pairs={{0,4},{1,5},{2,6},{3,7},{4,0},{5,1},{6,2},{7,3},{8,12},{9,13},{10,... | collective-permute-start | bytes 165896 | tf_op jit(solution)/shard_map/ppermute | solution.py:46
  13.9 1.2 copy.51
  16.1 1.2 and_select_fusion.refs_10_.refs_11_.refs_15_
  17.4 1.0 multiply_sine_fusion
  18.4 6.8 %collective-permute-start.1 = (bf16[2,216,128]{2,1,0:T(8,128)(2,1)S(1)}, bf16[2,216,128]{2,1,0:T(8,128)(2,1)S(1)}, u32[]{:S(2)}, u32[]{:S(2)}) collective-permute-start(bf16[2,216,128]{2,1,0:T(8,128)(2,1)S(1)} %pad_maximum_fusion.2), channel_id=1, source_target_pairs={{0,2},{1,3},{2,0},{3,1},{4,6},{5,7},{6,4},{7,5},{8,10},{9,11},{10,... | collective-permute-start | bytes 331784 | tf_op jit(solution)/shard_map/ppermute | solution.py:46
  25.2 6.3 %collective-permute-done.1 = bf16[2,216,128]{2,1,0:T(8,128)(2,1)S(1)} collective-permute-done((bf16[2,216,128]{2,1,0:T(8,128)(2,1)S(1)}, bf16[2,216,128]{2,1,0:T(8,128)(2,1)S(1)}, u32[]{:S(2)}, u32[]{:S(2)}) %collective-permute-start.1) | collective-permute-done | bytes 110624 | tf_op jit(solution)/shard_map/ppermute | solution.py:46
  31.5 3.6 %collective-permute-done.2 = bf16[1,2,128,576]{3,2,1,0:T(8,128)(2,1)S(1)} collective-permute-done((bf16[1,2,128,576]{3,2,1,0:T(8,128)(2,1)S(1)}, bf16[1,2,128,576]{3,2,1,0:T(8,128)(2,1)S(1)}, u32[]{:S(2)}, u32[]{:S(2)}) %collective-permute-start.2) | collective-permute-done | bytes 294944 | tf_op jit(solution)/shard_map/ppermute | solution.py:46
  35.2 1.7 collective-permute-start.3
  36.9 1.1 copy.52
  38.0 3.3 %collective-permute-done.3 = bf16[4,216,128]{2,1,0:T(8,128)(2,1)S(1)} collective-permute-done((bf16[4,216,128]{2,1,0:T(8,128)(2,1)S(1)}, bf16[4,216,128]{2,1,0:T(8,128)(2,1)S(1)}, u32[]{:S(2)}, u32[]{:S(2)}) %collective-permute-start.3) | collective-permute-done | bytes 221216 | tf_op jit(solution)/shard_map/ppermute | solution.py:46
  41.3 1.6 collective-permute-start.4
  42.9 13.9 %collective-permute-done.7 = bf16[2,2,128,576]{2,3,1,0:T(8,128)(2,1)S(1)} collective-permute-done((bf16[2,2,128,576]{2,3,1,0:T(8,128)(2,1)}, bf16[2,2,128,576]{2,3,1,0:T(8,128)(2,1)S(1)}, u32[]{:S(2)}, u32[]{:S(2)}) %collective-permute-start.7) | collective-permute-done | bytes 589856 | tf_op jit(solution)/shard_map/ppermute | solution.py:46
  57.7 1.1 copy.54.refs_5_
  58.8 2.2 %copy.55.refs_6_ = bf16[2,2,128,576]{3,2,1,0:T(8,128)(2,1)} copy(bf16[2,2,128,576]{2,3,1,0:T(8,128)(2,1)} %collective-permute-done.8) | data formatting | bytes 1179648 | tf_op jit(solution)/shard_map/ppermute | solution.py:46
  60.9 2.1 copy.56.refs_7_
  63.1 0.8 copy-done.28
  63.9 20.8 %shard_map.230 = (bf16[576,960]{1,0:T(8,128)(2,1)}, bf16[576,576]{1,0:T(8,128)(2,1)}, bf16[2,1024,576]{2,1,0:T(8,128)(2,1)}, bf16[2,576,128]{2,1,0:T(8,128)(2,1)...) custom-call(s32[32]{0:T(128)S(1)} %broadcast_xor_fusion.1.order.orde, ...), custom_call_target="tpu_custom_call" | custom-call | tf_op jit(solution)/shard_map/pallas_call | solution.py:268
  84.7 1.7 all-gather.2.cloned.1.call-done
  86.4 15.2 %shard_map.231 = (bf16[256,576]{1,0:T(8,128)(2,1)S(1)}, f32[256,576]{1,0:T(8,128)S(1)}, bf16[16,320,128]{2,1,0:T(8,128)(2,1)}, bf16[16,320,128]{2,1,0:T(8,128)(2...) custom-call(s32[32]{0:T(128)S(1)} %iota.26.straight, ...), custom_call_target="tpu_custom_call" | custom-call | tf_op jit(solution)/shard_map/pallas_call | solution.py:382
  102.2 1.6 convert_element_type.225
  103.9 1.8 convert_element_type.222
  105.7 12.2 %shard_map.232 = (bf16[576,128]{1,0:T(8,128)(2,1)S(1)}, bf16[8,384,128]{2,1,0:T(8,128)(2,1)}, f32[960,576]{1,0:T(8,128)}, f32[576,576]{1,0:T(8,128)}) custom-call(bf16[576,576]{1,0:T(8,128)(2,1)} %get-tuple-element.91.refs_0_.refs_4_, bf16[2,1024,576]{2,1,0:T(8,128)(2,1)} %get-tuple-element.92.refs_1_.refs_5_, ...), custom_call_target="tpu_custom_call" | custom-call | tf_op jit(solution)/shard_map/pallas_call | solution.py:568
  117.9 1.1 copy-done.23
  119.1 1.1 copy-done.24
  120.5 1.4 fusion.11
  121.9 0.9 copy-done.4
  122.8 1.5 fusion.14
  124.3 1.5 collective-permute-start.13
  126.5 15.8 %shard_map.233 = (bf16[16,216,128]{2,1,0:T(8,128)(2,1)}, bf16[16,216,128]{2,1,0:T(8,128)(2,1)}, bf16[2,576,128]{2,1,0:T(8,128)(2,1)S(1)}, bf16[4,2,384,128]{3,2,...) custom-call(s32[32]{0:T(128)S(1)} %broadcast_xor_fusion.1.order.order_one, ...), custom_call_target="tpu_custom_call" | custom-call | tf_op jit(solution)/shard_map/pallas_call | solution.py:568
  143.7 0.9 fusion.32
  144.5 1.5 collective-permute-start.17
  146.0 1.2 convert_element_type.231
  147.2 1.1 fusion.36
  149.4 0.8 copy-done.26
  150.3 7.3 %collective-permute-done.16 = bf16[4,320,128]{2,1,0:T(8,128)(2,1)} collective-permute-done((bf16[4,320,128]{2,1,0:T(8,128)(2,1)}, bf16[4,320,128]{2,1,0:T(8,128)(2,1)}, u32[]{:S(2)}, u32[]{:S(2)}) %collective-permute-start.16) | collective-permute-done | bytes 327712 | tf_op jit(solution)/shard_map/ppermute | solution.py:46
  158.0 2.0 collective-permute-start.23
  160.0 1.0 convert_element_type.249
  161.4 1.0 convert_element_type.245
  162.5 1.9 collective-permute-start.21
  164.4 1.3 convert_element_type.241
  165.9 0.8 collective-permute-start.19
  166.7 1.4 collective-permute-start.20
  168.1 7.7 %collective-permute-done.20 = f32[2,576]{1,0:T(2,128)S(1)} collective-permute-done((f32[2,576]{1,0:T(2,128)S(1)}, f32[2,576]{1,0:T(2,128)S(1)}, u32[]{:S(2)}, u32[]{:S(2)}) %collective-permute-start.20) | collective-permute-done | bytes 4640 | tf_op jit(solution)/shard_map/ppermute | solution.py:46
  175.9 0.7 fusion.30
  176.7 1.6 collective-permute-start.28
  178.3 0.7 fusion.45
  179.0 1.3 collective-permute-start.27
  180.6 0.8 collective-permute-start.24
  181.4 0.7 fusion.48
  182.1 2.3 %collective-permute-start.26 = (bf16[1,320,128]{2,1,0:T(8,128)(2,1)}, bf16[1,320,128]{2,1,0:T(8,128)(2,1)}, u32[]{:S(2)}, u32[]{:S(2)}) collective-permute-start(bf16[1,320,128]{2,1,0:T(8,128)(2,1)} %fusion.48), channel_id=1, source_target_pairs={{0,4},{1,5},{2,6},{3,7},{4,0},{5,1},{6,2},{7,3},{8,12},{9,13},{10,... | collective-permute-start | bytes 245768 | tf_op jit(solution)/shard_map/ppermute | solution.py:46
  185.0 0.6 slice_reduce_fusion
  185.6 1.0 copy.59
  186.6 0.9 copy.60
  188.0 4.8 %collective-permute-done.26 = bf16[1,320,128]{2,1,0:T(8,128)(2,1)} collective-permute-done((bf16[1,320,128]{2,1,0:T(8,128)(2,1)}, bf16[1,320,128]{2,1,0:T(8,128)(2,1)}, u32[]{:S(2)}, u32[]{:S(2)}) %collective-permute-start.26) | collective-permute-done | bytes 81952 | tf_op jit(solution)/shard_map/ppermute | solution.py:46
  193.1 2.1 collective-permute-start.29
  195.2 0.9 add_bitcast_fusion.1
  197.5 1.2 multiply_subtract_fusion
  198.6 2.6 %collective-permute-start.32 = (f32[2,576]{1,0:T(2,128)S(1)}, f32[2,576]{1,0:T(2,128)S(1)}, u32[]{:S(2)}, u32[]{:S(2)}) collective-permute-start(f32[2,576]{1,0:T(2,128)S(1)} %add.265), channel_id=1, source_target_pairs={{0,4},{1,5},{2,6},{3,7},{4,0},{5,1},{6,2},{7,3},{8,12},{9,13},{10,... | collective-permute-start | bytes 13832 | tf_op jit(solution)/shard_map/ppermute | solution.py:46
  201.8 0.9 fusion.21
  203.2 3.8 %collective-permute-done.31 = bf16[1,216,128]{2,1,0:T(8,128)(2,1)S(1)} collective-permute-done((bf16[1,216,128]{2,1,0:T(8,128)(2,1)S(1)}, bf16[1,216,128]{2,1,0:T(8,128)(2,1)S(1)}, u32[]{:S(2)}, u32[]{:S(2)}) %collective-permute-start.31) | collective-permute-done | bytes 55328 | tf_op jit(solution)/shard_map/ppermute | solution.py:46
  207.0 0.6 multiply_subtract_fusion.2
  207.7 0.8 multiply_subtract_fusion.1
  (177 shorter events, 11.3 us)
Async XLA Ops:
  7.2 8.5 %copy-start.41 = (s32[8]{0:T(128)S(1)}, s32[8]{0:T(128)}, u32[]{:S(2)}) copy-start(s32[8]{0:T(128)} %constant.28.clone) | copy-start | bytes 100
  7.2 7.9 %copy-start.37 = (s32[2,1,6]{2,1,0:T(1,128)S(1)}, s32[2,1,6]{2,1,0:T(1,128)}, u32[]{:S(2)}) copy-start(s32[2,1,6]{2,1,0:T(1,128)} %param.17) | copy-start | bytes 148
  7.2 79.2 %all-gather.2.cloned.1.call-start = ((), (), s32[]{:S(2)}) async-start(), calls=%async_computation | async-start | bytes 5474304 | tf_op jit(solution)/shard_map/all_gather | solution.py:630
  9.8 8.5 %collective-permute-start = (bf16[1,216,128]{2,1,0:T(8,128)(2,1)S(1)}, bf16[1,216,128]{2,1,0:T(8,128)(2,1)S(1)}, u32[]{:S(2)}, u32[]{:S(2)}) collective-permute-start(bf16[1,216,128]{2,1,0:T(8,128)(2,1)S(1)} %convert_bitcast_fusion.1), channel_id=1, source_target_pairs={{0,4},{1,5},{2,6},{3,7},{4,0},{5,1},{6,2},{7,3},{8,12},{9,13},{10,... | collective-permute-start | bytes 165896 | tf_op jit(solution)/shard_map/ppermute | solution.py:46
  15.0 20.1 %collective-permute-start.2 = (bf16[1,2,128,576]{3,2,1,0:T(8,128)(2,1)S(1)}, bf16[1,2,128,576]{3,2,1,0:T(8,128)(2,1)S(1)}, u32[]{:S(2)}, u32[]{:S(2)}) collective-permute-start(bf16[1,2,128,576]{3,2,1,0:T(8,128)(2,1)S(1)} %bitcast.51), channel_id=1, source_target_pairs={{0,4},{1,5},{2,6},{3,7},{4,0},{5,1},{6,2},{7,3},{8,12},{9,13},{10,... | collective-permute-start | bytes 884744 | tf_op jit(solution)/shard_map/ppermute | solution.py:46
  18.4 13.1 %collective-permute-start.1 = (bf16[2,216,128]{2,1,0:T(8,128)(2,1)S(1)}, bf16[2,216,128]{2,1,0:T(8,128)(2,1)S(1)}, u32[]{:S(2)}, u32[]{:S(2)}) collective-permute-start(bf16[2,216,128]{2,1,0:T(8,128)(2,1)S(1)} %pad_maximum_fusion.2), channel_id=1, source_target_pairs={{0,2},{1,3},{2,0},{3,1},{4,6},{5,7},{6,4},{7,5},{8,10},{9,11},{10,... | collective-permute-start | bytes 331784 | tf_op jit(solution)/shard_map/ppermute | solution.py:46
  35.2 21.8 %copy-start.5 = (bf16[2,2,128,576]{3,2,1,0:T(8,128)(2,1)}, bf16[2,2,128,576]{3,2,1,0:T(8,128)(2,1)S(1)}, u32[]{:S(2)}) copy-start(bf16[2,2,128,576]{3,2,1,0:T(8,128)(2,1)S(1)} %pad_maximum_fusion.refs_4_) | copy-start | bytes 1769476
  35.2 21.5 %copy-start.32 = (bf16[2,1,128,576]{2,3,1,0:T(8,128)(2,1)S(1)}, bf16[2,1,128,576]{2,3,1,0:T(8,128)(2,1)}, u32[]{:S(2)}) copy-start(bf16[2,1,128,576]{2,3,1,0:T(8,128)(2,1)} %param.16) | copy-start | bytes 884740
  35.2 22.4 %copy-start.40 = (s32[32]{0:T(128)S(1)}, s32[32]{0:T(128)}, u32[]{:S(2)}) copy-start(s32[32]{0:T(128)} %constant.29.clone) | copy-start | bytes 388
  35.2 22.4 %copy-start.39 = (s32[32]{0:T(128)S(1)}, s32[32]{0:T(128)}, u32[]{:S(2)}) copy-start(s32[32]{0:T(128)} %constant.30.clone) | copy-start | bytes 388
  35.2 6.0 %collective-permute-start.3 = (bf16[4,216,128]{2,1,0:T(8,128)(2,1)S(1)}, bf16[4,216,128]{2,1,0:T(8,128)(2,1)S(1)}, u32[]{:S(2)}, u32[]{:S(2)}) collective-permute-start(bf16[4,216,128]{2,1,0:T(8,128)(2,1)S(1)} %pad_maximum_fusion.1), channel_id=1, source_target_pairs={{0,16},{8,24},{16,0},{24,8},{1,17},{9,25},{17,1},{25,9},{2,18},{10... | collective-permute-start | bytes 663560 | tf_op jit(solution)/shard_map/ppermute | solution.py:46
  38.0 18.8 %collective-permute-start.7 = (bf16[2,2,128,576]{2,3,1,0:T(8,128)(2,1)}, bf16[2,2,128,576]{2,3,1,0:T(8,128)(2,1)S(1)}, u32[]{:S(2)}, u32[]{:S(2)}) collective-permute-start(bf16[2,2,128,576]{2,3,1,0:T(8,128)(2,1)} %copy.52), channel_id=1, source_target_pairs={{0,2},{1,3},{2,0},{3,1},{4,6},{5,7},{6,4},{7,5},{8,10},{9,11},{10,... | collective-permute-start | bytes 1769480 | tf_op jit(solution)/shard_map/ppermute | solution.py:46
  41.3 16.3 %collective-permute-start.4 = (bf16[8,216,128]{2,1,0:T(8,128)(2,1)S(1)}, bf16[8,216,128]{2,1,0:T(8,128)(2,1)S(1)}, u32[]{:S(2)}, u32[]{:S(2)}) collective-permute-start(bf16[8,216,128]{2,1,0:T(8,128)(2,1)S(1)} %constant_dynamic-update-slice_fusion.refs_0_), channel_id=1, source_target_pairs={{0,8},{8,0},{16,24},{24,16},{1,9},{9,1},{17,25},{25,17},{2,10},{10... | collective-permute-start | bytes 1327112 | tf_op jit(solution)/shard_map/ppermute | solution.py:46
  42.9 15.9 %collective-permute-start.8 = (bf16[2,2,128,576]{2,3,1,0:T(8,128)(2,1)}, bf16[2,2,128,576]{2,3,1,0:T(8,128)(2,1)}, u32[]{:S(2)}, u32[]{:S(2)}) collective-permute-start(bf16[2,2,128,576]{2,3,1,0:T(8,128)(2,1)} %copy.52), channel_id=1, source_target_pairs={{0,1},{1,0},{2,3},{3,2},{4,5},{5,4},{6,7},{7,6},{8,9},{9,8},{10,11... | collective-permute-start | bytes 1769480 | tf_op jit(solution)/shard_map/ppermute | solution.py:46
  56.7 4.2 %collective-permute-start.9 = (bf16[2,2,128,576]{2,3,1,0:T(8,128)(2,1)S(1)}, bf16[2,2,128,576]{2,3,1,0:T(8,128)(2,1)}, u32[]{:S(2)}, u32[]{:S(2)}) collective-permute-start(bf16[2,2,128,576]{2,3,1,0:T(8,128)(2,1)S(1)} %collective-permute-done.7), channel_id=1, source_target_pairs={{0,1},{1,0},{2,3},{3,2},{4,5},{5,4},{6,7},{7,6},{8,9},{9,8},{10,11... | collective-permute-start | bytes 1769480 | tf_op jit(solution)/shard_map/ppermute | solution.py:46
  57.0 6.1 %collective-permute-start.5 = (bf16[8,216,128]{2,1,0:T(8,128)(2,1)S(1)}, bf16[8,216,128]{2,1,0:T(8,128)(2,1)}, u32[]{:S(2)}, u32[]{:S(2)}) collective-permute-start(bf16[8,216,128]{2,1,0:T(8,128)(2,1)S(1)} %constant_dynamic-update-slice_fusion.refs_0_), channel_id=1, source_target_pairs={{0,1},{1,0},{2,3},{3,2},{4,5},{5,4},{6,7},{7,6},{8,9},{9,8},{10,11... | collective-permute-start | bytes 1327112 | tf_op jit(solution)/shard_map/ppermute | solution.py:46
  57.6 5.5 %collective-permute-start.6 = (bf16[8,216,128]{2,1,0:T(8,128)(2,1)S(1)}, bf16[8,216,128]{2,1,0:T(8,128)(2,1)S(1)}, u32[]{:S(2)}, u32[]{:S(2)}) collective-permute-start(bf16[8,216,128]{2,1,0:T(8,128)(2,1)S(1)} %collective-permute-done.4.refs_1_), channel_id=1, source_target_pairs={{0,1},{1,0},{2,3},{3,2},{4,5},{5,4},{6,7},{7,6},{8,9},{9,8},{10,11... | collective-permute-start | bytes 1327112 | tf_op jit(solution)/shard_map/ppermute | solution.py:46
  58.7 5.1 %copy-start.3 = (f32[2,576]{1,0:T(2,128)S(1)}, f32[2,576]{1,0:T(2,128)}, u32[]{:S(2)}) copy-start(f32[2,576]{1,0:T(2,128)} %gains.1) | copy-start | bytes 13828
  101.7 2.1 copy-start
  101.7 16.2 %collective-permute-start.11 = (bf16[16,328,128]{2,1,0:T(8,128)(2,1)}, bf16[16,328,128]{2,1,0:T(8,128)(2,1)S(1)}, u32[]{:S(2)}, u32[]{:S(2)}) collective-permute-start(bf16[16,328,128]{2,1,0:T(8,128)(2,1)} %get-tuple-element.90), channel_id=1, source_target_pairs={{0,1},{1,0},{2,3},{3,2},{4,5},{5,4},{6,7},{7,6},{8,9},{9,8},{10,11... | collective-permute-start | bytes 4030472 | tf_op jit(solution)/shard_map/ppermute | solution.py:46
  101.9 15.9 %collective-permute-start.10 = (bf16[16,320,128]{2,1,0:T(8,128)(2,1)}, bf16[16,320,128]{2,1,0:T(8,128)(2,1)S(1)}, u32[]{:S(2)}, u32[]{:S(2)}) collective-permute-start(bf16[16,320,128]{2,1,0:T(8,128)(2,1)} %get-tuple-element.89), channel_id=1, source_target_pairs={{0,1},{1,0},{2,3},{3,2},{4,5},{5,4},{6,7},{7,6},{8,9},{9,8},{10,11... | collective-permute-start | bytes 3932168 | tf_op jit(solution)/shard_map/ppermute | solution.py:46
  120.5 2.2 %copy-start.4 = (f32[16,320,128]{2,1,0:T(8,128)S(1)}, f32[16,320,128]{2,1,0:T(8,128)}, u32[]{:S(2)}) copy-start(f32[16,320,128]{2,1,0:T(8,128)} %convert_element_type.222) | copy-start | bytes 7864324
  124.3 18.4 %collective-permute-start.13 = (bf16[8,328,128]{2,1,0:T(8,128)(2,1)S(1)}, bf16[8,328,128]{2,1,0:T(8,128)(2,1)S(1)}, u32[]{:S(2)}, u32[]{:S(2)}) collective-permute-start(bf16[8,328,128]{2,1,0:T(8,128)(2,1)S(1)} %get-tuple-element.109), channel_id=1, source_target_pairs={{0,16},{8,24},{16,0},{24,8},{1,17},{9,25},{17,1},{25,9},{2,18},{10... | collective-permute-start | bytes 2015240 | tf_op jit(solution)/shard_map/ppermute | solution.py:46
  125.8 16.9 %collective-permute-start.12 = (bf16[8,320,128]{2,1,0:T(8,128)(2,1)}, bf16[8,320,128]{2,1,0:T(8,128)(2,1)}, u32[]{:S(2)}, u32[]{:S(2)}) collective-permute-start(bf16[8,320,128]{2,1,0:T(8,128)(2,1)} %get-tuple-element.108), channel_id=1, source_target_pairs={{0,8},{8,0},{16,24},{24,16},{1,9},{9,1},{17,25},{25,17},{2,10},{10... | collective-permute-start | bytes 1966088 | tf_op jit(solution)/shard_map/ppermute | solution.py:46
  142.8 14.8 %collective-permute-start.14 = (bf16[16,216,128]{2,1,0:T(8,128)(2,1)}, bf16[16,216,128]{2,1,0:T(8,128)(2,1)}, u32[]{:S(2)}, u32[]{:S(2)}) collective-permute-start(bf16[16,216,128]{2,1,0:T(8,128)(2,1)} %get-tuple-element.123), channel_id=1, source_target_pairs={{0,1},{1,0},{2,3},{3,2},{4,5},{5,4},{6,7},{7,6},{8,9},{9,8},{10,11... | collective-permute-start | bytes 2654216 | tf_op jit(solution)/shard_map/ppermute | solution.py:46
  142.9 14.8 %collective-permute-start.18 = (bf16[4,2,384,128]{3,2,1,0:T(8,128)(2,1)}, bf16[4,2,384,128]{3,2,1,0:T(8,128)(2,1)S(1)}, u32[]{:S(2)}, u32[]{:S(2)}) collective-permute-start(bf16[4,2,384,128]{3,2,1,0:T(8,128)(2,1)} %get-tuple-element.128), channel_id=1, source_target_pairs={{0,1},{1,0},{2,3},{3,2},{4,5},{5,4},{6,7},{7,6},{8,9},{9,8},{10,11... | collective-permute-start | bytes 2359304 | tf_op jit(solution)/shard_map/ppermute | solution.py:46
  144.5 2.7 %copy-start.7 = (f32[8,320,128]{2,1,0:T(8,128)S(1)}, f32[8,320,128]{2,1,0:T(8,128)}, u32[]{:S(2)}) copy-start(f32[8,320,128]{2,1,0:T(8,128)} %get-tuple-element.204) | copy-start | bytes 3932164
  144.5 13.1 %collective-permute-start.17 = (bf16[4,328,128]{2,1,0:T(8,128)(2,1)}, bf16[4,328,128]{2,1,0:T(8,128)(2,1)}, u32[]{:S(2)}, u32[]{:S(2)}) collective-permute-start(bf16[4,328,128]{2,1,0:T(8,128)(2,1)} %get-tuple-element.211), channel_id=1, source_target_pairs={{0,8},{8,0},{16,24},{24,16},{1,9},{9,1},{17,25},{25,17},{2,10},{10... | collective-permute-start | bytes 1007624 | tf_op jit(solution)/shard_map/ppermute | solution.py:46
  147.2 1.9 copy-start.10
  147.2 2.0 copy-start.27
  148.3 9.4 %collective-permute-start.16 = (bf16[4,320,128]{2,1,0:T(8,128)(2,1)}, bf16[4,320,128]{2,1,0:T(8,128)(2,1)}, u32[]{:S(2)}, u32[]{:S(2)}) collective-permute-start(bf16[4,320,128]{2,1,0:T(8,128)(2,1)} %get-tuple-element.213), channel_id=1, source_target_pairs={{0,16},{8,24},{16,0},{24,8},{1,17},{9,25},{17,1},{25,9},{2,18},{10... | collective-permute-start | bytes 983048 | tf_op jit(solution)/shard_map/ppermute | solution.py:46
  149.1 1.3 collective-permute-start.15
  158.0 17.9 %copy-start.8 = (f32[2,2,384,128]{3,2,1,0:T(8,128)}, f32[2,2,384,128]{3,2,1,0:T(8,128)S(1)}, u32[]{:S(2)}) copy-start(f32[2,2,384,128]{3,2,1,0:T(8,128)S(1)} %get-tuple-element.208) | copy-start | bytes 2359300
  158.0 17.8 %collective-permute-start.23 = (bf16[2,2,384,128]{3,2,1,0:T(8,128)(2,1)S(1)}, bf16[2,2,384,128]{3,2,1,0:T(8,128)(2,1)S(1)}, u32[]{:S(2)}, u32[]{:S(2)}) collective-permute-start(bf16[2,2,384,128]{3,2,1,0:T(8,128)(2,1)S(1)} %get-tuple-element.209), channel_id=1, source_target_pairs={{0,2},{1,3},{2,0},{3,1},{4,6},{5,7},{6,4},{7,5},{8,10},{9,11},{10,... | collective-permute-start | bytes 1179656 | tf_op jit(solution)/shard_map/ppermute | solution.py:46
  161.1 17.2 %copy-start.13 = (f32[2,328,128]{2,1,0:T(8,128)}, f32[2,328,128]{2,1,0:T(8,128)S(1)}, u32[]{:S(2)}) copy-start(f32[2,328,128]{2,1,0:T(8,128)S(1)} %get-tuple-element.216) | copy-start | bytes 1007620
  161.1 14.7 %collective-permute-start.22 = (bf16[2,328,128]{2,1,0:T(8,128)(2,1)S(1)}, bf16[2,328,128]{2,1,0:T(8,128)(2,1)S(1)}, u32[]{:S(2)}, u32[]{:S(2)}) collective-permute-start(bf16[2,328,128]{2,1,0:T(8,128)(2,1)S(1)} %get-tuple-element.217), channel_id=1, source_target_pairs={{0,2},{1,3},{2,0},{3,1},{4,6},{5,7},{6,4},{7,5},{8,10},{9,11},{10,... | collective-permute-start | bytes 503816 | tf_op jit(solution)/shard_map/ppermute | solution.py:46
  162.5 18.9 %copy-start.18 = (f32[2,320,128]{2,1,0:T(8,128)}, f32[2,320,128]{2,1,0:T(8,128)S(1)}, u32[]{:S(2)}) copy-start(f32[2,320,128]{2,1,0:T(8,128)S(1)} %get-tuple-element.218) | copy-start | bytes 983044
  162.5 13.3 %collective-permute-start.21 = (bf16[2,320,128]{2,1,0:T(8,128)(2,1)S(1)}, bf16[2,320,128]{2,1,0:T(8,128)(2,1)S(1)}, u32[]{:S(2)}, u32[]{:S(2)}) collective-permute-start(bf16[2,320,128]{2,1,0:T(8,128)(2,1)S(1)} %get-tuple-element.219), channel_id=1, source_target_pairs={{0,2},{1,3},{2,0},{3,1},{4,6},{5,7},{6,4},{7,5},{8,10},{9,11},{10,... | collective-permute-start | bytes 491528 | tf_op jit(solution)/shard_map/ppermute | solution.py:46
  165.9 9.9 %collective-permute-start.19 = (bf16[8,216,128]{2,1,0:T(8,128)(2,1)S(1)}, bf16[8,216,128]{2,1,0:T(8,128)(2,1)S(1)}, u32[]{:S(2)}, u32[]{:S(2)}) collective-permute-start(bf16[8,216,128]{2,1,0:T(8,128)(2,1)S(1)} %get-tuple-element.207), channel_id=1, source_target_pairs={{0,8},{8,0},{16,24},{24,16},{1,9},{9,1},{17,25},{25,17},{2,10},{10... | collective-permute-start | bytes 1327112 | tf_op jit(solution)/shard_map/ppermute | solution.py:46
  166.7 9.1 %collective-permute-start.20 = (f32[2,576]{1,0:T(2,128)S(1)}, f32[2,576]{1,0:T(2,128)S(1)}, u32[]{:S(2)}, u32[]{:S(2)}) collective-permute-start(f32[2,576]{1,0:T(2,128)S(1)} %fusion.62), channel_id=1, source_target_pairs={{0,8},{8,0},{16,24},{24,16},{1,9},{9,1},{17,25},{25,17},{2,10},{10... | collective-permute-start | bytes 13832 | tf_op jit(solution)/shard_map/ppermute | solution.py:46
  176.7 16.2 %collective-permute-start.28 = (bf16[1,2,384,128]{3,2,1,0:T(8,128)(2,1)}, bf16[1,2,384,128]{3,2,1,0:T(8,128)(2,1)S(1)}, u32[]{:S(2)}, u32[]{:S(2)}) collective-permute-start(bf16[1,2,384,128]{3,2,1,0:T(8,128)(2,1)} %fusion.30), channel_id=1, source_target_pairs={{0,4},{1,5},{2,6},{3,7},{4,0},{5,1},{6,2},{7,3},{8,12},{9,13},{10,... | collective-permute-start | bytes 589832 | tf_op jit(solution)/shard_map/ppermute | solution.py:46
  178.3 2.3 %copy-start.15 = (f32[2,328,128]{2,1,0:T(8,128)}, f32[2,328,128]{2,1,0:T(8,128)S(1)}, u32[]{:S(2)}) copy-start(f32[2,328,128]{2,1,0:T(8,128)S(1)} %convert_element_type.265) | copy-start | bytes 1007620
  179.0 13.8 %collective-permute-start.27 = (bf16[1,328,128]{2,1,0:T(8,128)(2,1)}, bf16[1,328,128]{2,1,0:T(8,128)(2,1)S(1)}, u32[]{:S(2)}, u32[]{:S(2)}) collective-permute-start(bf16[1,328,128]{2,1,0:T(8,128)(2,1)} %fusion.45), channel_id=1, source_target_pairs={{0,4},{1,5},{2,6},{3,7},{4,0},{5,1},{6,2},{7,3},{8,12},{9,13},{10,... | collective-permute-start | bytes 251912 | tf_op jit(solution)/shard_map/ppermute | solution.py:46
  180.5 5.1 %copy-start.1 = (f32[256,576]{1,0:T(8,128)S(1)}, f32[256,576]{1,0:T(8,128)}, u32[]{:S(2)}) copy-start(f32[256,576]{1,0:T(8,128)} %copy-done) | copy-start | bytes 1769476
  180.6 12.3 %collective-permute-start.24 = (bf16[4,216,128]{2,1,0:T(8,128)(2,1)S(1)}, bf16[4,216,128]{2,1,0:T(8,128)(2,1)S(1)}, u32[]{:S(2)}, u32[]{:S(2)}) collective-permute-start(bf16[4,216,128]{2,1,0:T(8,128)(2,1)S(1)} %get-tuple-element.215), channel_id=1, source_target_pairs={{0,16},{8,24},{16,0},{24,8},{1,17},{9,25},{17,1},{25,9},{2,18},{10... | collective-permute-start | bytes 663560 | tf_op jit(solution)/shard_map/ppermute | solution.py:46
  182.1 10.8 %collective-permute-start.26 = (bf16[1,320,128]{2,1,0:T(8,128)(2,1)}, bf16[1,320,128]{2,1,0:T(8,128)(2,1)}, u32[]{:S(2)}, u32[]{:S(2)}) collective-permute-start(bf16[1,320,128]{2,1,0:T(8,128)(2,1)} %fusion.48), channel_id=1, source_target_pairs={{0,4},{1,5},{2,6},{3,7},{4,0},{5,1},{6,2},{7,3},{8,12},{9,13},{10,... | collective-permute-start | bytes 245768 | tf_op jit(solution)/shard_map/ppermute | solution.py:46
  184.4 3.6 %collective-permute-start.25 = (f32[2,576]{1,0:T(2,128)S(1)}, f32[2,576]{1,0:T(2,128)S(1)}, u32[]{:S(2)}, u32[]{:S(2)}) collective-permute-start(f32[2,576]{1,0:T(2,128)S(1)} %add.249), channel_id=1, source_target_pairs={{0,16},{8,24},{16,0},{24,8},{1,17},{9,25},{17,1},{25,9},{2,18},{10... | collective-permute-start | bytes 13832 | tf_op jit(solution)/shard_map/ppermute | solution.py:46
  186.6 8.6 %copy-start.19 = (f32[2,320,128]{2,1,0:T(8,128)S(1)}, f32[2,320,128]{2,1,0:T(8,128)}, u32[]{:S(2)}) copy-start(f32[2,320,128]{2,1,0:T(8,128)} %copy-done.18) | copy-start | bytes 983044
  186.6 8.6 %copy-start.21 = (f32[2,320,128]{2,1,0:T(8,128)S(1)}, f32[2,320,128]{2,1,0:T(8,128)}, u32[]{:S(2)}) copy-start(f32[2,320,128]{2,1,0:T(8,128)} %copy-done.20) | copy-start | bytes 983044
  187.5 8.6 %copy-start.14 = (f32[2,328,128]{2,1,0:T(8,128)S(1)}, f32[2,328,128]{2,1,0:T(8,128)}, u32[]{:S(2)}) copy-start(f32[2,328,128]{2,1,0:T(8,128)} %copy-done.13) | copy-start | bytes 1007620
  187.5 8.6 %copy-start.16 = (f32[2,328,128]{2,1,0:T(8,128)S(1)}, f32[2,328,128]{2,1,0:T(8,128)}, u32[]{:S(2)}) copy-start(f32[2,328,128]{2,1,0:T(8,128)} %copy-done.15) | copy-start | bytes 1007620
  192.9 5.7 %collective-permute-start.30 = (f32[2,576]{1,0:T(2,128)S(1)}, f32[2,576]{1,0:T(2,128)S(1)}, u32[]{:S(2)}, u32[]{:S(2)}) collective-permute-start(f32[2,576]{1,0:T(2,128)S(1)} %add.262), channel_id=1, source_target_pairs={{0,2},{1,3},{2,0},{3,1},{4,6},{5,7},{6,4},{7,5},{8,10},{9,11},{10,... | collective-permute-start | bytes 13832 | tf_op jit(solution)/shard_map/ppermute | solution.py:46
  193.0 3.2 %copy-start.9 = (f32[2,2,384,128]{3,2,1,0:T(8,128)S(1)}, f32[2,2,384,128]{3,2,1,0:T(8,128)}, u32[]{:S(2)}) copy-start(f32[2,2,384,128]{3,2,1,0:T(8,128)} %copy-done.8) | copy-start | bytes 2359300
  193.1 3.2 %copy-start.25 = (bf16[576,960]{1,0:T(8,128)(2,1)S(1)}, bf16[576,960]{1,0:T(8,128)(2,1)}, u32[]{:S(2)}) copy-start(bf16[576,960]{1,0:T(8,128)(2,1)} %get-tuple-element.110.w_project) | copy-start | bytes 3317764
  193.1 3.2 %copy-start.38 = (f32[576]{0:T(1024)S(1)}, f32[576]{0:T(1024)}, u32[]{:S(2)}) copy-start(f32[576]{0:T(1024)} %slice_reduce_fusion) | copy-start | bytes 6916
  193.1 5.5 %collective-permute-start.29 = (bf16[2,216,128]{2,1,0:T(8,128)(2,1)S(1)}, bf16[2,216,128]{2,1,0:T(8,128)(2,1)S(1)}, u32[]{:S(2)}, u32[]{:S(2)}) collective-permute-start(bf16[2,216,128]{2,1,0:T(8,128)(2,1)S(1)} %get-tuple-element.221), channel_id=1, source_target_pairs={{0,2},{1,3},{2,0},{3,1},{4,6},{5,7},{6,4},{7,5},{8,10},{9,11},{10,... | collective-permute-start | bytes 331784 | tf_op jit(solution)/shard_map/ppermute | solution.py:46
  197.4 4.4 %copy-start.12 = (f32[2,128,576]{1,2,0:T(8,128)S(1)}, f32[2,128,576]{1,2,0:T(8,128)}, u32[]{:S(2)}) copy-start(f32[2,128,576]{1,2,0:T(8,128)} %copy.59) | copy-start | bytes 1769476
  198.6 4.6 %collective-permute-start.32 = (f32[2,576]{1,0:T(2,128)S(1)}, f32[2,576]{1,0:T(2,128)S(1)}, u32[]{:S(2)}, u32[]{:S(2)}) collective-permute-start(f32[2,576]{1,0:T(2,128)S(1)} %add.265), channel_id=1, source_target_pairs={{0,4},{1,5},{2,6},{3,7},{4,0},{5,1},{6,2},{7,3},{8,12},{9,13},{10,... | collective-permute-start | bytes 13832 | tf_op jit(solution)/shard_map/ppermute | solution.py:46
  201.2 5.8 %copy-start.35 = (f32[2,576]{1,0:T(2,128)S(1)}, f32[2,576]{1,0:T(2,128)}, u32[]{:S(2)}) copy-start(f32[2,576]{1,0:T(2,128)} %param.25) | copy-start | bytes 13828
  201.2 5.8 %copy-start.36 = (f32[2,576]{1,0:T(2,128)S(1)}, f32[2,576]{1,0:T(2,128)}, u32[]{:S(2)}) copy-start(f32[2,576]{1,0:T(2,128)} %param.26) | copy-start | bytes 13828
  201.2 6.4 %copy-start.29 = (f32[27648]{0:T(1024)S(1)}, f32[27648]{0:T(1024)}, u32[]{:S(2)}) copy-start(f32[27648]{0:T(1024)} %param.18) | copy-start | bytes 331780
  201.2 6.4 %copy-start.33 = (f32[27648]{0:T(1024)S(1)}, f32[27648]{0:T(1024)}, u32[]{:S(2)}) copy-start(f32[27648]{0:T(1024)} %param.21) | copy-start | bytes 331780
  201.3 6.4 %copy-start.34 = (f32[27648]{0:T(1024)S(1)}, f32[27648]{0:T(1024)}, u32[]{:S(2)}) copy-start(f32[27648]{0:T(1024)} %param.22) | copy-start | bytes 331780
  201.3 5.7 %collective-permute-start.31 = (bf16[1,216,128]{2,1,0:T(8,128)(2,1)S(1)}, bf16[1,216,128]{2,1,0:T(8,128)(2,1)S(1)}, u32[]{:S(2)}, u32[]{:S(2)}) collective-permute-start(bf16[1,216,128]{2,1,0:T(8,128)(2,1)S(1)} %get-tuple-element.223), channel_id=1, source_target_pairs={{0,4},{1,5},{2,6},{3,7},{4,0},{5,1},{6,2},{7,3},{8,12},{9,13},{10,... | collective-permute-start | bytes 165896 | tf_op jit(solution)/shard_map/ppermute | solution.py:46
  (12 other events, 14.8 us)
Sparse Core Ops, SparseCore 0:
  11.5 74.9 all-gather.1

commit v3 on v2

--- a/solution.py
+++ b/solution.py
@@ -1,3 +1,5 @@
+import functools
+
 import jax
 import jax.numpy as jnp
 from jax import lax
@@ -46,43 +48,22 @@
     return lax.ppermute(value, axis, [(place, place ^ bit) for place in range(count)])
 
 
-def gather_stages():
-    seq, dp = lax.axis_size("seq"), lax.axis_size("dp")
-    stages = []
-    bit = seq // 2
-    while bit > 1:
-        stages.append(("seq", bit, bit))
-        bit //= 2
-    bit = dp // 2
-    while bit >= 1:
-        stages.append(("dp", bit, bit * seq))
-        bit //= 2
-    if seq > 1:
-        stages.append(("seq", 1, 1))
-    return stages
-
-
-def block_order(stages):
-    order = [0]
-    for unused_axis, unused_bit, flat_bit in stages:
-        order = order + [place ^ flat_bit for place in order]
-    return order
-
-
-def swap_dp(stages):
-    turned = iter([stage for stage in reversed(stages) if stage[0] == "dp"])
-    return [next(turned) if stage[0] == "dp" else stage for stage in stages]
-
-
-def halve_step(kept, received):
-    half = kept.shape[0] // 2
-    kept, received = kept.astype(F32), received.astype(F32)
-    if half == 0:
-        return (kept + received, None)
-    return (
-        (kept[:half] + received[:half]).astype(BF16),
-        (kept[half:] + received[half:]).astype(BF16),
-    )
+def add_up(kept, news, parts):
+    size = kept.shape[0] // parts
+    results = []
+    for index in range(parts):
+        rows = slice(index * size, (index + 1) * size)
+        total = kept[rows].astype(F32)
+        for new in news:
+            total = total + new[rows].astype(F32)
+        results.append(total.astype(BF16) if index else total)
+    return results
+
+
+def pair_sum(values):
+    while len(values) > 1:
+        values = [one + two for one, two in zip(values[::2], values[1::2])]
+    return values[0]
 
 
 def together(*values):
@@ -90,14 +71,14 @@
 
 
 def unit_norm(inputs):
-    inverse_rms = lax.rsqrt(jnp.mean(inputs * inputs, axis=-1, keepdims=True) + NORM_EPSILON)
+    inverse_rms = lax.rsqrt(jnp.mean(inputs * inputs, axis=1, keepdims=True) + NORM_EPSILON)
     return (inputs * inverse_rms, inverse_rms)
 
 
 def norm_backward(d_normed, unit_rows, inverse_rms, gain_row):
     scaled = d_normed * gain_row
     return inverse_rms * (
-        scaled - unit_rows * jnp.mean(scaled * unit_rows, axis=-1, keepdims=True)
+        scaled - unit_rows * jnp.mean(scaled * unit_rows, axis=1, keepdims=True)
     )
 
 
@@ -205,8 +186,17 @@
     return jnp.concatenate([first * cosine - second * sine, second * cosine + first * sine], 0)
 
 
-def attention_forward_kernel(order, *refs):
-    weight_pieces, input_pieces, refs = refs[:4], refs[4:8], refs[8:]
+def three(rows, group):
+    pieces = []
+    for offset in range(GROUP):
+        start = pl.multiple_of((group * GROUP + offset) * HEAD_SIZE, HEAD_SIZE)
+        pieces.append(rows[pl.ds(start, HEAD_SIZE), :])
+    return jnp.concatenate(pieces, 1)
+
+
+def attention_forward_kernel(weight_count, input_count, order, *refs):
+    weight_pieces, refs = refs[:weight_count], refs[weight_count:]
+    input_pieces, refs = refs[:input_count], refs[input_count:]
     cosines, sines, bias, gains, w_project, w_output, normed, queries = refs[:8]
     keys_across, keys, values, log_totals, mixed_across, residual = refs[8:14]
     flat, planes_one, planes_two, w_across, values_across = refs[14:]
@@ -219,22 +209,22 @@
     unflatten_odd(flat, D * QKV_WIDTH // LANES, QUERY_WIDTH // 2, 4, planes_two)
     planes_to_matrix(planes_two, 4, w_output)
     blocks = [piece.at[place] for piece in input_pieces for place in range(piece.shape[0])]
-    gain = gains[0:1, :]
+    gain = jnp.broadcast_to(gains[...], (D, DEVICE_TOKENS))
 
     def one(micro, unused):
         for block, inputs in enumerate(blocks):
             rows = inputs[micro].astype(F32)
-            inverse = lax.rsqrt(jnp.mean(rows * rows, axis=-1, keepdims=True) + NORM_EPSILON)
-            normed[micro, block * DEVICE_TOKENS : (block + 1) * DEVICE_TOKENS, :] = (
+            inverse = lax.rsqrt(jnp.mean(rows * rows, axis=0, keepdims=True) + NORM_EPSILON)
+            normed[micro, :, block * DEVICE_TOKENS : (block + 1) * DEVICE_TOKENS] = (
                 rows * inverse * gain
             ).astype(BF16)
         cosine, sine = cosines[micro], sines[micro]
         own_cosine, own_sine = cosine[:, :DEVICE_TOKENS], sine[:, :DEVICE_TOKENS]
-        query = dot_nt(w_across[:QUERY_WIDTH, :], normed[micro, :DEVICE_TOKENS, :])
+        query = dot(w_across[:QUERY_WIDTH, :], normed[micro, :, :DEVICE_TOKENS])
         for head in range(QUERY_HEADS):
             rows = slice(head * HEAD_SIZE, (head + 1) * HEAD_SIZE)
             queries[micro, rows, :] = rotated(query[rows], own_cosine, own_sine).astype(BF16)
-        other = dot_nt(w_across[QUERY_WIDTH:, :], normed[micro])
+        other = dot(w_across[QUERY_WIDTH:, :], normed[micro])
         for head in range(KEY_VALUE_HEADS):
             rows = slice(head * HEAD_SIZE, (head + 1) * HEAD_SIZE)
             key = rotated(other[rows], cosine, sine)
@@ -243,19 +233,24 @@
             value = other[KV_WIDTH + head * HEAD_SIZE : KV_WIDTH + (head + 1) * HEAD_SIZE]
             values_across[rows, :] = value.astype(BF16)
             values[micro, head] = jnp.transpose(value).astype(BF16)
-        for head in range(QUERY_HEADS):
-            group = head // GROUP
-            rows = slice(head * HEAD_SIZE, (head + 1) * HEAD_SIZE)
+        bias_three = jnp.concatenate([bias[micro]] * GROUP, 1)
+        for group in range(KEY_VALUE_HEADS):
             group_rows = slice(group * HEAD_SIZE, (group + 1) * HEAD_SIZE)
-            scores = dot(keys[micro, group], queries[micro, rows, :] * SCALE) + bias[micro]
+            scores = dot(keys[micro, group], three(queries.at[micro], group) * SCALE) + bias_three
             top = jnp.max(scores, axis=0, keepdims=True)
             weights = jnp.exp(scores - top)
             total = jnp.sum(weights, axis=0, keepdims=True)
             low = (weights * (1.0 / total)).astype(BF16)
-            mixed_across[micro, rows, :] = dot(values_across[group_rows, :], low)
-            log_totals[micro, head : head + 1, :] = top + jnp.log(total)
+            mixed = dot(values_across[group_rows, :], low)
+            log_total = top + jnp.log(total)
+            for offset in range(GROUP):
+                head = group * GROUP + offset
+                lanes = slice(offset * DEVICE_TOKENS, (offset + 1) * DEVICE_TOKENS)
+                mixed_across[micro, head * HEAD_SIZE : (head + 1) * HEAD_SIZE, :] = mixed[:, lanes]
+                log_totals[micro, head : head + 1, :] = log_total[:, lanes]
         mixed = jnp.transpose(mixed_across[micro]).astype(BF16)
-        residual[micro] = blocks[0][micro].astype(F32) + dot(mixed, w_output[...])
+        inputs = jnp.transpose(blocks[0][micro].astype(F32))
+        residual[micro] = inputs + dot(mixed, w_output[...])
         return unused
 
     lax.fori_loop(0, MICRO, one, 0)
@@ -266,11 +261,11 @@
     shape = jax.ShapeDtypeStruct
     rows = sum(piece.shape[0] * piece.shape[1] for piece in weight_pieces)
     return pl.pallas_call(
-        attention_forward_kernel,
+        functools.partial(attention_forward_kernel, len(weight_pieces), len(input_pieces)),
         out_shape=(
             shape((D, QKV_WIDTH), BF16),
             shape((QUERY_WIDTH, D), BF16),
-            shape((MICRO, window, D), BF16),
+            shape((MICRO, D, window), BF16),
             shape((MICRO, QUERY_WIDTH, DEVICE_TOKENS), BF16),
             shape((MICRO, KV_WIDTH, window), BF16),
             shape((MICRO, KEY_VALUE_HEADS, window, HEAD_SIZE), BF16),
@@ -279,7 +274,7 @@
             shape((MICRO, QUERY_WIDTH, DEVICE_TOKENS), F32),
             shape((MICRO, DEVICE_TOKENS, D), F32),
         ),
-        in_specs=[smem()] + vmem(8 + len(tables)),
+        in_specs=[smem()] + vmem(len(weight_pieces) + len(input_pieces) + len(tables)),
         out_specs=tuple(vmem(10)),
         scratch_shapes=[
             pltpu.VMEM((rows, LANES), F32),
@@ -301,6 +296,7 @@
     cotangent,
     gains,
     block_output,
+    d_branch,
     d_residual,
     one_kept,
     one_sent,
@@ -322,12 +318,14 @@
         ].astype(BF16)
     unflatten_odd(flat, D * columns, FF // 2, 4, planes)
     planes_to_matrix(planes, 4, w_down)
-    gain = gains[1:2, :]
+    gain = gains[...]
     rows = jnp.concatenate([residual[micro] for micro in range(MICRO)], 0)
     inverse = lax.rsqrt(jnp.mean(rows * rows, axis=-1, keepdims=True) + NORM_EPSILON)
     unit = rows * inverse
     normed = (unit * gain).astype(BF16)
-    cotangent_low = jnp.concatenate([cotangent[micro, 0] for micro in range(MICRO)], 0)
+    cotangent_low = jnp.concatenate(
+        [jnp.transpose(cotangent[micro].astype(F32)) for micro in range(MICRO)], 0
+    ).astype(BF16)
     part = 256
     for start in range(0, FF, part):
         gate = dot(normed, w_gate_up[:, start : start + part])
@@ -340,12 +338,17 @@
             d_hidden * up * sigmoid * (1.0 + gate * (1.0 - sigmoid))
         ).astype(BF16)
         d_gate_up[:, FF + start : FF + start + part] = (d_hidden * activated).astype(BF16)
-    block_output[...] = (rows + dot(hidden[...], w_down[...])).astype(BF16)
+    result = rows + dot(hidden[...], w_down[...])
     d_normed = dot_nt(d_gate_up[...], w_gate_up[...])
     scaled = d_normed * gain
-    d_residual[...] = cotangent_low.astype(F32) + inverse * (
+    d_rows = cotangent_low.astype(F32) + inverse * (
         scaled - unit * jnp.mean(scaled * unit, axis=-1, keepdims=True)
     )
+    d_branch[...] = d_rows.astype(BF16)
+    for micro in range(MICRO):
+        own = slice(micro * DEVICE_TOKENS, (micro + 1) * DEVICE_TOKENS)
+        block_output[micro] = jnp.transpose(result[own]).astype(BF16)
+        d_residual[micro] = jnp.transpose(d_rows[own])
     normed_across = jnp.transpose(unit * gain).astype(BF16)
     total = jnp.zeros((D, LANES), F32)
     for start in range(0, 2 * FF, part):
@@ -382,8 +385,9 @@
     return pl.pallas_call(
         feedforward_kernel,
         out_shape=(
+            shape((MICRO, D, DEVICE_TOKENS), BF16),
             shape((tokens, D), BF16),
-            shape((tokens, D), F32),
+            shape((MICRO, D, DEVICE_TOKENS), F32),
             one,
             one,
             two,
@@ -391,7 +395,7 @@
             shape((D, 1), F32),
         ),
         in_specs=[smem()] * 3 + vmem(4),
-        out_specs=tuple(vmem(7)),
+        out_specs=tuple(vmem(8)),
         scratch_shapes=[
             pltpu.VMEM((rows, LANES), F32),
             pltpu.VMEM((5, FF, LANES), F32),
@@ -413,43 +417,45 @@
     values,
     log_totals,
     mixed_across,
-    d_residual,
+    d_branch,
     cosines,
     sines,
     bias,
     d_queries,
     d_window,
+    query_grad,
+    window_grad,
+    output_grad,
     d_window_across,
-    grad_across,
-    grad_output,
     d_mixed,
 ):
     blocks = d_window.shape[0]
     cosine, sine = cosines[...], sines[...]
     own_cosine, own_sine = cosine[:, :DEVICE_TOKENS], sine[:, :DEVICE_TOKENS]
-    d_branch = d_residual[...].astype(BF16)
-    d_mixed[...] = dot_nt(w_output[...], d_branch).astype(BF16)
+    d_mixed[...] = dot_nt(w_output[...], d_branch[...]).astype(BF16)
 
     def one(group, unused):
         group_rows = pl.ds(pl.multiple_of(group * HEAD_SIZE, HEAD_SIZE), HEAD_SIZE)
         value_rows = pl.ds(pl.multiple_of(KV_WIDTH + group * HEAD_SIZE, HEAD_SIZE), HEAD_SIZE)
-        d_key = d_value = jnp.zeros((HEAD_SIZE, cosine.shape[1]), F32)
+        query = three(queries, group) * SCALE
+        d_heads = three(d_mixed, group)
+        delta = jnp.sum(d_heads.astype(F32) * three(mixed_across, group), axis=0, keepdims=True)
+        log_total = jnp.concatenate(
+            [log_totals[pl.ds(group * GROUP + offset, 1), :] for offset in range(GROUP)], 1
+        )
+        bias_three = jnp.concatenate([bias[...]] * GROUP, 1)
+        probability = jnp.exp(dot(keys[group], query) + bias_three - log_total)
+        d_probs = dot(values[group], d_heads)
+        d_scores = (probability * (d_probs - delta)).astype(BF16)
+        d_query = dot(keys_across[group_rows, :], d_scores) * SCALE
         for offset in range(GROUP):
-            head = group * GROUP + offset
-            rows = pl.ds(pl.multiple_of(head * HEAD_SIZE, HEAD_SIZE), HEAD_SIZE)
-            query = queries[rows, :] * SCALE
-            d_mixed_head = d_mixed[rows, :]
-            delta = jnp.sum(
-                d_mixed_head.astype(F32) * mixed_across[rows, :], axis=0, keepdims=True
-            )
-            scores = dot(keys[group], query) + bias[...]
-            probability = jnp.exp(scores - log_totals[pl.ds(head, 1), :])
-            d_probs = dot(values[group], d_mixed_head)
-            d_scores = (probability * (d_probs - delta)).astype(BF16)
-            d_query = dot(keys_across[group_rows, :], d_scores) * SCALE
-            d_queries[rows, :] = rotated(d_query, own_cosine, -own_sine).astype(BF16)
-            d_key = d_key + dot_nt(query, d_scores)
-            d_value = d_value + dot_nt(d_mixed_head, probability.astype(BF16))
+            lanes = slice(offset * DEVICE_TOKENS, (offset + 1) * DEVICE_TOKENS)
+            start = pl.multiple_of((group * GROUP + offset) * HEAD_SIZE, HEAD_SIZE)
+            d_queries[pl.ds(start, HEAD_SIZE), :] = rotated(
+                d_query[:, lanes], own_cosine, -own_sine
+            ).astype(BF16)
+        d_key = dot_nt(query, d_scores)
+        d_value = dot_nt(d_heads, probability.astype(BF16))
         d_window_across[group_rows, :] = rotated(d_key, cosine, -sine).astype(BF16)
         d_window_across[value_rows, :] = d_value.astype(BF16)
         return unused
@@ -459,12 +465,9 @@
         d_window[block] = d_window_across[
             :, block * DEVICE_TOKENS : (block + 1) * DEVICE_TOKENS
         ]
-    query_grad = dot(d_queries[...], normed[:DEVICE_TOKENS, :])
-    window_grad = dot(d_window_across[...], normed[...])
-    output_grad = dot(mixed_across[...].astype(BF16), d_branch)
-    grad_across[:QUERY_WIDTH, :] = query_grad
-    grad_across[QUERY_WIDTH:, :] = window_grad
-    grad_output[...] = output_grad
+    query_grad[...] = dot_nt(normed[:, :DEVICE_TOKENS], d_queries[...])
+    window_grad[...] = dot_nt(normed[...], d_window_across[...])
+    output_grad[...] = dot(mixed_across[...].astype(BF16), d_branch[...])
 
 
 def micro_views(micro, operands):
@@ -475,27 +478,22 @@
 
 
 def attention_backward_first(*refs):
-    operands, (d_queries, d_window, grad_across, grad_output, across, d_mixed) = (
-        refs[:12],
-        refs[12:],
-    )
-    attention_backward_body(
-        *micro_views(0, operands), d_queries, d_window, across, grad_across, grad_output, d_mixed
-    )
+    attention_backward_body(*micro_views(0, refs[:12]), *refs[12:])
 
 
 def attention_backward_second(order, w_project, *refs):
-    first_queries, first_window, first_across, first_output = refs[:4]
-    operands, refs = refs[4:16], refs[16:]
+    first_queries, first_window, *first_grads = refs[:5]
+    operands, refs = refs[5:17], refs[17:]
     kept, sent, d_queries, window_kept, window_sent, gain_grad, flat, planes = refs[:8]
-    across, d_mixed, own_window, grad_across, grad_output = refs[8:]
+    across, d_mixed, own_window, query_grad, window_grad, output_grad = refs[8:]
     attention_backward_body(
         *micro_views(1, operands),
         d_queries.at[1],
         own_window,
+        query_grad,
+        window_grad,
+        output_grad,
         across,
-        grad_across,
-        grad_output,
         d_mixed,
     )
     d_queries[0] = first_queries[...]
@@ -504,24 +502,28 @@
         target, place = (window_kept, block) if block < early else (window_sent, block - early)
         target[place, 0] = first_window[block]
         target[place, 1] = own_window[block]
-    grad_across[...] += first_across[...]
-    grad_output[...] += first_output[...]
+    for sums, first in zip((query_grad, window_grad, output_grad), first_grads):
+        sums[...] += first[...]
     total = jnp.zeros((D, LANES), F32)
+    later = [window_grad[:, j * LANES : (j + 1) * LANES] for j in range(3)]
     for j in range(7):
-        piece = jnp.transpose(grad_across[j * LANES : (j + 1) * LANES, :])
+        if j < 4:
+            piece = query_grad[:, j * LANES : (j + 1) * LANES]
+        elif j == 4:
+            piece = jnp.concatenate([query_grad[:, j * LANES :], later[0][:, :HALF]], 1)
+        else:
+            piece = shift_half(later[j - 4], later[j - 5])
         planes[j] = piece
         total = total + piece * w_project[:, j * LANES : (j + 1) * LANES].astype(F32)
-    last = jnp.transpose(grad_across[QKV_WIDTH - LANES :, :])
-    last = pltpu.roll(last, HALF, 1)
-    planes[7] = last
-    last_sum = last[:, :HALF] * w_project[:, 7 * LANES :].astype(F32)
+    planes[7] = pltpu.roll(later[2], HALF, 1)
+    last_sum = planes[7, :, :HALF] * w_project[:, 7 * LANES :].astype(F32)
     gain_grad[...] = jnp.sum(total, axis=1, keepdims=True) + jnp.sum(
         last_sum, axis=1, keepdims=True
     )
     flatten_odd(planes, D // 2, 7, flat, 0)
     for j in range(4):
-        planes[j] = grad_output[:, j * LANES : (j + 1) * LANES]
-    planes[4, :, :HALF] = grad_output[:, 4 * LANES :]
+        planes[j] = output_grad[:, j * LANES : (j + 1) * LANES]
+    planes[4, :, :HALF] = output_grad[:, 4 * LANES :]
     flatten_odd(planes, QUERY_WIDTH // 2, 4, flat, D * QKV_WIDTH // LANES)
     store_blocks(order, flat, sent, sent.shape[1], 0, sent.shape[0])
     store_blocks(order, flat, kept, kept.shape[1], 0, 0)
@@ -529,9 +531,9 @@
 
 def attention_backward(operands, count, rows, final=()):
     shape = jax.ShapeDtypeStruct
-    window = operands[1].shape[1]
+    window = operands[1].shape[2]
     blocks = window // DEVICE_TOKENS
-    sums = [(QKV_WIDTH, D), (QUERY_WIDTH, D)]
+    sums = [(D, QUERY_WIDTH), (D, 2 * KV_WIDTH), (QUERY_WIDTH, D)]
     scratch = [
         pltpu.VMEM((2 * KV_WIDTH, window), BF16),
         pltpu.VMEM((QUERY_WIDTH, DEVICE_TOKENS), BF16),
@@ -615,13 +617,27 @@
     attention_length = attention_weights.shape[0]
     feedforward_length = feedforward_weights.shape[0]
     reach = min((DOC_MAX + DEVICE_TOKENS - 2) // DEVICE_TOKENS, seq_count - 1)
-    paired = is_power_of_two(seq_count) and reach == seq_count - 1
-    butterfly = is_power_of_two(owner_count) and attention_length % (8 * LANES) == 0
-    stages = gather_stages()
-    order = block_order(stages)
-    seq_stages = [stage for stage in stages if stage[0] == "seq"]
-
-    own_inputs = block_input[:, 0]
+    dp_count = lax.axis_size("dp")
+    butterfly = (
+        is_power_of_two(seq_count)
+        and seq_count >= 4
+        and reach == seq_count - 1
+        and dp_count == 4
+        and attention_length % (8 * LANES) == 0
+    )
+    pair = (0, 1)
+    line = range(0, seq_count, 2)
+    square = range(0, owner_count, seq_count)
+    order = [c ^ r ^ s for c in pair for r in square for s in line]
+    turned = [
+        c ^ x ^ y ^ s
+        for c in pair
+        for x in (0, seq_count)
+        for y in (0, 2 * seq_count)
+        for s in line
+    ]
+
+    own_inputs = jnp.swapaxes(block_input[:, 0], 1, 2)
     straight = jnp.arange(BLOCKS, dtype=jnp.int32)
     tiled_rows = feedforward_length % (8 * LANES) == 0
     feedforward_low = feedforward_weights.astype(BF16)
@@ -630,8 +646,8 @@
     feedforward_blocks = lax.all_gather(feedforward_low, both, axis=0, tiled=True)
     feedforward_blocks = feedforward_blocks.reshape(BLOCKS, -1, LANES)
 
-    if paired:
-        window_blocks = seq_place ^ jnp.array(block_order(seq_stages), jnp.int32)
+    if butterfly:
+        window_blocks = seq_place ^ jnp.array([c ^ s for c in pair for s in line], jnp.int32)
     else:
         window_blocks = seq_place - jnp.arange(reach + 1, dtype=jnp.int32)
     token = jnp.arange(DEVICE_TOKENS, dtype=jnp.int32)
@@ -652,32 +668,19 @@
 
     attention_low = attention_weights.astype(BF16)
     if butterfly:
-        orders = [
-            jnp.array(block_order(path), jnp.int32) ^ owner_place
-            for path in (stages, swap_dp(stages))
-        ]
-    else:
-        orders = [straight, straight]
-    if butterfly and paired:
+        orders = [jnp.array(path, jnp.int32) ^ owner_place for path in (turned, order)]
         weights = attention_low.reshape(1, attention_length // LANES, LANES)
         window_inputs = own_inputs[None]
-        inputs_far = exchange(window_inputs, "seq", seq_stages[0][1])
-        for index, (axis, bit, unused_flat) in enumerate(stages[:-1]):
-            far = exchange(weights, axis, bit)
-            if index == 0:
-                far, cosines, sines, bias = together(far, cosines, sines, bias)
-            if index < len(stages) - 2:
-                weights = jnp.concatenate([weights, far], 0)
-            if 0 < index < len(seq_stages) - 1:
-                window_inputs = jnp.concatenate([window_inputs, inputs_far], 0)
-                far_weights, window_inputs = together(weights, window_inputs)
-                weights = far_weights
-                inputs_far = exchange(window_inputs, "seq", seq_stages[index][1])
-        axis, bit, unused_flat = stages[-1]
-        weight_pieces = [weights, far]
-        weight_pieces += [exchange(piece, axis, bit) for piece in weight_pieces]
-        input_pieces = [window_inputs, inputs_far]
-        input_pieces += [exchange(piece, axis, bit) for piece in input_pieces]
+        news = [exchange(weights, "seq", place) for place in line[1:]]
+        inputs_near = [window_inputs]
+        inputs_near += [exchange(window_inputs, "seq", place) for place in line[1:]]
+        news = together(*news, cosines, sines, bias)
+        *news, cosines, sines, bias = news
+        weights = jnp.concatenate([weights, *news], 0)
+        weight_pieces = [weights]
+        weight_pieces += [exchange(weights, "dp", place) for place in range(1, dp_count)]
+        weight_pieces += [exchange(piece, "seq", 1) for piece in weight_pieces]
+        input_pieces = inputs_near + [exchange(piece, "seq", 1) for piece in inputs_near]
     else:
         weights = lax.all_gather(attention_low, both, axis=0, tiled=True)
         weights = weights.reshape(BLOCKS, -1, LANES)
@@ -709,12 +712,15 @@
         mixed_across,
         residual,
     ) = attention_forward(
-        orders[0], weight_pieces, input_pieces, cosines, sines, bias, norm_gains
-    )
-    block_output, d_residual, *parts, gain_two = feedforward(
-        (straight, *orders), feedforward_blocks, residual, out_grad, norm_gains
-    )
-    block_output = block_output.reshape(MICRO, DEVICE_TOKENS, D)
+        orders[1], weight_pieces, input_pieces, cosines, sines, bias, norm_gains[0][:, None]
+    )
+    block_output, d_branch, d_residual, *parts, gain_two = feedforward(
+        (straight, *orders),
+        feedforward_blocks,
+        residual,
+        jnp.swapaxes(out_grad[:, 0], 1, 2),
+        norm_gains[1:2],
+    )
     operands = (
         w_output,
         normed_one,
@@ -724,65 +730,71 @@
         values,
         log_totals,
         mixed_across,
-        d_residual,
+        d_branch,
         cosines,
         sines,
         bias,
     )
-    d_residual = d_residual.reshape(MICRO, DEVICE_TOKENS, D)
     attention_rows = D * (QKV_WIDTH + QUERY_WIDTH) // (LANES * BLOCKS)
-    if butterfly and paired:
-        paths = [stages[::-1], swap_dp(stages)[::-1]]
-        halving_seq = seq_stages[::-1]
-
-        def send(value, stage):
-            return exchange(value, stage[0], stage[1])
-
-        kept, sent = [parts[0], parts[2]], [parts[1], parts[3]]
-        arrived = [send(part, path[0]) for part, path in zip(sent, paths)]
+    if butterfly:
+        one_kept, one_sent, two_kept, two_sent = parts
+        one_new, two_new = exchange(one_sent, "seq", 1), exchange(two_sent, "seq", 1)
         first = attention_backward(operands, BLOCKS, attention_rows)
-        arrived = together(*arrived, *first)
-        first = arrived[2:]
-        kept, sent = zip(*[halve_step(part, new) for part, new in zip(kept, arrived)])
-        first_across, *sent = together(first[2], *sent)
-        arrived = [send(part, path[1]) for part, path in zip(sent, paths)]
+        one_new, two_new, *first = together(one_new, two_new, *first)
+        one_kept, one_sent = add_up(one_kept, [one_new], 2)
+        two_kept, two_sent = add_up(two_kept, [two_new], 2)
+        one_sent, two_sent, *first = together(one_sent, two_sent, *first)
+        one_new, two_new = exchange(one_sent, "dp", 1), exchange(two_sent, "dp", 2)
         second = attention_backward(
-            operands,
-            BLOCKS,
-            attention_rows,
-            (orders[0], w_project, first[0], first[1], first_across, first[3]),
+            operands, BLOCKS, attention_rows, (orders[1], w_project, *first)
         )
-        arrived = together(*arrived, *second)
-        attention_kept, attention_sent, d_queries, window_kept, window_sent, gain_one = arrived[2:]
-        kept, sent = zip(*[halve_step(part, new) for part, new in zip(kept, arrived)])
+        one_new, two_new, *second = together(one_new, two_new, *second)
+        kept, sent, d_queries, window_kept, window_sent, gain_one = second
+        one_kept, one_sent = add_up(one_kept, [one_new], 2)
+        two_kept, two_sent = add_up(two_kept, [two_new], 2)
         gains_total = jnp.stack([gain_one[:, 0], gain_two[:, 0]], 0) / norm_gains
-        for index, stage in enumerate(paths[0]):
-            arrivals = {}
-            if index + 2 < len(stages):
-                arrivals["one"] = send(sent[0], paths[0][index + 2])
-                arrivals["two"] = send(sent[1], paths[1][index + 2])
-            arrivals["attention"] = send(attention_sent, stage)
-            if index < len(halving_seq):
-                arrivals["window"] = send(window_sent, halving_seq[index])
-            arrivals["gains"] = send(gains_total, stage)
-            arrivals = lax.optimization_barrier(arrivals)
-            if "one" in arrivals:
-                news = [arrivals["one"], arrivals["two"]]
-                kept, sent = zip(*[halve_step(part, new) for part, new in zip(kept, news)])
-            attention_kept, attention_sent = halve_step(attention_kept, arrivals["attention"])
-            if "window" in arrivals:
-                window_kept, window_sent = halve_step(window_kept, arrivals["window"])
-            gains_total = gains_total + arrivals["gains"]
-        attention_owned = attention_kept.reshape(-1)
-        d_own = window_kept[0].astype(BF16)
-        feedforward_owned = jnp.concatenate([kept[0][0], kept[1][0]], 0).reshape(-1)
+
+        new = exchange(sent, "seq", 1)
+        one_new, two_new = exchange(one_sent, "dp", 2), exchange(two_sent, "dp", 1)
+        window_new = exchange(window_sent, "seq", 1)
+        gains_new = exchange(gains_total, "seq", 1)
+        new, one_new, two_new, window_new, gains_new = together(
+            new, one_new, two_new, window_new, gains_new
+        )
+        kept, *sent = add_up(kept, [new], dp_count)
+        gains_total = gains_total + gains_new
+        news = [exchange(part, "dp", place + 1) for place, part in enumerate(sent)]
+        gains_news = [exchange(gains_total, "dp", place) for place in range(1, dp_count)]
+
+        one_kept, *one_sent = add_up(one_kept, [one_new], len(line))
+        two_kept, *two_sent = add_up(two_kept, [two_new], len(line))
+        window_kept, *window_sent = add_up(window_kept, [window_new], len(line))
+
+        def along_line(parts):
+            return [exchange(part, "seq", place) for place, part in zip(line[1:], parts)]
+
+        one_news, two_news = along_line(one_sent), along_line(two_sent)
+        window_news = along_line(window_sent)
+
+        arrived = together(*news, *gains_news)
+        news, gains_news = arrived[: len(news)], arrived[len(news) :]
+        kept, *sent = add_up(kept, news, len(line))
+        gains_total = pair_sum([gains_total, *gains_news])
+        news = along_line(sent)
+        gains_news = along_line([gains_total] * len(sent))
+        gains_total = pair_sum([gains_total, *gains_news])
+        attention_owned = add_up(kept, news, 1)[0].reshape(-1)
+        feedforward_owned = jnp.concatenate(
+            [add_up(one_kept, one_news, 1)[0][0], add_up(two_kept, two_news, 1)[0][0]], 0
+        ).reshape(-1)
+        d_own = add_up(window_kept, window_news, 1)[0][0].astype(BF16)
     else:
         halves = [jnp.concatenate(parts[index : index + 2], 0) for index in (0, 2)]
         grads = jnp.concatenate(halves, 1).reshape(-1)
         feedforward_owned = lax.psum_scatter(grads, both, scatter_dimension=0, tiled=True)
         first = attention_backward(operands, BLOCKS, attention_rows)
         kept, sent, d_queries, window_kept, window_sent, gain_one = attention_backward(
-            operands, BLOCKS, attention_rows, (orders[0], w_project, *first)
+            operands, BLOCKS, attention_rows, (orders[1], w_project, *first)
         )
         attention_owned = lax.psum_scatter(
             jnp.concatenate([kept, sent], 0).reshape(-1), both, scatter_dimension=0, tiled=True
@@ -796,9 +808,11 @@
         d_own = d_own.astype(BF16)
         gains_total = jnp.stack([gain_one[:, 0], gain_two[:, 0]], 0) / norm_gains
         gains_total = lax.psum(gains_total, both)
-    d_normed_one = matmul("met,de->mtd", jnp.concatenate([d_queries, d_own], 1), w_project)
+    d_normed_one = matmul("de,met->mdt", w_project, jnp.concatenate([d_queries, d_own], 1))
     unit_one, inverse_one = unit_norm(own_inputs.astype(F32))
-    input_grad = d_residual + norm_backward(d_normed_one, unit_one, inverse_one, norm_gains[0])
+    input_grad = d_residual + norm_backward(
+        d_normed_one, unit_one, inverse_one, norm_gains[0][None, :, None]
+    )
 
     attention_place = owner_place * attention_length + jnp.arange(attention_length, dtype=jnp.int32)
     attention_rate = jnp.where(
@@ -828,8 +842,8 @@
     )
     new_gains = adam_update(norm_gains, gain_moment, gain_square, gains_total, GAIN_RATE, 0.0)
     return (
-        block_output[:, None],
-        input_grad[:, None],
+        jnp.swapaxes(block_output, 1, 2)[:, None],
+        jnp.swapaxes(input_grad, 1, 2)[:, None],
         *new_attention,
         *new_feedforward,
         *new_gains,

time: 216 us -> 223 us (1.032)
  waiting for transfers between devices: 53.9 us -> 74.1 us
  local copies, waits for them, and re-layouts: 16.4 us -> 1.75 us
  starting transfers between devices: 38.2 us -> 46.7 us
  Pallas kernels: 64.1 us -> 56.9 us
    all_gather x1, waiting for transfers between devices: 1.75 us -> 14 us  [on_device(): lax.all_gather(feedforward_low, both, axis=0, tiled=True)]
    convert_element_type x33 -> x6, other arithmetic: 16.7 us -> 6.09 us  [the longest x5 5.03 us: add_up(): results.append(total.astype(BF16) if index else total)]
    ppermute x33 -> x47, starting transfers between devices: 38.2 us -> 46.7 us  [exchange(): lax.ppermute(value, axis, [(place, place ^ bit) for place in range(count)])]
    ppermute x33 -> x47, waiting for transfers between devices: 52.1 us -> 60.1 us  [exchange(): lax.ppermute(value, axis, [(place, place ^ bit) for place in range(count)])]
    unnamed x88 -> x56, local copies, waits for them, and re-layouts: 8.15 us -> 0.75 us
    add x4 -> x6, other arithmetic: 0.03 us -> 7.29 us  [the longest x4 7.27 us: add_up(): total = total + new[rows].astype(F32)]
    ppermute x3 -> x0, local copies, waits for them, and re-layouts: 5.41 us -> none  [exchange(): lax.ppermute(value, axis, [(place, place ^ bit) for place in range(count)])]
    pallas_call x2, Pallas kernels: 36.1 us -> 31.5 us  [the longest x1 16.1 us: attention_forward(): pl.pallas_call(functools.partial(attention_forward_kernel, len(weight_pie...]
  transfers between devices with their start and end apart: 34 -> 48, of which waited for: 12 -> 20; matrix products, arithmetic and copies ran while one was open for 14% -> 11% of each run, Pallas kernels for 23% -> 19%
where the time goes in v3:
time: 223 us; the launch traced here: 222 us
  waiting for transfers between devices  74.1 us (33%)
  Pallas kernels  56.9 us (26%)
  starting transfers between devices  46.7 us (21%)
  other arithmetic  27.8 us (12%)
  between operations  14.5 us (7%)
    ppermute x47, waiting for transfers between devices, exchange(): lax.ppermute(value, axis, [(place, place ^ bit) for place in range(count)])  60.1 us
    ppermute x47, starting transfers between devices, exchange(): lax.ppermute(value, axis, [(place, place ^ bit) for place in range(count)])  46.7 us
    pallas_call x2, Pallas kernels, attention_backward(): pl.pallas_call(kernel, out_shape=outputs, in_specs=in_specs, out_specs=tu...  25.4 us
    pallas_call x1, Pallas kernels, attention_forward(): pl.pallas_call(functools.partial(attention_forward_kernel, len(weight_pie...  16.1 us
    pallas_call x1, Pallas kernels, feedforward(): pl.pallas_call(feedforward_kernel, out_shape=(shape((MICRO, D, DEVICE_TOK...  15.4 us
    all_gather x1, waiting for transfers between devices, on_device(): lax.all_gather(feedforward_low, both, axis=0, tiled=True)  14 us
    add x4, other arithmetic, add_up(): total = total + new[rows].astype(F32)  7.27 us
    convert_element_type x5, other arithmetic, add_up(): results.append(total.astype(BF16) if index else total)  5.03 us
  transfers between devices with their start and end apart: 48, of which 20 were waited for; matrix products, arithmetic and copies ran while one was open for 11% of the time, Pallas kernels for 19%

profile of v3, /device:TPU:0, one launch (start us, length us, event | category | flops | bytes accessed | tf_op | source)
XLA Modules:
  0.0 222.2 jit_solution(9496157490726674714)
XLA Ops:
  7.2 1.6 convert_bitcast_fusion
  8.9 0.9 convert_bitcast_fusion.1
  9.8 5.0 %collective-permute-start.2 = (bf16[1,216,128]{2,1,0:T(8,128)(2,1)S(1)}, bf16[1,216,128]{2,1,0:T(8,128)(2,1)S(1)}, u32[]{:S(2)}, u32[]{:S(2)}) collective-permute-start(bf16[1,216,128]{2,1,0:T(8,128)(2,1)S(1)} %convert_bitcast_fusion.1), channel_id=1, source_target_pairs={{0,6},{1,7},{2,4},{3,5},{4,2},{5,3},{6,0},{7,1},{8,14},{9,15},{10,... | collective-permute-start | bytes 165896 | tf_op jit(solution)/shard_map/ppermute | solution.py:48
  15.5 1.0 reduce_window_sum.12
  18.5 1.2 and_select_fusion.refs_18_.refs_11_.refs_16_
  19.7 1.8 multiply_sine_fusion
  21.7 2.7 %collective-permute-start.5 = (bf16[4,216,128]{2,1,0:T(8,128)(2,1)S(1)}, bf16[4,216,128]{2,1,0:T(8,128)(2,1)S(1)}, u32[]{:S(2)}, u32[]{:S(2)}) collective-permute-start(bf16[4,216,128]{2,1,0:T(8,128)(2,1)S(1)} %pad_maximum_fusion.refs_0_), channel_id=1, source_target_pairs={{0,24},{8,16},{16,8},{24,0},{1,25},{9,17},{17,9},{25,1},{2,26},{10... | collective-permute-start | bytes 663560 | tf_op jit(solution)/shard_map/ppermute | solution.py:48
  24.3 3.6 %collective-permute-start.12 = (bf16[1,2,576,128]{3,2,1,0:T(8,128)(2,1)S(1)}, bf16[1,2,576,128]{3,2,1,0:T(8,128)(2,1)S(1)}, u32[]{:S(2)}, u32[]{:S(2)}) collective-permute-start(bf16[1,2,576,128]{3,2,1,0:T(8,128)(2,1)S(1)} %bitcast.58), channel_id=1, source_target_pairs={{0,6},{1,7},{2,4},{3,5},{4,2},{5,3},{6,0},{7,1},{8,14},{9,15},{10,... | collective-permute-start | bytes 884744 | tf_op jit(solution)/shard_map/ppermute | solution.py:48
  27.9 0.8 collective-permute-start.10
  29.2 2.4 %collective-permute-done.5.refs_3_ = bf16[4,216,128]{2,1,0:T(8,128)(2,1)S(1)} collective-permute-done((bf16[4,216,128]{2,1,0:T(8,128)(2,1)S(1)}, bf16[4,216,128]{2,1,0:T(8,128)(2,1)S(1)}, u32[]{:S(2)}, u32[]{:S(2)}) %collective-permute-start.5) | collective-permute-done | bytes 221216 | tf_op jit(solution)/shard_map/ppermute | solution.py:48
  31.6 0.8 collective-permute-start.3
  32.4 3.9 %collective-permute-done.4.refs_2_ = bf16[4,216,128]{2,1,0:T(8,128)(2,1)S(1)} collective-permute-done((bf16[4,216,128]{2,1,0:T(8,128)(2,1)S(1)}, bf16[4,216,128]{2,1,0:T(8,128)(2,1)S(1)}, u32[]{:S(2)}, u32[]{:S(2)}) %collective-permute-start.4) | collective-permute-done | bytes 221216 | tf_op jit(solution)/shard_map/ppermute | solution.py:48
  36.3 2.6 %collective-permute-done.3.refs_1_ = bf16[4,216,128]{2,1,0:T(8,128)(2,1)S(1)} collective-permute-done((bf16[4,216,128]{2,1,0:T(8,128)(2,1)S(1)}, bf16[4,216,128]{2,1,0:T(8,128)(2,1)S(1)}, u32[]{:S(2)}, u32[]{:S(2)}) %collective-permute-start.3) | collective-permute-done | bytes 221216 | tf_op jit(solution)/shard_map/ppermute | solution.py:48
  39.4 18.6 %collective-permute-done.11.refs_10_ = bf16[1,2,576,128]{3,2,1,0:T(8,128)(2,1)S(1)} collective-permute-done((bf16[1,2,576,128]{3,2,1,0:T(8,128)(2,1)S(1)}, bf16[1,2,576,128]{3,2,1,0:T(8,128)(2,1)S(1)}, u32[]{:S(2)}, u32[]{:S(2)}) %collective-permute-start.11) | collective-permute-done | bytes 294944 | tf_op jit(solution)/shard_map/ppermute | solution.py:48
  58.5 0.9 copy.33.refs_19_
  60.9 0.7 collective-permute-done.7.refs_5_
  61.7 16.1 %shard_map.230 = (bf16[576,960]{1,0:T(8,128)(2,1)}, bf16[576,576]{1,0:T(8,128)(2,1)}, bf16[2,576,1024]{2,1,0:T(8,128)(2,1)}, bf16[2,576,128]{2,1,0:T(8,128)(2,1)...) custom-call(s32[32]{0:T(128)S(1)} %get-tuple-element.220.order.order, ...), custom_call_target="tpu_custom_call" | custom-call | tf_op jit(solution)/shard_map/pallas_call | solution.py:263
  77.7 14.0 %all-gather.2.cloned.1.call-done = bf16[20736,128]{1,0:T(8,128)(2,1)} async-done(((bf16[648,128]{1,0:T(8,128)(2,1)}), bf16[20736,128]{1,0:T(8,128)(2,1)}) %all-gather.2.cloned.1.call-update) | async-done | bytes 5308432 | tf_op jit(solution)/shard_map/all_gather | solution.py:646
  91.8 15.4 %shard_map.231 = (bf16[2,576,128]{2,1,0:T(8,128)(2,1)}, bf16[256,576]{1,0:T(8,128)(2,1)S(1)}, f32[2,576,128]{2,1,0:T(8,128)S(1)}, bf16[16,320,128]{2,1,0:T(8,128...) custom-call(s32[32]{0:T(128)S(1)} %iota.26.straight, ...), custom_call_target="tpu_custom_call" | custom-call | tf_op jit(solution)/shard_map/pallas_call | solution.py:385
  107.8 10.6 %shard_map.232 = (bf16[576,128]{1,0:T(8,128)(2,1)S(1)}, bf16[8,384,128]{2,1,0:T(8,128)(2,1)}, f32[576,576]{1,0:T(8,128)}, f32[576,384]{1,0:T(8,128)}, f32[576,576]{1,0:T(8,128)}) custom-call(bf16[576,576]{1,0:T(8,128)(2,1)} %get-tuple-element.91.refs_0_.refs_5_, bf16[2,576,1024]{2,1,0:T(8,128)(2,1)} %get-tuple-element.92.refs_1_.refs_6_, ...), custom_call_target="tpu_custom_call" | custom-call | tf_op jit(solution)/shard_map/pallas_call | solution.py:570
  118.4 1.6 convert_add_fusion.1
  120.0 1.4 convert_add_fusion
  121.3 1.5 collective-permute-start.20
  123.7 14.8 %shard_map.233 = (bf16[16,216,128]{2,1,0:T(8,128)(2,1)}, bf16[16,216,128]{2,1,0:T(8,128)(2,1)}, bf16[2,576,128]{2,1,0:T(8,128)(2,1)S(1)}, bf16[4,2,384,128]{3,2,...) custom-call(s32[32]{0:T(128)S(1)} %get-tuple-element.220.order.order_two, ...), custom_call_target="tpu_custom_call" | custom-call | tf_op jit(solution)/shard_map/pallas_call | solution.py:570
  138.5 1.3 collective-permute-done.19
  140.3 1.9 slice_add_fusion.2
  143.0 2.4 %slice_add_fusion = (f32[4,328,128]{2,1,0:T(8,128)S(1)}, bf16[4,328,128]{2,1,0:T(8,128)(2,1)}) fusion(f32[8,328,128]{2,1,0:T(8,128)} %get-tuple-element.189, bf16[8,328,128]{2,1,0:T(8,128)(2,1)} %collective-permute-done.20), kind=kLoop, calls=%fused_computation.12 | loop fusion | flops 839680 | bytes 3022848 | tf_op jit(solution)/shard_map/add | solution.py:58
  145.4 1.4 collective-permute-start.23
  146.9 1.1 collective-permute-done.25
  148.1 4.3 %collective-permute-done.22 = bf16[4,320,128]{2,1,0:T(8,128)(2,1)} collective-permute-done((bf16[4,320,128]{2,1,0:T(8,128)(2,1)}, bf16[4,320,128]{2,1,0:T(8,128)(2,1)}, u32[]{:S(2)}, u32[]{:S(2)}) %collective-permute-start.22) | collective-permute-done | bytes 327712 | tf_op jit(solution)/shard_map/ppermute | solution.py:48
  152.4 2.8 %collective-permute-done.23 = bf16[4,328,128]{2,1,0:T(8,128)(2,1)} collective-permute-done((bf16[4,328,128]{2,1,0:T(8,128)(2,1)}, bf16[4,328,128]{2,1,0:T(8,128)(2,1)}, u32[]{:S(2)}, u32[]{:S(2)}) %collective-permute-start.23) | collective-permute-done | bytes 335904 | tf_op jit(solution)/shard_map/ppermute | solution.py:48
  155.2 1.5 collective-permute-start.34
  156.8 1.4 collective-permute-start.33
  158.2 1.0 fusion.26
  159.2 2.0 collective-permute-start.38
  161.2 1.7 collective-permute-start.40
  162.9 1.5 add_convert_fusion.2
  164.5 1.3 add_convert_fusion.8
  165.8 1.1 fusion.19
  166.9 2.7 %collective-permute-start.41 = (bf16[1,328,128]{2,1,0:T(8,128)(2,1)S(1)}, bf16[1,328,128]{2,1,0:T(8,128)(2,1)S(1)}, u32[]{:S(2)}, u32[]{:S(2)}) collective-permute-start(bf16[1,328,128]{2,1,0:T(8,128)(2,1)S(1)} %get-tuple-element.207), channel_id=1, source_target_pairs={{0,2},{1,3},{2,0},{3,1},{4,6},{5,7},{6,4},{7,5},{8,10},{9,11},{10,... | collective-permute-start | bytes 251912 | tf_op jit(solution)/shard_map/ppermute | solution.py:48
  169.6 1.7 collective-permute-start.43
  171.3 0.9 fusion.30
  172.2 1.5 collective-permute-done.41
  173.7 1.3 collective-permute-start.26
  175.0 1.7 collective-permute-done.43
  176.7 1.7 collective-permute-start.28
  178.4 1.5 collective-permute-done.42
  179.9 0.9 fusion.23
  180.9 1.2 multiply_subtract_fusion
  182.7 4.0 %collective-permute-done.28 = bf16[1,2,384,128]{3,2,1,0:T(8,128)(2,1)S(1)} collective-permute-done((bf16[1,2,384,128]{3,2,1,0:T(8,128)(2,1)S(1)}, bf16[1,2,384,128]{3,2,1,0:T(8,128)(2,1)S(1)}, u32[]{:S(2)}, u32[]{:S(2)}) %collective-permute-start.28) | collective-permute-done | bytes 196640 | tf_op jit(solution)/shard_map/ppermute | solution.py:48
  186.7 1.5 collective-permute-start.31
  188.2 6.1 %collective-permute-done.27 = bf16[1,2,384,128]{3,2,1,0:T(8,128)(2,1)S(1)} collective-permute-done((bf16[1,2,384,128]{3,2,1,0:T(8,128)(2,1)S(1)}, bf16[1,2,384,128]{3,2,1,0:T(8,128)(2,1)S(1)}, u32[]{:S(2)}, u32[]{:S(2)}) %collective-permute-start.27) | collective-permute-done | bytes 196640 | tf_op jit(solution)/shard_map/ppermute | solution.py:48
  194.9 1.1 fusion.16
  196.5 1.5 collective-permute-start.29
  198.0 0.9 fusion.10
  199.0 1.2 collective-permute-done.30
  200.2 2.3 %collective-permute-done.29 = bf16[4,216,128]{2,1,0:T(8,128)(2,1)S(1)} collective-permute-done((bf16[4,216,128]{2,1,0:T(8,128)(2,1)S(1)}, bf16[4,216,128]{2,1,0:T(8,128)(2,1)S(1)}, u32[]{:S(2)}, u32[]{:S(2)}) %collective-permute-start.29) | collective-permute-done | bytes 221216 | tf_op jit(solution)/shard_map/ppermute | solution.py:48
  202.5 1.8 collective-permute-start.46
  204.4 2.5 %collective-permute-start.44 = (f32[2,576]{1,0:T(2,128)S(1)}, f32[2,576]{1,0:T(2,128)S(1)}, u32[]{:S(2)}, u32[]{:S(2)}) collective-permute-start(f32[2,576]{1,0:T(2,128)S(1)} %add_add_fusion.1), channel_id=1, source_target_pairs={{0,2},{1,3},{2,0},{3,1},{4,6},{5,7},{6,4},{7,5},{8,10},{9,11},{10,... | collective-permute-start | bytes 13832 | tf_op jit(solution)/shard_map/ppermute | solution.py:48
  207.1 1.8 collective-permute-start.37
  208.9 1.7 collective-permute-start.36
  211.3 2.0 collective-permute-done.37
  213.2 1.3 collective-permute-done.36
  214.6 0.8 multiply_subtract_fusion.1
  (140 shorter events, 11.4 us)
Async XLA Ops:
  7.2 84.6 %all-gather.2.cloned.1.call-start = ((), (), s32[]{:S(2)}) async-start(), calls=%async_computation | async-start | bytes 5474304 | tf_op jit(solution)/shard_map/all_gather | solution.py:646
  8.9 15.5 %copy-start.6 = (bf16[2,1,128,576]{2,3,1,0:T(8,128)(2,1)S(1)}, bf16[2,1,128,576]{2,3,1,0:T(8,128)(2,1)}, u32[]{:S(2)}) copy-start(bf16[2,1,128,576]{2,3,1,0:T(8,128)(2,1)} %param.15) | copy-start | bytes 884740
  8.9 49.6 %copy-start.23 = (f32[2,576]{1,0:T(2,128)S(1)}, f32[2,576]{1,0:T(2,128)}, u32[]{:S(2)}) copy-start(f32[2,576]{1,0:T(2,128)} %param.20) | copy-start | bytes 13828
  9.8 11.7 %collective-permute-start.2 = (bf16[1,216,128]{2,1,0:T(8,128)(2,1)S(1)}, bf16[1,216,128]{2,1,0:T(8,128)(2,1)S(1)}, u32[]{:S(2)}, u32[]{:S(2)}) collective-permute-start(bf16[1,216,128]{2,1,0:T(8,128)(2,1)S(1)} %convert_bitcast_fusion.1), channel_id=1, source_target_pairs={{0,6},{1,7},{2,4},{3,5},{4,2},{5,3},{6,0},{7,1},{8,14},{9,15},{10,... | collective-permute-start | bytes 165896 | tf_op jit(solution)/shard_map/ppermute | solution.py:48
  14.9 6.7 %collective-permute-start.1 = (bf16[1,216,128]{2,1,0:T(8,128)(2,1)S(1)}, bf16[1,216,128]{2,1,0:T(8,128)(2,1)S(1)}, u32[]{:S(2)}, u32[]{:S(2)}) collective-permute-start(bf16[1,216,128]{2,1,0:T(8,128)(2,1)S(1)} %convert_bitcast_fusion.1), channel_id=1, source_target_pairs={{0,4},{1,5},{2,6},{3,7},{4,0},{5,1},{6,2},{7,3},{8,12},{9,13},{10,... | collective-permute-start | bytes 165896 | tf_op jit(solution)/shard_map/ppermute | solution.py:48
  14.9 6.7 %collective-permute-start = (bf16[1,216,128]{2,1,0:T(8,128)(2,1)S(1)}, bf16[1,216,128]{2,1,0:T(8,128)(2,1)S(1)}, u32[]{:S(2)}, u32[]{:S(2)}) collective-permute-start(bf16[1,216,128]{2,1,0:T(8,128)(2,1)S(1)} %convert_bitcast_fusion.1), channel_id=1, source_target_pairs={{0,2},{1,3},{2,0},{3,1},{4,6},{5,7},{6,4},{7,5},{8,10},{9,11},{10,... | collective-permute-start | bytes 165896 | tf_op jit(solution)/shard_map/ppermute | solution.py:48
  17.2 43.0 %copy-start.26 = (s32[32]{0:T(128)S(1)}, s32[32]{0:T(128)}, u32[]{:S(2)}) copy-start(s32[32]{0:T(128)} %constant.30.clone) | copy-start | bytes 388
  17.2 43.0 %copy-start.27 = (s32[32]{0:T(128)S(1)}, s32[32]{0:T(128)}, u32[]{:S(2)}) copy-start(s32[32]{0:T(128)} %constant.29.clone) | copy-start | bytes 388
  21.6 7.1 %collective-permute-start.6 = (bf16[4,216,128]{2,1,0:T(8,128)(2,1)S(1)}, bf16[4,216,128]{2,1,0:T(8,128)(2,1)S(1)}, u32[]{:S(2)}, u32[]{:S(2)}) collective-permute-start(bf16[4,216,128]{2,1,0:T(8,128)(2,1)S(1)} %pad_maximum_fusion.refs_0_), channel_id=1, source_target_pairs={{0,1},{1,0},{2,3},{3,2},{4,5},{5,4},{6,7},{7,6},{8,9},{9,8},{10,11... | collective-permute-start | bytes 663560 | tf_op jit(solution)/shard_map/ppermute | solution.py:48
  21.7 10.0 %collective-permute-start.5 = (bf16[4,216,128]{2,1,0:T(8,128)(2,1)S(1)}, bf16[4,216,128]{2,1,0:T(8,128)(2,1)S(1)}, u32[]{:S(2)}, u32[]{:S(2)}) collective-permute-start(bf16[4,216,128]{2,1,0:T(8,128)(2,1)S(1)} %pad_maximum_fusion.refs_0_), channel_id=1, source_target_pairs={{0,24},{8,16},{16,8},{24,0},{1,25},{9,17},{17,9},{25,1},{2,26},{10... | collective-permute-start | bytes 663560 | tf_op jit(solution)/shard_map/ppermute | solution.py:48
  24.3 14.6 %collective-permute-start.12 = (bf16[1,2,576,128]{3,2,1,0:T(8,128)(2,1)S(1)}, bf16[1,2,576,128]{3,2,1,0:T(8,128)(2,1)S(1)}, u32[]{:S(2)}, u32[]{:S(2)}) collective-permute-start(bf16[1,2,576,128]{3,2,1,0:T(8,128)(2,1)S(1)} %bitcast.58), channel_id=1, source_target_pairs={{0,6},{1,7},{2,4},{3,5},{4,2},{5,3},{6,0},{7,1},{8,14},{9,15},{10,... | collective-permute-start | bytes 884744 | tf_op jit(solution)/shard_map/ppermute | solution.py:48
  27.9 30.0 %collective-permute-start.11 = (bf16[1,2,576,128]{3,2,1,0:T(8,128)(2,1)S(1)}, bf16[1,2,576,128]{3,2,1,0:T(8,128)(2,1)S(1)}, u32[]{:S(2)}, u32[]{:S(2)}) collective-permute-start(bf16[1,2,576,128]{3,2,1,0:T(8,128)(2,1)S(1)} %bitcast.59), channel_id=1, source_target_pairs={{0,4},{1,5},{2,6},{3,7},{4,0},{5,1},{6,2},{7,3},{8,12},{9,13},{10,... | collective-permute-start | bytes 884744 | tf_op jit(solution)/shard_map/ppermute | solution.py:48
  27.9 30.0 %collective-permute-start.10 = (bf16[1,2,576,128]{3,2,1,0:T(8,128)(2,1)S(1)}, bf16[1,2,576,128]{3,2,1,0:T(8,128)(2,1)S(1)}, u32[]{:S(2)}, u32[]{:S(2)}) collective-permute-start(bf16[1,2,576,128]{3,2,1,0:T(8,128)(2,1)S(1)} %bitcast.60), channel_id=1, source_target_pairs={{0,2},{1,3},{2,0},{3,1},{4,6},{5,7},{6,4},{7,5},{8,10},{9,11},{10,... | collective-permute-start | bytes 884744 | tf_op jit(solution)/shard_map/ppermute | solution.py:48
  28.7 7.6 %collective-permute-start.4 = (bf16[4,216,128]{2,1,0:T(8,128)(2,1)S(1)}, bf16[4,216,128]{2,1,0:T(8,128)(2,1)S(1)}, u32[]{:S(2)}, u32[]{:S(2)}) collective-permute-start(bf16[4,216,128]{2,1,0:T(8,128)(2,1)S(1)} %pad_maximum_fusion.refs_0_), channel_id=1, source_target_pairs={{0,16},{8,24},{16,0},{24,8},{1,17},{9,25},{17,1},{25,9},{2,18},{10... | collective-permute-start | bytes 663560 | tf_op jit(solution)/shard_map/ppermute | solution.py:48
  31.6 7.3 %collective-permute-start.3 = (bf16[4,216,128]{2,1,0:T(8,128)(2,1)S(1)}, bf16[4,216,128]{2,1,0:T(8,128)(2,1)S(1)}, u32[]{:S(2)}, u32[]{:S(2)}) collective-permute-start(bf16[4,216,128]{2,1,0:T(8,128)(2,1)S(1)} %pad_maximum_fusion.refs_0_), channel_id=1, source_target_pairs={{0,8},{8,0},{16,24},{24,16},{1,9},{9,1},{17,25},{25,17},{2,10},{10... | collective-permute-start | bytes 663560 | tf_op jit(solution)/shard_map/ppermute | solution.py:48
  36.3 23.1 %collective-permute-start.13 = (bf16[1,2,576,128]{3,2,1,0:T(8,128)(2,1)S(1)}, bf16[1,2,576,128]{3,2,1,0:T(8,128)(2,1)S(1)}, u32[]{:S(2)}, u32[]{:S(2)}) collective-permute-start(bf16[1,2,576,128]{3,2,1,0:T(8,128)(2,1)S(1)} %bitcast.61), channel_id=1, source_target_pairs={{0,1},{1,0},{2,3},{3,2},{4,5},{5,4},{6,7},{7,6},{8,9},{9,8},{10,11... | collective-permute-start | bytes 884744 | tf_op jit(solution)/shard_map/ppermute | solution.py:48
  38.9 20.6 %collective-permute-start.9 = (bf16[4,216,128]{2,1,0:T(8,128)(2,1)S(1)}, bf16[4,216,128]{2,1,0:T(8,128)(2,1)S(1)}, u32[]{:S(2)}, u32[]{:S(2)}) collective-permute-start(bf16[4,216,128]{2,1,0:T(8,128)(2,1)S(1)} %collective-permute-done.5.refs_3_), channel_id=1, source_target_pairs={{0,1},{1,0},{2,3},{3,2},{4,5},{5,4},{6,7},{7,6},{8,9},{9,8},{10,11... | collective-permute-start | bytes 663560 | tf_op jit(solution)/shard_map/ppermute | solution.py:48
  38.9 22.7 %copy-start.17 = (bf16[1,2,576,128]{3,2,1,0:T(8,128)(2,1)}, bf16[1,2,576,128]{3,2,1,0:T(8,128)(2,1)S(1)}, u32[]{:S(2)}) copy-start(bf16[1,2,576,128]{3,2,1,0:T(8,128)(2,1)S(1)} %collective-permute-done.12.refs_11_) | copy-start | bytes 884740
  38.9 22.7 %collective-permute-start.16 = (bf16[1,2,576,128]{3,2,1,0:T(8,128)(2,1)S(1)}, bf16[1,2,576,128]{3,2,1,0:T(8,128)(2,1)}, u32[]{:S(2)}, u32[]{:S(2)}) collective-permute-start(bf16[1,2,576,128]{3,2,1,0:T(8,128)(2,1)S(1)} %collective-permute-done.12.refs_11_), channel_id=1, source_target_pairs={{0,1},{1,0},{2,3},{3,2},{4,5},{5,4},{6,7},{7,6},{8,9},{9,8},{10,11... | collective-permute-start | bytes 884744 | tf_op jit(solution)/shard_map/ppermute | solution.py:48
  58.0 3.6 %collective-permute-start.15 = (bf16[1,2,576,128]{3,2,1,0:T(8,128)(2,1)S(1)}, bf16[1,2,576,128]{3,2,1,0:T(8,128)(2,1)}, u32[]{:S(2)}, u32[]{:S(2)}) collective-permute-start(bf16[1,2,576,128]{3,2,1,0:T(8,128)(2,1)S(1)} %collective-permute-done.11.refs_10_), channel_id=1, source_target_pairs={{0,1},{1,0},{2,3},{3,2},{4,5},{5,4},{6,7},{7,6},{8,9},{9,8},{10,11... | collective-permute-start | bytes 884744 | tf_op jit(solution)/shard_map/ppermute | solution.py:48
  58.0 3.6 %collective-permute-start.14 = (bf16[1,2,576,128]{3,2,1,0:T(8,128)(2,1)S(1)}, bf16[1,2,576,128]{3,2,1,0:T(8,128)(2,1)}, u32[]{:S(2)}, u32[]{:S(2)}) collective-permute-start(bf16[1,2,576,128]{3,2,1,0:T(8,128)(2,1)S(1)} %collective-permute-done.10.refs_9_), channel_id=1, source_target_pairs={{0,1},{1,0},{2,3},{3,2},{4,5},{5,4},{6,7},{7,6},{8,9},{9,8},{10,11... | collective-permute-start | bytes 884744 | tf_op jit(solution)/shard_map/ppermute | solution.py:48
  59.4 1.5 collective-permute-start.8
  60.1 1.5 collective-permute-start.7
  61.6 30.1 %copy-start.4 = (bf16[2,1,128,576]{2,3,1,0:T(8,128)(2,1)S(1)}, bf16[2,1,128,576]{2,3,1,0:T(8,128)(2,1)}, u32[]{:S(2)}) copy-start(bf16[2,1,128,576]{2,3,1,0:T(8,128)(2,1)} %param.16) | copy-start | bytes 884740
  91.8 16.0 %copy-start = (f32[2,32,1024]{2,1,0:T(8,128)S(1)}, f32[2,32,1024]{2,1,0:T(8,128)}, u32[]{:S(2)}) copy-start(f32[2,32,1024]{2,1,0:T(8,128)} %get-tuple-element.83.refs_17_.refs_10_.refs_15_) | copy-start | bytes 786436
  91.8 16.0 %copy-start.1 = (f32[2,32,1024]{2,1,0:T(8,128)S(1)}, f32[2,32,1024]{2,1,0:T(8,128)}, u32[]{:S(2)}) copy-start(f32[2,32,1024]{2,1,0:T(8,128)} %get-tuple-element.82.refs_16_.refs_9_.refs_14_) | copy-start | bytes 786436
  91.8 16.0 %copy-start.2 = (f32[2,576,128]{2,1,0:T(8,128)S(1)}, f32[2,576,128]{2,1,0:T(8,128)}, u32[]{:S(2)}) copy-start(f32[2,576,128]{2,1,0:T(8,128)} %get-tuple-element.98.refs_7_.refs_12_) | copy-start | bytes 1769476
  91.8 16.0 %copy-start.3 = (bf16[2,576,128]{2,1,0:T(8,128)(2,1)S(1)}, bf16[2,576,128]{2,1,0:T(8,128)(2,1)}, u32[]{:S(2)}) copy-start(bf16[2,576,128]{2,1,0:T(8,128)(2,1)} %get-tuple-element.93.refs_2_.refs_7_) | copy-start | bytes 884740
  107.2 11.1 %collective-permute-start.18 = (bf16[16,328,128]{2,1,0:T(8,128)(2,1)}, bf16[16,328,128]{2,1,0:T(8,128)(2,1)S(1)}, u32[]{:S(2)}, u32[]{:S(2)}) collective-permute-start(bf16[16,328,128]{2,1,0:T(8,128)(2,1)} %get-tuple-element.90), channel_id=1, source_target_pairs={{0,1},{1,0},{2,3},{3,2},{4,5},{5,4},{6,7},{7,6},{8,9},{9,8},{10,11... | collective-permute-start | bytes 4030472 | tf_op jit(solution)/shard_map/ppermute | solution.py:48
  107.5 10.8 %collective-permute-start.17 = (bf16[16,320,128]{2,1,0:T(8,128)(2,1)}, bf16[16,320,128]{2,1,0:T(8,128)(2,1)S(1)}, u32[]{:S(2)}, u32[]{:S(2)}) collective-permute-start(bf16[16,320,128]{2,1,0:T(8,128)(2,1)} %get-tuple-element.89), channel_id=1, source_target_pairs={{0,1},{1,0},{2,3},{3,2},{4,5},{5,4},{6,7},{7,6},{8,9},{9,8},{10,11... | collective-permute-start | bytes 3932168 | tf_op jit(solution)/shard_map/ppermute | solution.py:48
  121.3 18.4 %collective-permute-start.20 = (bf16[8,328,128]{2,1,0:T(8,128)(2,1)S(1)}, bf16[8,328,128]{2,1,0:T(8,128)(2,1)}, u32[]{:S(2)}, u32[]{:S(2)}) collective-permute-start(bf16[8,328,128]{2,1,0:T(8,128)(2,1)S(1)} %get-tuple-element.114), channel_id=1, source_target_pairs={{0,16},{8,24},{16,0},{24,8},{1,17},{9,25},{17,1},{25,9},{2,18},{10... | collective-permute-start | bytes 2015240 | tf_op jit(solution)/shard_map/ppermute | solution.py:48
  122.8 16.9 %collective-permute-start.19 = (bf16[8,320,128]{2,1,0:T(8,128)(2,1)}, bf16[8,320,128]{2,1,0:T(8,128)(2,1)}, u32[]{:S(2)}, u32[]{:S(2)}) collective-permute-start(bf16[8,320,128]{2,1,0:T(8,128)(2,1)} %get-tuple-element.113), channel_id=1, source_target_pairs={{0,8},{8,0},{16,24},{24,16},{1,9},{9,1},{17,25},{25,17},{2,10},{10... | collective-permute-start | bytes 1966088 | tf_op jit(solution)/shard_map/ppermute | solution.py:48
  123.6 16.6 %copy-start.5 = (f32[8,320,128]{2,1,0:T(8,128)S(1)}, f32[8,320,128]{2,1,0:T(8,128)}, u32[]{:S(2)}) copy-start(f32[8,320,128]{2,1,0:T(8,128)} %get-tuple-element.191) | copy-start | bytes 3932164
  139.7 15.5 %collective-permute-start.24 = (bf16[4,2,384,128]{3,2,1,0:T(8,128)(2,1)}, bf16[4,2,384,128]{3,2,1,0:T(8,128)(2,1)}, u32[]{:S(2)}, u32[]{:S(2)}) collective-permute-start(bf16[4,2,384,128]{3,2,1,0:T(8,128)(2,1)} %get-tuple-element.132), channel_id=1, source_target_pairs={{0,1},{1,0},{2,3},{3,2},{4,5},{5,4},{6,7},{7,6},{8,9},{9,8},{10,11... | collective-permute-start | bytes 2359304 | tf_op jit(solution)/shard_map/ppermute | solution.py:48
  139.8 15.5 %collective-permute-start.21 = (bf16[16,216,128]{2,1,0:T(8,128)(2,1)}, bf16[16,216,128]{2,1,0:T(8,128)(2,1)}, u32[]{:S(2)}, u32[]{:S(2)}) collective-permute-start(bf16[16,216,128]{2,1,0:T(8,128)(2,1)} %get-tuple-element.129), channel_id=1, source_target_pairs={{0,1},{1,0},{2,3},{3,2},{4,5},{5,4},{6,7},{7,6},{8,9},{9,8},{10,11... | collective-permute-start | bytes 2654216 | tf_op jit(solution)/shard_map/ppermute | solution.py:48
  142.4 10.0 %collective-permute-start.22 = (bf16[4,320,128]{2,1,0:T(8,128)(2,1)}, bf16[4,320,128]{2,1,0:T(8,128)(2,1)}, u32[]{:S(2)}, u32[]{:S(2)}) collective-permute-start(bf16[4,320,128]{2,1,0:T(8,128)(2,1)} %get-tuple-element.196), channel_id=1, source_target_pairs={{0,16},{8,24},{16,0},{24,8},{1,17},{9,25},{17,1},{25,9},{2,18},{10... | collective-permute-start | bytes 983048 | tf_op jit(solution)/shard_map/ppermute | solution.py:48
  143.0 19.9 %copy-start.12 = (bf16[16,216,128]{2,1,0:T(8,128)(2,1)S(1)}, bf16[16,216,128]{2,1,0:T(8,128)(2,1)}, u32[]{:S(2)}) copy-start(bf16[16,216,128]{2,1,0:T(8,128)(2,1)} %get-tuple-element.136) | copy-start | bytes 2654212
  145.4 9.8 %collective-permute-start.23 = (bf16[4,328,128]{2,1,0:T(8,128)(2,1)}, bf16[4,328,128]{2,1,0:T(8,128)(2,1)}, u32[]{:S(2)}, u32[]{:S(2)}) collective-permute-start(bf16[4,328,128]{2,1,0:T(8,128)(2,1)} %get-tuple-element.194), channel_id=1, source_target_pairs={{0,8},{8,0},{16,24},{24,16},{1,9},{9,1},{17,25},{25,17},{2,10},{10... | collective-permute-start | bytes 1007624 | tf_op jit(solution)/shard_map/ppermute | solution.py:48
  146.8 1.2 collective-permute-start.25
  155.2 41.3 %collective-permute-start.34 = (f32[2,576]{1,0:T(2,128)S(1)}, f32[2,576]{1,0:T(2,128)S(1)}, u32[]{:S(2)}, u32[]{:S(2)}) collective-permute-start(f32[2,576]{1,0:T(2,128)S(1)} %fusion.54), channel_id=1, source_target_pairs={{0,24},{8,16},{16,8},{24,0},{1,25},{9,17},{17,9},{25,1},{2,26},{10... | collective-permute-start | bytes 13832 | tf_op jit(solution)/shard_map/ppermute | solution.py:48
  156.8 42.2 %collective-permute-start.33 = (f32[2,576]{1,0:T(2,128)S(1)}, f32[2,576]{1,0:T(2,128)S(1)}, u32[]{:S(2)}, u32[]{:S(2)}) collective-permute-start(f32[2,576]{1,0:T(2,128)S(1)} %fusion.54), channel_id=1, source_target_pairs={{0,16},{8,24},{16,0},{24,8},{1,17},{9,25},{17,1},{25,9},{2,18},{10... | collective-permute-start | bytes 13832 | tf_op jit(solution)/shard_map/ppermute | solution.py:48
  159.2 7.7 %collective-permute-start.38 = (bf16[1,320,128]{2,1,0:T(8,128)(2,1)S(1)}, bf16[1,320,128]{2,1,0:T(8,128)(2,1)S(1)}, u32[]{:S(2)}, u32[]{:S(2)}) collective-permute-start(bf16[1,320,128]{2,1,0:T(8,128)(2,1)S(1)} %get-tuple-element.210), channel_id=1, source_target_pairs={{0,2},{1,3},{2,0},{3,1},{4,6},{5,7},{6,4},{7,5},{8,10},{9,11},{10,... | collective-permute-start | bytes 245768 | tf_op jit(solution)/shard_map/ppermute | solution.py:48
  161.2 8.4 %collective-permute-start.40 = (bf16[1,320,128]{2,1,0:T(8,128)(2,1)S(1)}, bf16[1,320,128]{2,1,0:T(8,128)(2,1)S(1)}, u32[]{:S(2)}, u32[]{:S(2)}) collective-permute-start(bf16[1,320,128]{2,1,0:T(8,128)(2,1)S(1)} %get-tuple-element.211), channel_id=1, source_target_pairs={{0,6},{1,7},{2,4},{3,5},{4,2},{5,3},{6,0},{7,1},{8,14},{9,15},{10,... | collective-permute-start | bytes 245768 | tf_op jit(solution)/shard_map/ppermute | solution.py:48
  162.9 8.4 %collective-permute-start.39 = (bf16[1,320,128]{2,1,0:T(8,128)(2,1)S(1)}, bf16[1,320,128]{2,1,0:T(8,128)(2,1)S(1)}, u32[]{:S(2)}, u32[]{:S(2)}) collective-permute-start(bf16[1,320,128]{2,1,0:T(8,128)(2,1)S(1)} %get-tuple-element.212), channel_id=1, source_target_pairs={{0,4},{1,5},{2,6},{3,7},{4,0},{5,1},{6,2},{7,3},{8,12},{9,13},{10,... | collective-permute-start | bytes 245768 | tf_op jit(solution)/shard_map/ppermute | solution.py:48
  165.8 15.1 %copy-start.9 = (f32[82944]{0:T(1024)S(1)}, f32[82944]{0:T(1024)}, u32[]{:S(2)}) copy-start(f32[82944]{0:T(1024)} %param.19) | copy-start | bytes 995332
  166.9 6.8 %collective-permute-start.41 = (bf16[1,328,128]{2,1,0:T(8,128)(2,1)S(1)}, bf16[1,328,128]{2,1,0:T(8,128)(2,1)S(1)}, u32[]{:S(2)}, u32[]{:S(2)}) collective-permute-start(bf16[1,328,128]{2,1,0:T(8,128)(2,1)S(1)} %get-tuple-element.207), channel_id=1, source_target_pairs={{0,2},{1,3},{2,0},{3,1},{4,6},{5,7},{6,4},{7,5},{8,10},{9,11},{10,... | collective-permute-start | bytes 251912 | tf_op jit(solution)/shard_map/ppermute | solution.py:48
  169.6 7.1 %collective-permute-start.43 = (bf16[1,328,128]{2,1,0:T(8,128)(2,1)S(1)}, bf16[1,328,128]{2,1,0:T(8,128)(2,1)S(1)}, u32[]{:S(2)}, u32[]{:S(2)}) collective-permute-start(bf16[1,328,128]{2,1,0:T(8,128)(2,1)S(1)} %get-tuple-element.208), channel_id=1, source_target_pairs={{0,6},{1,7},{2,4},{3,5},{4,2},{5,3},{6,0},{7,1},{8,14},{9,15},{10,... | collective-permute-start | bytes 251912 | tf_op jit(solution)/shard_map/ppermute | solution.py:48
  171.3 8.6 %collective-permute-start.42 = (bf16[1,328,128]{2,1,0:T(8,128)(2,1)S(1)}, bf16[1,328,128]{2,1,0:T(8,128)(2,1)S(1)}, u32[]{:S(2)}, u32[]{:S(2)}) collective-permute-start(bf16[1,328,128]{2,1,0:T(8,128)(2,1)S(1)} %get-tuple-element.209), channel_id=1, source_target_pairs={{0,4},{1,5},{2,6},{3,7},{4,0},{5,1},{6,2},{7,3},{8,12},{9,13},{10,... | collective-permute-start | bytes 251912 | tf_op jit(solution)/shard_map/ppermute | solution.py:48
  173.7 8.4 %collective-permute-start.26 = (bf16[1,2,384,128]{3,2,1,0:T(8,128)(2,1)S(1)}, bf16[1,2,384,128]{3,2,1,0:T(8,128)(2,1)S(1)}, u32[]{:S(2)}, u32[]{:S(2)}) collective-permute-start(bf16[1,2,384,128]{3,2,1,0:T(8,128)(2,1)S(1)} %get-tuple-element.201), channel_id=1, source_target_pairs={{0,2},{1,3},{2,0},{3,1},{4,6},{5,7},{6,4},{7,5},{8,10},{9,11},{10,... | collective-permute-start | bytes 589832 | tf_op jit(solution)/shard_map/ppermute | solution.py:48
  176.7 10.0 %collective-permute-start.28 = (bf16[1,2,384,128]{3,2,1,0:T(8,128)(2,1)S(1)}, bf16[1,2,384,128]{3,2,1,0:T(8,128)(2,1)S(1)}, u32[]{:S(2)}, u32[]{:S(2)}) collective-permute-start(bf16[1,2,384,128]{3,2,1,0:T(8,128)(2,1)S(1)} %get-tuple-element.202), channel_id=1, source_target_pairs={{0,6},{1,7},{2,4},{3,5},{4,2},{5,3},{6,0},{7,1},{8,14},{9,15},{10,... | collective-permute-start | bytes 589832 | tf_op jit(solution)/shard_map/ppermute | solution.py:48
  179.9 14.3 %collective-permute-start.27 = (bf16[1,2,384,128]{3,2,1,0:T(8,128)(2,1)S(1)}, bf16[1,2,384,128]{3,2,1,0:T(8,128)(2,1)S(1)}, u32[]{:S(2)}, u32[]{:S(2)}) collective-permute-start(bf16[1,2,384,128]{3,2,1,0:T(8,128)(2,1)S(1)} %get-tuple-element.203), channel_id=1, source_target_pairs={{0,4},{1,5},{2,6},{3,7},{4,0},{5,1},{6,2},{7,3},{8,12},{9,13},{10,... | collective-permute-start | bytes 589832 | tf_op jit(solution)/shard_map/ppermute | solution.py:48
  182.1 16.9 %collective-permute-start.32 = (f32[2,576]{1,0:T(2,128)S(1)}, f32[2,576]{1,0:T(2,128)S(1)}, u32[]{:S(2)}, u32[]{:S(2)}) collective-permute-start(f32[2,576]{1,0:T(2,128)S(1)} %fusion.54), channel_id=1, source_target_pairs={{0,8},{8,0},{16,24},{24,16},{1,9},{9,1},{17,25},{25,17},{2,10},{10... | collective-permute-start | bytes 13832 | tf_op jit(solution)/shard_map/ppermute | solution.py:48
  186.7 12.3 %collective-permute-start.31 = (bf16[4,216,128]{2,1,0:T(8,128)(2,1)S(1)}, bf16[4,216,128]{2,1,0:T(8,128)(2,1)S(1)}, u32[]{:S(2)}, u32[]{:S(2)}) collective-permute-start(bf16[4,216,128]{2,1,0:T(8,128)(2,1)S(1)} %get-tuple-element.197), channel_id=1, source_target_pairs={{0,24},{8,16},{16,8},{24,0},{1,25},{9,17},{17,9},{25,1},{2,26},{10... | collective-permute-start | bytes 663560 | tf_op jit(solution)/shard_map/ppermute | solution.py:48
  194.3 5.9 %collective-permute-start.30 = (bf16[4,216,128]{2,1,0:T(8,128)(2,1)S(1)}, bf16[4,216,128]{2,1,0:T(8,128)(2,1)S(1)}, u32[]{:S(2)}, u32[]{:S(2)}) collective-permute-start(bf16[4,216,128]{2,1,0:T(8,128)(2,1)S(1)} %get-tuple-element.198), channel_id=1, source_target_pairs={{0,16},{8,24},{16,0},{24,8},{1,17},{9,25},{17,1},{25,9},{2,18},{10... | collective-permute-start | bytes 663560 | tf_op jit(solution)/shard_map/ppermute | solution.py:48
  196.5 6.0 %collective-permute-start.29 = (bf16[4,216,128]{2,1,0:T(8,128)(2,1)S(1)}, bf16[4,216,128]{2,1,0:T(8,128)(2,1)S(1)}, u32[]{:S(2)}, u32[]{:S(2)}) collective-permute-start(bf16[4,216,128]{2,1,0:T(8,128)(2,1)S(1)} %get-tuple-element.199), channel_id=1, source_target_pairs={{0,8},{8,0},{16,24},{24,16},{1,9},{9,1},{17,25},{25,17},{2,10},{10... | collective-permute-start | bytes 663560 | tf_op jit(solution)/shard_map/ppermute | solution.py:48
  198.0 16.5 %copy-start.14 = (f32[27648]{0:T(1024)S(1)}, f32[27648]{0:T(1024)}, u32[]{:S(2)}) copy-start(f32[27648]{0:T(1024)} %param.18) | copy-start | bytes 331780
  198.0 16.5 %copy-start.21 = (f32[27648]{0:T(1024)S(1)}, f32[27648]{0:T(1024)}, u32[]{:S(2)}) copy-start(f32[27648]{0:T(1024)} %param.21) | copy-start | bytes 331780
  198.0 16.5 %copy-start.22 = (f32[27648]{0:T(1024)S(1)}, f32[27648]{0:T(1024)}, u32[]{:S(2)}) copy-start(f32[27648]{0:T(1024)} %param.22) | copy-start | bytes 331780
  202.5 6.4 %collective-permute-start.46 = (f32[2,576]{1,0:T(2,128)S(1)}, f32[2,576]{1,0:T(2,128)S(1)}, u32[]{:S(2)}, u32[]{:S(2)}) collective-permute-start(f32[2,576]{1,0:T(2,128)S(1)} %add_add_fusion.1), channel_id=1, source_target_pairs={{0,6},{1,7},{2,4},{3,5},{4,2},{5,3},{6,0},{7,1},{8,14},{9,15},{10,... | collective-permute-start | bytes 13832 | tf_op jit(solution)/shard_map/ppermute | solution.py:48
  204.3 6.3 %collective-permute-start.45 = (f32[2,576]{1,0:T(2,128)S(1)}, f32[2,576]{1,0:T(2,128)S(1)}, u32[]{:S(2)}, u32[]{:S(2)}) collective-permute-start(f32[2,576]{1,0:T(2,128)S(1)} %add_add_fusion.1), channel_id=1, source_target_pairs={{0,4},{1,5},{2,6},{3,7},{4,0},{5,1},{6,2},{7,3},{8,12},{9,13},{10,... | collective-permute-start | bytes 13832 | tf_op jit(solution)/shard_map/ppermute | solution.py:48
  204.4 6.2 %collective-permute-start.44 = (f32[2,576]{1,0:T(2,128)S(1)}, f32[2,576]{1,0:T(2,128)S(1)}, u32[]{:S(2)}, u32[]{:S(2)}) collective-permute-start(f32[2,576]{1,0:T(2,128)S(1)} %add_add_fusion.1), channel_id=1, source_target_pairs={{0,2},{1,3},{2,0},{3,1},{4,6},{5,7},{6,4},{7,5},{8,10},{9,11},{10,... | collective-permute-start | bytes 13832 | tf_op jit(solution)/shard_map/ppermute | solution.py:48
  207.0 4.2 %collective-permute-start.35 = (bf16[1,216,128]{2,1,0:T(8,128)(2,1)S(1)}, bf16[1,216,128]{2,1,0:T(8,128)(2,1)S(1)}, u32[]{:S(2)}, u32[]{:S(2)}) collective-permute-start(bf16[1,216,128]{2,1,0:T(8,128)(2,1)S(1)} %get-tuple-element.204), channel_id=1, source_target_pairs={{0,2},{1,3},{2,0},{3,1},{4,6},{5,7},{6,4},{7,5},{8,10},{9,11},{10,... | collective-permute-start | bytes 165896 | tf_op jit(solution)/shard_map/ppermute | solution.py:48
  207.1 6.1 %collective-permute-start.37 = (bf16[1,216,128]{2,1,0:T(8,128)(2,1)S(1)}, bf16[1,216,128]{2,1,0:T(8,128)(2,1)S(1)}, u32[]{:S(2)}, u32[]{:S(2)}) collective-permute-start(bf16[1,216,128]{2,1,0:T(8,128)(2,1)S(1)} %get-tuple-element.205), channel_id=1, source_target_pairs={{0,6},{1,7},{2,4},{3,5},{4,2},{5,3},{6,0},{7,1},{8,14},{9,15},{10,... | collective-permute-start | bytes 165896 | tf_op jit(solution)/shard_map/ppermute | solution.py:48
  208.9 5.6 %collective-permute-start.36 = (bf16[1,216,128]{2,1,0:T(8,128)(2,1)S(1)}, bf16[1,216,128]{2,1,0:T(8,128)(2,1)S(1)}, u32[]{:S(2)}, u32[]{:S(2)}) collective-permute-start(bf16[1,216,128]{2,1,0:T(8,128)(2,1)S(1)} %get-tuple-element.206), channel_id=1, source_target_pairs={{0,4},{1,5},{2,6},{3,7},{4,0},{5,1},{6,2},{7,3},{8,12},{9,13},{10,... | collective-permute-start | bytes 165896 | tf_op jit(solution)/shard_map/ppermute | solution.py:48
  (12 other events, 95.7 us)
Sparse Core Ops, SparseCore 0:
  10.9 80.8 all-gather.1

commit v4 on v3

--- a/solution.py
+++ b/solution.py
@@ -39,13 +39,12 @@
 F32 = jnp.float32
 
 
-def is_power_of_two(count):
-    return count & (count - 1) == 0
-
-
-def exchange(value, axis, bit):
+def exchange(value, axis, bit, way=0):
     count = lax.axis_size(axis)
-    return lax.ppermute(value, axis, [(place, place ^ bit) for place in range(count)])
+    pairs = [(place, place ^ bit) for place in range(count)]
+    if way:
+        pairs = [(source, target) for source, target in pairs if (target - source) * way > 0]
+    return lax.ppermute(value, axis, pairs)
 
 
 def add_up(kept, news, parts):
@@ -60,10 +59,9 @@
     return results
 
 
-def pair_sum(values):
-    while len(values) > 1:
-        values = [one + two for one, two in zip(values[::2], values[1::2])]
-    return values[0]
+def both_bits(total, axis, one, two):
+    total = total + exchange(total, axis, one)
+    return total + exchange(total, axis, two)
 
 
 def together(*values):
@@ -619,8 +617,7 @@
     reach = min((DOC_MAX + DEVICE_TOKENS - 2) // DEVICE_TOKENS, seq_count - 1)
     dp_count = lax.axis_size("dp")
     butterfly = (
-        is_power_of_two(seq_count)
-        and seq_count >= 4
+        seq_count == 8
         and reach == seq_count - 1
         and dp_count == 4
         and attention_length % (8 * LANES) == 0
@@ -629,12 +626,11 @@
     line = range(0, seq_count, 2)
     square = range(0, owner_count, seq_count)
     order = [c ^ r ^ s for c in pair for r in square for s in line]
-    turned = [
-        c ^ x ^ y ^ s
-        for c in pair
-        for x in (0, seq_count)
-        for y in (0, 2 * seq_count)
-        for s in line
+    window_line = (0, 4, 2, 6)
+    across_x, across_y = (0, seq_count), (0, 2 * seq_count)
+    paths = [
+        [c ^ one ^ two ^ s for c in pair for one in first for two in second for s in window_line]
+        for first, second in ((across_x, across_y), (across_y, across_x))
     ]
 
     own_inputs = jnp.swapaxes(block_input[:, 0], 1, 2)
@@ -647,7 +643,7 @@
     feedforward_blocks = feedforward_blocks.reshape(BLOCKS, -1, LANES)
 
     if butterfly:
-        window_blocks = seq_place ^ jnp.array([c ^ s for c in pair for s in line], jnp.int32)
+        window_blocks = seq_place ^ jnp.array([c ^ s for c in pair for s in window_line], jnp.int32)
     else:
         window_blocks = seq_place - jnp.arange(reach + 1, dtype=jnp.int32)
     token = jnp.arange(DEVICE_TOKENS, dtype=jnp.int32)
@@ -668,19 +664,21 @@
 
     attention_low = attention_weights.astype(BF16)
     if butterfly:
-        orders = [jnp.array(path, jnp.int32) ^ owner_place for path in (turned, order)]
+        orders = [jnp.array(path, jnp.int32) ^ owner_place for path in (order, *paths)]
         weights = attention_low.reshape(1, attention_length // LANES, LANES)
         window_inputs = own_inputs[None]
-        news = [exchange(weights, "seq", place) for place in line[1:]]
-        inputs_near = [window_inputs]
-        inputs_near += [exchange(window_inputs, "seq", place) for place in line[1:]]
-        news = together(*news, cosines, sines, bias)
-        *news, cosines, sines, bias = news
-        weights = jnp.concatenate([weights, *news], 0)
-        weight_pieces = [weights]
-        weight_pieces += [exchange(weights, "dp", place) for place in range(1, dp_count)]
+        inputs_far = exchange(window_inputs, "seq", 4, 1)
+        far, cosines, sines, bias = together(exchange(weights, "seq", 2), cosines, sines, bias)
+        weights = jnp.concatenate([weights, far], 0)
+        weights = jnp.concatenate([weights, exchange(weights, "seq", 4)], 0)
+        window_inputs = jnp.concatenate([window_inputs, inputs_far], 0)
+        weights, window_inputs = together(weights, window_inputs)
+        inputs_far = exchange(window_inputs, "seq", 2)
+        weights = jnp.concatenate([weights, exchange(weights, "dp", 1)], 0)
+        weight_pieces = [weights, exchange(weights, "dp", 2)]
         weight_pieces += [exchange(piece, "seq", 1) for piece in weight_pieces]
-        input_pieces = inputs_near + [exchange(piece, "seq", 1) for piece in inputs_near]
+        input_pieces = [window_inputs, inputs_far]
+        input_pieces += [exchange(piece, "seq", 1) for piece in input_pieces]
     else:
         weights = lax.all_gather(attention_low, both, axis=0, tiled=True)
         weights = weights.reshape(BLOCKS, -1, LANES)
@@ -698,7 +696,7 @@
         quarter = (reach + 1) // 4
         cuts = [0, quarter, 2 * quarter, 3 * quarter, reach + 1]
         input_pieces = [window_inputs[a:b] for a, b in zip(cuts, cuts[1:])]
-        orders = [straight, straight]
+        orders = [straight] * 3
 
     (
         w_project,
@@ -712,10 +710,10 @@
         mixed_across,
         residual,
     ) = attention_forward(
-        orders[1], weight_pieces, input_pieces, cosines, sines, bias, norm_gains[0][:, None]
+        orders[0], weight_pieces, input_pieces, cosines, sines, bias, norm_gains[0][:, None]
     )
     block_output, d_branch, d_residual, *parts, gain_two = feedforward(
-        (straight, *orders),
+        (straight, *orders[1:]),
         feedforward_blocks,
         residual,
         jnp.swapaxes(out_grad[:, 0], 1, 2),
@@ -746,7 +744,7 @@
         one_sent, two_sent, *first = together(one_sent, two_sent, *first)
         one_new, two_new = exchange(one_sent, "dp", 1), exchange(two_sent, "dp", 2)
         second = attention_backward(
-            operands, BLOCKS, attention_rows, (orders[1], w_project, *first)
+            operands, BLOCKS, attention_rows, (orders[0], w_project, *first)
         )
         one_new, two_new, *second = together(one_new, two_new, *second)
         kept, sent, d_queries, window_kept, window_sent, gain_one = second
@@ -754,47 +752,52 @@
         two_kept, two_sent = add_up(two_kept, [two_new], 2)
         gains_total = jnp.stack([gain_one[:, 0], gain_two[:, 0]], 0) / norm_gains
 
-        new = exchange(sent, "seq", 1)
-        one_new, two_new = exchange(one_sent, "dp", 2), exchange(two_sent, "dp", 1)
-        window_new = exchange(window_sent, "seq", 1)
-        gains_new = exchange(gains_total, "seq", 1)
         new, one_new, two_new, window_new, gains_new = together(
-            new, one_new, two_new, window_new, gains_new
+            exchange(sent, "seq", 1),
+            exchange(one_sent, "dp", 2),
+            exchange(two_sent, "dp", 1),
+            exchange(window_sent, "seq", 1),
+            exchange(gains_total, "seq", 1),
         )
         kept, *sent = add_up(kept, [new], dp_count)
+        one_kept, one_sent = add_up(one_kept, [one_new], 2)
+        two_kept, two_sent = add_up(two_kept, [two_new], 2)
+        window_kept, window_sent = add_up(window_kept, [window_new], 2)
         gains_total = gains_total + gains_new
-        news = [exchange(part, "dp", place + 1) for place, part in enumerate(sent)]
-        gains_news = [exchange(gains_total, "dp", place) for place in range(1, dp_count)]
-
-        one_kept, *one_sent = add_up(one_kept, [one_new], len(line))
-        two_kept, *two_sent = add_up(two_kept, [two_new], len(line))
-        window_kept, *window_sent = add_up(window_kept, [window_new], len(line))
-
-        def along_line(parts):
-            return [exchange(part, "seq", place) for place, part in zip(line[1:], parts)]
-
-        one_news, two_news = along_line(one_sent), along_line(two_sent)
-        window_news = along_line(window_sent)
-
-        arrived = together(*news, *gains_news)
-        news, gains_news = arrived[: len(news)], arrived[len(news) :]
-        kept, *sent = add_up(kept, news, len(line))
-        gains_total = pair_sum([gains_total, *gains_news])
-        news = along_line(sent)
-        gains_news = along_line([gains_total] * len(sent))
-        gains_total = pair_sum([gains_total, *gains_news])
-        attention_owned = add_up(kept, news, 1)[0].reshape(-1)
+
+        arrived = together(
+            *[exchange(part, "dp", place) for place, part in enumerate(sent, 1)],
+            both_bits(gains_total, "dp", 1, 2),
+            exchange(one_sent, "seq", 2),
+            exchange(two_sent, "seq", 2),
+            exchange(window_sent, "seq", 2),
+        )
+        kept, *sent = add_up(kept, arrived[:3], len(line))
+        gains_total = arrived[3]
+        one_kept, one_sent = add_up(one_kept, [arrived[4]], 2)
+        two_kept, two_sent = add_up(two_kept, [arrived[5]], 2)
+        window_kept, window_sent = add_up(window_kept, [arrived[6]], 2)
+
+        arrived = together(
+            *[exchange(part, "seq", place) for place, part in zip(line[1:], sent)],
+            both_bits(gains_total, "seq", 2, 4),
+            exchange(one_sent, "seq", 4),
+            exchange(two_sent, "seq", 4),
+            exchange(window_sent, "seq", 4),
+        )
+        attention_owned = add_up(kept, arrived[:3], 1)[0].reshape(-1)
+        gains_total = arrived[3]
         feedforward_owned = jnp.concatenate(
-            [add_up(one_kept, one_news, 1)[0][0], add_up(two_kept, two_news, 1)[0][0]], 0
+            [add_up(one_kept, [arrived[4]], 1)[0][0], add_up(two_kept, [arrived[5]], 1)[0][0]], 0
         ).reshape(-1)
-        d_own = add_up(window_kept, window_news, 1)[0][0].astype(BF16)
+        d_own = add_up(window_kept, [arrived[6]], 1)[0][0].astype(BF16)
     else:
         halves = [jnp.concatenate(parts[index : index + 2], 0) for index in (0, 2)]
         grads = jnp.concatenate(halves, 1).reshape(-1)
         feedforward_owned = lax.psum_scatter(grads, both, scatter_dimension=0, tiled=True)
         first = attention_backward(operands, BLOCKS, attention_rows)
         kept, sent, d_queries, window_kept, window_sent, gain_one = attention_backward(
-            operands, BLOCKS, attention_rows, (orders[1], w_project, *first)
+            operands, BLOCKS, attention_rows, (orders[0], w_project, *first)
         )
         attention_owned = lax.psum_scatter(
             jnp.concatenate([kept, sent], 0).reshape(-1), both, scatter_dimension=0, tiled=True

time: 223 us -> 220 us (0.987)
  starting transfers between devices: 46.7 us -> 42.3 us
    ppermute x47 -> x35, waiting for transfers between devices: 60.1 us -> 68.7 us  [exchange(): return lax.ppermute(value, axis, pairs)]
    all_gather x1, waiting for transfers between devices: 14 us -> 5.66 us  [on_device(): lax.all_gather(feedforward_low, both, axis=0, tiled=True)]
    ppermute x47 -> x35, starting transfers between devices: 46.7 us -> 42.3 us  [exchange(): return lax.ppermute(value, axis, pairs)]
    add x4 -> x7, other arithmetic: 7.27 us -> 5.35 us  [add_up(): total = total + new[rows].astype(F32)]
  transfers between devices with their start and end apart: 48 -> 36, of which waited for: 20 -> 14; matrix products, arithmetic and copies ran while one was open for 11% -> 8% of each run, Pallas kernels for 19% -> 19%
where the time goes in v4:
time: 220 us; the launch traced here: 219 us
  waiting for transfers between devices  74.3 us (34%)
  Pallas kernels  57.4 us (26%)
  starting transfers between devices  42.3 us (19%)
  other arithmetic  25.8 us (12%)
  between operations  14.6 us (7%)
  local copies, waits for them, and re-layouts  3.35 us (2%)
    ppermute x35, waiting for transfers between devices, exchange(): return lax.ppermute(value, axis, pairs)  68.7 us
    ppermute x35, starting transfers between devices, exchange(): return lax.ppermute(value, axis, pairs)  42.3 us
    pallas_call x2, Pallas kernels, attention_backward(): pl.pallas_call(kernel, out_shape=outputs, in_specs=in_specs, out_specs=tu...  25.3 us
    pallas_call x1, Pallas kernels, attention_forward(): pl.pallas_call(functools.partial(attention_forward_kernel, len(weight_pie...  16.7 us
    pallas_call x1, Pallas kernels, feedforward(): pl.pallas_call(feedforward_kernel, out_shape=(shape((MICRO, D, DEVICE_TOK...  15.3 us
    all_gather x1, waiting for transfers between devices, on_device(): lax.all_gather(feedforward_low, both, axis=0, tiled=True)  5.66 us
    add x7, other arithmetic, add_up(): total = total + new[rows].astype(F32)  5.35 us
  transfers between devices with their start and end apart: 36, of which 14 were waited for; matrix products, arithmetic and copies ran while one was open for 8% of the time, Pallas kernels for 19%

profile of v4, /device:TPU:0, one launch (start us, length us, event | category | flops | bytes accessed | tf_op | source)
XLA Modules:
  0.0 219.0 jit_solution(11216206882680009403)
XLA Ops:
  7.2 1.7 convert_bitcast_fusion
  8.9 0.9 convert_bitcast_fusion.1
  9.9 3.0 %collective-permute-start = (bf16[1,216,128]{2,1,0:T(8,128)(2,1)S(1)}, bf16[1,216,128]{2,1,0:T(8,128)(2,1)S(1)}, u32[]{:S(2)}, u32[]{:S(2)}) collective-permute-start(bf16[1,216,128]{2,1,0:T(8,128)(2,1)S(1)} %convert_bitcast_fusion.1), channel_id=1, source_target_pairs={{0,2},{1,3},{2,0},{3,1},{4,6},{5,7},{6,4},{7,5},{8,10},{9,11},{10,... | collective-permute-start | bytes 165896 | tf_op jit(solution)/shard_map/ppermute | solution.py:47
  12.9 4.5 %collective-permute-start.2 = (bf16[1,2,576,128]{3,2,1,0:T(8,128)(2,1)}, bf16[1,2,576,128]{3,2,1,0:T(8,128)(2,1)S(1)}, u32[]{:S(2)}, u32[]{:S(2)}) collective-permute-start(bf16[1,2,576,128]{3,2,1,0:T(8,128)(2,1)} %bitcast.57), channel_id=1, source_target_pairs={{0,4},{1,5},{2,6},{3,7},{8,12},{9,13},{10,14},{11,15},{16,20},{17,... | collective-permute-start | bytes 884744 | tf_op jit(solution)/shard_map/ppermute | solution.py:47
  17.4 1.0 reduce_window_sum.12
  18.4 0.7 sub.30
  19.3 0.7 xor_multiply_fusion
  20.4 1.2 and_select_fusion.refs_10_.refs_11_.refs_16_
  21.6 1.0 multiply_sine_fusion
  22.7 9.5 %collective-permute-done.1 = bf16[2,216,128]{2,1,0:T(8,128)(2,1)S(1)} collective-permute-done((bf16[2,216,128]{2,1,0:T(8,128)(2,1)S(1)}, bf16[2,216,128]{2,1,0:T(8,128)(2,1)S(1)}, u32[]{:S(2)}, u32[]{:S(2)}) %collective-permute-start.1) | collective-permute-done | bytes 110624 | tf_op jit(solution)/shard_map/ppermute | solution.py:47
  32.3 0.9 pad_maximum_fusion.refs_4_
  33.2 6.4 %collective-permute-start.7 = (bf16[2,2,576,128]{3,2,1,0:T(8,128)(2,1)}, bf16[2,2,576,128]{3,2,1,0:T(8,128)(2,1)}, u32[]{:S(2)}, u32[]{:S(2)}) collective-permute-start(bf16[2,2,576,128]{3,2,1,0:T(8,128)(2,1)} %pad_maximum_fusion.refs_4_), channel_id=1, source_target_pairs={{0,2},{1,3},{2,0},{3,1},{4,6},{5,7},{6,4},{7,5},{8,10},{9,11},{10,... | collective-permute-start | bytes 1769480 | tf_op jit(solution)/shard_map/ppermute | solution.py:47
  39.5 1.5 collective-permute-start.3
  41.1 7.0 %collective-permute-done.3 = bf16[4,216,128]{2,1,0:T(8,128)(2,1)S(1)} collective-permute-done((bf16[4,216,128]{2,1,0:T(8,128)(2,1)S(1)}, bf16[4,216,128]{2,1,0:T(8,128)(2,1)S(1)}, u32[]{:S(2)}, u32[]{:S(2)}) %collective-permute-start.3) | collective-permute-done | bytes 221216 | tf_op jit(solution)/shard_map/ppermute | solution.py:47
  48.1 1.1 collective-permute-start.4
  49.2 10.2 %collective-permute-done.7.refs_5_ = bf16[2,2,576,128]{3,2,1,0:T(8,128)(2,1)} collective-permute-done((bf16[2,2,576,128]{3,2,1,0:T(8,128)(2,1)}, bf16[2,2,576,128]{3,2,1,0:T(8,128)(2,1)}, u32[]{:S(2)}, u32[]{:S(2)}) %collective-permute-start.7) | collective-permute-done | bytes 589856 | tf_op jit(solution)/shard_map/ppermute | solution.py:47
  60.9 1.3 collective-permute-done.5.refs_2_
  62.2 0.6 collective-permute-done.6.refs_3_
  63.6 16.7 %shard_map.239 = (bf16[576,960]{1,0:T(8,128)(2,1)}, bf16[576,576]{1,0:T(8,128)(2,1)}, bf16[2,576,1024]{2,1,0:T(8,128)(2,1)}, bf16[2,576,128]{2,1,0:T(8,128)(2,1)...) custom-call(s32[32]{0:T(128)S(1)} %broadcast_xor_fusion.order, ...), custom_call_target="tpu_custom_call" | custom-call | tf_op jit(solution)/shard_map/pallas_call | solution.py:261
  80.3 5.7 %all-gather.2.cloned.1.call-done = bf16[20736,128]{1,0:T(8,128)(2,1)} async-done(((bf16[648,128]{1,0:T(8,128)(2,1)}), bf16[20736,128]{1,0:T(8,128)(2,1)}) %all-gather.2.cloned.1.call-update) | async-done | bytes 5308432 | tf_op jit(solution)/shard_map/all_gather | solution.py:642
  86.0 15.3 %shard_map.240 = (bf16[2,576,128]{2,1,0:T(8,128)(2,1)}, bf16[256,576]{1,0:T(8,128)(2,1)S(1)}, f32[2,576,128]{2,1,0:T(8,128)S(1)}, bf16[16,320,128]{2,1,0:T(8,128...) custom-call(s32[32]{0:T(128)S(1)} %iota.26.straight, ...), custom_call_target="tpu_custom_call" | custom-call | tf_op jit(solution)/shard_map/pallas_call | solution.py:383
  101.8 10.5 %shard_map.241 = (bf16[576,128]{1,0:T(8,128)(2,1)S(1)}, bf16[8,384,128]{2,1,0:T(8,128)(2,1)}, f32[576,576]{1,0:T(8,128)}, f32[576,384]{1,0:T(8,128)}, f32[576,576]{1,0:T(8,128)}) custom-call(bf16[576,576]{1,0:T(8,128)(2,1)} %get-tuple-element.99.refs_0_.refs_5_, bf16[2,576,1024]{2,1,0:T(8,128)(2,1)} %get-tuple-element.100.refs_1_.refs_6_, ...), custom_call_target="tpu_custom_call" | custom-call | tf_op jit(solution)/shard_map/pallas_call | solution.py:568
  112.7 1.0 copy-done.3
  114.0 1.5 collective-permute-start.13
  116.1 14.7 %shard_map.242 = (bf16[16,216,128]{2,1,0:T(8,128)(2,1)}, bf16[16,216,128]{2,1,0:T(8,128)(2,1)}, bf16[2,576,128]{2,1,0:T(8,128)(2,1)S(1)}, bf16[4,2,384,128]{3,2,...) custom-call(s32[32]{0:T(128)S(1)} %broadcast_xor_fusion.order, ...), custom_call_target="tpu_custom_call" | custom-call | tf_op jit(solution)/shard_map/pallas_call | solution.py:568
  130.9 1.3 collective-permute-done.12
  132.8 0.7 collective-permute-start.16
  133.5 1.0 slice_add_fusion.2
  134.5 1.4 collective-permute-start.15
  136.4 1.2 collective-permute-done.18
  137.6 6.6 %collective-permute-done.15 = bf16[4,320,128]{2,1,0:T(8,128)(2,1)} collective-permute-done((bf16[4,320,128]{2,1,0:T(8,128)(2,1)}, bf16[4,320,128]{2,1,0:T(8,128)(2,1)}, u32[]{:S(2)}, u32[]{:S(2)}) %collective-permute-start.15) | collective-permute-done | bytes 327712 | tf_op jit(solution)/shard_map/ppermute | solution.py:47
  144.2 1.5 collective-permute-start.22
  145.7 1.2 slice_add_fusion.8
  147.0 2.0 collective-permute-start.24
  149.0 1.7 add_convert_fusion.3
  150.7 1.5 collective-permute-start.21
  152.2 0.6 collective-permute-start.20
  152.8 1.4 collective-permute-start.19
  154.3 0.7 collective-permute-start.23
  155.0 1.3 convert_add_fusion.2
  156.3 5.9 %collective-permute-done.23 = f32[2,576]{1,0:T(2,128)S(1)} collective-permute-done((f32[2,576]{1,0:T(2,128)S(1)}, f32[2,576]{1,0:T(2,128)S(1)}, u32[]{:S(2)}, u32[]{:S(2)}) %collective-permute-start.23) | collective-permute-done | bytes 4640 | tf_op jit(solution)/shard_map/ppermute | solution.py:47
  162.6 1.1 slice_add_fusion.6
  163.7 1.6 collective-permute-start.25
  165.4 10.8 %collective-permute-done.25 = bf16[2,328,128]{2,1,0:T(8,128)(2,1)S(1)} collective-permute-done((bf16[2,328,128]{2,1,0:T(8,128)(2,1)S(1)}, bf16[2,328,128]{2,1,0:T(8,128)(2,1)S(1)}, u32[]{:S(2)}, u32[]{:S(2)}) %collective-permute-start.25) | collective-permute-done | bytes 167968 | tf_op jit(solution)/shard_map/ppermute | solution.py:47
  176.3 0.7 collective-permute-start.30
  177.0 0.7 fusion.27
  177.6 1.6 collective-permute-start.32
  179.3 1.4 collective-permute-start.33
  180.7 0.7 fusion.37
  181.4 1.6 collective-permute-start.29
  183.0 1.2 collective-permute-start.28
  184.2 1.8 collective-permute-start.31
  186.1 5.8 %collective-permute-done.31 = f32[2,576]{1,0:T(2,128)S(1)} collective-permute-done((f32[2,576]{1,0:T(2,128)S(1)}, f32[2,576]{1,0:T(2,128)S(1)}, u32[]{:S(2)}, u32[]{:S(2)}) %collective-permute-start.31) | collective-permute-done | bytes 4640 | tf_op jit(solution)/shard_map/ppermute | solution.py:47
  192.5 1.6 collective-permute-start.34
  194.1 0.8 add.292
  194.9 1.6 collective-permute-done.27
  196.5 6.8 %collective-permute-done.34 = bf16[1,2,384,128]{3,2,1,0:T(8,128)(2,1)S(1)} collective-permute-done((bf16[1,2,384,128]{3,2,1,0:T(8,128)(2,1)S(1)}, bf16[1,2,384,128]{3,2,1,0:T(8,128)(2,1)S(1)}, u32[]{:S(2)}, u32[]{:S(2)}) %collective-permute-start.34) | collective-permute-done | bytes 196640 | tf_op jit(solution)/shard_map/ppermute | solution.py:47
  203.4 1.0 fusion.23
  204.3 1.0 fusion.26
  205.3 1.0 fusion.21
  206.3 1.2 fusion.6
  207.6 0.9 fusion.10
  209.2 1.2 multiply_subtract_fusion
  210.3 1.8 multiply_subtract_fusion.1
  (135 shorter events, 7.8 us)
Async XLA Ops:
  7.2 78.8 %all-gather.2.cloned.1.call-start = ((), (), s32[]{:S(2)}) async-start(), calls=%async_computation | async-start | bytes 5474304 | tf_op jit(solution)/shard_map/all_gather | solution.py:642
  8.9 23.4 %copy-start.2 = (bf16[2,1,128,576]{2,3,1,0:T(8,128)(2,1)S(1)}, bf16[2,1,128,576]{2,3,1,0:T(8,128)(2,1)}, u32[]{:S(2)}) copy-start(bf16[2,1,128,576]{2,3,1,0:T(8,128)(2,1)} %param.16) | copy-start | bytes 884740
  9.9 12.7 %collective-permute-start = (bf16[1,216,128]{2,1,0:T(8,128)(2,1)S(1)}, bf16[1,216,128]{2,1,0:T(8,128)(2,1)S(1)}, u32[]{:S(2)}, u32[]{:S(2)}) collective-permute-start(bf16[1,216,128]{2,1,0:T(8,128)(2,1)S(1)} %convert_bitcast_fusion.1), channel_id=1, source_target_pairs={{0,2},{1,3},{2,0},{3,1},{4,6},{5,7},{6,4},{7,5},{8,10},{9,11},{10,... | collective-permute-start | bytes 165896 | tf_op jit(solution)/shard_map/ppermute | solution.py:47
  12.9 19.4 %collective-permute-start.2 = (bf16[1,2,576,128]{3,2,1,0:T(8,128)(2,1)}, bf16[1,2,576,128]{3,2,1,0:T(8,128)(2,1)S(1)}, u32[]{:S(2)}, u32[]{:S(2)}) collective-permute-start(bf16[1,2,576,128]{3,2,1,0:T(8,128)(2,1)} %bitcast.57), channel_id=1, source_target_pairs={{0,4},{1,5},{2,6},{3,7},{8,12},{9,13},{10,14},{11,15},{16,20},{17,... | collective-permute-start | bytes 884744 | tf_op jit(solution)/shard_map/ppermute | solution.py:47
  22.6 36.8 %copy-start.23 = (f32[2,576]{1,0:T(2,128)S(1)}, f32[2,576]{1,0:T(2,128)}, u32[]{:S(2)}) copy-start(f32[2,576]{1,0:T(2,128)} %param.21) | copy-start | bytes 13828
  22.6 38.2 %copy-start.31 = (s32[32]{0:T(128)S(1)}, s32[32]{0:T(128)}, u32[]{:S(2)}) copy-start(s32[32]{0:T(128)} %constant.30.clone) | copy-start | bytes 388
  22.6 38.2 %copy-start.29 = (s32[32]{0:T(128)S(1)}, s32[32]{0:T(128)}, u32[]{:S(2)}) copy-start(s32[32]{0:T(128)} %constant.100.clone) | copy-start | bytes 388
  22.6 38.2 %copy-start.30 = (s32[32]{0:T(128)S(1)}, s32[32]{0:T(128)}, u32[]{:S(2)}) copy-start(s32[32]{0:T(128)} %constant.31.clone) | copy-start | bytes 388
  22.7 9.6 %collective-permute-start.1 = (bf16[2,216,128]{2,1,0:T(8,128)(2,1)S(1)}, bf16[2,216,128]{2,1,0:T(8,128)(2,1)S(1)}, u32[]{:S(2)}, u32[]{:S(2)}) collective-permute-start(bf16[2,216,128]{2,1,0:T(8,128)(2,1)S(1)} %pad_maximum_fusion.2), channel_id=1, source_target_pairs={{0,4},{1,5},{2,6},{3,7},{4,0},{5,1},{6,2},{7,3},{8,12},{9,13},{10,... | collective-permute-start | bytes 331784 | tf_op jit(solution)/shard_map/ppermute | solution.py:47
  33.2 26.2 %collective-permute-start.7 = (bf16[2,2,576,128]{3,2,1,0:T(8,128)(2,1)}, bf16[2,2,576,128]{3,2,1,0:T(8,128)(2,1)}, u32[]{:S(2)}, u32[]{:S(2)}) collective-permute-start(bf16[2,2,576,128]{3,2,1,0:T(8,128)(2,1)} %pad_maximum_fusion.refs_4_), channel_id=1, source_target_pairs={{0,2},{1,3},{2,0},{3,1},{4,6},{5,7},{6,4},{7,5},{8,10},{9,11},{10,... | collective-permute-start | bytes 1769480 | tf_op jit(solution)/shard_map/ppermute | solution.py:47
  39.5 8.5 %collective-permute-start.3 = (bf16[4,216,128]{2,1,0:T(8,128)(2,1)S(1)}, bf16[4,216,128]{2,1,0:T(8,128)(2,1)S(1)}, u32[]{:S(2)}, u32[]{:S(2)}) collective-permute-start(bf16[4,216,128]{2,1,0:T(8,128)(2,1)S(1)} %pad_maximum_fusion.1), channel_id=1, source_target_pairs={{0,8},{8,0},{16,24},{24,16},{1,9},{9,1},{17,25},{25,17},{2,10},{10... | collective-permute-start | bytes 663560 | tf_op jit(solution)/shard_map/ppermute | solution.py:47
  48.1 12.6 %collective-permute-start.4 = (bf16[8,216,128]{2,1,0:T(8,128)(2,1)S(1)}, bf16[8,216,128]{2,1,0:T(8,128)(2,1)S(1)}, u32[]{:S(2)}, u32[]{:S(2)}) collective-permute-start(bf16[8,216,128]{2,1,0:T(8,128)(2,1)S(1)} %constant_dynamic-update-slice_fusion.refs_0_), channel_id=1, source_target_pairs={{0,16},{8,24},{16,0},{24,8},{1,17},{9,25},{17,1},{25,9},{2,18},{10... | collective-permute-start | bytes 1327112 | tf_op jit(solution)/shard_map/ppermute | solution.py:47
  49.2 11.7 %collective-permute-start.8 = (bf16[2,2,576,128]{3,2,1,0:T(8,128)(2,1)}, bf16[2,2,576,128]{3,2,1,0:T(8,128)(2,1)}, u32[]{:S(2)}, u32[]{:S(2)}) collective-permute-start(bf16[2,2,576,128]{3,2,1,0:T(8,128)(2,1)} %pad_maximum_fusion.refs_4_), channel_id=1, source_target_pairs={{0,1},{1,0},{2,3},{3,2},{4,5},{5,4},{6,7},{7,6},{8,9},{9,8},{10,11... | collective-permute-start | bytes 1769480 | tf_op jit(solution)/shard_map/ppermute | solution.py:47
  59.4 3.4 %collective-permute-start.9 = (bf16[2,2,576,128]{3,2,1,0:T(8,128)(2,1)}, bf16[2,2,576,128]{3,2,1,0:T(8,128)(2,1)}, u32[]{:S(2)}, u32[]{:S(2)}) collective-permute-start(bf16[2,2,576,128]{3,2,1,0:T(8,128)(2,1)} %collective-permute-done.7.refs_5_), channel_id=1, source_target_pairs={{0,1},{1,0},{2,3},{3,2},{4,5},{5,4},{6,7},{7,6},{8,9},{9,8},{10,11... | collective-permute-start | bytes 1769480 | tf_op jit(solution)/shard_map/ppermute | solution.py:47
  60.2 2.0 collective-permute-start.5
  60.8 2.0 collective-permute-start.6
  60.9 25.1 %copy-start.1 = (bf16[2,1,128,576]{2,3,1,0:T(8,128)(2,1)S(1)}, bf16[2,1,128,576]{2,3,1,0:T(8,128)(2,1)}, u32[]{:S(2)}) copy-start(bf16[2,1,128,576]{2,3,1,0:T(8,128)(2,1)} %param.17) | copy-start | bytes 884740
  86.0 15.9 %copy-start = (f32[2,576,128]{2,1,0:T(8,128)S(1)}, f32[2,576,128]{2,1,0:T(8,128)}, u32[]{:S(2)}) copy-start(f32[2,576,128]{2,1,0:T(8,128)} %get-tuple-element.106.refs_7_.refs_12_) | copy-start | bytes 1769476
  101.3 11.1 %collective-permute-start.11 = (bf16[16,328,128]{2,1,0:T(8,128)(2,1)}, bf16[16,328,128]{2,1,0:T(8,128)(2,1)S(1)}, u32[]{:S(2)}, u32[]{:S(2)}) collective-permute-start(bf16[16,328,128]{2,1,0:T(8,128)(2,1)} %get-tuple-element.98), channel_id=1, source_target_pairs={{0,1},{1,0},{2,3},{3,2},{4,5},{5,4},{6,7},{7,6},{8,9},{9,8},{10,11... | collective-permute-start | bytes 4030472 | tf_op jit(solution)/shard_map/ppermute | solution.py:47
  101.6 10.8 %collective-permute-start.10 = (bf16[16,320,128]{2,1,0:T(8,128)(2,1)}, bf16[16,320,128]{2,1,0:T(8,128)(2,1)S(1)}, u32[]{:S(2)}, u32[]{:S(2)}) collective-permute-start(bf16[16,320,128]{2,1,0:T(8,128)(2,1)} %get-tuple-element.97), channel_id=1, source_target_pairs={{0,1},{1,0},{2,3},{3,2},{4,5},{5,4},{6,7},{7,6},{8,9},{9,8},{10,11... | collective-permute-start | bytes 3932168 | tf_op jit(solution)/shard_map/ppermute | solution.py:47
  101.8 10.5 %copy-start.5 = (bf16[16,320,128]{2,1,0:T(8,128)(2,1)S(1)}, bf16[16,320,128]{2,1,0:T(8,128)(2,1)}, u32[]{:S(2)}) copy-start(bf16[16,320,128]{2,1,0:T(8,128)(2,1)} %get-tuple-element.96) | copy-start | bytes 3932164
  112.4 1.3 copy-start.3
  114.0 18.2 %collective-permute-start.13 = (bf16[8,328,128]{2,1,0:T(8,128)(2,1)S(1)}, bf16[8,328,128]{2,1,0:T(8,128)(2,1)S(1)}, u32[]{:S(2)}, u32[]{:S(2)}) collective-permute-start(bf16[8,328,128]{2,1,0:T(8,128)(2,1)S(1)} %get-tuple-element.122), channel_id=1, source_target_pairs={{0,16},{8,24},{16,0},{24,8},{1,17},{9,25},{17,1},{25,9},{2,18},{10... | collective-permute-start | bytes 2015240 | tf_op jit(solution)/shard_map/ppermute | solution.py:47
  115.6 16.6 %collective-permute-start.12 = (bf16[8,320,128]{2,1,0:T(8,128)(2,1)S(1)}, bf16[8,320,128]{2,1,0:T(8,128)(2,1)S(1)}, u32[]{:S(2)}, u32[]{:S(2)}) collective-permute-start(bf16[8,320,128]{2,1,0:T(8,128)(2,1)S(1)} %get-tuple-element.121), channel_id=1, source_target_pairs={{0,8},{8,0},{16,24},{24,16},{1,9},{9,1},{17,25},{25,17},{2,10},{10... | collective-permute-start | bytes 1966088 | tf_op jit(solution)/shard_map/ppermute | solution.py:47
  132.2 12.0 %collective-permute-start.14 = (bf16[16,216,128]{2,1,0:T(8,128)(2,1)}, bf16[16,216,128]{2,1,0:T(8,128)(2,1)}, u32[]{:S(2)}, u32[]{:S(2)}) collective-permute-start(bf16[16,216,128]{2,1,0:T(8,128)(2,1)} %get-tuple-element.137), channel_id=1, source_target_pairs={{0,1},{1,0},{2,3},{3,2},{4,5},{5,4},{6,7},{7,6},{8,9},{9,8},{10,11... | collective-permute-start | bytes 2654216 | tf_op jit(solution)/shard_map/ppermute | solution.py:47
  132.2 12.0 %collective-permute-start.17 = (bf16[4,2,384,128]{3,2,1,0:T(8,128)(2,1)}, bf16[4,2,384,128]{3,2,1,0:T(8,128)(2,1)}, u32[]{:S(2)}, u32[]{:S(2)}) collective-permute-start(bf16[4,2,384,128]{3,2,1,0:T(8,128)(2,1)} %get-tuple-element.140), channel_id=1, source_target_pairs={{0,1},{1,0},{2,3},{3,2},{4,5},{5,4},{6,7},{7,6},{8,9},{9,8},{10,11... | collective-permute-start | bytes 2359304 | tf_op jit(solution)/shard_map/ppermute | solution.py:47
  132.8 11.4 %collective-permute-start.16 = (bf16[4,328,128]{2,1,0:T(8,128)(2,1)S(1)}, bf16[4,328,128]{2,1,0:T(8,128)(2,1)}, u32[]{:S(2)}, u32[]{:S(2)}) collective-permute-start(bf16[4,328,128]{2,1,0:T(8,128)(2,1)S(1)} %get-tuple-element.210), channel_id=1, source_target_pairs={{0,8},{8,0},{16,24},{24,16},{1,9},{9,1},{17,25},{25,17},{2,10},{10... | collective-permute-start | bytes 1007624 | tf_op jit(solution)/shard_map/ppermute | solution.py:47
  134.5 9.7 %collective-permute-start.15 = (bf16[4,320,128]{2,1,0:T(8,128)(2,1)}, bf16[4,320,128]{2,1,0:T(8,128)(2,1)}, u32[]{:S(2)}, u32[]{:S(2)}) collective-permute-start(bf16[4,320,128]{2,1,0:T(8,128)(2,1)} %get-tuple-element.212), channel_id=1, source_target_pairs={{0,16},{8,24},{16,0},{24,8},{1,17},{9,25},{17,1},{25,9},{2,18},{10... | collective-permute-start | bytes 983048 | tf_op jit(solution)/shard_map/ppermute | solution.py:47
  136.3 1.2 collective-permute-start.18
  144.2 10.1 %collective-permute-start.22 = (f32[2,576]{1,0:T(2,128)S(1)}, f32[2,576]{1,0:T(2,128)S(1)}, u32[]{:S(2)}, u32[]{:S(2)}) collective-permute-start(f32[2,576]{1,0:T(2,128)S(1)} %fusion.51), channel_id=1, source_target_pairs={{0,8},{8,0},{16,24},{24,16},{1,9},{9,1},{17,25},{25,17},{2,10},{10... | collective-permute-start | bytes 13832 | tf_op jit(solution)/shard_map/ppermute | solution.py:47
  146.9 30.0 %copy-start.6 = (f32[2,320,128]{2,1,0:T(8,128)}, f32[2,320,128]{2,1,0:T(8,128)S(1)}, u32[]{:S(2)}) copy-start(f32[2,320,128]{2,1,0:T(8,128)S(1)} %get-tuple-element.224) | copy-start | bytes 983044
  147.0 8.0 %copy-start.9 = (bf16[4,2,384,128]{3,2,1,0:T(8,128)(2,1)S(1)}, bf16[4,2,384,128]{3,2,1,0:T(8,128)(2,1)}, u32[]{:S(2)}) copy-start(bf16[4,2,384,128]{3,2,1,0:T(8,128)(2,1)} %get-tuple-element.136) | copy-start | bytes 2359300
  147.0 16.7 %collective-permute-start.24 = (bf16[2,320,128]{2,1,0:T(8,128)(2,1)S(1)}, bf16[2,320,128]{2,1,0:T(8,128)(2,1)S(1)}, u32[]{:S(2)}, u32[]{:S(2)}) collective-permute-start(bf16[2,320,128]{2,1,0:T(8,128)(2,1)S(1)} %get-tuple-element.225), channel_id=1, source_target_pairs={{0,2},{1,3},{2,0},{3,1},{4,6},{5,7},{6,4},{7,5},{8,10},{9,11},{10,... | collective-permute-start | bytes 491528 | tf_op jit(solution)/shard_map/ppermute | solution.py:47
  150.7 25.5 %collective-permute-start.21 = (bf16[4,216,128]{2,1,0:T(8,128)(2,1)S(1)}, bf16[4,216,128]{2,1,0:T(8,128)(2,1)S(1)}, u32[]{:S(2)}, u32[]{:S(2)}) collective-permute-start(bf16[4,216,128]{2,1,0:T(8,128)(2,1)S(1)} %get-tuple-element.213), channel_id=1, source_target_pairs={{0,24},{8,16},{16,8},{24,0},{1,25},{9,17},{17,9},{25,1},{2,26},{10... | collective-permute-start | bytes 663560 | tf_op jit(solution)/shard_map/ppermute | solution.py:47
  152.2 24.0 %collective-permute-start.20 = (bf16[4,216,128]{2,1,0:T(8,128)(2,1)S(1)}, bf16[4,216,128]{2,1,0:T(8,128)(2,1)S(1)}, u32[]{:S(2)}, u32[]{:S(2)}) collective-permute-start(bf16[4,216,128]{2,1,0:T(8,128)(2,1)S(1)} %get-tuple-element.215), channel_id=1, source_target_pairs={{0,16},{8,24},{16,0},{24,8},{1,17},{9,25},{17,1},{25,9},{2,18},{10... | collective-permute-start | bytes 663560 | tf_op jit(solution)/shard_map/ppermute | solution.py:47
  152.8 23.4 %collective-permute-start.19 = (bf16[4,216,128]{2,1,0:T(8,128)(2,1)S(1)}, bf16[4,216,128]{2,1,0:T(8,128)(2,1)S(1)}, u32[]{:S(2)}, u32[]{:S(2)}) collective-permute-start(bf16[4,216,128]{2,1,0:T(8,128)(2,1)S(1)} %get-tuple-element.216), channel_id=1, source_target_pairs={{0,8},{8,0},{16,24},{24,16},{1,9},{9,1},{17,25},{25,17},{2,10},{10... | collective-permute-start | bytes 663560 | tf_op jit(solution)/shard_map/ppermute | solution.py:47
  154.3 7.9 %collective-permute-start.23 = (f32[2,576]{1,0:T(2,128)S(1)}, f32[2,576]{1,0:T(2,128)S(1)}, u32[]{:S(2)}, u32[]{:S(2)}) collective-permute-start(f32[2,576]{1,0:T(2,128)S(1)} %add.273), channel_id=1, source_target_pairs={{0,16},{8,24},{16,0},{24,8},{1,17},{9,25},{17,1},{25,9},{2,18},{10... | collective-permute-start | bytes 13832 | tf_op jit(solution)/shard_map/ppermute | solution.py:47
  162.1 14.1 %collective-permute-start.26 = (bf16[2,2,384,128]{3,2,1,0:T(8,128)(2,1)S(1)}, bf16[2,2,384,128]{3,2,1,0:T(8,128)(2,1)S(1)}, u32[]{:S(2)}, u32[]{:S(2)}) collective-permute-start(bf16[2,2,384,128]{3,2,1,0:T(8,128)(2,1)S(1)} %get-tuple-element.218), channel_id=1, source_target_pairs={{0,2},{1,3},{2,0},{3,1},{4,6},{5,7},{6,4},{7,5},{8,10},{9,11},{10,... | collective-permute-start | bytes 1179656 | tf_op jit(solution)/shard_map/ppermute | solution.py:47
  163.7 22.4 %copy-start.20 = (bf16[2,320,128]{2,1,0:T(8,128)(2,1)}, bf16[2,320,128]{2,1,0:T(8,128)(2,1)S(1)}, u32[]{:S(2)}) copy-start(bf16[2,320,128]{2,1,0:T(8,128)(2,1)S(1)} %collective-permute-done.24) | copy-start | bytes 491524
  163.7 12.5 %collective-permute-start.25 = (bf16[2,328,128]{2,1,0:T(8,128)(2,1)S(1)}, bf16[2,328,128]{2,1,0:T(8,128)(2,1)S(1)}, u32[]{:S(2)}, u32[]{:S(2)}) collective-permute-start(bf16[2,328,128]{2,1,0:T(8,128)(2,1)S(1)} %get-tuple-element.223), channel_id=1, source_target_pairs={{0,2},{1,3},{2,0},{3,1},{4,6},{5,7},{6,4},{7,5},{8,10},{9,11},{10,... | collective-permute-start | bytes 503816 | tf_op jit(solution)/shard_map/ppermute | solution.py:47
  176.2 3.1 %copy-start.19 = (bf16[2,328,128]{2,1,0:T(8,128)(2,1)}, bf16[2,328,128]{2,1,0:T(8,128)(2,1)S(1)}, u32[]{:S(2)}) copy-start(bf16[2,328,128]{2,1,0:T(8,128)(2,1)S(1)} %collective-permute-done.25) | copy-start | bytes 503812
  176.2 9.9 %copy-start.16 = (bf16[4,216,128]{2,1,0:T(8,128)(2,1)}, bf16[4,216,128]{2,1,0:T(8,128)(2,1)S(1)}, u32[]{:S(2)}) copy-start(bf16[4,216,128]{2,1,0:T(8,128)(2,1)S(1)} %collective-permute-done.21) | copy-start | bytes 663556
  176.2 15.7 %copy-start.17 = (bf16[4,216,128]{2,1,0:T(8,128)(2,1)}, bf16[4,216,128]{2,1,0:T(8,128)(2,1)S(1)}, u32[]{:S(2)}) copy-start(bf16[4,216,128]{2,1,0:T(8,128)(2,1)S(1)} %collective-permute-done.20) | copy-start | bytes 663556
  176.2 15.7 %copy-start.18 = (bf16[4,216,128]{2,1,0:T(8,128)(2,1)}, bf16[4,216,128]{2,1,0:T(8,128)(2,1)S(1)}, u32[]{:S(2)}) copy-start(bf16[4,216,128]{2,1,0:T(8,128)(2,1)S(1)} %collective-permute-done.19) | copy-start | bytes 663556
  176.2 9.8 %copy-start.13 = (bf16[2,2,384,128]{3,2,1,0:T(8,128)(2,1)}, bf16[2,2,384,128]{3,2,1,0:T(8,128)(2,1)S(1)}, u32[]{:S(2)}) copy-start(bf16[2,2,384,128]{3,2,1,0:T(8,128)(2,1)S(1)} %collective-permute-done.26) | copy-start | bytes 1179652
  176.3 8.0 %collective-permute-start.30 = (f32[2,576]{1,0:T(2,128)S(1)}, f32[2,576]{1,0:T(2,128)S(1)}, u32[]{:S(2)}, u32[]{:S(2)}) collective-permute-start(f32[2,576]{1,0:T(2,128)S(1)} %add.274), channel_id=1, source_target_pairs={{0,2},{1,3},{2,0},{3,1},{4,6},{5,7},{6,4},{7,5},{8,10},{9,11},{10,... | collective-permute-start | bytes 13832 | tf_op jit(solution)/shard_map/ppermute | solution.py:47
  177.6 26.7 %copy-start.7 = (f32[2,320,128]{2,1,0:T(8,128)S(1)}, f32[2,320,128]{2,1,0:T(8,128)}, u32[]{:S(2)}) copy-start(f32[2,320,128]{2,1,0:T(8,128)} %copy-done.6) | copy-start | bytes 983044
  177.6 18.9 %collective-permute-start.32 = (bf16[1,320,128]{2,1,0:T(8,128)(2,1)}, bf16[1,320,128]{2,1,0:T(8,128)(2,1)}, u32[]{:S(2)}, u32[]{:S(2)}) collective-permute-start(bf16[1,320,128]{2,1,0:T(8,128)(2,1)} %fusion.27), channel_id=1, source_target_pairs={{0,4},{1,5},{2,6},{3,7},{4,0},{5,1},{6,2},{7,3},{8,12},{9,13},{10,... | collective-permute-start | bytes 245768 | tf_op jit(solution)/shard_map/ppermute | solution.py:47
  179.3 17.2 %collective-permute-start.33 = (bf16[1,328,128]{2,1,0:T(8,128)(2,1)S(1)}, bf16[1,328,128]{2,1,0:T(8,128)(2,1)}, u32[]{:S(2)}, u32[]{:S(2)}) collective-permute-start(bf16[1,328,128]{2,1,0:T(8,128)(2,1)S(1)} %fusion.24), channel_id=1, source_target_pairs={{0,4},{1,5},{2,6},{3,7},{4,0},{5,1},{6,2},{7,3},{8,12},{9,13},{10,... | collective-permute-start | bytes 251912 | tf_op jit(solution)/shard_map/ppermute | solution.py:47
  181.4 11.1 %collective-permute-start.29 = (bf16[1,216,128]{2,1,0:T(8,128)(2,1)S(1)}, bf16[1,216,128]{2,1,0:T(8,128)(2,1)}, u32[]{:S(2)}, u32[]{:S(2)}) collective-permute-start(bf16[1,216,128]{2,1,0:T(8,128)(2,1)S(1)} %get-tuple-element.219), channel_id=1, source_target_pairs={{0,6},{1,7},{2,4},{3,5},{4,2},{5,3},{6,0},{7,1},{8,14},{9,15},{10,... | collective-permute-start | bytes 165896 | tf_op jit(solution)/shard_map/ppermute | solution.py:47
  183.0 11.9 %collective-permute-start.28 = (bf16[1,216,128]{2,1,0:T(8,128)(2,1)}, bf16[1,216,128]{2,1,0:T(8,128)(2,1)}, u32[]{:S(2)}, u32[]{:S(2)}) collective-permute-start(bf16[1,216,128]{2,1,0:T(8,128)(2,1)} %get-tuple-element.220), channel_id=1, source_target_pairs={{0,4},{1,5},{2,6},{3,7},{4,0},{5,1},{6,2},{7,3},{8,12},{9,13},{10,... | collective-permute-start | bytes 165896 | tf_op jit(solution)/shard_map/ppermute | solution.py:47
  184.2 7.7 %copy-start.25 = (f32[2,576]{1,0:T(2,128)}, f32[2,576]{1,0:T(2,128)S(1)}, u32[]{:S(2)}) copy-start(f32[2,576]{1,0:T(2,128)S(1)} %add.291) | copy-start | bytes 13828
  184.2 7.6 %collective-permute-start.31 = (f32[2,576]{1,0:T(2,128)S(1)}, f32[2,576]{1,0:T(2,128)S(1)}, u32[]{:S(2)}, u32[]{:S(2)}) collective-permute-start(f32[2,576]{1,0:T(2,128)S(1)} %add.291), channel_id=1, source_target_pairs={{0,4},{1,5},{2,6},{3,7},{4,0},{5,1},{6,2},{7,3},{8,12},{9,13},{10,... | collective-permute-start | bytes 13832 | tf_op jit(solution)/shard_map/ppermute | solution.py:47
  191.9 4.6 %collective-permute-start.27 = (bf16[1,216,128]{2,1,0:T(8,128)(2,1)}, bf16[1,216,128]{2,1,0:T(8,128)(2,1)}, u32[]{:S(2)}, u32[]{:S(2)}) collective-permute-start(bf16[1,216,128]{2,1,0:T(8,128)(2,1)} %get-tuple-element.221), channel_id=1, source_target_pairs={{0,2},{1,3},{2,0},{3,1},{4,6},{5,7},{6,4},{7,5},{8,10},{9,11},{10,... | collective-permute-start | bytes 165896 | tf_op jit(solution)/shard_map/ppermute | solution.py:47
  192.5 10.9 %collective-permute-start.34 = (bf16[1,2,384,128]{3,2,1,0:T(8,128)(2,1)S(1)}, bf16[1,2,384,128]{3,2,1,0:T(8,128)(2,1)S(1)}, u32[]{:S(2)}, u32[]{:S(2)}) collective-permute-start(bf16[1,2,384,128]{3,2,1,0:T(8,128)(2,1)S(1)} %fusion.15), channel_id=1, source_target_pairs={{0,4},{1,5},{2,6},{3,7},{4,0},{5,1},{6,2},{7,3},{8,12},{9,13},{10,... | collective-permute-start | bytes 589832 | tf_op jit(solution)/shard_map/ppermute | solution.py:47
  194.1 12.2 %copy-start.8 = (bf16[576,960]{1,0:T(8,128)(2,1)S(1)}, bf16[576,960]{1,0:T(8,128)(2,1)}, u32[]{:S(2)}) copy-start(bf16[576,960]{1,0:T(8,128)(2,1)} %get-tuple-element.123.w_project) | copy-start | bytes 3317764
  207.5 1.0 copy-start.24
  207.5 1.0 copy-start.26
  207.5 1.6 copy-start.4
  207.5 1.6 copy-start.14
  207.5 1.6 copy-start.15
  208.5 1.8 copy-start.12
  208.5 1.8 copy-start.21
  208.5 1.8 copy-start.22
  (4 other events, 3.2 us)
Sparse Core Ops, SparseCore 0:
  11.4 74.4 all-gather.1

commit v5 on v4

--- a/solution.py
+++ b/solution.py
@@ -759,38 +759,42 @@
             exchange(window_sent, "seq", 1),
             exchange(gains_total, "seq", 1),
         )
-        kept, *sent = add_up(kept, [new], dp_count)
+        kept, sent = add_up(kept, [new], 2)
         one_kept, one_sent = add_up(one_kept, [one_new], 2)
         two_kept, two_sent = add_up(two_kept, [two_new], 2)
         window_kept, window_sent = add_up(window_kept, [window_new], 2)
         gains_total = gains_total + gains_new
 
-        arrived = together(
-            *[exchange(part, "dp", place) for place, part in enumerate(sent, 1)],
-            both_bits(gains_total, "dp", 1, 2),
+        new, one_new, two_new, window_new, gains_new = together(
+            exchange(sent, "dp", 2),
             exchange(one_sent, "seq", 2),
             exchange(two_sent, "seq", 2),
             exchange(window_sent, "seq", 2),
-        )
-        kept, *sent = add_up(kept, arrived[:3], len(line))
-        gains_total = arrived[3]
-        one_kept, one_sent = add_up(one_kept, [arrived[4]], 2)
-        two_kept, two_sent = add_up(two_kept, [arrived[5]], 2)
-        window_kept, window_sent = add_up(window_kept, [arrived[6]], 2)
-
-        arrived = together(
-            *[exchange(part, "seq", place) for place, part in zip(line[1:], sent)],
-            both_bits(gains_total, "seq", 2, 4),
+            exchange(gains_total, "dp", 2),
+        )
+        kept, sent = add_up(kept, [new], 2)
+        one_kept, one_sent = add_up(one_kept, [one_new], 2)
+        two_kept, two_sent = add_up(two_kept, [two_new], 2)
+        window_kept, window_sent = add_up(window_kept, [window_new], 2)
+        gains_total = gains_total + gains_new
+
+        new, one_new, two_new, window_new, gains_new = together(
+            exchange(sent, "dp", 1),
             exchange(one_sent, "seq", 4),
             exchange(two_sent, "seq", 4),
             exchange(window_sent, "seq", 4),
-        )
-        attention_owned = add_up(kept, arrived[:3], 1)[0].reshape(-1)
-        gains_total = arrived[3]
+            exchange(gains_total, "dp", 1),
+        )
+        kept, *sent = add_up(kept, [new], len(line))
+        gains_total = gains_total + gains_new
         feedforward_owned = jnp.concatenate(
-            [add_up(one_kept, [arrived[4]], 1)[0][0], add_up(two_kept, [arrived[5]], 1)[0][0]], 0
+            [add_up(one_kept, [one_new], 1)[0][0], add_up(two_kept, [two_new], 1)[0][0]], 0
         ).reshape(-1)
-        d_own = add_up(window_kept, [arrived[6]], 1)[0][0].astype(BF16)
+        d_own = add_up(window_kept, [window_new], 1)[0][0].astype(BF16)
+
+        news = [exchange(part, "seq", place) for place, part in zip(line[1:], sent)]
+        gains_total = both_bits(gains_total, "seq", 2, 4)
+        attention_owned = add_up(kept, news, 1)[0].reshape(-1)
     else:
         halves = [jnp.concatenate(parts[index : index + 2], 0) for index in (0, 2)]
         grads = jnp.concatenate(halves, 1).reshape(-1)

time: 220 us -> 207 us (0.941)
  waiting for transfers between devices: 74.3 us -> 63.8 us
  other arithmetic: 25.8 us -> 23.4 us
    ppermute x35 -> x34, waiting for transfers between devices: 68.7 us -> 56.3 us  [exchange(): return lax.ppermute(value, axis, pairs)]
    ppermute x35 -> x34, starting transfers between devices: 42.3 us -> 43.3 us  [exchange(): return lax.ppermute(value, axis, pairs)]
    add x7 -> x8, other arithmetic: 5.35 us -> 4.66 us  [add_up(): total = total + new[rows].astype(F32)]
  transfers between devices with their start and end apart: 36 -> 35, of which waited for: 14 -> 15; matrix products, arithmetic and copies ran while one was open for 8% -> 9% of each run, Pallas kernels for 19% -> 20%
where the time goes in v5:
time: 207 us
  waiting for transfers between devices  63.8 us (31%)
  Pallas kernels  56.7 us (27%)
  starting transfers between devices  43.3 us (21%)
  other arithmetic  23.4 us (11%)
  between operations  14.6 us (7%)
  local copies, waits for them, and re-layouts  3.53 us (2%)
    ppermute x34, waiting for transfers between devices, exchange(): return lax.ppermute(value, axis, pairs)  56.3 us
    ppermute x34, starting transfers between devices, exchange(): return lax.ppermute(value, axis, pairs)  43.3 us
    pallas_call x2, Pallas kernels, attention_backward(): pl.pallas_call(kernel, out_shape=outputs, in_specs=in_specs, out_specs=tu...  25.3 us
    pallas_call x1, Pallas kernels, attention_forward(): pl.pallas_call(functools.partial(attention_forward_kernel, len(weight_pie...  16.1 us
    pallas_call x1, Pallas kernels, feedforward(): pl.pallas_call(feedforward_kernel, out_shape=(shape((MICRO, D, DEVICE_TOK...  15.4 us
    all_gather x1, waiting for transfers between devices, on_device(): lax.all_gather(feedforward_low, both, axis=0, tiled=True)  7.5 us
    add x8, other arithmetic, add_up(): total = total + new[rows].astype(F32)  4.66 us
  transfers between devices with their start and end apart: 35, of which 15 were waited for; matrix products, arithmetic and copies ran while one was open for 9% of the time, Pallas kernels for 20%

profile of v5, /device:TPU:0, one launch (start us, length us, event | category | flops | bytes accessed | tf_op | source)
XLA Modules:
  0.0 206.6 jit_solution(3155469726303368470)
XLA Ops:
  7.2 1.7 convert_bitcast_fusion
  8.9 0.9 convert_bitcast_fusion.1
  9.9 3.0 %collective-permute-start = (bf16[1,216,128]{2,1,0:T(8,128)(2,1)S(1)}, bf16[1,216,128]{2,1,0:T(8,128)(2,1)S(1)}, u32[]{:S(2)}, u32[]{:S(2)}) collective-permute-start(bf16[1,216,128]{2,1,0:T(8,128)(2,1)S(1)} %convert_bitcast_fusion.1), channel_id=1, source_target_pairs={{0,2},{1,3},{2,0},{3,1},{4,6},{5,7},{6,4},{7,5},{8,10},{9,11},{10,... | collective-permute-start | bytes 165896 | tf_op jit(solution)/shard_map/ppermute | solution.py:47
  12.9 4.5 %collective-permute-start.2 = (bf16[1,2,576,128]{3,2,1,0:T(8,128)(2,1)}, bf16[1,2,576,128]{3,2,1,0:T(8,128)(2,1)S(1)}, u32[]{:S(2)}, u32[]{:S(2)}) collective-permute-start(bf16[1,2,576,128]{3,2,1,0:T(8,128)(2,1)} %bitcast.63), channel_id=1, source_target_pairs={{0,4},{1,5},{2,6},{3,7},{8,12},{9,13},{10,14},{11,15},{16,20},{17,... | collective-permute-start | bytes 884744 | tf_op jit(solution)/shard_map/ppermute | solution.py:47
  17.4 1.0 reduce_window_sum.12
  18.4 0.7 sub.30
  19.3 0.7 xor_multiply_fusion
  20.4 1.2 and_select_fusion.refs_10_.refs_11_.refs_16_
  21.6 1.0 multiply_sine_fusion
  22.7 9.5 %collective-permute-done.1 = bf16[2,216,128]{2,1,0:T(8,128)(2,1)S(1)} collective-permute-done((bf16[2,216,128]{2,1,0:T(8,128)(2,1)S(1)}, bf16[2,216,128]{2,1,0:T(8,128)(2,1)S(1)}, u32[]{:S(2)}, u32[]{:S(2)}) %collective-permute-start.1) | collective-permute-done | bytes 110624 | tf_op jit(solution)/shard_map/ppermute | solution.py:47
  32.4 6.4 %collective-permute-start.7 = (bf16[2,2,576,128]{3,2,1,0:T(8,128)(2,1)S(1)}, bf16[2,2,576,128]{3,2,1,0:T(8,128)(2,1)}, u32[]{:S(2)}, u32[]{:S(2)}) collective-permute-start(bf16[2,2,576,128]{3,2,1,0:T(8,128)(2,1)S(1)} %pad_maximum_fusion.refs_4_), channel_id=1, source_target_pairs={{0,2},{1,3},{2,0},{3,1},{4,6},{5,7},{6,4},{7,5},{8,10},{9,11},{10,... | collective-permute-start | bytes 1769480 | tf_op jit(solution)/shard_map/ppermute | solution.py:47
  38.8 1.5 collective-permute-start.3
  40.3 5.4 %collective-permute-done.3 = bf16[4,216,128]{2,1,0:T(8,128)(2,1)S(1)} collective-permute-done((bf16[4,216,128]{2,1,0:T(8,128)(2,1)S(1)}, bf16[4,216,128]{2,1,0:T(8,128)(2,1)S(1)}, u32[]{:S(2)}, u32[]{:S(2)}) %collective-permute-start.3) | collective-permute-done | bytes 221216 | tf_op jit(solution)/shard_map/ppermute | solution.py:47
  45.7 1.2 collective-permute-start.4
  46.9 10.8 %collective-permute-done.7.refs_5_ = bf16[2,2,576,128]{3,2,1,0:T(8,128)(2,1)} collective-permute-done((bf16[2,2,576,128]{3,2,1,0:T(8,128)(2,1)S(1)}, bf16[2,2,576,128]{3,2,1,0:T(8,128)(2,1)}, u32[]{:S(2)}, u32[]{:S(2)}) %collective-permute-start.7) | collective-permute-done | bytes 589856 | tf_op jit(solution)/shard_map/ppermute | solution.py:47
  59.2 1.3 collective-permute-done.5.refs_2_
  60.5 0.6 collective-permute-done.6.refs_3_
  61.3 0.6 copy-done.10
  61.9 16.1 %shard_map.239 = (bf16[576,960]{1,0:T(8,128)(2,1)}, bf16[576,576]{1,0:T(8,128)(2,1)}, bf16[2,576,1024]{2,1,0:T(8,128)(2,1)}, bf16[2,576,128]{2,1,0:T(8,128)(2,1)...) custom-call(s32[32]{0:T(128)S(1)} %broadcast_xor_fusion.order, ...), custom_call_target="tpu_custom_call" | custom-call | tf_op jit(solution)/shard_map/pallas_call | solution.py:261
  78.0 7.5 %all-gather.2.cloned.1.call-done = bf16[20736,128]{1,0:T(8,128)(2,1)} async-done(((bf16[648,128]{1,0:T(8,128)(2,1)}), bf16[20736,128]{1,0:T(8,128)(2,1)}) %all-gather.2.cloned.1.call-update) | async-done | bytes 5308432 | tf_op jit(solution)/shard_map/all_gather | solution.py:642
  85.5 15.4 %shard_map.240 = (bf16[2,576,128]{2,1,0:T(8,128)(2,1)}, bf16[256,576]{1,0:T(8,128)(2,1)S(1)}, f32[2,576,128]{2,1,0:T(8,128)S(1)}, bf16[16,320,128]{2,1,0:T(8,128...) custom-call(s32[32]{0:T(128)S(1)} %iota.26.straight, ...), custom_call_target="tpu_custom_call" | custom-call | tf_op jit(solution)/shard_map/pallas_call | solution.py:383
  101.4 10.6 %shard_map.241 = (bf16[576,128]{1,0:T(8,128)(2,1)S(1)}, bf16[8,384,128]{2,1,0:T(8,128)(2,1)}, f32[576,576]{1,0:T(8,128)}, f32[576,384]{1,0:T(8,128)}, f32[576,576]{1,0:T(8,128)}) custom-call(bf16[576,576]{1,0:T(8,128)(2,1)} %get-tuple-element.95.refs_0_.refs_5_, bf16[2,576,1024]{2,1,0:T(8,128)(2,1)} %get-tuple-element.96.refs_1_.refs_6_, ...), custom_call_target="tpu_custom_call" | custom-call | tf_op jit(solution)/shard_map/pallas_call | solution.py:568
  112.3 1.0 copy-done.4
  113.6 1.5 collective-permute-start.13
  115.7 14.7 %shard_map.242 = (bf16[16,216,128]{2,1,0:T(8,128)(2,1)}, bf16[16,216,128]{2,1,0:T(8,128)(2,1)}, bf16[2,576,128]{2,1,0:T(8,128)(2,1)S(1)}, bf16[4,2,384,128]{3,2,...) custom-call(s32[32]{0:T(128)S(1)} %broadcast_xor_fusion.order, ...), custom_call_target="tpu_custom_call" | custom-call | tf_op jit(solution)/shard_map/pallas_call | solution.py:568
  130.4 1.4 collective-permute-done.12
  132.4 0.6 collective-permute-start.16
  133.1 1.0 slice_add_fusion.2
  134.1 1.4 collective-permute-start.15
  136.0 1.2 collective-permute-done.18
  137.1 6.6 %collective-permute-done.15 = bf16[4,320,128]{2,1,0:T(8,128)(2,1)} collective-permute-done((bf16[4,320,128]{2,1,0:T(8,128)(2,1)}, bf16[4,320,128]{2,1,0:T(8,128)(2,1)}, u32[]{:S(2)}, u32[]{:S(2)}) %collective-permute-start.15) | collective-permute-done | bytes 327712 | tf_op jit(solution)/shard_map/ppermute | solution.py:47
  143.8 0.7 copy-done.13
  144.5 1.2 slice_add_fusion.10
  145.7 2.0 collective-permute-start.20
  147.7 1.5 convert_add_fusion.3
  149.5 1.3 add_convert_fusion.2
  150.9 1.5 collective-permute-start.19
  152.4 1.9 collective-permute-start.21
  154.3 0.7 collective-permute-start.23
  155.1 6.5 %collective-permute-done.23 = f32[2,576]{1,0:T(2,128)S(1)} collective-permute-done((f32[2,576]{1,0:T(2,128)S(1)}, f32[2,576]{1,0:T(2,128)S(1)}, u32[]{:S(2)}, u32[]{:S(2)}) %collective-permute-start.23) | collective-permute-done | bytes 4640 | tf_op jit(solution)/shard_map/ppermute | solution.py:47
  161.6 1.6 collective-permute-done.21
  163.2 1.5 collective-permute-start.28
  164.7 0.7 fusion.28
  165.3 2.0 collective-permute-start.25
  167.3 0.7 fusion.25
  168.0 1.0 collective-permute-start.26
  168.9 0.7 fusion.16
  169.6 2.0 collective-permute-start.27
  171.7 0.6 collective-permute-start.24
  172.9 5.8 %collective-permute-done.25 = bf16[1,320,128]{2,1,0:T(8,128)(2,1)} collective-permute-done((bf16[1,320,128]{2,1,0:T(8,128)(2,1)}, bf16[1,320,128]{2,1,0:T(8,128)(2,1)}, u32[]{:S(2)}, u32[]{:S(2)}) %collective-permute-start.25) | collective-permute-done | bytes 81952 | tf_op jit(solution)/shard_map/ppermute | solution.py:47
  178.7 1.8 collective-permute-done.26
  180.5 2.6 %collective-permute-done.27 = bf16[1,2,384,128]{3,2,1,0:T(8,128)(2,1)} collective-permute-done((bf16[1,2,384,128]{3,2,1,0:T(8,128)(2,1)}, bf16[1,2,384,128]{3,2,1,0:T(8,128)(2,1)}, u32[]{:S(2)}, u32[]{:S(2)}) %collective-permute-start.27) | collective-permute-done | bytes 196640 | tf_op jit(solution)/shard_map/ppermute | solution.py:47
  183.1 1.0 fusion.24
  184.1 1.0 fusion.27
  185.0 1.1 fusion.22
  186.3 1.3 fusion.6
  187.6 1.2 multiply_subtract_fusion
  188.8 2.1 %collective-permute-start.29 = (bf16[1,216,128]{2,1,0:T(8,128)(2,1)S(1)}, bf16[1,216,128]{2,1,0:T(8,128)(2,1)S(1)}, u32[]{:S(2)}, u32[]{:S(2)}) collective-permute-start(bf16[1,216,128]{2,1,0:T(8,128)(2,1)S(1)} %get-tuple-element.215), channel_id=1, source_target_pairs={{0,2},{1,3},{2,0},{3,1},{4,6},{5,7},{6,4},{7,5},{8,10},{9,11},{10,... | collective-permute-start | bytes 165896 | tf_op jit(solution)/shard_map/ppermute | solution.py:47
  190.9 2.2 %collective-permute-start.31 = (bf16[1,216,128]{2,1,0:T(8,128)(2,1)S(1)}, bf16[1,216,128]{2,1,0:T(8,128)(2,1)S(1)}, u32[]{:S(2)}, u32[]{:S(2)}) collective-permute-start(bf16[1,216,128]{2,1,0:T(8,128)(2,1)S(1)} %get-tuple-element.216), channel_id=1, source_target_pairs={{0,6},{1,7},{2,4},{3,5},{4,2},{5,3},{6,0},{7,1},{8,14},{9,15},{10,... | collective-permute-start | bytes 165896 | tf_op jit(solution)/shard_map/ppermute | solution.py:47
  193.1 3.0 %collective-permute-start.33 = (f32[2,576]{1,0:T(2,128)S(1)}, f32[2,576]{1,0:T(2,128)S(1)}, u32[]{:S(2)}, u32[]{:S(2)}) collective-permute-start(f32[2,576]{1,0:T(2,128)S(1)} %add.290), channel_id=1, source_target_pairs={{0,4},{1,5},{2,6},{3,7},{4,0},{5,1},{6,2},{7,3},{8,12},{9,13},{10,... | collective-permute-start | bytes 13832 | tf_op jit(solution)/shard_map/ppermute | solution.py:47
  196.1 0.9 fusion.10
  197.1 1.2 collective-permute-done.33
  198.2 0.6 multiply_subtract_fusion.2
  198.9 0.8 multiply_subtract_fusion.1
  (127 shorter events, 6.5 us)
Async XLA Ops:
  7.2 78.3 %all-gather.2.cloned.1.call-start = ((), (), s32[]{:S(2)}) async-start(), calls=%async_computation | async-start | bytes 5474304 | tf_op jit(solution)/shard_map/all_gather | solution.py:642
  8.9 23.4 %copy-start.2 = (bf16[2,1,128,576]{2,3,1,0:T(8,128)(2,1)S(1)}, bf16[2,1,128,576]{2,3,1,0:T(8,128)(2,1)}, u32[]{:S(2)}) copy-start(bf16[2,1,128,576]{2,3,1,0:T(8,128)(2,1)} %param.16) | copy-start | bytes 884740
  9.9 12.7 %collective-permute-start = (bf16[1,216,128]{2,1,0:T(8,128)(2,1)S(1)}, bf16[1,216,128]{2,1,0:T(8,128)(2,1)S(1)}, u32[]{:S(2)}, u32[]{:S(2)}) collective-permute-start(bf16[1,216,128]{2,1,0:T(8,128)(2,1)S(1)} %convert_bitcast_fusion.1), channel_id=1, source_target_pairs={{0,2},{1,3},{2,0},{3,1},{4,6},{5,7},{6,4},{7,5},{8,10},{9,11},{10,... | collective-permute-start | bytes 165896 | tf_op jit(solution)/shard_map/ppermute | solution.py:47
  12.9 19.4 %collective-permute-start.2 = (bf16[1,2,576,128]{3,2,1,0:T(8,128)(2,1)}, bf16[1,2,576,128]{3,2,1,0:T(8,128)(2,1)S(1)}, u32[]{:S(2)}, u32[]{:S(2)}) collective-permute-start(bf16[1,2,576,128]{3,2,1,0:T(8,128)(2,1)} %bitcast.63), channel_id=1, source_target_pairs={{0,4},{1,5},{2,6},{3,7},{8,12},{9,13},{10,14},{11,15},{16,20},{17,... | collective-permute-start | bytes 884744 | tf_op jit(solution)/shard_map/ppermute | solution.py:47
  22.6 35.2 %copy-start.21 = (f32[2,576]{1,0:T(2,128)S(1)}, f32[2,576]{1,0:T(2,128)}, u32[]{:S(2)}) copy-start(f32[2,576]{1,0:T(2,128)} %param.21) | copy-start | bytes 13828
  22.6 36.6 %copy-start.28 = (s32[32]{0:T(128)S(1)}, s32[32]{0:T(128)}, u32[]{:S(2)}) copy-start(s32[32]{0:T(128)} %constant.30.clone) | copy-start | bytes 388
  22.6 36.6 %copy-start.26 = (s32[32]{0:T(128)S(1)}, s32[32]{0:T(128)}, u32[]{:S(2)}) copy-start(s32[32]{0:T(128)} %constant.100.clone) | copy-start | bytes 388
  22.6 36.6 %copy-start.27 = (s32[32]{0:T(128)S(1)}, s32[32]{0:T(128)}, u32[]{:S(2)}) copy-start(s32[32]{0:T(128)} %constant.31.clone) | copy-start | bytes 388
  22.7 9.6 %collective-permute-start.1 = (bf16[2,216,128]{2,1,0:T(8,128)(2,1)S(1)}, bf16[2,216,128]{2,1,0:T(8,128)(2,1)S(1)}, u32[]{:S(2)}, u32[]{:S(2)}) collective-permute-start(bf16[2,216,128]{2,1,0:T(8,128)(2,1)S(1)} %pad_maximum_fusion.2), channel_id=1, source_target_pairs={{0,4},{1,5},{2,6},{3,7},{4,0},{5,1},{6,2},{7,3},{8,12},{9,13},{10,... | collective-permute-start | bytes 331784 | tf_op jit(solution)/shard_map/ppermute | solution.py:47
  32.4 28.8 %copy-start.3 = (bf16[2,2,576,128]{3,2,1,0:T(8,128)(2,1)}, bf16[2,2,576,128]{3,2,1,0:T(8,128)(2,1)S(1)}, u32[]{:S(2)}) copy-start(bf16[2,2,576,128]{3,2,1,0:T(8,128)(2,1)S(1)} %pad_maximum_fusion.refs_4_) | copy-start | bytes 1769476
  32.4 25.4 %collective-permute-start.7 = (bf16[2,2,576,128]{3,2,1,0:T(8,128)(2,1)S(1)}, bf16[2,2,576,128]{3,2,1,0:T(8,128)(2,1)}, u32[]{:S(2)}, u32[]{:S(2)}) collective-permute-start(bf16[2,2,576,128]{3,2,1,0:T(8,128)(2,1)S(1)} %pad_maximum_fusion.refs_4_), channel_id=1, source_target_pairs={{0,2},{1,3},{2,0},{3,1},{4,6},{5,7},{6,4},{7,5},{8,10},{9,11},{10,... | collective-permute-start | bytes 1769480 | tf_op jit(solution)/shard_map/ppermute | solution.py:47
  38.8 6.9 %collective-permute-start.3 = (bf16[4,216,128]{2,1,0:T(8,128)(2,1)S(1)}, bf16[4,216,128]{2,1,0:T(8,128)(2,1)S(1)}, u32[]{:S(2)}, u32[]{:S(2)}) collective-permute-start(bf16[4,216,128]{2,1,0:T(8,128)(2,1)S(1)} %pad_maximum_fusion.1), channel_id=1, source_target_pairs={{0,8},{8,0},{16,24},{24,16},{1,9},{9,1},{17,25},{25,17},{2,10},{10... | collective-permute-start | bytes 663560 | tf_op jit(solution)/shard_map/ppermute | solution.py:47
  45.7 13.4 %collective-permute-start.4 = (bf16[8,216,128]{2,1,0:T(8,128)(2,1)S(1)}, bf16[8,216,128]{2,1,0:T(8,128)(2,1)S(1)}, u32[]{:S(2)}, u32[]{:S(2)}) collective-permute-start(bf16[8,216,128]{2,1,0:T(8,128)(2,1)S(1)} %constant_dynamic-update-slice_fusion.refs_0_), channel_id=1, source_target_pairs={{0,16},{8,24},{16,0},{24,8},{1,17},{9,25},{17,1},{25,9},{2,18},{10... | collective-permute-start | bytes 1327112 | tf_op jit(solution)/shard_map/ppermute | solution.py:47
  46.9 12.3 %collective-permute-start.8 = (bf16[2,2,576,128]{3,2,1,0:T(8,128)(2,1)S(1)}, bf16[2,2,576,128]{3,2,1,0:T(8,128)(2,1)}, u32[]{:S(2)}, u32[]{:S(2)}) collective-permute-start(bf16[2,2,576,128]{3,2,1,0:T(8,128)(2,1)S(1)} %pad_maximum_fusion.refs_4_), channel_id=1, source_target_pairs={{0,1},{1,0},{2,3},{3,2},{4,5},{5,4},{6,7},{7,6},{8,9},{9,8},{10,11... | collective-permute-start | bytes 1769480 | tf_op jit(solution)/shard_map/ppermute | solution.py:47
  57.8 3.4 %collective-permute-start.9 = (bf16[2,2,576,128]{3,2,1,0:T(8,128)(2,1)}, bf16[2,2,576,128]{3,2,1,0:T(8,128)(2,1)}, u32[]{:S(2)}, u32[]{:S(2)}) collective-permute-start(bf16[2,2,576,128]{3,2,1,0:T(8,128)(2,1)} %collective-permute-done.7.refs_5_), channel_id=1, source_target_pairs={{0,1},{1,0},{2,3},{3,2},{4,5},{5,4},{6,7},{7,6},{8,9},{9,8},{10,11... | collective-permute-start | bytes 1769480 | tf_op jit(solution)/shard_map/ppermute | solution.py:47
  58.5 2.0 collective-permute-start.5
  59.1 2.0 collective-permute-start.6
  59.2 26.3 %copy-start.1 = (bf16[2,1,128,576]{2,3,1,0:T(8,128)(2,1)S(1)}, bf16[2,1,128,576]{2,3,1,0:T(8,128)(2,1)}, u32[]{:S(2)}) copy-start(bf16[2,1,128,576]{2,3,1,0:T(8,128)(2,1)} %param.17) | copy-start | bytes 884740
  60.5 0.8 copy-start.9
  61.2 0.8 copy-start.10
  85.5 15.9 %copy-start = (f32[2,576,128]{2,1,0:T(8,128)S(1)}, f32[2,576,128]{2,1,0:T(8,128)}, u32[]{:S(2)}) copy-start(f32[2,576,128]{2,1,0:T(8,128)} %get-tuple-element.102.refs_7_.refs_12_) | copy-start | bytes 1769476
  100.9 11.1 %collective-permute-start.11 = (bf16[16,328,128]{2,1,0:T(8,128)(2,1)}, bf16[16,328,128]{2,1,0:T(8,128)(2,1)S(1)}, u32[]{:S(2)}, u32[]{:S(2)}) collective-permute-start(bf16[16,328,128]{2,1,0:T(8,128)(2,1)} %get-tuple-element.94), channel_id=1, source_target_pairs={{0,1},{1,0},{2,3},{3,2},{4,5},{5,4},{6,7},{7,6},{8,9},{9,8},{10,11... | collective-permute-start | bytes 4030472 | tf_op jit(solution)/shard_map/ppermute | solution.py:47
  101.1 10.8 %collective-permute-start.10 = (bf16[16,320,128]{2,1,0:T(8,128)(2,1)}, bf16[16,320,128]{2,1,0:T(8,128)(2,1)S(1)}, u32[]{:S(2)}, u32[]{:S(2)}) collective-permute-start(bf16[16,320,128]{2,1,0:T(8,128)(2,1)} %get-tuple-element.93), channel_id=1, source_target_pairs={{0,1},{1,0},{2,3},{3,2},{4,5},{5,4},{6,7},{7,6},{8,9},{9,8},{10,11... | collective-permute-start | bytes 3932168 | tf_op jit(solution)/shard_map/ppermute | solution.py:47
  101.4 10.6 %copy-start.6 = (bf16[16,320,128]{2,1,0:T(8,128)(2,1)S(1)}, bf16[16,320,128]{2,1,0:T(8,128)(2,1)}, u32[]{:S(2)}) copy-start(bf16[16,320,128]{2,1,0:T(8,128)(2,1)} %get-tuple-element.92) | copy-start | bytes 3932164
  112.0 1.3 copy-start.4
  113.6 18.2 %collective-permute-start.13 = (bf16[8,328,128]{2,1,0:T(8,128)(2,1)S(1)}, bf16[8,328,128]{2,1,0:T(8,128)(2,1)S(1)}, u32[]{:S(2)}, u32[]{:S(2)}) collective-permute-start(bf16[8,328,128]{2,1,0:T(8,128)(2,1)S(1)} %get-tuple-element.118), channel_id=1, source_target_pairs={{0,16},{8,24},{16,0},{24,8},{1,17},{9,25},{17,1},{25,9},{2,18},{10... | collective-permute-start | bytes 2015240 | tf_op jit(solution)/shard_map/ppermute | solution.py:47
  115.2 16.6 %collective-permute-start.12 = (bf16[8,320,128]{2,1,0:T(8,128)(2,1)S(1)}, bf16[8,320,128]{2,1,0:T(8,128)(2,1)S(1)}, u32[]{:S(2)}, u32[]{:S(2)}) collective-permute-start(bf16[8,320,128]{2,1,0:T(8,128)(2,1)S(1)} %get-tuple-element.117), channel_id=1, source_target_pairs={{0,8},{8,0},{16,24},{24,16},{1,9},{9,1},{17,25},{25,17},{2,10},{10... | collective-permute-start | bytes 1966088 | tf_op jit(solution)/shard_map/ppermute | solution.py:47
  131.8 12.0 %collective-permute-start.14 = (bf16[16,216,128]{2,1,0:T(8,128)(2,1)}, bf16[16,216,128]{2,1,0:T(8,128)(2,1)}, u32[]{:S(2)}, u32[]{:S(2)}) collective-permute-start(bf16[16,216,128]{2,1,0:T(8,128)(2,1)} %get-tuple-element.133), channel_id=1, source_target_pairs={{0,1},{1,0},{2,3},{3,2},{4,5},{5,4},{6,7},{7,6},{8,9},{9,8},{10,11... | collective-permute-start | bytes 2654216 | tf_op jit(solution)/shard_map/ppermute | solution.py:47
  131.8 12.0 %collective-permute-start.17 = (bf16[4,2,384,128]{3,2,1,0:T(8,128)(2,1)}, bf16[4,2,384,128]{3,2,1,0:T(8,128)(2,1)}, u32[]{:S(2)}, u32[]{:S(2)}) collective-permute-start(bf16[4,2,384,128]{3,2,1,0:T(8,128)(2,1)} %get-tuple-element.136), channel_id=1, source_target_pairs={{0,1},{1,0},{2,3},{3,2},{4,5},{5,4},{6,7},{7,6},{8,9},{9,8},{10,11... | collective-permute-start | bytes 2359304 | tf_op jit(solution)/shard_map/ppermute | solution.py:47
  132.4 11.4 %collective-permute-start.16 = (bf16[4,328,128]{2,1,0:T(8,128)(2,1)S(1)}, bf16[4,328,128]{2,1,0:T(8,128)(2,1)S(1)}, u32[]{:S(2)}, u32[]{:S(2)}) collective-permute-start(bf16[4,328,128]{2,1,0:T(8,128)(2,1)S(1)} %get-tuple-element.202), channel_id=1, source_target_pairs={{0,8},{8,0},{16,24},{24,16},{1,9},{9,1},{17,25},{25,17},{2,10},{10... | collective-permute-start | bytes 1007624 | tf_op jit(solution)/shard_map/ppermute | solution.py:47
  134.1 9.7 %collective-permute-start.15 = (bf16[4,320,128]{2,1,0:T(8,128)(2,1)}, bf16[4,320,128]{2,1,0:T(8,128)(2,1)}, u32[]{:S(2)}, u32[]{:S(2)}) collective-permute-start(bf16[4,320,128]{2,1,0:T(8,128)(2,1)} %get-tuple-element.204), channel_id=1, source_target_pairs={{0,16},{8,24},{16,0},{24,8},{1,17},{9,25},{17,1},{25,9},{2,18},{10... | collective-permute-start | bytes 983048 | tf_op jit(solution)/shard_map/ppermute | solution.py:47
  135.9 1.2 collective-permute-start.18
  143.8 0.7 copy-start.13
  145.7 3.8 %copy-start.8 = (bf16[16,216,128]{2,1,0:T(8,128)(2,1)S(1)}, bf16[16,216,128]{2,1,0:T(8,128)(2,1)}, u32[]{:S(2)}) copy-start(bf16[16,216,128]{2,1,0:T(8,128)(2,1)} %get-tuple-element.140) | copy-start | bytes 2654212
  145.7 15.8 %collective-permute-start.20 = (bf16[2,320,128]{2,1,0:T(8,128)(2,1)S(1)}, bf16[2,320,128]{2,1,0:T(8,128)(2,1)S(1)}, u32[]{:S(2)}, u32[]{:S(2)}) collective-permute-start(bf16[2,320,128]{2,1,0:T(8,128)(2,1)S(1)} %get-tuple-element.214), channel_id=1, source_target_pairs={{0,2},{1,3},{2,0},{3,1},{4,6},{5,7},{6,4},{7,5},{8,10},{9,11},{10,... | collective-permute-start | bytes 491528 | tf_op jit(solution)/shard_map/ppermute | solution.py:47
  149.3 3.1 %copy-start.14 = (bf16[4,328,128]{2,1,0:T(8,128)(2,1)S(1)}, bf16[4,328,128]{2,1,0:T(8,128)(2,1)}, u32[]{:S(2)}) copy-start(bf16[4,328,128]{2,1,0:T(8,128)(2,1)} %copy-done.13) | copy-start | bytes 1007620
  149.3 13.9 %collective-permute-start.22 = (bf16[2,2,384,128]{3,2,1,0:T(8,128)(2,1)S(1)}, bf16[2,2,384,128]{3,2,1,0:T(8,128)(2,1)S(1)}, u32[]{:S(2)}, u32[]{:S(2)}) collective-permute-start(bf16[2,2,384,128]{3,2,1,0:T(8,128)(2,1)S(1)} %get-tuple-element.208), channel_id=1, source_target_pairs={{0,2},{1,3},{2,0},{3,1},{4,6},{5,7},{6,4},{7,5},{8,10},{9,11},{10,... | collective-permute-start | bytes 1179656 | tf_op jit(solution)/shard_map/ppermute | solution.py:47
  150.9 12.3 %collective-permute-start.19 = (bf16[8,216,128]{2,1,0:T(8,128)(2,1)S(1)}, bf16[8,216,128]{2,1,0:T(8,128)(2,1)S(1)}, u32[]{:S(2)}, u32[]{:S(2)}) collective-permute-start(bf16[8,216,128]{2,1,0:T(8,128)(2,1)S(1)} %get-tuple-element.205), channel_id=1, source_target_pairs={{0,16},{8,24},{16,0},{24,8},{1,17},{9,25},{17,1},{25,9},{2,18},{10... | collective-permute-start | bytes 1327112 | tf_op jit(solution)/shard_map/ppermute | solution.py:47
  152.4 10.7 %collective-permute-start.21 = (bf16[2,328,128]{2,1,0:T(8,128)(2,1)S(1)}, bf16[2,328,128]{2,1,0:T(8,128)(2,1)S(1)}, u32[]{:S(2)}, u32[]{:S(2)}) collective-permute-start(bf16[2,328,128]{2,1,0:T(8,128)(2,1)S(1)} %get-tuple-element.212), channel_id=1, source_target_pairs={{0,2},{1,3},{2,0},{3,1},{4,6},{5,7},{6,4},{7,5},{8,10},{9,11},{10,... | collective-permute-start | bytes 503816 | tf_op jit(solution)/shard_map/ppermute | solution.py:47
  154.3 7.2 %collective-permute-start.23 = (f32[2,576]{1,0:T(2,128)S(1)}, f32[2,576]{1,0:T(2,128)S(1)}, u32[]{:S(2)}, u32[]{:S(2)}) collective-permute-start(f32[2,576]{1,0:T(2,128)S(1)} %fusion.44), channel_id=1, source_target_pairs={{0,16},{8,24},{16,0},{24,8},{1,17},{9,25},{17,1},{25,9},{2,18},{10... | collective-permute-start | bytes 13832 | tf_op jit(solution)/shard_map/ppermute | solution.py:47
  161.6 10.1 %copy-start.18 = (bf16[2,320,128]{2,1,0:T(8,128)(2,1)}, bf16[2,320,128]{2,1,0:T(8,128)(2,1)S(1)}, u32[]{:S(2)}) copy-start(bf16[2,320,128]{2,1,0:T(8,128)(2,1)S(1)} %collective-permute-done.20) | copy-start | bytes 491524
  163.1 9.2 %copy-start.17 = (bf16[2,328,128]{2,1,0:T(8,128)(2,1)}, bf16[2,328,128]{2,1,0:T(8,128)(2,1)S(1)}, u32[]{:S(2)}) copy-start(bf16[2,328,128]{2,1,0:T(8,128)(2,1)S(1)} %collective-permute-done.21) | copy-start | bytes 503812
  163.1 8.5 %copy-start.12 = (bf16[2,2,384,128]{3,2,1,0:T(8,128)(2,1)}, bf16[2,2,384,128]{3,2,1,0:T(8,128)(2,1)S(1)}, u32[]{:S(2)}) copy-start(bf16[2,2,384,128]{3,2,1,0:T(8,128)(2,1)S(1)} %collective-permute-done.22) | copy-start | bytes 1179652
  163.2 9.7 %collective-permute-start.28 = (f32[2,576]{1,0:T(2,128)S(1)}, f32[2,576]{1,0:T(2,128)S(1)}, u32[]{:S(2)}, u32[]{:S(2)}) collective-permute-start(f32[2,576]{1,0:T(2,128)S(1)} %add.260), channel_id=1, source_target_pairs={{0,8},{8,0},{16,24},{24,16},{1,9},{9,1},{17,25},{25,17},{2,10},{10... | collective-permute-start | bytes 13832 | tf_op jit(solution)/shard_map/ppermute | solution.py:47
  165.3 13.4 %collective-permute-start.25 = (bf16[1,320,128]{2,1,0:T(8,128)(2,1)}, bf16[1,320,128]{2,1,0:T(8,128)(2,1)}, u32[]{:S(2)}, u32[]{:S(2)}) collective-permute-start(bf16[1,320,128]{2,1,0:T(8,128)(2,1)} %fusion.28), channel_id=1, source_target_pairs={{0,4},{1,5},{2,6},{3,7},{4,0},{5,1},{6,2},{7,3},{8,12},{9,13},{10,... | collective-permute-start | bytes 245768 | tf_op jit(solution)/shard_map/ppermute | solution.py:47
  168.0 12.6 %collective-permute-start.26 = (bf16[1,328,128]{2,1,0:T(8,128)(2,1)}, bf16[1,328,128]{2,1,0:T(8,128)(2,1)}, u32[]{:S(2)}, u32[]{:S(2)}) collective-permute-start(bf16[1,328,128]{2,1,0:T(8,128)(2,1)} %fusion.25), channel_id=1, source_target_pairs={{0,4},{1,5},{2,6},{3,7},{4,0},{5,1},{6,2},{7,3},{8,12},{9,13},{10,... | collective-permute-start | bytes 251912 | tf_op jit(solution)/shard_map/ppermute | solution.py:47
  169.6 13.5 %collective-permute-start.27 = (bf16[1,2,384,128]{3,2,1,0:T(8,128)(2,1)}, bf16[1,2,384,128]{3,2,1,0:T(8,128)(2,1)}, u32[]{:S(2)}, u32[]{:S(2)}) collective-permute-start(bf16[1,2,384,128]{3,2,1,0:T(8,128)(2,1)} %fusion.16), channel_id=1, source_target_pairs={{0,4},{1,5},{2,6},{3,7},{4,0},{5,1},{6,2},{7,3},{8,12},{9,13},{10,... | collective-permute-start | bytes 589832 | tf_op jit(solution)/shard_map/ppermute | solution.py:47
  171.7 11.4 %collective-permute-start.24 = (bf16[4,216,128]{2,1,0:T(8,128)(2,1)S(1)}, bf16[4,216,128]{2,1,0:T(8,128)(2,1)S(1)}, u32[]{:S(2)}, u32[]{:S(2)}) collective-permute-start(bf16[4,216,128]{2,1,0:T(8,128)(2,1)S(1)} %get-tuple-element.210), channel_id=1, source_target_pairs={{0,8},{8,0},{16,24},{24,16},{1,9},{9,1},{17,25},{25,17},{2,10},{10... | collective-permute-start | bytes 663560 | tf_op jit(solution)/shard_map/ppermute | solution.py:47
  172.9 13.4 %copy-start.7 = (bf16[576,960]{1,0:T(8,128)(2,1)S(1)}, bf16[576,960]{1,0:T(8,128)(2,1)}, u32[]{:S(2)}) copy-start(bf16[576,960]{1,0:T(8,128)(2,1)} %get-tuple-element.119.w_project) | copy-start | bytes 3317764
  172.9 13.4 %copy-start.25 = (f32[2,128]{1,0:T(2,128)S(1)}, f32[2,128]{1,0:T(2,128)}, u32[]{:S(2)}) copy-start(f32[2,128]{1,0:T(2,128)} %add_rsqrt_fusion) | copy-start | bytes 3076
  186.1 7.0 %collective-permute-start.32 = (f32[2,576]{1,0:T(2,128)S(1)}, f32[2,576]{1,0:T(2,128)S(1)}, u32[]{:S(2)}, u32[]{:S(2)}) collective-permute-start(f32[2,576]{1,0:T(2,128)S(1)} %add.289), channel_id=1, source_target_pairs={{0,2},{1,3},{2,0},{3,1},{4,6},{5,7},{6,4},{7,5},{8,10},{9,11},{10,... | collective-permute-start | bytes 13832 | tf_op jit(solution)/shard_map/ppermute | solution.py:47
  186.3 1.3 copy-start.5
  186.3 1.3 copy-start.15
  186.3 1.3 copy-start.16
  188.8 9.5 %copy-start.22 = (f32[2,576]{1,0:T(2,128)S(1)}, f32[2,576]{1,0:T(2,128)}, u32[]{:S(2)}) copy-start(f32[2,576]{1,0:T(2,128)} %param.21) | copy-start | bytes 13828
  188.8 9.5 %copy-start.23 = (f32[2,576]{1,0:T(2,128)S(1)}, f32[2,576]{1,0:T(2,128)}, u32[]{:S(2)}) copy-start(f32[2,576]{1,0:T(2,128)} %param.26) | copy-start | bytes 13828
  188.8 9.5 %copy-start.24 = (f32[2,576]{1,0:T(2,128)S(1)}, f32[2,576]{1,0:T(2,128)}, u32[]{:S(2)}) copy-start(f32[2,576]{1,0:T(2,128)} %param.27) | copy-start | bytes 13828
  188.8 10.1 %copy-start.11 = (f32[27648]{0:T(1024)S(1)}, f32[27648]{0:T(1024)}, u32[]{:S(2)}) copy-start(f32[27648]{0:T(1024)} %param.19) | copy-start | bytes 331780
  188.8 10.1 %copy-start.19 = (f32[27648]{0:T(1024)S(1)}, f32[27648]{0:T(1024)}, u32[]{:S(2)}) copy-start(f32[27648]{0:T(1024)} %param.22) | copy-start | bytes 331780
  188.8 10.1 %copy-start.20 = (f32[27648]{0:T(1024)S(1)}, f32[27648]{0:T(1024)}, u32[]{:S(2)}) copy-start(f32[27648]{0:T(1024)} %param.23) | copy-start | bytes 331780
  188.8 10.1 %collective-permute-start.29 = (bf16[1,216,128]{2,1,0:T(8,128)(2,1)S(1)}, bf16[1,216,128]{2,1,0:T(8,128)(2,1)S(1)}, u32[]{:S(2)}, u32[]{:S(2)}) collective-permute-start(bf16[1,216,128]{2,1,0:T(8,128)(2,1)S(1)} %get-tuple-element.215), channel_id=1, source_target_pairs={{0,2},{1,3},{2,0},{3,1},{4,6},{5,7},{6,4},{7,5},{8,10},{9,11},{10,... | collective-permute-start | bytes 165896 | tf_op jit(solution)/shard_map/ppermute | solution.py:47
  190.9 8.0 %collective-permute-start.31 = (bf16[1,216,128]{2,1,0:T(8,128)(2,1)S(1)}, bf16[1,216,128]{2,1,0:T(8,128)(2,1)S(1)}, u32[]{:S(2)}, u32[]{:S(2)}) collective-permute-start(bf16[1,216,128]{2,1,0:T(8,128)(2,1)S(1)} %get-tuple-element.216), channel_id=1, source_target_pairs={{0,6},{1,7},{2,4},{3,5},{4,2},{5,3},{6,0},{7,1},{8,14},{9,15},{10,... | collective-permute-start | bytes 165896 | tf_op jit(solution)/shard_map/ppermute | solution.py:47
  193.1 5.8 %collective-permute-start.30 = (bf16[1,216,128]{2,1,0:T(8,128)(2,1)S(1)}, bf16[1,216,128]{2,1,0:T(8,128)(2,1)S(1)}, u32[]{:S(2)}, u32[]{:S(2)}) collective-permute-start(bf16[1,216,128]{2,1,0:T(8,128)(2,1)S(1)} %get-tuple-element.217), channel_id=1, source_target_pairs={{0,4},{1,5},{2,6},{3,7},{4,0},{5,1},{6,2},{7,3},{8,12},{9,13},{10,... | collective-permute-start | bytes 165896 | tf_op jit(solution)/shard_map/ppermute | solution.py:47
  193.1 5.1 %collective-permute-start.33 = (f32[2,576]{1,0:T(2,128)S(1)}, f32[2,576]{1,0:T(2,128)S(1)}, u32[]{:S(2)}, u32[]{:S(2)}) collective-permute-start(f32[2,576]{1,0:T(2,128)S(1)} %add.290), channel_id=1, source_target_pairs={{0,4},{1,5},{2,6},{3,7},{4,0},{5,1},{6,2},{7,3},{8,12},{9,13},{10,... | collective-permute-start | bytes 13832 | tf_op jit(solution)/shard_map/ppermute | solution.py:47
Sparse Core Ops, SparseCore 0:
  11.4 74.0 all-gather.1

commit v6 on v5

--- a/solution.py
+++ b/solution.py
@@ -57,11 +57,6 @@
             total = total + new[rows].astype(F32)
         results.append(total.astype(BF16) if index else total)
     return results
-
-
-def both_bits(total, axis, one, two):
-    total = total + exchange(total, axis, one)
-    return total + exchange(total, axis, two)
 
 
 def together(*values):
@@ -787,13 +782,18 @@
         )
         kept, *sent = add_up(kept, [new], len(line))
         gains_total = gains_total + gains_new
+
+        news = [exchange(part, "seq", place) for place, part in zip(line[1:], sent)]
+        gains_new = exchange(gains_total, "seq", 2)
+        gains_new, one_new, two_new, window_new = together(
+            gains_new, one_new, two_new, window_new
+        )
+        gains_total = gains_total + gains_new
+        gains_total = gains_total + exchange(gains_total, "seq", 4)
         feedforward_owned = jnp.concatenate(
             [add_up(one_kept, [one_new], 1)[0][0], add_up(two_kept, [two_new], 1)[0][0]], 0
         ).reshape(-1)
         d_own = add_up(window_kept, [window_new], 1)[0][0].astype(BF16)
-
-        news = [exchange(part, "seq", place) for place, part in zip(line[1:], sent)]
-        gains_total = both_bits(gains_total, "seq", 2, 4)
         attention_owned = add_up(kept, news, 1)[0].reshape(-1)
     else:
         halves = [jnp.concatenate(parts[index : index + 2], 0) for index in (0, 2)]

time: 207 us -> 208 us (level)
  other arithmetic: 23.4 us -> 26.8 us
  waiting for transfers between devices: 63.8 us -> 61.6 us
    add x8 -> x9, other arithmetic: 4.66 us -> 7.7 us  [add_up(): total = total + new[rows].astype(F32)]
    ppermute x34, waiting for transfers between devices: 56.3 us -> 54.1 us  [exchange(): return lax.ppermute(value, axis, pairs)]
  transfers between devices with their start and end apart: 35 -> 35, of which waited for: 15 -> 14; matrix products, arithmetic and copies ran while one was open for 9% -> 11% of each run, Pallas kernels for 20% -> 20%
where the time goes in v6:
time: 208 us; the launch traced here: 207 us
  waiting for transfers between devices  61.6 us (30%)
  Pallas kernels  56.6 us (27%)
  starting transfers between devices  43.7 us (21%)
  other arithmetic  26.8 us (13%)
  between operations  14.5 us (7%)
  local copies, waits for them, and re-layouts  2.82 us (1%)
    ppermute x34, waiting for transfers between devices, exchange(): return lax.ppermute(value, axis, pairs)  54.1 us
    ppermute x34, starting transfers between devices, exchange(): return lax.ppermute(value, axis, pairs)  43.7 us
    pallas_call x2, Pallas kernels, attention_backward(): pl.pallas_call(kernel, out_shape=outputs, in_specs=in_specs, out_specs=tu...  25.3 us
    pallas_call x1, Pallas kernels, attention_forward(): pl.pallas_call(functools.partial(attention_forward_kernel, len(weight_pie...  16 us
    pallas_call x1, Pallas kernels, feedforward(): pl.pallas_call(feedforward_kernel, out_shape=(shape((MICRO, D, DEVICE_TOK...  15.4 us
    add x9, other arithmetic, add_up(): total = total + new[rows].astype(F32)  7.7 us
    all_gather x1, waiting for transfers between devices, on_device(): lax.all_gather(feedforward_low, both, axis=0, tiled=True)  7.56 us
  transfers between devices with their start and end apart: 35, of which 14 were waited for; matrix products, arithmetic and copies ran while one was open for 11% of the time, Pallas kernels for 20%

profile of v6, /device:TPU:0, one launch (start us, length us, event | category | flops | bytes accessed | tf_op | source)
XLA Modules:
  0.0 207.4 jit_solution(14106596493284980919)
XLA Ops:
  7.2 1.7 convert_bitcast_fusion
  8.9 0.9 convert_bitcast_fusion.1
  9.9 3.0 %collective-permute-start = (bf16[1,216,128]{2,1,0:T(8,128)(2,1)S(1)}, bf16[1,216,128]{2,1,0:T(8,128)(2,1)S(1)}, u32[]{:S(2)}, u32[]{:S(2)}) collective-permute-start(bf16[1,216,128]{2,1,0:T(8,128)(2,1)S(1)} %convert_bitcast_fusion.1), channel_id=1, source_target_pairs={{0,2},{1,3},{2,0},{3,1},{4,6},{5,7},{6,4},{7,5},{8,10},{9,11},{10,... | collective-permute-start | bytes 165896 | tf_op jit(solution)/shard_map/ppermute | solution.py:47
  12.9 4.5 %collective-permute-start.2 = (bf16[1,2,576,128]{3,2,1,0:T(8,128)(2,1)}, bf16[1,2,576,128]{3,2,1,0:T(8,128)(2,1)S(1)}, u32[]{:S(2)}, u32[]{:S(2)}) collective-permute-start(bf16[1,2,576,128]{3,2,1,0:T(8,128)(2,1)} %bitcast.63), channel_id=1, source_target_pairs={{0,4},{1,5},{2,6},{3,7},{8,12},{9,13},{10,14},{11,15},{16,20},{17,... | collective-permute-start | bytes 884744 | tf_op jit(solution)/shard_map/ppermute | solution.py:47
  17.4 1.0 reduce_window_sum.12
  18.4 0.7 sub.30
  19.3 0.7 xor_multiply_fusion
  20.4 1.2 and_select_fusion.refs_10_.refs_11_.refs_16_
  21.6 1.0 multiply_sine_fusion
  22.7 9.5 %collective-permute-done.1 = bf16[2,216,128]{2,1,0:T(8,128)(2,1)S(1)} collective-permute-done((bf16[2,216,128]{2,1,0:T(8,128)(2,1)S(1)}, bf16[2,216,128]{2,1,0:T(8,128)(2,1)S(1)}, u32[]{:S(2)}, u32[]{:S(2)}) %collective-permute-start.1) | collective-permute-done | bytes 110624 | tf_op jit(solution)/shard_map/ppermute | solution.py:47
  32.4 6.4 %collective-permute-start.7 = (bf16[2,2,576,128]{3,2,1,0:T(8,128)(2,1)S(1)}, bf16[2,2,576,128]{3,2,1,0:T(8,128)(2,1)}, u32[]{:S(2)}, u32[]{:S(2)}) collective-permute-start(bf16[2,2,576,128]{3,2,1,0:T(8,128)(2,1)S(1)} %pad_maximum_fusion.refs_4_), channel_id=1, source_target_pairs={{0,2},{1,3},{2,0},{3,1},{4,6},{5,7},{6,4},{7,5},{8,10},{9,11},{10,... | collective-permute-start | bytes 1769480 | tf_op jit(solution)/shard_map/ppermute | solution.py:47
  38.8 1.5 collective-permute-start.3
  40.3 5.4 %collective-permute-done.3 = bf16[4,216,128]{2,1,0:T(8,128)(2,1)S(1)} collective-permute-done((bf16[4,216,128]{2,1,0:T(8,128)(2,1)S(1)}, bf16[4,216,128]{2,1,0:T(8,128)(2,1)S(1)}, u32[]{:S(2)}, u32[]{:S(2)}) %collective-permute-start.3) | collective-permute-done | bytes 221216 | tf_op jit(solution)/shard_map/ppermute | solution.py:47
  45.7 1.2 collective-permute-start.4
  46.9 10.8 %collective-permute-done.7.refs_5_ = bf16[2,2,576,128]{3,2,1,0:T(8,128)(2,1)} collective-permute-done((bf16[2,2,576,128]{3,2,1,0:T(8,128)(2,1)S(1)}, bf16[2,2,576,128]{3,2,1,0:T(8,128)(2,1)}, u32[]{:S(2)}, u32[]{:S(2)}) %collective-permute-start.7) | collective-permute-done | bytes 589856 | tf_op jit(solution)/shard_map/ppermute | solution.py:47
  59.2 1.3 collective-permute-done.5.refs_2_
  60.5 0.6 collective-permute-done.6.refs_3_
  61.9 16.0 %shard_map.239 = (bf16[576,960]{1,0:T(8,128)(2,1)}, bf16[576,576]{1,0:T(8,128)(2,1)}, bf16[2,576,1024]{2,1,0:T(8,128)(2,1)}, bf16[2,576,128]{2,1,0:T(8,128)(2,1)...) custom-call(s32[32]{0:T(128)S(1)} %broadcast_xor_fusion.order, ...), custom_call_target="tpu_custom_call" | custom-call | tf_op jit(solution)/shard_map/pallas_call | solution.py:256
  77.9 7.6 %all-gather.2.cloned.1.call-done = bf16[20736,128]{1,0:T(8,128)(2,1)} async-done(((bf16[648,128]{1,0:T(8,128)(2,1)}), bf16[20736,128]{1,0:T(8,128)(2,1)}) %all-gather.2.cloned.1.call-update) | async-done | bytes 5308432 | tf_op jit(solution)/shard_map/all_gather | solution.py:637
  85.5 15.4 %shard_map.240 = (bf16[2,576,128]{2,1,0:T(8,128)(2,1)}, bf16[256,576]{1,0:T(8,128)(2,1)S(1)}, f32[2,576,128]{2,1,0:T(8,128)S(1)}, bf16[16,320,128]{2,1,0:T(8,128...) custom-call(s32[32]{0:T(128)S(1)} %iota.26.straight, ...), custom_call_target="tpu_custom_call" | custom-call | tf_op jit(solution)/shard_map/pallas_call | solution.py:378
  101.4 10.5 %shard_map.241 = (bf16[576,128]{1,0:T(8,128)(2,1)S(1)}, bf16[8,384,128]{2,1,0:T(8,128)(2,1)}, f32[576,576]{1,0:T(8,128)}, f32[576,384]{1,0:T(8,128)}, f32[576,576]{1,0:T(8,128)}) custom-call(bf16[576,576]{1,0:T(8,128)(2,1)} %get-tuple-element.99.refs_0_.refs_5_, bf16[2,576,1024]{2,1,0:T(8,128)(2,1)} %get-tuple-element.100.refs_1_.refs_6_, ...), custom_call_target="tpu_custom_call" | custom-call | tf_op jit(solution)/shard_map/pallas_call | solution.py:563
  112.3 1.0 copy-done.4
  113.6 1.5 collective-permute-start.13
  115.7 14.7 %shard_map.242 = (bf16[16,216,128]{2,1,0:T(8,128)(2,1)}, bf16[16,216,128]{2,1,0:T(8,128)(2,1)}, bf16[2,576,128]{2,1,0:T(8,128)(2,1)S(1)}, bf16[4,2,384,128]{3,2,...) custom-call(s32[32]{0:T(128)S(1)} %broadcast_xor_fusion.order, ...), custom_call_target="tpu_custom_call" | custom-call | tf_op jit(solution)/shard_map/pallas_call | solution.py:563
  130.4 1.3 collective-permute-done.12
  132.4 0.6 collective-permute-start.16
  133.0 1.0 slice_add_fusion.2
  134.1 1.4 collective-permute-start.15
  136.0 1.2 collective-permute-done.18
  137.1 6.6 %collective-permute-done.15 = bf16[4,320,128]{2,1,0:T(8,128)(2,1)} collective-permute-done((bf16[4,320,128]{2,1,0:T(8,128)(2,1)}, bf16[4,320,128]{2,1,0:T(8,128)(2,1)}, u32[]{:S(2)}, u32[]{:S(2)}) %collective-permute-start.15) | collective-permute-done | bytes 327712 | tf_op jit(solution)/shard_map/ppermute | solution.py:47
  143.8 1.2 slice_add_fusion.10
  145.0 2.0 collective-permute-start.20
  147.0 1.5 convert_add_fusion.3
  148.8 1.3 convert_add_fusion.2
  150.1 1.5 collective-permute-start.19
  151.6 1.1 slice_add_fusion.8
  152.7 1.9 collective-permute-start.21
  154.6 0.7 collective-permute-start.23
  155.4 5.5 %collective-permute-done.23 = f32[2,576]{1,0:T(2,128)S(1)} collective-permute-done((f32[2,576]{1,0:T(2,128)S(1)}, f32[2,576]{1,0:T(2,128)S(1)}, u32[]{:S(2)}, u32[]{:S(2)}) %collective-permute-start.23) | collective-permute-done | bytes 4640 | tf_op jit(solution)/shard_map/ppermute | solution.py:47
  160.8 1.6 collective-permute-done.21
  162.4 0.7 add.253
  163.1 1.4 collective-permute-start.28
  164.5 0.7 fusion.28
  165.2 1.9 collective-permute-start.25
  167.1 1.1 collective-permute-start.26
  168.2 0.7 fusion.16
  168.9 1.9 collective-permute-start.27
  170.8 0.8 slice_add_fusion.4
  171.6 0.6 collective-permute-start.24
  172.3 5.8 %collective-permute-done.25 = bf16[1,320,128]{2,1,0:T(8,128)(2,1)} collective-permute-done((bf16[1,320,128]{2,1,0:T(8,128)(2,1)}, bf16[1,320,128]{2,1,0:T(8,128)(2,1)}, u32[]{:S(2)}, u32[]{:S(2)}) %collective-permute-start.25) | collective-permute-done | bytes 81952 | tf_op jit(solution)/shard_map/ppermute | solution.py:47
  178.0 1.8 collective-permute-done.26
  179.8 2.7 %collective-permute-done.27 = bf16[1,2,384,128]{3,2,1,0:T(8,128)(2,1)} collective-permute-done((bf16[1,2,384,128]{3,2,1,0:T(8,128)(2,1)}, bf16[1,2,384,128]{3,2,1,0:T(8,128)(2,1)}, u32[]{:S(2)}, u32[]{:S(2)}) %collective-permute-start.27) | collective-permute-done | bytes 196640 | tf_op jit(solution)/shard_map/ppermute | solution.py:47
  182.5 0.7 add.261
  183.2 0.9 fusion.32
  184.1 2.1 %collective-permute-start.30 = (bf16[1,216,128]{2,1,0:T(8,128)(2,1)S(1)}, bf16[1,216,128]{2,1,0:T(8,128)(2,1)S(1)}, u32[]{:S(2)}, u32[]{:S(2)}) collective-permute-start(bf16[1,216,128]{2,1,0:T(8,128)(2,1)S(1)} %get-tuple-element.223), channel_id=1, source_target_pairs={{0,2},{1,3},{2,0},{3,1},{4,6},{5,7},{6,4},{7,5},{8,10},{9,11},{10,... | collective-permute-start | bytes 165896 | tf_op jit(solution)/shard_map/ppermute | solution.py:47
  186.2 2.7 %collective-permute-start.32 = (bf16[1,216,128]{2,1,0:T(8,128)(2,1)S(1)}, bf16[1,216,128]{2,1,0:T(8,128)(2,1)S(1)}, u32[]{:S(2)}, u32[]{:S(2)}) collective-permute-start(bf16[1,216,128]{2,1,0:T(8,128)(2,1)S(1)} %get-tuple-element.224), channel_id=1, source_target_pairs={{0,6},{1,7},{2,4},{3,5},{4,2},{5,3},{6,0},{7,1},{8,14},{9,15},{10,... | collective-permute-start | bytes 165896 | tf_op jit(solution)/shard_map/ppermute | solution.py:47
  188.9 1.0 fusion.24
  189.9 1.0 fusion.27
  190.8 1.0 fusion.22
  191.9 1.3 fusion.6
  193.2 3.0 %collective-permute-start.33 = (f32[2,576]{1,0:T(2,128)S(1)}, f32[2,576]{1,0:T(2,128)S(1)}, u32[]{:S(2)}, u32[]{:S(2)}) collective-permute-start(f32[2,576]{1,0:T(2,128)S(1)} %add.290), channel_id=1, source_target_pairs={{0,4},{1,5},{2,6},{3,7},{4,0},{5,1},{6,2},{7,3},{8,12},{9,13},{10,... | collective-permute-start | bytes 13832 | tf_op jit(solution)/shard_map/ppermute | solution.py:47
  196.2 1.1 multiply_subtract_fusion
  197.3 0.9 fusion.10
  199.0 1.6 multiply_subtract_fusion.1
  (123 shorter events, 7.0 us)
Async XLA Ops:
  7.2 78.3 %all-gather.2.cloned.1.call-start = ((), (), s32[]{:S(2)}) async-start(), calls=%async_computation | async-start | bytes 5474304 | tf_op jit(solution)/shard_map/all_gather | solution.py:637
  8.9 23.4 %copy-start.2 = (bf16[2,1,128,576]{2,3,1,0:T(8,128)(2,1)S(1)}, bf16[2,1,128,576]{2,3,1,0:T(8,128)(2,1)}, u32[]{:S(2)}) copy-start(bf16[2,1,128,576]{2,3,1,0:T(8,128)(2,1)} %param.16) | copy-start | bytes 884740
  9.9 12.7 %collective-permute-start = (bf16[1,216,128]{2,1,0:T(8,128)(2,1)S(1)}, bf16[1,216,128]{2,1,0:T(8,128)(2,1)S(1)}, u32[]{:S(2)}, u32[]{:S(2)}) collective-permute-start(bf16[1,216,128]{2,1,0:T(8,128)(2,1)S(1)} %convert_bitcast_fusion.1), channel_id=1, source_target_pairs={{0,2},{1,3},{2,0},{3,1},{4,6},{5,7},{6,4},{7,5},{8,10},{9,11},{10,... | collective-permute-start | bytes 165896 | tf_op jit(solution)/shard_map/ppermute | solution.py:47
  12.9 19.4 %collective-permute-start.2 = (bf16[1,2,576,128]{3,2,1,0:T(8,128)(2,1)}, bf16[1,2,576,128]{3,2,1,0:T(8,128)(2,1)S(1)}, u32[]{:S(2)}, u32[]{:S(2)}) collective-permute-start(bf16[1,2,576,128]{3,2,1,0:T(8,128)(2,1)} %bitcast.63), channel_id=1, source_target_pairs={{0,4},{1,5},{2,6},{3,7},{8,12},{9,13},{10,14},{11,15},{16,20},{17,... | collective-permute-start | bytes 884744 | tf_op jit(solution)/shard_map/ppermute | solution.py:47
  22.6 35.2 %copy-start.20 = (f32[2,576]{1,0:T(2,128)S(1)}, f32[2,576]{1,0:T(2,128)}, u32[]{:S(2)}) copy-start(f32[2,576]{1,0:T(2,128)} %param.21) | copy-start | bytes 13828
  22.6 36.6 %copy-start.26 = (s32[32]{0:T(128)S(1)}, s32[32]{0:T(128)}, u32[]{:S(2)}) copy-start(s32[32]{0:T(128)} %constant.30.clone) | copy-start | bytes 388
  22.6 36.6 %copy-start.24 = (s32[32]{0:T(128)S(1)}, s32[32]{0:T(128)}, u32[]{:S(2)}) copy-start(s32[32]{0:T(128)} %constant.100.clone) | copy-start | bytes 388
  22.6 36.6 %copy-start.25 = (s32[32]{0:T(128)S(1)}, s32[32]{0:T(128)}, u32[]{:S(2)}) copy-start(s32[32]{0:T(128)} %constant.31.clone) | copy-start | bytes 388
  22.7 9.6 %collective-permute-start.1 = (bf16[2,216,128]{2,1,0:T(8,128)(2,1)S(1)}, bf16[2,216,128]{2,1,0:T(8,128)(2,1)S(1)}, u32[]{:S(2)}, u32[]{:S(2)}) collective-permute-start(bf16[2,216,128]{2,1,0:T(8,128)(2,1)S(1)} %pad_maximum_fusion.2), channel_id=1, source_target_pairs={{0,4},{1,5},{2,6},{3,7},{4,0},{5,1},{6,2},{7,3},{8,12},{9,13},{10,... | collective-permute-start | bytes 331784 | tf_op jit(solution)/shard_map/ppermute | solution.py:47
  32.4 28.8 %copy-start.3 = (bf16[2,2,576,128]{3,2,1,0:T(8,128)(2,1)}, bf16[2,2,576,128]{3,2,1,0:T(8,128)(2,1)S(1)}, u32[]{:S(2)}) copy-start(bf16[2,2,576,128]{3,2,1,0:T(8,128)(2,1)S(1)} %pad_maximum_fusion.refs_4_) | copy-start | bytes 1769476
  32.4 25.4 %collective-permute-start.7 = (bf16[2,2,576,128]{3,2,1,0:T(8,128)(2,1)S(1)}, bf16[2,2,576,128]{3,2,1,0:T(8,128)(2,1)}, u32[]{:S(2)}, u32[]{:S(2)}) collective-permute-start(bf16[2,2,576,128]{3,2,1,0:T(8,128)(2,1)S(1)} %pad_maximum_fusion.refs_4_), channel_id=1, source_target_pairs={{0,2},{1,3},{2,0},{3,1},{4,6},{5,7},{6,4},{7,5},{8,10},{9,11},{10,... | collective-permute-start | bytes 1769480 | tf_op jit(solution)/shard_map/ppermute | solution.py:47
  38.8 6.9 %collective-permute-start.3 = (bf16[4,216,128]{2,1,0:T(8,128)(2,1)S(1)}, bf16[4,216,128]{2,1,0:T(8,128)(2,1)S(1)}, u32[]{:S(2)}, u32[]{:S(2)}) collective-permute-start(bf16[4,216,128]{2,1,0:T(8,128)(2,1)S(1)} %pad_maximum_fusion.1), channel_id=1, source_target_pairs={{0,8},{8,0},{16,24},{24,16},{1,9},{9,1},{17,25},{25,17},{2,10},{10... | collective-permute-start | bytes 663560 | tf_op jit(solution)/shard_map/ppermute | solution.py:47
  45.7 13.4 %collective-permute-start.4 = (bf16[8,216,128]{2,1,0:T(8,128)(2,1)S(1)}, bf16[8,216,128]{2,1,0:T(8,128)(2,1)S(1)}, u32[]{:S(2)}, u32[]{:S(2)}) collective-permute-start(bf16[8,216,128]{2,1,0:T(8,128)(2,1)S(1)} %constant_dynamic-update-slice_fusion.refs_0_), channel_id=1, source_target_pairs={{0,16},{8,24},{16,0},{24,8},{1,17},{9,25},{17,1},{25,9},{2,18},{10... | collective-permute-start | bytes 1327112 | tf_op jit(solution)/shard_map/ppermute | solution.py:47
  46.9 12.3 %collective-permute-start.8 = (bf16[2,2,576,128]{3,2,1,0:T(8,128)(2,1)S(1)}, bf16[2,2,576,128]{3,2,1,0:T(8,128)(2,1)}, u32[]{:S(2)}, u32[]{:S(2)}) collective-permute-start(bf16[2,2,576,128]{3,2,1,0:T(8,128)(2,1)S(1)} %pad_maximum_fusion.refs_4_), channel_id=1, source_target_pairs={{0,1},{1,0},{2,3},{3,2},{4,5},{5,4},{6,7},{7,6},{8,9},{9,8},{10,11... | collective-permute-start | bytes 1769480 | tf_op jit(solution)/shard_map/ppermute | solution.py:47
  57.8 3.4 %collective-permute-start.9 = (bf16[2,2,576,128]{3,2,1,0:T(8,128)(2,1)}, bf16[2,2,576,128]{3,2,1,0:T(8,128)(2,1)}, u32[]{:S(2)}, u32[]{:S(2)}) collective-permute-start(bf16[2,2,576,128]{3,2,1,0:T(8,128)(2,1)} %collective-permute-done.7.refs_5_), channel_id=1, source_target_pairs={{0,1},{1,0},{2,3},{3,2},{4,5},{5,4},{6,7},{7,6},{8,9},{9,8},{10,11... | collective-permute-start | bytes 1769480 | tf_op jit(solution)/shard_map/ppermute | solution.py:47
  58.5 2.0 collective-permute-start.5
  59.1 2.0 collective-permute-start.6
  59.2 26.3 %copy-start.1 = (bf16[2,1,128,576]{2,3,1,0:T(8,128)(2,1)S(1)}, bf16[2,1,128,576]{2,3,1,0:T(8,128)(2,1)}, u32[]{:S(2)}) copy-start(bf16[2,1,128,576]{2,3,1,0:T(8,128)(2,1)} %param.17) | copy-start | bytes 884740
  60.5 0.8 copy-start.9
  61.2 0.8 copy-start.10
  85.5 15.9 %copy-start = (f32[2,576,128]{2,1,0:T(8,128)S(1)}, f32[2,576,128]{2,1,0:T(8,128)}, u32[]{:S(2)}) copy-start(f32[2,576,128]{2,1,0:T(8,128)} %get-tuple-element.106.refs_7_.refs_12_) | copy-start | bytes 1769476
  100.9 11.1 %collective-permute-start.11 = (bf16[16,328,128]{2,1,0:T(8,128)(2,1)}, bf16[16,328,128]{2,1,0:T(8,128)(2,1)S(1)}, u32[]{:S(2)}, u32[]{:S(2)}) collective-permute-start(bf16[16,328,128]{2,1,0:T(8,128)(2,1)} %get-tuple-element.98), channel_id=1, source_target_pairs={{0,1},{1,0},{2,3},{3,2},{4,5},{5,4},{6,7},{7,6},{8,9},{9,8},{10,11... | collective-permute-start | bytes 4030472 | tf_op jit(solution)/shard_map/ppermute | solution.py:47
  101.1 10.8 %collective-permute-start.10 = (bf16[16,320,128]{2,1,0:T(8,128)(2,1)}, bf16[16,320,128]{2,1,0:T(8,128)(2,1)S(1)}, u32[]{:S(2)}, u32[]{:S(2)}) collective-permute-start(bf16[16,320,128]{2,1,0:T(8,128)(2,1)} %get-tuple-element.97), channel_id=1, source_target_pairs={{0,1},{1,0},{2,3},{3,2},{4,5},{5,4},{6,7},{7,6},{8,9},{9,8},{10,11... | collective-permute-start | bytes 3932168 | tf_op jit(solution)/shard_map/ppermute | solution.py:47
  101.4 10.6 %copy-start.6 = (bf16[16,320,128]{2,1,0:T(8,128)(2,1)S(1)}, bf16[16,320,128]{2,1,0:T(8,128)(2,1)}, u32[]{:S(2)}) copy-start(bf16[16,320,128]{2,1,0:T(8,128)(2,1)} %get-tuple-element.96) | copy-start | bytes 3932164
  112.0 1.3 copy-start.4
  113.6 18.2 %collective-permute-start.13 = (bf16[8,328,128]{2,1,0:T(8,128)(2,1)S(1)}, bf16[8,328,128]{2,1,0:T(8,128)(2,1)S(1)}, u32[]{:S(2)}, u32[]{:S(2)}) collective-permute-start(bf16[8,328,128]{2,1,0:T(8,128)(2,1)S(1)} %get-tuple-element.122), channel_id=1, source_target_pairs={{0,16},{8,24},{16,0},{24,8},{1,17},{9,25},{17,1},{25,9},{2,18},{10... | collective-permute-start | bytes 2015240 | tf_op jit(solution)/shard_map/ppermute | solution.py:47
  115.1 16.6 %collective-permute-start.12 = (bf16[8,320,128]{2,1,0:T(8,128)(2,1)S(1)}, bf16[8,320,128]{2,1,0:T(8,128)(2,1)S(1)}, u32[]{:S(2)}, u32[]{:S(2)}) collective-permute-start(bf16[8,320,128]{2,1,0:T(8,128)(2,1)S(1)} %get-tuple-element.121), channel_id=1, source_target_pairs={{0,8},{8,0},{16,24},{24,16},{1,9},{9,1},{17,25},{25,17},{2,10},{10... | collective-permute-start | bytes 1966088 | tf_op jit(solution)/shard_map/ppermute | solution.py:47
  131.8 12.0 %collective-permute-start.14 = (bf16[16,216,128]{2,1,0:T(8,128)(2,1)}, bf16[16,216,128]{2,1,0:T(8,128)(2,1)}, u32[]{:S(2)}, u32[]{:S(2)}) collective-permute-start(bf16[16,216,128]{2,1,0:T(8,128)(2,1)} %get-tuple-element.137), channel_id=1, source_target_pairs={{0,1},{1,0},{2,3},{3,2},{4,5},{5,4},{6,7},{7,6},{8,9},{9,8},{10,11... | collective-permute-start | bytes 2654216 | tf_op jit(solution)/shard_map/ppermute | solution.py:47
  131.8 12.0 %collective-permute-start.17 = (bf16[4,2,384,128]{3,2,1,0:T(8,128)(2,1)}, bf16[4,2,384,128]{3,2,1,0:T(8,128)(2,1)}, u32[]{:S(2)}, u32[]{:S(2)}) collective-permute-start(bf16[4,2,384,128]{3,2,1,0:T(8,128)(2,1)} %get-tuple-element.140), channel_id=1, source_target_pairs={{0,1},{1,0},{2,3},{3,2},{4,5},{5,4},{6,7},{7,6},{8,9},{9,8},{10,11... | collective-permute-start | bytes 2359304 | tf_op jit(solution)/shard_map/ppermute | solution.py:47
  132.4 11.4 %collective-permute-start.16 = (bf16[4,328,128]{2,1,0:T(8,128)(2,1)S(1)}, bf16[4,328,128]{2,1,0:T(8,128)(2,1)}, u32[]{:S(2)}, u32[]{:S(2)}) collective-permute-start(bf16[4,328,128]{2,1,0:T(8,128)(2,1)S(1)} %get-tuple-element.210), channel_id=1, source_target_pairs={{0,8},{8,0},{16,24},{24,16},{1,9},{9,1},{17,25},{25,17},{2,10},{10... | collective-permute-start | bytes 1007624 | tf_op jit(solution)/shard_map/ppermute | solution.py:47
  134.1 9.7 %collective-permute-start.15 = (bf16[4,320,128]{2,1,0:T(8,128)(2,1)}, bf16[4,320,128]{2,1,0:T(8,128)(2,1)}, u32[]{:S(2)}, u32[]{:S(2)}) collective-permute-start(bf16[4,320,128]{2,1,0:T(8,128)(2,1)} %get-tuple-element.212), channel_id=1, source_target_pairs={{0,16},{8,24},{16,0},{24,8},{1,17},{9,25},{17,1},{25,9},{2,18},{10... | collective-permute-start | bytes 983048 | tf_op jit(solution)/shard_map/ppermute | solution.py:47
  135.9 1.2 collective-permute-start.18
  145.0 3.8 %copy-start.8 = (bf16[16,216,128]{2,1,0:T(8,128)(2,1)S(1)}, bf16[16,216,128]{2,1,0:T(8,128)(2,1)}, u32[]{:S(2)}) copy-start(bf16[16,216,128]{2,1,0:T(8,128)(2,1)} %get-tuple-element.144) | copy-start | bytes 2654212
  145.0 15.8 %collective-permute-start.20 = (bf16[2,320,128]{2,1,0:T(8,128)(2,1)S(1)}, bf16[2,320,128]{2,1,0:T(8,128)(2,1)S(1)}, u32[]{:S(2)}, u32[]{:S(2)}) collective-permute-start(bf16[2,320,128]{2,1,0:T(8,128)(2,1)S(1)} %get-tuple-element.222), channel_id=1, source_target_pairs={{0,2},{1,3},{2,0},{3,1},{4,6},{5,7},{6,4},{7,5},{8,10},{9,11},{10,... | collective-permute-start | bytes 491528 | tf_op jit(solution)/shard_map/ppermute | solution.py:47
  148.5 13.9 %collective-permute-start.22 = (bf16[2,2,384,128]{3,2,1,0:T(8,128)(2,1)S(1)}, bf16[2,2,384,128]{3,2,1,0:T(8,128)(2,1)S(1)}, u32[]{:S(2)}, u32[]{:S(2)}) collective-permute-start(bf16[2,2,384,128]{3,2,1,0:T(8,128)(2,1)S(1)} %get-tuple-element.216), channel_id=1, source_target_pairs={{0,2},{1,3},{2,0},{3,1},{4,6},{5,7},{6,4},{7,5},{8,10},{9,11},{10,... | collective-permute-start | bytes 1179656 | tf_op jit(solution)/shard_map/ppermute | solution.py:47
  150.1 12.3 %collective-permute-start.19 = (bf16[8,216,128]{2,1,0:T(8,128)(2,1)S(1)}, bf16[8,216,128]{2,1,0:T(8,128)(2,1)S(1)}, u32[]{:S(2)}, u32[]{:S(2)}) collective-permute-start(bf16[8,216,128]{2,1,0:T(8,128)(2,1)S(1)} %get-tuple-element.214), channel_id=1, source_target_pairs={{0,16},{8,24},{16,0},{24,8},{1,17},{9,25},{17,1},{25,9},{2,18},{10... | collective-permute-start | bytes 1327112 | tf_op jit(solution)/shard_map/ppermute | solution.py:47
  152.7 9.7 %collective-permute-start.21 = (bf16[2,328,128]{2,1,0:T(8,128)(2,1)S(1)}, bf16[2,328,128]{2,1,0:T(8,128)(2,1)S(1)}, u32[]{:S(2)}, u32[]{:S(2)}) collective-permute-start(bf16[2,328,128]{2,1,0:T(8,128)(2,1)S(1)} %get-tuple-element.220), channel_id=1, source_target_pairs={{0,2},{1,3},{2,0},{3,1},{4,6},{5,7},{6,4},{7,5},{8,10},{9,11},{10,... | collective-permute-start | bytes 503816 | tf_op jit(solution)/shard_map/ppermute | solution.py:47
  154.6 6.2 %collective-permute-start.23 = (f32[2,576]{1,0:T(2,128)S(1)}, f32[2,576]{1,0:T(2,128)S(1)}, u32[]{:S(2)}, u32[]{:S(2)}) collective-permute-start(f32[2,576]{1,0:T(2,128)S(1)} %fusion.44), channel_id=1, source_target_pairs={{0,16},{8,24},{16,0},{24,8},{1,17},{9,25},{17,1},{25,9},{2,18},{10... | collective-permute-start | bytes 13832 | tf_op jit(solution)/shard_map/ppermute | solution.py:47
  160.8 10.8 %copy-start.17 = (bf16[2,320,128]{2,1,0:T(8,128)(2,1)}, bf16[2,320,128]{2,1,0:T(8,128)(2,1)S(1)}, u32[]{:S(2)}) copy-start(bf16[2,320,128]{2,1,0:T(8,128)(2,1)S(1)} %collective-permute-done.20) | copy-start | bytes 491524
  162.4 9.2 %copy-start.16 = (bf16[2,328,128]{2,1,0:T(8,128)(2,1)}, bf16[2,328,128]{2,1,0:T(8,128)(2,1)S(1)}, u32[]{:S(2)}) copy-start(bf16[2,328,128]{2,1,0:T(8,128)(2,1)S(1)} %collective-permute-done.21) | copy-start | bytes 503812
  162.4 9.2 %copy-start.12 = (bf16[2,2,384,128]{3,2,1,0:T(8,128)(2,1)}, bf16[2,2,384,128]{3,2,1,0:T(8,128)(2,1)S(1)}, u32[]{:S(2)}) copy-start(bf16[2,2,384,128]{3,2,1,0:T(8,128)(2,1)S(1)} %collective-permute-done.22) | copy-start | bytes 1179652
  163.1 9.2 %collective-permute-start.28 = (f32[2,576]{1,0:T(2,128)}, f32[2,576]{1,0:T(2,128)}, u32[]{:S(2)}, u32[]{:S(2)}) collective-permute-start(f32[2,576]{1,0:T(2,128)} %add.253), channel_id=1, source_target_pairs={{0,8},{8,0},{16,24},{24,16},{1,9},{9,1},{17,25},{25,17},{2,10},{10... | collective-permute-start | bytes 13832 | tf_op jit(solution)/shard_map/ppermute | solution.py:47
  165.2 12.9 %collective-permute-start.25 = (bf16[1,320,128]{2,1,0:T(8,128)(2,1)}, bf16[1,320,128]{2,1,0:T(8,128)(2,1)}, u32[]{:S(2)}, u32[]{:S(2)}) collective-permute-start(bf16[1,320,128]{2,1,0:T(8,128)(2,1)} %fusion.28), channel_id=1, source_target_pairs={{0,4},{1,5},{2,6},{3,7},{4,0},{5,1},{6,2},{7,3},{8,12},{9,13},{10,... | collective-permute-start | bytes 245768 | tf_op jit(solution)/shard_map/ppermute | solution.py:47
  167.1 12.7 %collective-permute-start.26 = (bf16[1,328,128]{2,1,0:T(8,128)(2,1)S(1)}, bf16[1,328,128]{2,1,0:T(8,128)(2,1)}, u32[]{:S(2)}, u32[]{:S(2)}) collective-permute-start(bf16[1,328,128]{2,1,0:T(8,128)(2,1)S(1)} %fusion.25), channel_id=1, source_target_pairs={{0,4},{1,5},{2,6},{3,7},{4,0},{5,1},{6,2},{7,3},{8,12},{9,13},{10,... | collective-permute-start | bytes 251912 | tf_op jit(solution)/shard_map/ppermute | solution.py:47
  168.9 13.6 %collective-permute-start.27 = (bf16[1,2,384,128]{3,2,1,0:T(8,128)(2,1)}, bf16[1,2,384,128]{3,2,1,0:T(8,128)(2,1)}, u32[]{:S(2)}, u32[]{:S(2)}) collective-permute-start(bf16[1,2,384,128]{3,2,1,0:T(8,128)(2,1)} %fusion.16), channel_id=1, source_target_pairs={{0,4},{1,5},{2,6},{3,7},{4,0},{5,1},{6,2},{7,3},{8,12},{9,13},{10,... | collective-permute-start | bytes 589832 | tf_op jit(solution)/shard_map/ppermute | solution.py:47
  171.6 19.2 %copy-start.13 = (bf16[2,2,384,128]{3,2,1,0:T(8,128)(2,1)S(1)}, bf16[2,2,384,128]{3,2,1,0:T(8,128)(2,1)}, u32[]{:S(2)}) copy-start(bf16[2,2,384,128]{3,2,1,0:T(8,128)(2,1)} %copy-done.12) | copy-start | bytes 1179652
  171.6 10.9 %collective-permute-start.24 = (bf16[4,216,128]{2,1,0:T(8,128)(2,1)}, bf16[4,216,128]{2,1,0:T(8,128)(2,1)}, u32[]{:S(2)}, u32[]{:S(2)}) collective-permute-start(bf16[4,216,128]{2,1,0:T(8,128)(2,1)} %get-tuple-element.218), channel_id=1, source_target_pairs={{0,8},{8,0},{16,24},{24,16},{1,9},{9,1},{17,25},{25,17},{2,10},{10... | collective-permute-start | bytes 663560 | tf_op jit(solution)/shard_map/ppermute | solution.py:47
  172.3 19.6 %copy-start.7 = (bf16[576,960]{1,0:T(8,128)(2,1)S(1)}, bf16[576,960]{1,0:T(8,128)(2,1)}, u32[]{:S(2)}) copy-start(bf16[576,960]{1,0:T(8,128)(2,1)} %get-tuple-element.123.w_project) | copy-start | bytes 3317764
  183.2 5.7 %collective-permute-start.29 = (f32[2,576]{1,0:T(2,128)S(1)}, f32[2,576]{1,0:T(2,128)S(1)}, u32[]{:S(2)}, u32[]{:S(2)}) collective-permute-start(f32[2,576]{1,0:T(2,128)S(1)} %add.261), channel_id=1, source_target_pairs={{0,2},{1,3},{2,0},{3,1},{4,6},{5,7},{6,4},{7,5},{8,10},{9,11},{10,... | collective-permute-start | bytes 13832 | tf_op jit(solution)/shard_map/ppermute | solution.py:47
  184.1 14.8 %collective-permute-start.30 = (bf16[1,216,128]{2,1,0:T(8,128)(2,1)S(1)}, bf16[1,216,128]{2,1,0:T(8,128)(2,1)S(1)}, u32[]{:S(2)}, u32[]{:S(2)}) collective-permute-start(bf16[1,216,128]{2,1,0:T(8,128)(2,1)S(1)} %get-tuple-element.223), channel_id=1, source_target_pairs={{0,2},{1,3},{2,0},{3,1},{4,6},{5,7},{6,4},{7,5},{8,10},{9,11},{10,... | collective-permute-start | bytes 165896 | tf_op jit(solution)/shard_map/ppermute | solution.py:47
  186.2 12.7 %collective-permute-start.32 = (bf16[1,216,128]{2,1,0:T(8,128)(2,1)S(1)}, bf16[1,216,128]{2,1,0:T(8,128)(2,1)S(1)}, u32[]{:S(2)}, u32[]{:S(2)}) collective-permute-start(bf16[1,216,128]{2,1,0:T(8,128)(2,1)S(1)} %get-tuple-element.224), channel_id=1, source_target_pairs={{0,6},{1,7},{2,4},{3,5},{4,2},{5,3},{6,0},{7,1},{8,14},{9,15},{10,... | collective-permute-start | bytes 165896 | tf_op jit(solution)/shard_map/ppermute | solution.py:47
  188.9 10.0 %collective-permute-start.31 = (bf16[1,216,128]{2,1,0:T(8,128)(2,1)S(1)}, bf16[1,216,128]{2,1,0:T(8,128)(2,1)S(1)}, u32[]{:S(2)}, u32[]{:S(2)}) collective-permute-start(bf16[1,216,128]{2,1,0:T(8,128)(2,1)S(1)} %get-tuple-element.225), channel_id=1, source_target_pairs={{0,4},{1,5},{2,6},{3,7},{4,0},{5,1},{6,2},{7,3},{8,12},{9,13},{10,... | collective-permute-start | bytes 165896 | tf_op jit(solution)/shard_map/ppermute | solution.py:47
  191.8 4.3 %copy-start.5 = (f32[82944]{0:T(1024)S(1)}, f32[82944]{0:T(1024)}, u32[]{:S(2)}) copy-start(f32[82944]{0:T(1024)} %param.20) | copy-start | bytes 995332
  191.9 4.3 %copy-start.14 = (f32[82944]{0:T(1024)S(1)}, f32[82944]{0:T(1024)}, u32[]{:S(2)}) copy-start(f32[82944]{0:T(1024)} %param.24) | copy-start | bytes 995332
  191.9 4.3 %copy-start.15 = (f32[82944]{0:T(1024)S(1)}, f32[82944]{0:T(1024)}, u32[]{:S(2)}) copy-start(f32[82944]{0:T(1024)} %param.25) | copy-start | bytes 995332
  193.2 5.1 %collective-permute-start.33 = (f32[2,576]{1,0:T(2,128)S(1)}, f32[2,576]{1,0:T(2,128)S(1)}, u32[]{:S(2)}, u32[]{:S(2)}) collective-permute-start(f32[2,576]{1,0:T(2,128)S(1)} %add.290), channel_id=1, source_target_pairs={{0,4},{1,5},{2,6},{3,7},{4,0},{5,1},{6,2},{7,3},{8,12},{9,13},{10,... | collective-permute-start | bytes 13832 | tf_op jit(solution)/shard_map/ppermute | solution.py:47
  197.3 1.0 copy-start.21
  197.3 1.0 copy-start.22
  197.3 1.0 copy-start.23
  197.3 1.6 copy-start.11
  197.3 1.6 copy-start.18
  197.3 1.6 copy-start.19
Sparse Core Ops, SparseCore 0:
  11.4 74.0 all-gather.1
